TPU v7x, 32 devices: a whole 2x2x4 slice. The times are simulated.
32 devices in a mesh: seq: 4 (over y, core), blk: 8 (over z, x).
Axes of the slice: x: 2, y: 2, z: 4, core: 2. Of those that a mesh axis runs over, the one named last changes fastest.
Arguments:
- inputs: bfloat16 [2, 3072, 2048], P(None, ('seq', 'blk')), may hold values from -6 to 6
- seg_ids: int32 [2, 3072], P(None, 'seq'), may hold values from 0 to 1, as said below
- norm_in: bfloat16 [2048], P(('seq', 'blk')), may hold values from 0.099609375 to 1.8984375
- proj_y: bfloat16 [2048, 2560], P(('seq', 'blk')), may hold values from -0.125 to 0.125
- proj_x: bfloat16 [2048, 2560], P(('seq', 'blk')), may hold values from -0.125 to 0.125
- conv_weight: float32 [4, 2560], P(None, 'blk'), may hold values from -3 to 3
- conv_bias: float32 [2560], P('blk'), may hold values from -2 to 2
- rate_weight: bfloat16 [16, 160, 160], P('blk'), may hold values from -0.5 to 0.5
- rate_bias: float32 [2560], P('blk'), may hold values from -4 to 4
- input_weight: bfloat16 [16, 160, 160], P('blk'), may hold values from -0.5 to 0.5
- input_bias: float32 [2560], P('blk'), may hold values from -4 to 4
- decay_param: float32 [2560], P('blk'), may hold values from 3 to 12
- proj_out: bfloat16 [2048, 2560], P(('seq', 'blk')), may hold values from -0.5 to 0.5
- norm_mlp: bfloat16 [2048], P(('seq', 'blk')), may hold values from 0.099609375 to 1.8984375
- mlp_gate: bfloat16 [2048, 6144], P(('seq', 'blk')), may hold values from -0.125 to 0.125
- mlp_up: bfloat16 [2048, 6144], P(('seq', 'blk')), may hold values from -0.125 to 0.125
- mlp_down: bfloat16 [2048, 6144], P(('seq', 'blk')), may hold values from -0.15625 to 0.15625
- cotangent: bfloat16 [2, 3072, 2048], P(None, ('seq', 'blk')), may hold values from -6 to 6
Outputs:
- output: bfloat16 [2, 3072, 2048], P(None, ('seq', 'blk'))
- grad_inputs: bfloat16 [2, 3072, 2048], P(None, ('seq', 'blk'))
- grad_norm_in: float32 [2048], P(('seq', 'blk'))
- grad_proj_y: float32 [2048, 2560], P(('seq', 'blk'))
- grad_proj_x: float32 [2048, 2560], P(('seq', 'blk'))
- grad_conv_weight: float32 [4, 2560], P(None, 'blk')
- grad_conv_bias: float32 [2560], P('blk')
- grad_rate_weight: float32 [16, 160, 160], P('blk')
- grad_rate_bias: float32 [2560], P('blk')
- grad_input_weight: float32 [16, 160, 160], P('blk')
- grad_input_bias: float32 [2560], P('blk')
- grad_decay_param: float32 [2560], P('blk')
- grad_proj_out: float32 [2048, 2560], P(('seq', 'blk'))
- grad_norm_mlp: float32 [2048], P(('seq', 'blk'))
- grad_mlp_gate: float32 [2048, 6144], P(('seq', 'blk'))
- grad_mlp_up: float32 [2048, 6144], P(('seq', 'blk'))
- grad_mlp_down: float32 [2048, 6144], P(('seq', 'blk'))
Inputs may be any that keep to these rules, and one draw needn't show every extreme that they name: `seg_ids`: for each micro-batch and sequence group, ids are 0 before a cut and 1 from it on, the cut lying after the group's first token; each group holds two sequences.
All inputs are finite; a program needn't handle non-finite values.
Results may differ from a plain program's by a relative error of at most 0.014.
Values may be sent and summed in bfloat16 or wider, within the bound.
No kernel may reach another device: no remote copies, remote signals or barrier semaphores. Data moves between devices by JAX's collectives and lax.ppermute only.
A program may use at most 576 MiB of HBM per device.

v0:
```python
import jax
import jax.numpy as jnp
from jax import lax
from jax.sharding import PartitionSpec as P

NORM_EPS = 1e-06


def recurrence(
    values,
    segments,
    conv_weight,
    conv_bias,
    rate_weight,
    rate_bias,
    input_weight,
    input_bias,
    decay_param,
):
    taps = conv_weight.shape[0]
    length = values.shape[1]
    filtered = conv_bias + values * conv_weight[0]
    for offset in range(1, taps):
        shifted = jnp.pad(values, ((0, 0), (offset, 0), (0, 0)))[:, :length]
        same_doc = (
            jnp.pad(segments, ((0, 0), (offset, 0)), constant_values=-1)[:, :length] == segments
        )
        filtered = filtered + jnp.where(same_doc[..., None], shifted, 0.0) * conv_weight[offset]
    blocks = rate_weight.shape[0]
    block_width = rate_weight.shape[1]
    grouped = filtered.reshape(filtered.shape[0], length, blocks, block_width)
    pre_rate = (
        jnp.einsum("blhi,hij->blhj", grouped, rate_weight, precision=lax.Precision.HIGHEST).reshape(
            filtered.shape
        )
        + rate_bias
    )
    pre_input = (
        jnp.einsum(
            "blhi,hij->blhj", grouped, input_weight, precision=lax.Precision.HIGHEST
        ).reshape(filtered.shape)
        + input_bias
    )
    rate_gate = jax.nn.sigmoid(pre_rate)
    input_gate = jax.nn.sigmoid(pre_input)
    log_decay = -8.0 * rate_gate * jax.nn.softplus(-decay_param)
    previous = jnp.pad(segments, ((0, 0), (1, 0)), constant_values=-1)[:, :length]
    seg_start = previous != segments
    decay_now = jnp.where(seg_start[..., None], 0.0, jnp.exp(log_decay))
    input_scale = jnp.sqrt(-jnp.expm1(2.0 * log_decay))
    driven = input_scale * input_gate * filtered

    def combine(earlier, later):
        return (earlier[0] * later[0], later[0] * earlier[1] + later[1])

    scanned = lax.associative_scan(combine, (decay_now, driven), axis=1)
    return scanned[1]


def norm_back(grad_in, rows_in, scale_vec, gain_vec):
    weighted = grad_in * gain_vec
    return scale_vec * weighted - rows_in * scale_vec**3 * jnp.mean(
        weighted * rows_in, axis=-1, keepdims=True
    )


def local_set(
    conv_weight, conv_bias, rate_weight, rate_bias, input_weight, input_bias, decay_param
):
    return (
        conv_weight,
        conv_bias,
        rate_weight.astype(jnp.float32),
        rate_bias,
        input_weight.astype(jnp.float32),
        input_bias,
        decay_param,
    )


def run_pass(
    inputs,
    seg_ids,
    cotangent,
    norm_in,
    proj_y,
    proj_x,
    local_params,
    proj_out,
    norm_mlp,
    mlp_gate,
    mlp_up,
    mlp_down,
):
    batch_count, tok_rows, model_width = inputs.shape
    rows_all = batch_count * tok_rows
    source = inputs.astype(jnp.float32).reshape(rows_all, model_width)
    mix_y, mix_x, mix_out, gain_in = (
        lax.all_gather(proj_y, ("seq", "blk"), axis=0, tiled=True),
        lax.all_gather(proj_x, ("seq", "blk"), axis=0, tiled=True),
        lax.all_gather(proj_out, ("seq", "blk"), axis=0, tiled=True),
        lax.all_gather(norm_in, ("seq", "blk"), axis=0, tiled=True),
    )
    scale_in = lax.rsqrt(jnp.mean(source * source, axis=-1, keepdims=True) + NORM_EPS)
    normed = (source * scale_in * gain_in.astype(jnp.float32)).astype(jnp.bfloat16)
    pre_y = jnp.dot(normed, mix_y, preferred_element_type=jnp.float32)
    branch_y, gelu_y_back = jax.vjp(jax.nn.gelu, pre_y)
    drive_in = (
        jnp.dot(normed, mix_x, preferred_element_type=jnp.float32)
        .astype(jnp.bfloat16)
        .reshape(batch_count, tok_rows, -1)
    )
    channels = lax.all_to_all(drive_in, "blk", split_axis=2, concat_axis=1, tiled=True)

    def scan_part(values, *params):
        return recurrence(values, seg_ids, *params)

    scan_state, scan_back = jax.vjp(scan_part, channels.astype(jnp.float32), *local_params)
    state_tokens = lax.all_to_all(
        scan_state.astype(jnp.bfloat16), "blk", split_axis=1, concat_axis=2, tiled=True
    ).reshape(rows_all, -1)
    hidden_f = state_tokens.astype(jnp.float32)
    mixed_in = (branch_y * hidden_f).astype(jnp.bfloat16)
    resid = source + jnp.einsum("rc,dc->rd", mixed_in, mix_out, preferred_element_type=jnp.float32)
    ff_gate, ff_up, ff_down, gain_mlp = (
        lax.all_gather(mlp_gate, ("seq", "blk"), axis=0, tiled=True),
        lax.all_gather(mlp_up, ("seq", "blk"), axis=0, tiled=True),
        lax.all_gather(mlp_down, ("seq", "blk"), axis=0, tiled=True),
        lax.all_gather(norm_mlp, ("seq", "blk"), axis=0, tiled=True),
    )
    scale_mlp = lax.rsqrt(jnp.mean(resid * resid, axis=-1, keepdims=True) + NORM_EPS)
    normed_mlp = (resid * scale_mlp * gain_mlp.astype(jnp.float32)).astype(jnp.bfloat16)
    pre_gate = jnp.dot(normed_mlp, ff_gate, preferred_element_type=jnp.float32)
    pre_up = jnp.dot(normed_mlp, ff_up, preferred_element_type=jnp.float32)
    activated, gelu_gate_back = jax.vjp(jax.nn.gelu, pre_gate)
    product = (activated * pre_up).astype(jnp.bfloat16)
    block_out = (
        resid + jnp.einsum("rf,df->rd", product, ff_down, preferred_element_type=jnp.float32)
    ).astype(jnp.bfloat16)
    grad_out = cotangent.astype(jnp.float32).reshape(rows_all, model_width)
    grad_low = cotangent.reshape(rows_all, model_width)
    back_gate, back_up, back_down, back_gain = (
        lax.all_gather(mlp_gate, ("seq", "blk"), axis=0, tiled=True),
        lax.all_gather(mlp_up, ("seq", "blk"), axis=0, tiled=True),
        lax.all_gather(mlp_down, ("seq", "blk"), axis=0, tiled=True),
        lax.all_gather(norm_mlp, ("seq", "blk"), axis=0, tiled=True),
    )
    grad_prod = jnp.einsum("rd,df->rf", grad_low, back_down, preferred_element_type=jnp.float32)
    grad_gate = gelu_gate_back(grad_prod * pre_up)[0].astype(jnp.bfloat16)
    grad_up = (grad_prod * activated).astype(jnp.bfloat16)
    grad_norm_mlp = jnp.einsum(
        "rf,df->rd", grad_gate, back_gate, preferred_element_type=jnp.float32
    ) + jnp.einsum("rf,df->rd", grad_up, back_up, preferred_element_type=jnp.float32)
    term_gate = jnp.einsum("rd,rf->df", normed_mlp, grad_gate, preferred_element_type=jnp.float32)
    term_up = jnp.einsum("rd,rf->df", normed_mlp, grad_up, preferred_element_type=jnp.float32)
    term_down = jnp.einsum("rd,rf->df", grad_low, product, preferred_element_type=jnp.float32)
    term_gain_mlp = jnp.sum(grad_norm_mlp * resid * scale_mlp, axis=0)
    mlp_sums = (
        lax.psum_scatter(term_gate, ("seq", "blk"), scatter_dimension=0, tiled=True),
        lax.psum_scatter(term_up, ("seq", "blk"), scatter_dimension=0, tiled=True),
        lax.psum_scatter(term_down, ("seq", "blk"), scatter_dimension=0, tiled=True),
        lax.psum_scatter(term_gain_mlp, ("seq", "blk"), scatter_dimension=0, tiled=True),
    )
    grad_resid = grad_out + norm_back(
        grad_norm_mlp, resid, scale_mlp, back_gain.astype(jnp.float32)
    )
    grad_branch = grad_resid.astype(jnp.bfloat16)
    back_y, back_x, back_out, back_gain_in = (
        lax.all_gather(proj_y, ("seq", "blk"), axis=0, tiled=True),
        lax.all_gather(proj_x, ("seq", "blk"), axis=0, tiled=True),
        lax.all_gather(proj_out, ("seq", "blk"), axis=0, tiled=True),
        lax.all_gather(norm_in, ("seq", "blk"), axis=0, tiled=True),
    )
    grad_mixed = jnp.einsum("rd,dc->rc", grad_branch, back_out, preferred_element_type=jnp.float32)
    term_out = jnp.einsum("rd,rc->dc", grad_branch, mixed_in, preferred_element_type=jnp.float32)
    grad_y = grad_mixed * hidden_f
    grad_state = (grad_mixed * branch_y).astype(jnp.bfloat16).reshape(batch_count, tok_rows, -1)
    grad_channels = lax.all_to_all(grad_state, "blk", split_axis=2, concat_axis=1, tiled=True)
    scan_grads = scan_back(grad_channels.astype(jnp.float32))
    grad_drive = lax.all_to_all(
        scan_grads[0].astype(jnp.bfloat16), "blk", split_axis=1, concat_axis=2, tiled=True
    ).reshape(rows_all, -1)
    grad_pre_y = gelu_y_back(grad_y)[0].astype(jnp.bfloat16)
    grad_normed = jnp.einsum(
        "rc,dc->rd", grad_pre_y, back_y, preferred_element_type=jnp.float32
    ) + jnp.einsum("rc,dc->rd", grad_drive, back_x, preferred_element_type=jnp.float32)
    term_y = jnp.einsum("rd,rc->dc", normed, grad_pre_y, preferred_element_type=jnp.float32)
    term_x = jnp.einsum("rd,rc->dc", normed, grad_drive, preferred_element_type=jnp.float32)
    term_gain_in = jnp.sum(grad_normed * source * scale_in, axis=0)
    mixer_sums = (
        lax.psum_scatter(term_y, ("seq", "blk"), scatter_dimension=0, tiled=True),
        lax.psum_scatter(term_x, ("seq", "blk"), scatter_dimension=0, tiled=True),
        lax.psum_scatter(term_out, ("seq", "blk"), scatter_dimension=0, tiled=True),
        lax.psum_scatter(term_gain_in, ("seq", "blk"), scatter_dimension=0, tiled=True),
    )
    grad_source = grad_resid + norm_back(
        grad_normed, source, scale_in, back_gain_in.astype(jnp.float32)
    )
    grad_source = grad_source.astype(jnp.bfloat16).reshape(batch_count, tok_rows, model_width)
    return (
        block_out.reshape(batch_count, tok_rows, model_width),
        grad_source,
        mixer_sums,
        mlp_sums,
        tuple(scan_grads[1:]),
    )


def on_device(
    inputs,
    seg_ids,
    norm_in,
    proj_y,
    proj_x,
    conv_weight,
    conv_bias,
    rate_weight,
    rate_bias,
    input_weight,
    input_bias,
    decay_param,
    proj_out,
    norm_mlp,
    mlp_gate,
    mlp_up,
    mlp_down,
    cotangent,
):
    local_params = local_set(
        conv_weight, conv_bias, rate_weight, rate_bias, input_weight, input_bias, decay_param
    )
    small_total = None
    mixer_total = None
    mlp_total = None
    results = run_pass(
        inputs,
        seg_ids,
        cotangent,
        norm_in,
        proj_y,
        proj_x,
        local_params,
        proj_out,
        norm_mlp,
        mlp_gate,
        mlp_up,
        mlp_down,
    )
    outputs = results[0]
    grad_rows = results[1]
    mixer_total = results[2]
    mlp_total = results[3]
    small_total = results[4]
    grad_y_w, grad_x_w, grad_out_w, grad_gain_in = (
        mixer_total[0],
        mixer_total[1],
        mixer_total[2],
        mixer_total[3],
    )
    grad_gate_w, grad_up_w, grad_down_w, grad_gain_mlp = (
        mlp_total[0],
        mlp_total[1],
        mlp_total[2],
        mlp_total[3],
    )
    summed = (
        lax.psum(small_total[0].astype(jnp.bfloat16), "seq").astype(jnp.float32),
        lax.psum(small_total[1].astype(jnp.bfloat16), "seq").astype(jnp.float32),
        lax.psum(small_total[2].astype(jnp.bfloat16), "seq").astype(jnp.float32),
        lax.psum(small_total[3].astype(jnp.bfloat16), "seq").astype(jnp.float32),
        lax.psum(small_total[4].astype(jnp.bfloat16), "seq").astype(jnp.float32),
        lax.psum(small_total[5].astype(jnp.bfloat16), "seq").astype(jnp.float32),
        lax.psum(small_total[6].astype(jnp.bfloat16), "seq").astype(jnp.float32),
    )
    return (
        outputs,
        grad_rows,
        grad_gain_in,
        grad_y_w,
        grad_x_w,
        summed[0],
        summed[1],
        summed[2],
        summed[3],
        summed[4],
        summed[5],
        summed[6],
        grad_out_w,
        grad_gain_mlp,
        grad_gate_w,
        grad_up_w,
        grad_down_w,
    )


def solution(mesh):
    placed = (
        P(None, ("seq", "blk"), None),
        P(None, "seq"),
        P(("seq", "blk")),
        P(("seq", "blk"), None),
        P(("seq", "blk"), None),
        P(None, "blk"),
        P("blk"),
        P("blk", None, None),
        P("blk"),
        P("blk", None, None),
        P("blk"),
        P("blk"),
        P(("seq", "blk"), None),
        P(("seq", "blk")),
        P(("seq", "blk"), None),
        P(("seq", "blk"), None),
        P(("seq", "blk"), None),
        P(None, ("seq", "blk"), None),
    )
    return jax.shard_map(
        on_device,
        mesh=mesh,
        in_specs=placed,
        out_specs=(
            P(None, ("seq", "blk"), None),
            P(None, ("seq", "blk"), None),
            P(("seq", "blk")),
            P(("seq", "blk"), None),
            P(("seq", "blk"), None),
            P(None, "blk"),
            P("blk"),
            P("blk", None, None),
            P("blk"),
            P("blk", None, None),
            P("blk"),
            P("blk"),
            P(("seq", "blk"), None),
            P(("seq", "blk")),
            P(("seq", "blk"), None),
            P(("seq", "blk"), None),
            P(("seq", "blk"), None),
        ),
        check_vma=False,
    )
```

profile of v0, /device:TPU:0, one launch (start us, length us, event | category | flops | bytes accessed | tf_op | source)
XLA Modules:
  0.0 3736.7 jit_solution(1673145084533346647)
XLA Ops:
  11.7 42.9 %all-reduce.106 = (bf16[2048]{0:T(1024)(128)(2,1)S(1)}, bf16[2048]{0:T(1024)(128)(2,1)}) all-reduce(bf16[2048]{0:T(1024)(128)(2,1)S(1)} %dynamic-update-slice, bf16[2048]{0:T(1024)(128)(2,1)S(1)} %dynamic-update-slice.1), channel_id=1, replica_groups=mesh['seq'=4,'blk'=8] {'seq','blk'}, use_global_device_ids=true, to_apply=%add.101 | all-reduce | flops 4096 | bytes 16384
  56.1 45.1 %all-gather.9.cloned.1.call-done = bf16[2048,2560]{1,0:T(8,128)(2,1)} async-done(((bf16[64,2560]{1,0:T(8,128)(2,1)}), bf16[2048,2560]{1,0:T(8,128)(2,1)}) %all-gather.9.cloned.1.call-update) | async-done | bytes 10485776 | tf_op jit(solution)/shard_map/all_gather | solution.py:100
  101.1 6.2 convolution_convert_fusion
  109.6 4.1 all-to-all-start
  113.9 50.2 %all-to-all-done = bf16[2,96,2560]{1,0,2:T(2,128)(2,1)S(1)} async-done(((bf16[2,96,2560]{1,0,2:T(2,128)(2,1)}), bf16[2,96,2560]{1,0,2:T(2,128)(2,1)S(1)}, u32[]{:S(2)}, u32[]{:S(2)}) %all-to-all-start) | async-done | bytes 983072 | tf_op jit(solution)/shard_map/all_to_all | solution.py:113
  189.9 7.8 exponential_select_fusion
  197.7 6.7 slice.328
  204.4 3.7 slice.329
  208.0 5.3 slice.327
  213.4 6.9 slice.331
  226.8 4.4 slice.335
  282.4 4.4 slice.332
  286.8 4.3 slice.391
  292.4 6.6 slice.326
  299.0 3.7 slice.393
  316.1 5.5 pad.421
  324.6 6.1 pad.420
  335.5 4.3 all-to-all-start.1
  339.9 51.4 %all-to-all-done.1 = bf16[2,768,320]{2,0,1:T(2,128)(2,1)} async-done(((bf16[2,768,320]{2,0,1:T(2,128)(2,1)}), bf16[2,768,320]{2,0,1:T(2,128)(2,1)}, u32[]{:S(2)}, u32[]{:S(2)}) %all-to-all-start.1) | async-done | bytes 983072 | tf_op jit(solution)/shard_map/all_to_all | solution.py:119
  399.4 9.0 multiply_convert_fusion.3
  408.4 8.0 multiply_reduce_fusion.9
  417.8 53.6 %all-gather.13.cloned.1.call-done = bf16[2048,6144]{1,0:T(8,128)(2,1)} async-done(((bf16[64,6144]{1,0:T(8,128)(2,1)}), bf16[2048,6144]{1,0:T(8,128)(2,1)}) %all-gather.13.cloned.1.call-update) | async-done | bytes 25165840 | tf_op jit(solution)/shard_map/all_gather | solution.py:126
  471.4 13.0 fusion.117
  484.4 142.7 %all-gather.15.cloned.1.call-done = bf16[2048,6144]{1,0:T(8,128)(2,1)} async-done(((bf16[64,6144]{1,0:T(8,128)(2,1)}), bf16[2048,6144]{1,0:T(8,128)(2,1)}) %all-gather.15.cloned.1.call-update) | async-done | bytes 25165840 | tf_op jit(solution)/shard_map/all_gather | solution.py:127
  627.1 13.0 fusion.118
  640.2 142.7 %all-gather.17.cloned.1.call-done = bf16[2048,6144]{1,0:T(8,128)(2,1)} async-done(((bf16[64,6144]{1,0:T(8,128)(2,1)}), bf16[2048,6144]{1,0:T(8,128)(2,1)}) %all-gather.17.cloned.1.call-update) | async-done | bytes 25165840 | tf_op jit(solution)/shard_map/all_gather | solution.py:128
  782.9 17.3 multiply_convert_fusion
  800.2 14.7 fusion.119
  814.9 16.3 multiply_reduce_fusion.5
  834.3 8.2 multiply_convert_fusion.2
  844.7 36.7 all_to_all.42
  890.4 6.5 slice.394
  900.6 5.3 slice.395
  907.3 4.2 slice.396
  962.5 5.5 pad.481
  968.1 4.5 multiply_add_fusion.3
  972.5 5.5 pad.507
  981.7 3.7 pad.482
  985.3 4.0 pad.424
  989.5 5.7 pad.483
  995.3 10.1 multiply_reduce_fusion
  1006.1 6.6 fusion.82
  1015.8 4.7 fusion.41
  1023.5 4.8 fusion.42
  1028.4 10.2 fusion.43
  1039.7 9.9 fusion.121
  1058.1 7.1 fusion.81
  1074.1 37.3 all-to-all-done.3
  1115.0 8.9 fusion.122
  1125.1 21.7 fusion.123
  1146.8 21.3 fusion.124
  1169.8 20.8 convolution_bitcast_fusion
  1190.6 49.1 %copy.142 = f32[2048,6144]{1,0:T(8,128)} copy(f32[2048,6144]{0,1:T(8,128)} %convolution_bitcast_fusion) | data formatting | bytes 100663296
  1240.4 9.1 fusion.120
  1249.6 14.8 fusion.7
  1264.5 6.5 all-reduce.107
  1277.2 9.3 multiply_reduce_fusion.6
  1286.5 53.8 %all-reduce.105 = (f32[2048]{0:T(1024)S(1)}, f32[2048]{0:T(1024)S(1)}) all-reduce(f32[2048]{0:T(1024)S(1)} %get-tuple-element.112, f32[2048]{0:T(1024)S(1)} %copy-done.167), channel_id=2, replica_groups=mesh['seq'=4,'blk'=8] {'seq','blk'}, use_global_device_ids=true, to_apply=%region_5.6.clone | all-reduce | flops 4096 | bytes 32768
  1344.3 177.1 %reduce-scatter.13.cloned.1.call-done = f32[64,2560]{1,0:T(8,128)} async-done(((f32[2048,2560]{1,0:T(8,128)}), f32[64,2560]{1,0:T(8,128)}) %reduce-scatter.13.cloned.1.call-update) | async-done | bytes 655376 | tf_op jit(solution)/shard_map/reduce_scatter | solution.py:193
  1521.4 447.8 %reduce-scatter.9.cloned.1.call-done = f32[64,2560]{1,0:T(8,128)} async-done(((f32[2048,2560]{1,0:T(8,128)}), f32[64,2560]{1,0:T(8,128)}) %reduce-scatter.9.cloned.1.call-update) | async-done | bytes 655376 | tf_op jit(solution)/shard_map/reduce_scatter | solution.py:191
  1969.2 447.2 %reduce-scatter.11.cloned.1.call-done = f32[64,2560]{1,0:T(8,128)} async-done(((f32[2048,2560]{1,0:T(8,128)}), f32[64,2560]{1,0:T(8,128)}) %reduce-scatter.11.cloned.1.call-update) | async-done | bytes 655376 | tf_op jit(solution)/shard_map/reduce_scatter | solution.py:192
  2416.5 438.5 %reduce-scatter.15.cloned.1.call-done = f32[64,6144]{1,0:T(8,128)} async-done(((f32[2048,6144]{1,0:T(8,128)}), f32[64,6144]{1,0:T(8,128)}) %reduce-scatter.15.cloned.1.call-update) | async-done | bytes 1572880 | tf_op jit(solution)/shard_map/reduce_scatter | solution.py:159
  2855.0 437.4 %reduce-scatter.17.cloned.1.call-done = f32[64,6144]{1,0:T(8,128)} async-done(((f32[2048,6144]{1,0:T(8,128)}), f32[64,6144]{1,0:T(8,128)}) %reduce-scatter.17.cloned.1.call-update) | async-done | bytes 1572880 | tf_op jit(solution)/shard_map/reduce_scatter | solution.py:160
  3292.4 437.6 %reduce-scatter.19.cloned.1.call-done = f32[64,6144]{1,0:T(8,128)} async-done(((f32[2048,6144]{1,0:T(8,128)}), f32[64,6144]{1,0:T(8,128)}) %reduce-scatter.19.cloned.1.call-update) | async-done | bytes 1572880
  (656 shorter events, 238.3 us)
Async XLA Ops:
  7.2 168.2 %copy-start = (bf16[2,160,160]{2,1,0:T(8,128)(2,1)S(1)}, bf16[2,160,160]{2,1,0:T(8,128)(2,1)}, u32[]{:S(2)}) copy-start(bf16[2,160,160]{2,1,0:T(8,128)(2,1)} %param.25) | copy-start | bytes 307204
  7.2 47.4 %copy-start.6 = (bf16[2,96,2048]{2,1,0:T(8,128)(2,1)S(1)}, bf16[2,96,2048]{2,1,0:T(8,128)(2,1)}, u32[]{:S(2)}) copy-start(bf16[2,96,2048]{2,1,0:T(8,128)(2,1)} %param.18) | copy-start | bytes 2359300
  7.2 93.9 %all-gather.9.cloned.1.call-start = ((), (), s32[]{:S(2)}) async-start(), calls=%async_computation.11 | async-start | bytes 10813440 | tf_op jit(solution)/shard_map/all_gather | solution.py:100
  8.0 391.5 %all-gather.7.cloned.1.call-start = ((), (), s32[]{:S(2)}) async-start(), calls=%async_computation.10 | async-start | bytes 10813440 | tf_op jit(solution)/shard_map/all_gather | solution.py:99
  8.7 399.7 %all-gather.11.cloned.1.call-start = ((), (), s32[]{:S(2)}) async-start(), calls=%async_computation.12 | async-start | bytes 10813440 | tf_op jit(solution)/shard_map/all_gather | solution.py:101
  9.5 462.0 %all-gather.13.cloned.1.call-start = ((), (), s32[]{:S(2)}) async-start(), calls=%async_computation.13 | async-start | bytes 25952256 | tf_op jit(solution)/shard_map/all_gather | solution.py:126
  10.0 617.1 %all-gather.15.cloned.1.call-start = ((), (), s32[]{:S(2)}) async-start(), calls=%async_computation.14 | async-start | bytes 25952256 | tf_op jit(solution)/shard_map/all_gather | solution.py:127
  10.6 772.2 %all-gather.17.cloned.1.call-start = ((), (), s32[]{:S(2)}) async-start(), calls=%async_computation.15 | async-start | bytes 25952256 | tf_op jit(solution)/shard_map/all_gather | solution.py:128
  56.1 51.3 %copy-start.46 = (bf16[192,2048]{1,0:T(8,128)(2,1)}, bf16[192,2048]{1,0:T(8,128)(2,1)S(1)}, u32[]{:S(2)}) copy-start(bf16[192,2048]{1,0:T(8,128)(2,1)S(1)} %multiply_convert_fusion.6) | copy-start | bytes 2359300
  109.6 54.6 %all-to-all-start = ((bf16[2,96,2560]{1,0,2:T(2,128)(2,1)}), bf16[2,96,2560]{1,0,2:T(2,128)(2,1)S(1)}, u32[]{:S(2)}, u32[]{:S(2)}) async-start(bf16[2,96,2560]{1,0,2:T(2,128)(2,1)} %copy.107), calls=%async_computation | async-start | bytes 2621440 | tf_op jit(solution)/shard_map/all_to_all | solution.py:113
  113.7 76.1 %copy-start.127 = (f32[320]{0:T(512)}, f32[320]{0:T(512)S(1)}, u32[]{:S(2)}) copy-start(f32[320]{0:T(512)S(1)} %get-tuple-element.114) | copy-start | bytes 3844
  113.7 76.1 %copy-start.129 = (f32[320]{0:T(512)}, f32[320]{0:T(512)S(1)}, u32[]{:S(2)}) copy-start(f32[320]{0:T(512)S(1)} %get-tuple-element.115) | copy-start | bytes 3844
  113.7 76.1 %copy-start.131 = (f32[320]{0:T(512)}, f32[320]{0:T(512)S(1)}, u32[]{:S(2)}) copy-start(f32[320]{0:T(512)S(1)} %get-tuple-element.116) | copy-start | bytes 3844
  113.7 76.1 %copy-start.133 = (f32[320]{0:T(512)}, f32[320]{0:T(512)S(1)}, u32[]{:S(2)}) copy-start(f32[320]{0:T(512)S(1)} %get-tuple-element.117) | copy-start | bytes 3844
  113.8 76.0 %copy-start.137 = (f32[320]{0:T(512)}, f32[320]{0:T(512)S(1)}, u32[]{:S(2)}) copy-start(f32[320]{0:T(512)S(1)} %broadcast_multiply_fusion) | copy-start | bytes 3844
  113.9 75.9 %copy-start.111 = (pred[2,768]{1,0:T(4,128)(4,1)}, pred[2,768]{1,0:T(4,128)(4,1)S(1)}, u32[]{:S(2)}) copy-start(pred[2,768]{1,0:T(4,128)(4,1)S(1)} %get-tuple-element.246) | copy-start | bytes 4612
  113.9 75.9 %copy-start.113 = (pred[2,768]{1,0:T(4,128)(4,1)}, pred[2,768]{1,0:T(4,128)(4,1)S(1)}, u32[]{:S(2)}) copy-start(pred[2,768]{1,0:T(4,128)(4,1)S(1)} %get-tuple-element.247) | copy-start | bytes 4612
  113.9 75.9 %copy-start.115 = (pred[2,768]{1,0:T(4,128)(4,1)}, pred[2,768]{1,0:T(4,128)(4,1)S(1)}, u32[]{:S(2)}) copy-start(pred[2,768]{1,0:T(4,128)(4,1)S(1)} %get-tuple-element.248) | copy-start | bytes 4612
  113.9 75.9 %copy-start.149 = (pred[2,768]{1,0:T(4,128)(4,1)}, pred[2,768]{1,0:T(4,128)(4,1)S(1)}, u32[]{:S(2)}) copy-start(pred[2,768]{1,0:T(4,128)(4,1)S(1)} %get-tuple-element.245) | copy-start | bytes 4612
  169.1 20.8 copy-start.2
  208.0 12.2 copy-start.17
  237.0 13.8 copy-start.53
  238.9 39.8 %copy-start.68 = (f32[2,48,320]{2,1,0:T(8,128)}, f32[2,48,320]{2,1,0:T(8,128)S(1)}, u32[]{:S(2)}) copy-start(f32[2,48,320]{2,1,0:T(8,128)S(1)} %slice.346) | copy-start | bytes 368644
  240.7 40.2 %copy-start.58 = (f32[2,48,320]{2,1,0:T(8,128)}, f32[2,48,320]{2,1,0:T(8,128)S(1)}, u32[]{:S(2)}) copy-start(f32[2,48,320]{2,1,0:T(8,128)S(1)} %slice.345) | copy-start | bytes 368644
  241.8 39.1 %copy-start.70 = (f32[2,48,320]{2,1,0:T(8,128)}, f32[2,48,320]{2,1,0:T(8,128)S(1)}, u32[]{:S(2)}) copy-start(f32[2,48,320]{2,1,0:T(8,128)S(1)} %slice.349) | copy-start | bytes 368644
  243.5 35.2 copy-start.66
  246.6 31.3 copy-start.67
  247.6 39.1 %copy-start.74 = (f32[2,24,320]{2,1,0:T(8,128)}, f32[2,24,320]{2,1,0:T(8,128)S(1)}, u32[]{:S(2)}) copy-start(f32[2,24,320]{2,1,0:T(8,128)S(1)} %slice.351) | copy-start | bytes 184324
  251.7 30.0 copy-start.92
  254.2 27.6 copy-start.82
  255.1 26.6 copy-start.94
  255.9 25.8 copy-start.103
  256.6 25.2 copy-start.97
  256.6 34.4 copy-start.105
  282.3 16.6 copy-start.14
  292.3 11.0 copy-start.121
  292.3 11.0 copy-start.140
  292.3 11.1 copy-start.135
  292.4 11.1 copy-start.153
  292.4 11.2 copy-start.157
  335.5 55.8 %all-to-all-start.1 = ((bf16[2,768,320]{2,0,1:T(2,128)(2,1)}), bf16[2,768,320]{2,0,1:T(2,128)(2,1)}, u32[]{:S(2)}, u32[]{:S(2)}) async-start(bf16[2,768,320]{2,0,1:T(2,128)(2,1)} %copy.119), calls=%async_computation.1 | async-start | bytes 2359296 | tf_op jit(solution)/shard_map/all_to_all | solution.py:119
  339.8 934.1 %all-reduce.111.cloned.1.call-start = ((), (), s32[]{:S(2)}) async-start(), calls=%async_computation.22 | async-start | bytes 655360 | tf_op jit(solution)/shard_map/psum | solution.py:269
  417.8 209.3 %copy-start.25 = (bf16[192,2048]{1,0:T(8,128)(2,1)}, bf16[192,2048]{1,0:T(8,128)(2,1)S(1)}, u32[]{:S(2)}) copy-start(bf16[192,2048]{1,0:T(8,128)(2,1)S(1)} %multiply_convert_fusion.5) | copy-start | bytes 2359300
  814.9 16.3 copy-start.50
  1028.3 493.1 %reduce-scatter.13.cloned.1.call-start = ((), (), s32[]{:S(2)}) async-start(), calls=%async_computation.18 | async-start | bytes 21626880 | tf_op jit(solution)/shard_map/reduce_scatter | solution.py:193
  1038.6 930.7 %reduce-scatter.9.cloned.1.call-start = ((), (), s32[]{:S(2)}) async-start(), calls=%async_computation.16 | async-start | bytes 21626880 | tf_op jit(solution)/shard_map/reduce_scatter | solution.py:191
  1069.3 42.1 %all-to-all-start.3 = ((bf16[2,768,320]{2,0,1:T(2,128)(2,1)}), bf16[2,768,320]{2,0,1:T(2,128)(2,1)S(1)}, u32[]{:S(2)}, u32[]{:S(2)}) async-start(bf16[2,768,320]{2,0,1:T(2,128)(2,1)} %copy.131), calls=%async_computation.3 | async-start | bytes 2359296 | tf_op jit(solution)/shard_map/all_to_all | solution.py:180
  1072.9 1343.6 %reduce-scatter.11.cloned.1.call-start = ((), (), s32[]{:S(2)}) async-start(), calls=%async_computation.17 | async-start | bytes 21626880 | tf_op jit(solution)/shard_map/reduce_scatter | solution.py:192
  1074.1 40.9 %copy-start.48 = (bf16[2,96,2048]{2,1,0:T(8,128)(2,1)S(1)}, bf16[2,96,2048]{2,1,0:T(8,128)(2,1)}, u32[]{:S(2)}) copy-start(bf16[2,96,2048]{2,1,0:T(8,128)(2,1)} %multiply_convert_fusion.4) | copy-start | bytes 2359300
  1124.0 1731.0 %reduce-scatter.15.cloned.1.call-start = ((), (), s32[]{:S(2)}) async-start(), calls=%async_computation.19 | async-start | bytes 51904512 | tf_op jit(solution)/shard_map/reduce_scatter | solution.py:159
  1146.8 2145.6 %reduce-scatter.17.cloned.1.call-start = ((), (), s32[]{:S(2)}) async-start(), calls=%async_computation.20 | async-start | bytes 51904512 | tf_op jit(solution)/shard_map/reduce_scatter | solution.py:160
  1168.2 2561.8 %reduce-scatter.19.cloned.1.call-start = ((), (), s32[]{:S(2)}) async-start(), calls=%async_computation.21 | async-start | bytes 51904512
  1249.5 14.9 copy-start.164
  1249.5 14.9 copy-start.163
  1249.5 14.9 copy-start.162
  1249.5 14.9 copy-start.161
  1249.5 14.9 copy-start.170
  1249.5 14.9 copy-start.171
  1249.5 14.9 copy-start.172
  1249.5 14.9 copy-start.174
  1249.5 27.7 copy-start.8
  1249.6 27.7 copy-start.110
  1277.2 64.3 %copy-start.16 = (f32[192,2048]{1,0:T(8,128)S(1)}, f32[192,2048]{1,0:T(8,128)}, u32[]{:S(2)}) copy-start(f32[192,2048]{1,0:T(8,128)} %copy-done.15) | copy-start | bytes 4718596
  1341.5 2388.5 %copy-start.1 = (bf16[2,160,160]{2,1,0:T(8,128)(2,1)S(1)}, bf16[2,160,160]{2,1,0:T(8,128)(2,1)}, u32[]{:S(2)}) copy-start(bf16[2,160,160]{2,1,0:T(8,128)(2,1)} %param.25) | copy-start | bytes 307204
  (130 other events, 530.4 us)
Sparse Core Ops, SparseCore 0:
  11.0 90.1 all-gather.8
  104.0 100.7 all-gather.6
  207.7 85.3 all-gather.10
  295.9 175.4 all-gather.12
  474.2 152.8 all-gather.14
  630.0 152.8 all-gather.16
  1028.4 31.4 all-reduce.110
  1062.9 458.5 reduce-scatter.12
  1524.3 444.8 reduce-scatter.8
  1972.0 444.4 reduce-scatter.10
  2423.5 431.4 reduce-scatter.14
  2861.8 430.4 reduce-scatter.16
  3299.4 430.5 reduce-scatter.18
where the time goes:
time: 3750 us; the launch traced here: 3740 us
  waiting for transfers between devices  2910 us (78%)
  local copies, waits for them, and re-layouts  302 us (8%)
  matrix products  251 us (7%)
  blocking collectives  140 us (4%)
  other arithmetic  102 us (3%)
    reduce_scatter x1, waiting for transfers between devices, run_pass(): lax.psum_scatter(term_y, ('seq', 'blk'), scatter_dimension=0, tiled=True)  448 us
    reduce_scatter x1, waiting for transfers between devices, run_pass(): lax.psum_scatter(term_x, ('seq', 'blk'), scatter_dimension=0, tiled=True)  447 us
    unnamed x14, waiting for transfers between devices  441 us
    reduce_scatter x1, waiting for transfers between devices, run_pass(): lax.psum_scatter(term_gate, ('seq', 'blk'), scatter_dimension=0, tiled=True)  439 us
    reduce_scatter x1, waiting for transfers between devices, run_pass(): lax.psum_scatter(term_up, ('seq', 'blk'), scatter_dimension=0, tiled=True)  437 us
    reduce_scatter x1, waiting for transfers between devices, run_pass(): lax.psum_scatter(term_out, ('seq', 'blk'), scatter_dimension=0, tiled=True)  177 us
    all_gather x1, waiting for transfers between devices, run_pass(): lax.all_gather(mlp_up, ('seq', 'blk'), axis=0, tiled=True)  143 us
    all_gather x1, waiting for transfers between devices, run_pass(): lax.all_gather(mlp_down, ('seq', 'blk'), axis=0, tiled=True)  143 us
  transfers between devices with their start and end apart: 16, of which 13 were waited for; matrix products, arithmetic and copies ran while one was open for 12% of the time, Pallas kernels for 0%

commit v1 on v0

v1 whole, which is shorter than its diff:
```python
import functools

import jax
import jax.numpy as jnp
from jax import lax
from jax.experimental import pallas as pl
from jax.experimental.pallas import tpu as pltpu
from jax.sharding import PartitionSpec as P

NORM_EPS = 1e-06
F32 = jnp.float32
BF16 = jnp.bfloat16
TAPS = 4
HALO = 8


class Grid:
    def __init__(self, n_seq, n_blk):
        core = 2 if n_seq % 2 == 0 else 1
        nx = max(d for d in range(1, n_blk + 1) if d * d <= n_blk and n_blk % d == 0)
        self.n = {"y": n_seq // core, "c": core, "z": n_blk // nx, "x": nx}
        self.n_blk = n_blk

    def index(self, part):
        seq, blk = lax.axis_index("seq"), lax.axis_index("blk")
        return {
            "y": seq // self.n["c"],
            "c": seq % self.n["c"],
            "z": blk // self.n["x"],
            "x": blk % self.n["x"],
        }[part]

    def shift(self, value, part, by, wrap=True):
        outer, inner, axis = {
            "y": ("y", "c", "seq"),
            "c": ("y", "c", "seq"),
            "z": ("z", "x", "blk"),
            "x": ("z", "x", "blk"),
        }[part]
        pairs = []
        for o in range(self.n[outer]):
            for i in range(self.n[inner]):
                p = (o if part == outer else i) + by
                if not wrap and not 0 <= p < self.n[part]:
                    continue
                p = p % self.n[part]
                to = (p, i) if part == outer else (o, p)
                pairs.append((o * self.n[inner] + i, to[0] * self.n[inner] + to[1]))
        return lax.ppermute(value, axis, pairs)

    def gather_abs(self, value, part, ring=False):
        n, me = self.n[part], self.index(part)
        out = jnp.zeros((n, *value.shape), value.dtype)
        held = value
        for r in range(n):
            if r:
                held = self.shift(held, part, 1) if ring else self.shift(value, part, r)
            out = lax.dynamic_update_index_in_dim(out, held, (me - r) % n, 0)
        return out

    def scatter_sum(self, value, part, dim):
        n, me = self.n[part], self.index(part)
        total = lax.dynamic_index_in_dim(value, me, dim, keepdims=False)
        for r in range(1, n):
            piece = lax.dynamic_index_in_dim(value, (me + r) % n, dim, keepdims=False)
            total = total + self.shift(piece, part, r)
        return total

    def total(self, value, part):
        out = value.astype(F32)
        for r in range(1, self.n[part]):
            out = out + self.shift(value, part, r).astype(F32)
        return out.astype(value.dtype)

    def spread(self, shard, first):
        nx, ny = self.n["x"], self.n["y"]
        got = {(0, 0): shard}
        for r in range(1, nx):
            got[0, r] = self.shift(shard, "x", r)
        for r in range(1, ny):
            got[r, 0] = self.shift(shard, "y", r)
        for ry in range(1, ny):
            for rx in range(1, nx):
                if first == "x":
                    got[ry, rx] = self.shift(got[0, rx], "y", ry)
                else:
                    got[ry, rx] = self.shift(got[ry, 0], "x", rx)
        return jnp.concatenate([got[ry, rx] for ry in range(ny) for rx in range(nx)], axis=0)

    def collect(self, partial, first):
        nx, ny = self.n["x"], self.n["y"]
        part = partial.reshape(ny, nx, partial.shape[0] // (ny * nx), partial.shape[1])
        total = part[0, 0].astype(F32)
        if first == "y":
            for rx in range(1, nx):
                held = part[0, rx]
                if ny > 1:
                    held = held.astype(F32)
                    for ry in range(1, ny):
                        held = held + self.shift(part[ry, rx], "y", -ry).astype(F32)
                total = total + self.shift(held.astype(BF16), "x", -rx).astype(F32)
            for ry in range(1, ny):
                total = total + self.shift(part[ry, 0], "y", -ry).astype(F32)
        else:
            for ry in range(1, ny):
                held = part[ry, 0]
                if nx > 1:
                    held = held.astype(F32)
                    for rx in range(1, nx):
                        held = held + self.shift(part[ry, rx], "x", -rx).astype(F32)
                total = total + self.shift(held.astype(BF16), "y", -ry).astype(F32)
            for rx in range(1, nx):
                total = total + self.shift(part[0, rx], "x", -rx).astype(F32)
        return total

    def columns_of(self, pieces):
        nx, ny, nz, nc = self.n["x"], self.n["y"], self.n["z"], self.n["c"]
        x, y, z, c = (self.index(p) for p in "xyzc")
        rows = pieces[0].shape[0]

        def take(yy, xx):
            out = []
            for w in pieces:
                width = w.shape[1] // (nx * ny)
                out.append(lax.dynamic_slice_in_dim(w, (yy * nx + xx) * width, width, 1))
            return out[0] if len(out) == 1 else jnp.concatenate(out, axis=1)

        def for_x(xx):
            return jnp.stack([take(yy, xx) for yy in range(ny)])

        width = sum(w.shape[1] for w in pieces) // (nx * ny)
        mine = jnp.zeros((ny, nx, rows, width), BF16)
        for r in range(nx):
            got = for_x((x + r) % nx)
            if r:
                got = self.shift(got, "x", r)
            mine = lax.dynamic_update_slice_in_dim(mine, got[:, None], (x - r) % nx, 1)
        block = jnp.zeros((ny, nx, rows, width), BF16)
        for r in range(ny):
            got = lax.dynamic_index_in_dim(mine, (y + r) % ny, 0, keepdims=False)
            if r:
                got = self.shift(got, "y", r)
            block = lax.dynamic_update_index_in_dim(block, got, (y - r) % ny, 0)
        whole = jnp.zeros((ny, nc, nz, nx * rows, width), BF16)
        held = block.reshape(ny, 1, 1, nx * rows, width)
        for r in range(nz):
            if r:
                held = self.shift(held, "z", 1)
            for s in range(nc):
                other = self.shift(held, "c", s) if s else held
                whole = lax.dynamic_update_slice(whole, other, (0, (c - s) % nc, (z - r) % nz, 0, 0))
        return whole.reshape(ny * nc * nz * nx * rows, width)

    def weight_grad(self, left, right, widths):
        nx, ny, nz, nc = self.n["x"], self.n["y"], self.n["z"], self.n["c"]
        x, y, z, c = (self.index(p) for p in "xyzc")
        tokens, depth = left.shape
        rows = depth // (nx * ny * nz * nc)
        wide = left.reshape(tokens, ny, nc, nz, nx * rows)

        def part(core):
            cut = lax.dynamic_index_in_dim(wide, core, 2, keepdims=False)
            cut = cut.transpose(0, 2, 1, 3).reshape(tokens, depth // nc)
            return cut

        def product(core):
            return lax.dot_general(
                part(core), right, (((0,), (0,)), ((), ())), preferred_element_type=F32
            )

        mine = product(c)
        for s in range(1, nc):
            mine = mine + self.shift(product((c + s) % nc).astype(BF16), "c", s).astype(F32)
        mine = mine.reshape(nz, depth // (nc * nz), right.shape[1])

        def slab(r):
            return lax.dynamic_index_in_dim(mine, (z - r) % nz, 0, keepdims=False)

        if nz > 1:
            held = slab(1).astype(BF16)
            for r in range(2, nz):
                held = (slab(r) + self.shift(held, "z", 1).astype(F32)).astype(BF16)
            done = slab(0) + self.shift(held, "z", 1).astype(F32)
        else:
            done = slab(0)
        done = done.astype(BF16).reshape(ny, nx, rows, right.shape[1])
        side = jnp.zeros((ny, nx, rows, right.shape[1]), BF16)
        for r in range(ny):
            got = lax.dynamic_index_in_dim(done, (y + r) % ny, 0, keepdims=False)
            if r:
                got = self.shift(got, "y", r)
            side = lax.dynamic_update_index_in_dim(side, got, (y - r) % ny, 0)
        outs = [jnp.zeros((rows, w * nx * ny), F32) for w in widths]
        for r in range(nx):
            got = lax.dynamic_index_in_dim(side, (x + r) % nx, 1, keepdims=False)
            if r:
                got = self.shift(got, "x", r)
            got = got.astype(F32)
            for yy in range(ny):
                at = 0
                for i, w in enumerate(widths):
                    column = (yy * nx + (x - r) % nx) * w
                    outs[i] = lax.dynamic_update_slice(
                        outs[i], got[yy, :, at : at + w], (0, column)
                    )
                    at += w
        return outs


def decay_terms(rate, slope):
    log_decay = rate * slope
    small = 1.0 / 40320.0
    for div in (5040.0, 720.0, 120.0, 24.0, 6.0, 2.0, 1.0):
        small = small * log_decay + 1.0 / div
    less = jnp.where(log_decay < -0.4, jnp.exp(log_decay) - 1.0, log_decay * small)
    decay = 1.0 + less
    square = -less * (1.0 + decay)
    return decay, square


def split_dot(value, weight):
    high = value.astype(BF16)
    rest = (value - high.astype(F32)).astype(BF16)
    return jnp.dot(high, weight, preferred_element_type=F32) + jnp.dot(
        rest, weight, preferred_element_type=F32
    )


def forward_kernel(order, u, halo, same, vec, gates, conv, rate, gate_in, state, prods, ends, rows, keep_a, keep_b):
    nx, step = u.shape[1], u.shape[2]
    length = nx * step
    rows[0:HALO] = halo[0]
    for i in range(nx):
        rows[HALO + i * step : HALO + (i + 1) * step] = u[0, order[i]].astype(F32)
    filtered = vec[4:5] + rows[HALO : HALO + length] * vec[0:1]
    for k in range(1, TAPS):
        filtered = filtered + rows[HALO - k : HALO - k + length] * same[0, :, k : k + 1] * vec[k : k + 1]
    conv[0] = filtered
    r_gate = jax.nn.sigmoid(split_dot(filtered, gates[0]) + vec[5:6])
    i_gate = jax.nn.sigmoid(split_dot(filtered, gates[1]) + vec[6:7])
    rate[0] = r_gate
    gate_in[0] = i_gate
    decay, square = decay_terms(r_gate, vec[7:8])
    a = decay * same[0, :, 1:2]
    b = jnp.sqrt(square) * i_gate * filtered
    width = a.shape[1]
    tiles = length // 8
    a = a.reshape(tiles, 8, width)
    b = b.reshape(tiles, 8, width)
    row = lax.broadcasted_iota(jnp.int32, (tiles, 8, width), 1)
    for d in (1, 2, 4):
        a_back = jnp.where(row >= d, pltpu.roll(a, d, 1), 1.0)
        b_back = jnp.where(row >= d, pltpu.roll(b, d, 1), 0.0)
        b = b + a * b_back
        a = a * a_back
    keep_a[...] = a.reshape(length, width)
    keep_b[...] = b.reshape(length, width)
    carry_s = jnp.zeros((1, width), F32)
    carry_a = jnp.ones((1, width), F32)
    for t in range(tiles):
        at = keep_a[t * 8 : t * 8 + 8]
        bt = keep_b[t * 8 : t * 8 + 8]
        s = bt + at * carry_s
        p = at * carry_a
        state[0, t * 8 : t * 8 + 8] = s
        prods[0, t * 8 : t * 8 + 8] = p
        carry_s = s[7:8]
        carry_a = p[7:8]
    ends[0, 0:1] = carry_a
    ends[0, 1:2] = carry_s
    ends[0, 2:8] = jnp.zeros((6, width), F32)


def reverse_kernel(order, d_state, same, vec, rate, grads, prods, ends, keep_g, keep_a):
    nx, step = d_state.shape[1], d_state.shape[2]
    length = nx * step
    width = rate.shape[2]
    decay, _ = decay_terms(rate[0], vec[7:8])
    a = decay * same[0, :, 1:2]
    keep_a[0:length] = a
    keep_a[length : length + 8] = jnp.ones((8, width), F32)
    for i in range(nx):
        keep_g[i * step : (i + 1) * step] = d_state[0, order[i]].astype(F32)
    first = a[0:1]
    tiles = length // 8
    nxt = keep_a[1 : length + 1].reshape(tiles, 8, width)
    g = keep_g[...].reshape(tiles, 8, width)
    row = lax.broadcasted_iota(jnp.int32, (tiles, 8, width), 1)
    p = nxt
    for d in (1, 2, 4):
        g_ahead = jnp.where(row < 8 - d, pltpu.roll(g, 8 - d, 1), 0.0)
        p_ahead = jnp.where(row < 8 - d, pltpu.roll(p, 8 - d, 1), 1.0)
        g = g + p * g_ahead
        p = p * p_ahead
    keep_g[...] = g.reshape(length, width)
    keep_a[0:length] = p.reshape(length, width)
    carry_g = jnp.zeros((1, width), F32)
    carry_p = jnp.ones((1, width), F32)
    for t in reversed(range(tiles)):
        pt = keep_a[t * 8 : t * 8 + 8]
        gt = keep_g[t * 8 : t * 8 + 8] + pt * carry_g
        pt = pt * carry_p
        grads[0, t * 8 : t * 8 + 8] = gt
        prods[0, t * 8 : t * 8 + 8] = pt
        carry_g = gt[0:1]
        carry_p = pt[0:1]
    ends[0, 0:1] = first * carry_p
    ends[0, 1:2] = first * carry_g
    ends[0, 2:8] = jnp.zeros((6, width), F32)


def final_kernel(
    order, u, halo, same, vec, gates, conv, rate, gate_in, state, prods, start, grads, back, carry,
    d_u, head, d_rate, d_input, sums, rows, tail,
):
    nx, step = u.shape[1], u.shape[2]
    length = nx * step
    width = conv.shape[2]
    d_s = grads[0] + back[0] * carry[0, 0:1]
    s_now = state[0] + prods[0] * start[0, 0:1]
    rows[HALO : HALO + length] = s_now
    rows[HALO - 1 : HALO] = start[0, 0:1]
    s_prev = rows[HALO - 1 : HALO - 1 + length]
    r_gate, i_gate, filtered = rate[0], gate_in[0], conv[0]
    decay, square = decay_terms(r_gate, vec[7:8])
    inverse = lax.rsqrt(jnp.maximum(square, 1e-37))
    scale = square * inverse
    a = decay * same[0, :, 1:2]
    d_scaled = d_s * i_gate * filtered
    d_log = d_s * s_prev * a - d_scaled * (decay * decay) * inverse
    d_i = d_s * scale * filtered * i_gate * (1.0 - i_gate)
    d_r = d_log * vec[7:8] * r_gate * (1.0 - r_gate)
    d_r_low = d_r.astype(BF16)
    d_i_low = d_i.astype(BF16)
    d_rate[0] = d_r_low
    d_input[0] = d_i_low
    back_dims = (((1,), (1,)), ((), ()))
    d_c = (
        d_s * scale * i_gate
        + lax.dot_general(d_r_low, gates[0], back_dims, preferred_element_type=F32)
        + lax.dot_general(d_i_low, gates[1], back_dims, preferred_element_type=F32)
    )
    rows[0:HALO] = halo[0]
    for i in range(nx):
        rows[HALO + i * step : HALO + (i + 1) * step] = u[0, order[i]].astype(F32)

    def column(value):
        return jnp.sum(value, axis=0, keepdims=True)

    parts = [column(d_c * rows[HALO : HALO + length])]
    tail[0:HALO] = jnp.zeros((HALO, width), F32)
    tail[HALO + length : 2 * HALO + length] = jnp.zeros((HALO, width), F32)
    d_rows = d_c * vec[0:1]
    d_head = jnp.zeros((HALO, width), F32)
    for k in range(1, TAPS):
        masked = d_c * same[0, :, k : k + 1]
        parts.append(column(masked * rows[HALO - k : HALO - k + length]))
        tail[HALO : HALO + length] = masked * vec[k : k + 1]
        d_rows = d_rows + tail[HALO + k : HALO + k + length]
        d_head = d_head + tail[k : k + HALO]
    for i in range(nx):
        d_u[0, order[i]] = d_rows[i * step : (i + 1) * step]
    head[0] = d_head
    parts += [column(d_c), column(d_r), column(d_i), column(d_log * r_gate)]

    @pl.when(pl.program_id(0) == 0)
    def _():
        sums[...] = jnp.zeros_like(sums)

    for i, value in enumerate(parts):
        sums[i : i + 1] += value


def chain_spec(*dims):
    return pl.BlockSpec((1, *dims), lambda i: (i,) + (0,) * len(dims))


def whole_spec(*dims):
    return pl.BlockSpec(dims, lambda i: (0,) * len(dims))


def scan_call(kernel, chains, operands, outs, scratch, flops):
    specs = [pl.BlockSpec(memory_space=pltpu.SMEM)]
    for value, chained in operands[1:]:
        specs.append(chain_spec(*value.shape[1:]) if chained else whole_spec(*value.shape))
    shapes, out_specs = [], []
    for shape, dtype, chained in outs:
        shapes.append(jax.ShapeDtypeStruct(shape, dtype))
        out_specs.append(chain_spec(*shape[1:]) if chained else whole_spec(*shape))
    moved = sum(v.size * v.dtype.itemsize for v, _ in operands)
    moved += sum(s.size * s.dtype.itemsize for s in shapes)
    return pl.pallas_call(
        kernel,
        grid=(chains,),
        in_specs=specs,
        out_specs=out_specs,
        out_shape=shapes,
        scratch_shapes=[pltpu.VMEM(s, F32) for s in scratch],
        compiler_params=pltpu.CompilerParams(vmem_limit_bytes=48 * 1024 * 1024),
        cost_estimate=pl.CostEstimate(flops=flops, bytes_accessed=moved, transcendentals=0),
    )(*[v for v, _ in operands])


def norm_back(grad_in, rows_in, scale_vec, gain_vec):
    weighted = grad_in * gain_vec
    return scale_vec * weighted - rows_in * scale_vec**3 * jnp.mean(
        weighted * rows_in, axis=-1, keepdims=True
    )


def mix(left, right):
    return jnp.dot(left, right, preferred_element_type=F32)


def mix_back(left, right):
    return lax.dot_general(left, right, (((1,), (1,)), ((), ())), preferred_element_type=F32)


def on_device(
    grid,
    inputs,
    seg_ids,
    norm_in,
    proj_y,
    proj_x,
    conv_weight,
    conv_bias,
    rate_weight,
    rate_bias,
    input_weight,
    input_bias,
    decay_param,
    proj_out,
    norm_mlp,
    mlp_gate,
    mlp_up,
    mlp_down,
    cotangent,
):
    nx, ny, nz, nc = (grid.n[p] for p in "xyzc")
    x, y, z, c = (grid.index(p) for p in "xyzc")
    planes = nx * ny
    micro, step, depth = inputs.shape
    chains = micro * ny
    length = nx * step
    local = planes * step
    firsts = ["x" if m % 2 == 0 else "y" for m in range(micro)]

    def spread(shard):
        return jnp.concatenate(
            [grid.spread(shard[m], firsts[m]) for m in range(micro)], axis=0
        )

    def collect(partial):
        partial = partial.reshape(micro, local, partial.shape[1])
        return jnp.stack(
            [grid.collect(partial[m], "y" if firsts[m] == "x" else "x") for m in range(micro)]
        )

    source = inputs.astype(F32)
    rows_in = spread(inputs)
    mix_x = grid.columns_of([proj_x])
    mix_y = grid.columns_of([proj_y])
    mix_out = grid.columns_of([proj_out])
    width = mix_x.shape[1]
    ff_in = grid.columns_of([mlp_gate, mlp_up])
    ff_down = grid.columns_of([mlp_down])
    ff_width = ff_down.shape[1]
    rows_cot = spread(cotangent)

    slope = -8.0 * jax.nn.softplus(-decay_param)
    slope_back = 8.0 * jax.nn.sigmoid(-decay_param)
    small = jnp.concatenate(
        [
            conv_weight,
            conv_bias[None],
            rate_bias[None],
            input_bias[None],
            slope[None],
        ],
        axis=0,
    )
    share = small.shape[1]
    gain_pair = jnp.stack([norm_in, norm_mlp]).astype(F32)
    gate_pair = jnp.stack([rate_weight, input_weight], axis=1)
    heads, block = gate_pair.shape[0], gate_pair.shape[2]
    per = nz // ny

    def own_channels(value):
        by_z = grid.gather_abs(value, "z", ring=True)
        part = lax.dynamic_slice_in_dim(by_z, y * per, per, 0)
        by_x = grid.gather_abs(part, "x")
        flat = jnp.moveaxis(by_x, 0, 1).reshape(per * nx, *value.shape)
        return lax.dynamic_slice_in_dim(flat, x * per, per, 0)

    vec = jnp.moveaxis(own_channels(small), 0, 1).reshape(8, width)
    gate_own = own_channels(gate_pair).reshape(per * heads, 2, block, block)
    dense = [jnp.zeros((width, width), BF16) for _ in range(2)]
    for h in range(per * heads):
        for g in range(2):
            dense[g] = lax.dynamic_update_slice(dense[g], gate_own[h, g], (h * block, h * block))
    gates = jnp.stack(dense)
    gains = gain_pair
    for part in "xzcy":
        gains = grid.gather_abs(gains, part)
    gains = jnp.moveaxis(gains, -2, 0).reshape(2, depth)
    gain_in, gain_mlp = gains[0], gains[1]

    segments = jnp.stack([seg_ids] + [grid.shift(seg_ids, "y", r) for r in range(1, ny)], axis=1)
    padded = jnp.pad(segments, ((0, 0), (0, 0), (HALO, 0)), constant_values=-1)
    near = lax.dynamic_slice_in_dim(padded, z * length, length + HALO, 2)
    here = near[:, :, HALO:]
    same = [jnp.ones_like(here, dtype=F32)]
    for k in range(1, TAPS):
        same.append((near[:, :, HALO - k : HALO - k + length] == here).astype(F32))
    same = jnp.stack(same + [jnp.zeros_like(same[0])] * (8 - TAPS), axis=-1)
    same = same.reshape(chains, length, 8)
    order = ((x - jnp.arange(nx, dtype=jnp.int32)) % nx).astype(jnp.int32)

    wide = rows_in.astype(F32)
    scale_wide = lax.rsqrt(jnp.mean(wide * wide, axis=-1, keepdims=True) + NORM_EPS)
    normed = (wide * scale_wide * gain_in).astype(BF16)
    drive = mix(normed, mix_x).astype(BF16).reshape(chains, nx, step, width)
    pre_y = mix(normed, mix_y)
    branch_y, gelu_y_back = jax.vjp(jax.nn.gelu, pre_y)
    last = lax.dynamic_index_in_dim(drive, (x - (nx - 1)) % nx, 1, keepdims=False)
    halo = grid.shift(last[:, step - HALO :].astype(F32), "z", 1, wrap=False)
    shape = (chains, length, width)
    conv, rate, gate_in, state, prods, ends = scan_call(
        forward_kernel,
        chains,
        [(order, False), (drive, True), (halo, True), (same, True), (vec, False), (gates, False)],
        [(shape, F32, True)] * 5 + [((chains, 8, width), F32, True)],
        [(length + HALO, width), (length, width), (length, width)],
        flops=8 * chains * length * width * width,
    )

    def carry_from(summary, sign):
        carry = jnp.zeros((chains, 1, width), F32)
        for r in reversed(range(1, nz)):
            got = grid.shift(summary, "z", sign * r, wrap=False)
            carry = got[:, 1:2] + got[:, 0:1] * carry
        return carry

    start = carry_from(ends[:, 0:2], 1)
    hidden = (state + prods * start).astype(BF16).reshape(chains, nx, step, width)

    def relative(value):
        return jnp.concatenate(
            [
                lax.dynamic_index_in_dim(value, (x - r) % nx, 1, keepdims=True) for r in range(nx)
            ],
            axis=1,
        ).reshape(chains * length, width)

    hidden_f = relative(hidden).astype(F32)
    mixed = (branch_y * hidden_f).astype(BF16)
    resid = source + collect(mix_back(mixed, mix_out).astype(BF16))

    scale_mlp = lax.rsqrt(jnp.mean(resid * resid, axis=-1, keepdims=True) + NORM_EPS)
    normed_mlp = spread((resid * scale_mlp * gain_mlp).astype(BF16))
    pre_ff = mix(normed_mlp, ff_in)
    pre_gate, pre_up = pre_ff[:, :ff_width], pre_ff[:, ff_width:]
    activated, gelu_gate_back = jax.vjp(jax.nn.gelu, pre_gate)
    product = (activated * pre_up).astype(BF16)
    grad_prod = mix(rows_cot, ff_down)
    grad_gate = gelu_gate_back(grad_prod * pre_up)[0].astype(BF16)
    grad_up = (grad_prod * activated).astype(BF16)
    grad_ff = jnp.concatenate([grad_gate, grad_up], axis=1)
    grad_norm_mlp = collect(mix_back(grad_ff, ff_in).astype(BF16))
    block_out = (resid + collect(mix_back(product, ff_down).astype(BF16))).astype(BF16)
    grad_gate_w, grad_up_w = grid.weight_grad(normed_mlp, grad_ff, [ff_width, ff_width])
    (grad_down_w,) = grid.weight_grad(rows_cot, product, [ff_width])
    term_gain_mlp = jnp.sum(grad_norm_mlp * resid * scale_mlp, axis=(0, 1))
    grad_resid = cotangent.astype(F32) + norm_back(grad_norm_mlp, resid, scale_mlp, gain_mlp)
    grad_branch = spread(grad_resid.astype(BF16))

    grad_mixed = mix(grad_branch, mix_out)
    grad_pre_y = gelu_y_back(grad_mixed * hidden_f)[0].astype(BF16)
    grad_state = (grad_mixed * branch_y).astype(BF16).reshape(chains, nx, step, width)
    d_local, d_prods, d_ends = scan_call(
        reverse_kernel,
        chains,
        [(order, False), (grad_state, True), (same, True), (vec, False), (rate, True)],
        [(shape, F32, True)] * 2 + [((chains, 8, width), F32, True)],
        [(length, width), (length + HALO, width)],
        flops=40 * chains * length * width,
    )
    d_carry = carry_from(d_ends[:, 0:2], -1)
    d_drive, head, *d_pre, sums = scan_call(
        final_kernel,
        chains,
        [
            (order, False),
            (drive, True),
            (halo, True),
            (same, True),
            (vec, False),
            (gates, False),
            (conv, True),
            (rate, True),
            (gate_in, True),
            (state, True),
            (prods, True),
            (start, True),
            (d_local, True),
            (d_prods, True),
            (d_carry, True),
        ],
        [
            ((chains, nx, step, width), F32, True),
            ((chains, HALO, width), F32, True),
            (shape, BF16, True),
            (shape, BF16, True),
            ((8, width), F32, False),
        ],
        [(length + HALO, width), (length + 2 * HALO, width)],
        flops=8 * chains * length * width * width,
    )
    after = grid.shift(head, "z", -1, wrap=False)
    chunk = lax.broadcasted_iota(jnp.int32, (1, nx, 1, 1), 1)
    tail = jnp.pad(after, ((0, 0), (step - HALO, 0), (0, 0)))[:, None]
    d_drive = d_drive + jnp.where(chunk == (x - (nx - 1)) % nx, tail, 0.0)
    grad_drive = d_drive.astype(BF16).reshape(chains * length, width)
    both = jnp.concatenate([grad_pre_y, grad_drive], axis=1)
    grad_normed = collect(
        (mix_back(grad_pre_y, mix_y) + mix_back(grad_drive, mix_x)).astype(BF16)
    )
    grad_y_w, grad_x_w = grid.weight_grad(normed, both, [width, width])
    (grad_out_w,) = grid.weight_grad(grad_branch, mixed, [width])
    scale_in = lax.rsqrt(jnp.mean(source * source, axis=-1, keepdims=True) + NORM_EPS)
    term_gain_in = jnp.sum(grad_normed * source * scale_in, axis=(0, 1))
    grad_source = (grad_resid + norm_back(grad_normed, source, scale_in, gain_in)).astype(BF16)

    terms = jnp.stack([term_gain_in, term_gain_mlp]).reshape(2, ny, nc, nz, nx, -1)
    for part, dim in (("c", 2), ("y", 1), ("z", 1), ("x", 1)):
        terms = grid.scatter_sum(terms, part, dim)
    conv_low = conv.reshape(chains * length, width).astype(BF16)
    gate_dense = [
        lax.dot_general(
            conv_low,
            d.reshape(chains * length, width),
            (((0,), (0,)), ((), ())),
            preferred_element_type=F32,
        )
        for d in d_pre
    ]
    gate_grads = jnp.stack(
        [
            jnp.stack([d[h * block : (h + 1) * block, h * block : (h + 1) * block] for d in gate_dense])
            for h in range(per * heads)
        ]
    )

    def own_share(value):
        value = grid.total(grid.total(value, "c"), "z")
        by_y = grid.gather_abs(grid.gather_abs(value, "x"), "y")
        flat = by_y.reshape(ny * nx * per, *value.shape[1:])
        return lax.dynamic_index_in_dim(flat, z * nx + x, 0, keepdims=False)

    gate_share = own_share(gate_grads.astype(BF16).reshape(per, heads, 2, block, block)).astype(F32)
    sum_share = own_share(jnp.moveaxis(sums.reshape(8, per, share), 0, 1))
    return (
        block_out,
        grad_source,
        terms[0],
        grad_y_w,
        grad_x_w,
        sum_share[0:4],
        sum_share[4],
        gate_share[:, 0],
        sum_share[5],
        gate_share[:, 1],
        sum_share[6],
        sum_share[7] * slope_back,
        grad_out_w,
        terms[1],
        grad_gate_w,
        grad_up_w,
        grad_down_w,
    )


def solution(mesh):
    grid = Grid(mesh.shape["seq"], mesh.shape["blk"])
    every = ("seq", "blk")
    placed = (
        P(None, every, None),
        P(None, "seq"),
        P(every),
        P(every, None),
        P(every, None),
        P(None, "blk"),
        P("blk"),
        P("blk", None, None),
        P("blk"),
        P("blk", None, None),
        P("blk"),
        P("blk"),
        P(every, None),
        P(every),
        P(every, None),
        P(every, None),
        P(every, None),
        P(None, every, None),
    )
    return jax.shard_map(
        functools.partial(on_device, grid),
        mesh=mesh,
        in_specs=placed,
        out_specs=(
            P(None, every, None),
            P(None, every, None),
            P(every),
            P(every, None),
            P(every, None),
            P(None, "blk"),
            P("blk"),
            P("blk", None, None),
            P("blk"),
            P("blk", None, None),
            P("blk"),
            P("blk"),
            P(every, None),
            P(every),
            P(every, None),
            P(every, None),
            P(every, None),
        ),
        check_vma=False,
    )
```

time: 3750 us -> 1230 us (0.33)
  waiting for transfers between devices: 2910 us -> 526 us
  blocking collectives: 140 us -> 0 us
  starting transfers between devices: 12.5 us -> 147 us
  matrix products: 251 us -> 117 us
  other arithmetic: 102 us -> 41.6 us
  local copies, waits for them, and re-layouts: 302 us -> 351 us
    reduce_scatter x5 -> x0, waiting for transfers between devices: 1950 us -> none  [the longest x1 448 us: run_pass(): lax.psum_scatter(term_y, ('seq', 'blk'), scatter_dimension=0, tiled=True)]
    ppermute x0 -> x158, waiting for transfers between devices: none -> 526 us  [shift(): return lax.ppermute(value, axis, pairs)]
    unnamed x14 -> x0, waiting for transfers between devices: 441 us -> none
    all_gather x6 -> x0, waiting for transfers between devices: 384 us -> none  [the longest x1 143 us: run_pass(): lax.all_gather(mlp_up, ('seq', 'blk'), axis=0, tiled=True)]
    ppermute x0 -> x158, starting transfers between devices: none -> 147 us  [shift(): return lax.ppermute(value, axis, pairs)]
    concatenate x0 -> x73, local copies, waits for them, and re-layouts: none -> 141 us  [the longest x72 140 us: spread(): jnp.concatenate([grid.spread(shard[m], firsts[m]) for m in range(micro)],...]
    all_to_all x3 -> x0, waiting for transfers between devices: 139 us -> none  [the longest x1 51.4 us: run_pass(): lax.all_to_all(scan_state.astype(jnp.bfloat16), 'blk', split_axis=1, conc...]
    dot_general x24 -> x20, matrix products: 251 us -> 117 us  [the longest x5 43.1 us: mix(): return jnp.dot(left, right, preferred_element_type=F32)]
  transfers between devices with their start and end apart: 16 -> 158, of which waited for: 13 -> 70; matrix products, arithmetic and copies ran while one was open for 12% -> 37% of each run, Pallas kernels for 0% -> 2%
where the time goes in v1:
time: 1230 us; the launch traced here: 1220 us
  waiting for transfers between devices  526 us (43%)
  local copies, waits for them, and re-layouts  351 us (29%)
  starting transfers between devices  147 us (12%)
  matrix products  117 us (10%)
  other arithmetic  41.6 us (3%)
  Pallas kernels  28.7 us (2%)
    ppermute x158, waiting for transfers between devices, shift(): return lax.ppermute(value, axis, pairs)  526 us
    ppermute x158, starting transfers between devices, shift(): return lax.ppermute(value, axis, pairs)  147 us
    concatenate x72, local copies, waits for them, and re-layouts, spread(): jnp.concatenate([grid.spread(shard[m], firsts[m]) for m in range(micro)],...  140 us
    dynamic_update_slice x40, local copies, waits for them, and re-layouts, columns_of(): lax.dynamic_update_slice(whole, other, (0, (c - s) % nc, (z - r) % nz, 0,...  58.4 us
    unnamed x250, local copies, waits for them, and re-layouts  48.4 us
    dot_general x5, matrix products, mix(): return jnp.dot(left, right, preferred_element_type=F32)  43.1 us
    dot_general x8, matrix products, product(): lax.dot_general(part(core), right, (((0,), (0,)), ((), ())), preferred_el...  35.4 us
    dot_general x5, matrix products, mix_back(): lax.dot_general(left, right, (((1,), (1,)), ((), ())), preferred_element_...  35.3 us
  transfers between devices with their start and end apart: 158, of which 70 were waited for; matrix products, arithmetic and copies ran while one was open for 37% of the time, Pallas kernels for 2%

profile of v1, /device:TPU:0, one launch (start us, length us, event | category | flops | bytes accessed | tf_op | source)
XLA Modules:
  0.0 1216.0 jit_solution(10182925111432016044)
XLA Ops:
  48.1 3.8 collective-permute-done.7
  76.7 4.2 collective-permute-done.33
  82.0 4.3 collective-permute-done.34
  92.0 5.1 collective-permute-done.21
  111.3 6.2 collective-permute-done.36
  124.4 5.6 collective-permute-done.13
  131.9 4.4 collective-permute-done.44
  192.7 9.0 collective-permute-done.38
  229.1 10.3 collective-permute-done.90
  266.7 6.7 concatenate.140
  290.1 6.5 concatenate.168
  296.6 3.9 constant_dynamic-slice_fusion.2
  309.8 4.4 collective-permute-done.48
  340.1 6.6 collective-permute-done.19
  348.3 5.5 collective-permute-done.50
  359.2 11.3 collective-permute-done.76
  372.7 6.1 broadcast_in_dim.279
  382.4 4.4 convolution_convert_fusion.7
  389.9 16.7 %collective-permute-done.30.halo = f32[4,8,640]{2,1,0:T(8,128)S(1)} collective-permute-done((f32[4,8,640]{2,1,0:T(8,128)S(1)}, f32[4,8,640]{2,1,0:T(8,128)S(1)}, u32[]{:S(2)}, u32[]{:S(2)}) %collective-permute-start.30) | collective-permute-done | bytes 81952 | tf_op jit(solution)/shard_map/ppermute | solution.py:49
  406.6 10.4 shard_map.305
  420.8 4.4 collective-permute-start.40
  430.7 6.2 fusion.13
  436.9 4.9 convolution_convert_fusion.3
  444.4 17.2 %collective-permute-done.55 = bf16[96,2048]{1,0:T(8,128)(2,1)S(1)} collective-permute-done((bf16[96,2048]{1,0:T(8,128)(2,1)S(1)}, bf16[96,2048]{1,0:T(8,128)(2,1)S(1)}, u32[]{:S(2)}, u32[]{:S(2)}) %collective-permute-start.55) | collective-permute-done | bytes 393248 | tf_op jit(solution)/shard_map/ppermute | solution.py:49
  462.5 9.2 collective-permute-done.52
  475.0 8.7 collective-permute-done.56
  484.4 4.6 collective-permute-done.54
  550.7 6.9 concatenate.159
  562.0 9.7 collective-permute-done.69
  581.8 27.8 %collective-permute-done.71 = bf16[2,1,1,128,3072]{4,3,0,2,1:T(8,128)(2,1)S(1)} collective-permute-done((bf16[2,1,1,128,3072]{4,3,0,2,1:T(8,128)(2,1)}, bf16[2,1,1,128,3072]{4,3,0,2,1:T(8,128)(2,1)S(1)}, u32[]{:S(2)}, u32[]{:S(2)}) %collective-permute-start.71) | collective-permute-done | bytes 1572896 | tf_op jit(solution)/shard_map/ppermute | solution.py:49
  616.2 12.9 %fusion.147 = f32[768,3072]{1,0:T(8,128)S(1)} fusion(bf16[768,2048]{1,0:T(8,128)(2,1)S(1)} %constant_dynamic-update-slice_fusion.8, bf16[2048,3072]{1,0:T(8,128)(2,1)} %bitcast.742), kind=kOutput, calls=%fused_computation.561 | convolution fusion | flops 9663676416 | bytes 25165824 | tf_op jit(solution)/shard_map/dot_general | solution.py:412
  629.1 12.2 %fusion.9 = (bf16[768,1536]{1,0:T(8,128)(2,1)S(1)}, bf16[768,1536]{1,0:T(8,128)(2,1)S(1)}, bf16[768,1536]{1,0:T(8,128)(2,1)}) fusion(f32[768,3072]{1,0:T(8,128)S(1)} %fusion.147, bf16[768,2048]{1,0:T(8,128)(2,1)} %constant_dynamic-update-slice_fusion.16, bf16[2048,1536]{1,0:T(8,128)(2,1)} %bitcast.128), kind=kOutput, calls=%fused_computation.19 | convolution fusion | flops 4862509056 | bytes 25952256 | tf_op jit(solution)/shard_map/dot_general | solution.py:412
  641.4 14.6 %convolution_convert_fusion.4 = bf16[768,2048]{1,0:T(8,128)(2,1)S(1)} fusion(bf16[2048,3072]{1,0:T(8,128)(2,1)} %bitcast.743, bf16[768,1536]{1,0:T(8,128)(2,1)S(1)} %get-tuple-element.60, bf16[768,1536]{1,0:T(8,128)(2,1)S(1)} %get-tuple-element.59), kind=kOutput, calls=%fused_computation.27 | convolution fusion | flops 9674686464 | bytes 20447232 | tf_op jit(solution)/shard_map/dot_general | solution.py:416
  660.8 8.2 convolution_convert_fusion.5
  672.6 7.2 convolution_convert_fusion
  679.8 4.0 convolution_convert_fusion.1
  687.1 8.0 collective-permute-done.85
  696.6 8.0 collective-permute-done.82
  706.6 6.6 collective-permute-done.98
  715.7 6.4 collective-permute-done.95
  770.9 7.4 fusion.20
  778.3 7.3 shard_map.306
  800.3 6.4 concatenate.150
  812.6 11.1 shard_map.307
  828.9 5.7 collective-permute-start.131
  848.8 4.8 add_convert_fusion
  863.1 8.7 collective-permute-done.113
  873.7 7.3 collective-permute-done.110
  901.0 39.6 %collective-permute-done.136 = bf16[2,2,2,160,160]{4,3,2,1,0:T(8,128)(2,1)} collective-permute-done((bf16[2,2,2,160,160]{4,3,2,1,0:T(8,128)(2,1)S(1)}, bf16[2,2,2,160,160]{4,3,2,1,0:T(8,128)(2,1)}, u32[]{:S(2)}, u32[]{:S(2)}) %collective-permute-start.136) | collective-permute-done | bytes 409632 | tf_op jit(solution)/shard_map/ppermute | solution.py:49
  962.2 8.9 collective-permute-done.138
  973.9 4.5 convert_add_fusion.1
  982.4 15.0 %collective-permute-done.139 = bf16[2,2,2,2,160,160]{5,4,2,3,1,0:T(8,128)(2,1)S(1)} collective-permute-done((bf16[2,2,2,2,160,160]{5,4,2,3,1,0:T(8,128)(2,1)S(1)}, bf16[2,2,2,2,160,160]{5,4,2,3,1,0:T(8,128)(2,1)S(1)}, u32[]{:S(2)}, u32[]{:S(2)}) %collective-permute-start.139) | collective-permute-done | bytes 819232 | tf_op jit(solution)/shard_map/ppermute | solution.py:49
  998.4 7.2 collective-permute-done.143
  1019.4 10.7 collective-permute-done.154
  1030.4 13.7 %collective-permute-done.123 = bf16[256,1280]{1,0:T(8,128)(2,1)S(1)} collective-permute-done((bf16[256,1280]{1,0:T(8,128)(2,1)S(1)}, bf16[256,1280]{1,0:T(8,128)(2,1)S(1)}, u32[]{:S(2)}, u32[]{:S(2)}) %collective-permute-start.123) | collective-permute-done | bytes 655392 | tf_op jit(solution)/shard_map/ppermute | solution.py:49
  1044.4 16.6 %collective-permute-done.155 = bf16[256,1536]{1,0:T(8,128)(2,1)S(1)} collective-permute-done((bf16[256,1536]{1,0:T(8,128)(2,1)S(1)}, bf16[256,1536]{1,0:T(8,128)(2,1)S(1)}, u32[]{:S(2)}, u32[]{:S(2)}) %collective-permute-start.155) | collective-permute-done | bytes 786464 | tf_op jit(solution)/shard_map/ppermute | solution.py:49
  1064.7 8.6 convert_add_fusion
  1074.1 38.6 %collective-permute-done.147 = bf16[256,3072]{1,0:T(8,128)(2,1)S(1)} collective-permute-done((bf16[256,3072]{1,0:T(8,128)(2,1)S(1)}, bf16[256,3072]{1,0:T(8,128)(2,1)S(1)}, u32[]{:S(2)}, u32[]{:S(2)}) %collective-permute-start.147) | collective-permute-done | bytes 1572896 | tf_op jit(solution)/shard_map/ppermute | solution.py:49
  1115.6 11.1 collective-permute-done.125
  1128.7 26.7 %collective-permute-done.148 = bf16[256,3072]{1,0:T(8,128)(2,1)S(1)} collective-permute-done((bf16[256,3072]{1,0:T(8,128)(2,1)S(1)}, bf16[256,3072]{1,0:T(8,128)(2,1)S(1)}, u32[]{:S(2)}, u32[]{:S(2)}) %collective-permute-start.148) | collective-permute-done | bytes 1572896 | tf_op jit(solution)/shard_map/ppermute | solution.py:49
  1158.6 28.0 %collective-permute-done.149 = bf16[256,3072]{1,0:T(8,128)(2,1)S(1)} collective-permute-done((bf16[256,3072]{1,0:T(8,128)(2,1)S(1)}, bf16[256,3072]{1,0:T(8,128)(2,1)S(1)}, u32[]{:S(2)}, u32[]{:S(2)}) %collective-permute-start.149) | collective-permute-done | bytes 1572896 | tf_op jit(solution)/shard_map/ppermute | solution.py:49
  1188.5 11.0 collective-permute-done.150
  1199.8 4.1 collective-permute-start.151
  1204.2 9.6 collective-permute-done.151
  (921 shorter events, 576.5 us)
Async XLA Ops:
  3.0 133.9 %collective-permute-start = (bf16[96,2048]{1,0:T(8,128)(2,1)}, bf16[96,2048]{1,0:T(8,128)(2,1)}, u32[]{:S(2)}, u32[]{:S(2)}) collective-permute-start(bf16[96,2048]{1,0:T(8,128)(2,1)} %get-tuple-element.136), channel_id=1, source_target_pairs={{0,1},{1,0},{2,3},{3,2},{4,5},{5,4},{6,7},{7,6},{8,9},{9,8},{10,11... | collective-permute-start | bytes 1179656 | tf_op jit(solution)/shard_map/ppermute | solution.py:49
  6.0 132.5 %collective-permute-start.1 = (bf16[96,2048]{1,0:T(8,128)(2,1)}, bf16[96,2048]{1,0:T(8,128)(2,1)}, u32[]{:S(2)}, u32[]{:S(2)}) collective-permute-start(bf16[96,2048]{1,0:T(8,128)(2,1)} %get-tuple-element.136), channel_id=1, source_target_pairs={{0,16},{8,24},{16,0},{24,8},{1,17},{9,25},{17,1},{25,9},{2,18},{10... | collective-permute-start | bytes 1179656 | tf_op jit(solution)/shard_map/ppermute | solution.py:49
  7.5 131.5 %collective-permute-start.3 = (bf16[96,2048]{1,0:T(8,128)(2,1)}, bf16[96,2048]{1,0:T(8,128)(2,1)}, u32[]{:S(2)}, u32[]{:S(2)}) collective-permute-start(bf16[96,2048]{1,0:T(8,128)(2,1)} %get-tuple-element.135), channel_id=1, source_target_pairs={{0,1},{1,0},{2,3},{3,2},{4,5},{5,4},{6,7},{7,6},{8,9},{9,8},{10,11... | collective-permute-start | bytes 1179656 | tf_op jit(solution)/shard_map/ppermute | solution.py:49
  8.0 132.3 %collective-permute-start.4 = (bf16[96,2048]{1,0:T(8,128)(2,1)}, bf16[96,2048]{1,0:T(8,128)(2,1)}, u32[]{:S(2)}, u32[]{:S(2)}) collective-permute-start(bf16[96,2048]{1,0:T(8,128)(2,1)} %get-tuple-element.135), channel_id=1, source_target_pairs={{0,16},{8,24},{16,0},{24,8},{1,17},{9,25},{17,1},{25,9},{2,18},{10... | collective-permute-start | bytes 1179656 | tf_op jit(solution)/shard_map/ppermute | solution.py:49
  9.3 36.5 %collective-permute-start.6 = (f32[2,64]{1,0:T(2,128)}, f32[2,64]{1,0:T(2,128)}, u32[]{:S(2)}, u32[]{:S(2)}) collective-permute-start(f32[2,64]{1,0:T(2,128)} %maximum_convert_fusion.1), channel_id=1, source_target_pairs={{0,1},{1,0},{2,3},{3,2},{4,5},{5,4},{6,7},{7,6},{8,9},{9,8},{10,11... | collective-permute-start | bytes 1544 | tf_op jit(solution)/shard_map/ppermute | solution.py:49
  136.3 26.5 %collective-permute-start.88 = (bf16[96,2048]{1,0:T(8,128)(2,1)}, bf16[96,2048]{1,0:T(8,128)(2,1)}, u32[]{:S(2)}, u32[]{:S(2)}) collective-permute-start(bf16[96,2048]{1,0:T(8,128)(2,1)} %get-tuple-element.123), channel_id=1, source_target_pairs={{0,1},{1,0},{2,3},{3,2},{4,5},{5,4},{6,7},{7,6},{8,9},{9,8},{10,11... | collective-permute-start | bytes 1179656 | tf_op jit(solution)/shard_map/ppermute | solution.py:49
  136.9 31.4 %collective-permute-start.89 = (bf16[96,2048]{1,0:T(8,128)(2,1)}, bf16[96,2048]{1,0:T(8,128)(2,1)}, u32[]{:S(2)}, u32[]{:S(2)}) collective-permute-start(bf16[96,2048]{1,0:T(8,128)(2,1)} %get-tuple-element.123), channel_id=1, source_target_pairs={{0,16},{8,24},{16,0},{24,8},{1,17},{9,25},{17,1},{25,9},{2,18},{10... | collective-permute-start | bytes 1179656 | tf_op jit(solution)/shard_map/ppermute | solution.py:49
  138.4 34.0 %collective-permute-start.91 = (bf16[96,2048]{1,0:T(8,128)(2,1)}, bf16[96,2048]{1,0:T(8,128)(2,1)}, u32[]{:S(2)}, u32[]{:S(2)}) collective-permute-start(bf16[96,2048]{1,0:T(8,128)(2,1)} %get-tuple-element.124), channel_id=1, source_target_pairs={{0,1},{1,0},{2,3},{3,2},{4,5},{5,4},{6,7},{7,6},{8,9},{9,8},{10,11... | collective-permute-start | bytes 1179656 | tf_op jit(solution)/shard_map/ppermute | solution.py:49
  139.0 37.6 %collective-permute-start.92 = (bf16[96,2048]{1,0:T(8,128)(2,1)}, bf16[96,2048]{1,0:T(8,128)(2,1)}, u32[]{:S(2)}, u32[]{:S(2)}) collective-permute-start(bf16[96,2048]{1,0:T(8,128)(2,1)} %get-tuple-element.124), channel_id=1, source_target_pairs={{0,16},{8,24},{16,0},{24,8},{1,17},{9,25},{17,1},{25,9},{2,18},{10... | collective-permute-start | bytes 1179656 | tf_op jit(solution)/shard_map/ppermute | solution.py:49
  140.3 40.4 %collective-permute-start.73 = (bf16[2,64,1536]{2,1,0:T(8,128)(2,1)}, bf16[2,64,1536]{2,1,0:T(8,128)(2,1)}, u32[]{:S(2)}, u32[]{:S(2)}) collective-permute-start(bf16[2,64,1536]{2,1,0:T(8,128)(2,1)} %pad_maximum_fusion.17), channel_id=1, source_target_pairs={{0,1},{1,0},{2,3},{3,2},{4,5},{5,4},{6,7},{7,6},{8,9},{9,8},{10,11... | collective-permute-start | bytes 1179656 | tf_op jit(solution)/shard_map/ppermute | solution.py:49
  162.7 78.2 %collective-permute-start.64 = (bf16[2,64,3072]{2,1,0:T(8,128)(2,1)}, bf16[2,64,3072]{2,1,0:T(8,128)(2,1)}, u32[]{:S(2)}, u32[]{:S(2)}) collective-permute-start(bf16[2,64,3072]{2,1,0:T(8,128)(2,1)} %pad_maximum_fusion.15), channel_id=1, source_target_pairs={{0,1},{1,0},{2,3},{3,2},{4,5},{5,4},{6,7},{7,6},{8,9},{9,8},{10,11... | collective-permute-start | bytes 2359304 | tf_op jit(solution)/shard_map/ppermute | solution.py:49
  172.4 32.7 %collective-permute-start.23 = (bf16[2,1,1,128,640]{4,3,2,1,0:T(8,128)(2,1)}, bf16[2,1,1,128,640]{4,3,2,1,0:T(8,128)(2,1)}, u32[]{:S(2)}, u32[]{:S(2)}) collective-permute-start(bf16[2,1,1,128,640]{4,3,2,1,0:T(8,128)(2,1)} %bitcast.806), channel_id=1, source_target_pairs={{0,8},{8,0},{16,24},{24,16},{1,9},{9,1},{17,25},{25,17},{2,10},{10... | collective-permute-start | bytes 983048 | tf_op jit(solution)/shard_map/ppermute | solution.py:49
  176.6 30.6 %collective-permute-start.24 = (bf16[2,1,1,128,640]{4,3,2,1,0:T(8,128)(2,1)}, bf16[2,1,1,128,640]{4,3,2,1,0:T(8,128)(2,1)}, u32[]{:S(2)}, u32[]{:S(2)}) collective-permute-start(bf16[2,1,1,128,640]{4,3,2,1,0:T(8,128)(2,1)} %bitcast.807), channel_id=1, source_target_pairs={{0,2},{1,3},{2,4},{3,5},{4,6},{5,7},{6,0},{7,1},{8,10},{9,11},{10,... | collective-permute-start | bytes 983048 | tf_op jit(solution)/shard_map/ppermute | solution.py:49
  180.7 30.6 %collective-permute-start.14 = (bf16[2,1,1,128,640]{4,3,2,1,0:T(8,128)(2,1)}, bf16[2,1,1,128,640]{4,3,2,1,0:T(8,128)(2,1)S(1)}, u32[]{:S(2)}, u32[]{:S(2)}) collective-permute-start(bf16[2,1,1,128,640]{4,3,2,1,0:T(8,128)(2,1)} %bitcast.809), channel_id=1, source_target_pairs={{0,8},{8,0},{16,24},{24,16},{1,9},{9,1},{17,25},{25,17},{2,10},{10... | collective-permute-start | bytes 983048 | tf_op jit(solution)/shard_map/ppermute | solution.py:49
  213.2 35.2 %collective-permute-start.74 = (bf16[2,64,1536]{2,1,0:T(8,128)(2,1)S(1)}, bf16[2,64,1536]{2,1,0:T(8,128)(2,1)S(1)}, u32[]{:S(2)}, u32[]{:S(2)}) collective-permute-start(bf16[2,64,1536]{2,1,0:T(8,128)(2,1)S(1)} %get-tuple-element.139), channel_id=1, source_target_pairs={{0,16},{8,24},{16,0},{24,8},{1,17},{9,25},{17,1},{25,9},{2,18},{10... | collective-permute-start | bytes 1179656 | tf_op jit(solution)/shard_map/ppermute | solution.py:49
  223.5 52.5 %collective-permute-start.93 = (bf16[96,2048]{1,0:T(8,128)(2,1)}, bf16[96,2048]{1,0:T(8,128)(2,1)}, u32[]{:S(2)}, u32[]{:S(2)}) collective-permute-start(bf16[96,2048]{1,0:T(8,128)(2,1)} %collective-permute-done.92), channel_id=1, source_target_pairs={{0,1},{1,0},{2,3},{3,2},{4,5},{5,4},{6,7},{7,6},{8,9},{9,8},{10,11... | collective-permute-start | bytes 1179656 | tf_op jit(solution)/shard_map/ppermute | solution.py:49
  228.1 86.8 %collective-permute-start.39 = (bf16[2,2,2,160,160]{4,3,1,2,0:T(8,128)(2,1)}, bf16[2,2,2,160,160]{4,3,1,2,0:T(8,128)(2,1)}, u32[]{:S(2)}, u32[]{:S(2)}) collective-permute-start(bf16[2,2,2,160,160]{4,3,1,2,0:T(8,128)(2,1)} %get-tuple-element.56), channel_id=1, source_target_pairs={{0,1},{1,0},{2,3},{3,2},{4,5},{5,4},{6,7},{7,6},{8,9},{9,8},{10,11... | collective-permute-start | bytes 1228808 | tf_op jit(solution)/shard_map/ppermute | solution.py:49
  239.4 61.1 %collective-permute-start.25 = (bf16[2,1,1,128,640]{4,3,2,1,0:T(8,128)(2,1)}, bf16[2,1,1,128,640]{4,3,2,1,0:T(8,128)(2,1)}, u32[]{:S(2)}, u32[]{:S(2)}) collective-permute-start(bf16[2,1,1,128,640]{4,3,2,1,0:T(8,128)(2,1)} %collective-permute-done.24), channel_id=1, source_target_pairs={{0,8},{8,0},{16,24},{24,16},{1,9},{9,1},{17,25},{25,17},{2,10},{10... | collective-permute-start | bytes 983048 | tf_op jit(solution)/shard_map/ppermute | solution.py:49
  241.0 61.5 %collective-permute-start.26 = (bf16[2,1,1,128,640]{4,3,2,1,0:T(8,128)(2,1)}, bf16[2,1,1,128,640]{4,3,2,1,0:T(8,128)(2,1)}, u32[]{:S(2)}, u32[]{:S(2)}) collective-permute-start(bf16[2,1,1,128,640]{4,3,2,1,0:T(8,128)(2,1)} %collective-permute-done.24), channel_id=1, source_target_pairs={{0,2},{1,3},{2,4},{3,5},{4,6},{5,7},{6,0},{7,1},{8,10},{9,11},{10,... | collective-permute-start | bytes 983048 | tf_op jit(solution)/shard_map/ppermute | solution.py:49
  248.4 56.2 %collective-permute-start.16 = (bf16[2,1,1,128,640]{4,3,2,1,0:T(8,128)(2,1)}, bf16[2,1,1,128,640]{4,3,2,1,0:T(8,128)(2,1)}, u32[]{:S(2)}, u32[]{:S(2)}) collective-permute-start(bf16[2,1,1,128,640]{4,3,2,1,0:T(8,128)(2,1)} %collective-permute-done.15), channel_id=1, source_target_pairs={{0,8},{8,0},{16,24},{24,16},{1,9},{9,1},{17,25},{25,17},{2,10},{10... | collective-permute-start | bytes 983048 | tf_op jit(solution)/shard_map/ppermute | solution.py:49
  276.1 30.4 %collective-permute-start.17 = (bf16[2,1,1,128,640]{4,3,2,1,0:T(8,128)(2,1)}, bf16[2,1,1,128,640]{4,3,2,1,0:T(8,128)(2,1)}, u32[]{:S(2)}, u32[]{:S(2)}) collective-permute-start(bf16[2,1,1,128,640]{4,3,2,1,0:T(8,128)(2,1)} %collective-permute-done.15), channel_id=1, source_target_pairs={{0,2},{1,3},{2,4},{3,5},{4,6},{5,7},{6,0},{7,1},{8,10},{9,11},{10,... | collective-permute-start | bytes 983048 | tf_op jit(solution)/shard_map/ppermute | solution.py:49
  304.6 52.4 %collective-permute-start.75 = (bf16[2,1,1,128,1536]{4,3,2,1,0:T(8,128)(2,1)}, bf16[2,1,1,128,1536]{4,3,2,1,0:T(8,128)(2,1)}, u32[]{:S(2)}, u32[]{:S(2)}) collective-permute-start(bf16[2,1,1,128,1536]{4,3,2,1,0:T(8,128)(2,1)} %bitcast.127), channel_id=1, source_target_pairs={{0,8},{8,0},{16,24},{24,16},{1,9},{9,1},{17,25},{25,17},{2,10},{10... | collective-permute-start | bytes 2359304 | tf_op jit(solution)/shard_map/ppermute | solution.py:49
  306.4 48.1 %collective-permute-start.65 = (bf16[2,64,3072]{2,1,0:T(8,128)(2,1)}, bf16[2,64,3072]{2,1,0:T(8,128)(2,1)}, u32[]{:S(2)}, u32[]{:S(2)}) collective-permute-start(bf16[2,64,3072]{2,1,0:T(8,128)(2,1)} %get-tuple-element.102), channel_id=1, source_target_pairs={{0,16},{8,24},{16,0},{24,8},{1,17},{9,25},{17,1},{25,9},{2,18},{10... | collective-permute-start | bytes 2359304 | tf_op jit(solution)/shard_map/ppermute | solution.py:49
  308.9 25.2 %collective-permute-start.27 = (bf16[2,1,1,128,640]{4,3,2,1,0:T(8,128)(2,1)}, bf16[2,1,1,128,640]{4,3,2,1,0:T(8,128)(2,1)}, u32[]{:S(2)}, u32[]{:S(2)}) collective-permute-start(bf16[2,1,1,128,640]{4,3,2,1,0:T(8,128)(2,1)} %collective-permute-done.26), channel_id=1, source_target_pairs={{0,8},{8,0},{16,24},{24,16},{1,9},{9,1},{17,25},{25,17},{2,10},{10... | collective-permute-start | bytes 983048 | tf_op jit(solution)/shard_map/ppermute | solution.py:49
  347.5 34.2 %collective-permute-start.29 = (bf16[2,1,1,128,640]{4,3,2,1,0:T(8,128)(2,1)S(1)}, bf16[2,1,1,128,640]{4,3,2,1,0:T(8,128)(2,1)S(1)}, u32[]{:S(2)}, u32[]{:S(2)}) collective-permute-start(bf16[2,1,1,128,640]{4,3,2,1,0:T(8,128)(2,1)S(1)} %collective-permute-done.28), channel_id=1, source_target_pairs={{0,8},{8,0},{16,24},{24,16},{1,9},{9,1},{17,25},{25,17},{2,10},{10... | collective-permute-start | bytes 983048 | tf_op jit(solution)/shard_map/ppermute | solution.py:49
  353.7 35.5 %collective-permute-start.20 = (bf16[2,1,1,128,640]{4,3,2,1,0:T(8,128)(2,1)S(1)}, bf16[2,1,1,128,640]{4,3,2,1,0:T(8,128)(2,1)S(1)}, u32[]{:S(2)}, u32[]{:S(2)}) collective-permute-start(bf16[2,1,1,128,640]{4,3,2,1,0:T(8,128)(2,1)S(1)} %collective-permute-done.19), channel_id=1, source_target_pairs={{0,8},{8,0},{16,24},{24,16},{1,9},{9,1},{17,25},{25,17},{2,10},{10... | collective-permute-start | bytes 983048 | tf_op jit(solution)/shard_map/ppermute | solution.py:49
  354.5 70.7 %collective-permute-start.51 = (bf16[2,1,1,128,640]{4,3,2,1,0:T(8,128)(2,1)S(1)}, bf16[2,1,1,128,640]{4,3,2,1,0:T(8,128)(2,1)S(1)}, u32[]{:S(2)}, u32[]{:S(2)}) collective-permute-start(bf16[2,1,1,128,640]{4,3,2,1,0:T(8,128)(2,1)S(1)} %collective-permute-done.50), channel_id=1, source_target_pairs={{0,8},{8,0},{16,24},{24,16},{1,9},{9,1},{17,25},{25,17},{2,10},{10... | collective-permute-start | bytes 983048 | tf_op jit(solution)/shard_map/ppermute | solution.py:49
  357.1 172.5 %collective-permute-start.66 = (bf16[2,1,1,128,3072]{4,3,0,2,1:T(8,128)(2,1)}, bf16[2,1,1,128,3072]{4,3,0,2,1:T(8,128)(2,1)}, u32[]{:S(2)}, u32[]{:S(2)}) collective-permute-start(bf16[2,1,1,128,3072]{4,3,0,2,1:T(8,128)(2,1)} %bitcast.109), channel_id=1, source_target_pairs={{0,8},{8,0},{16,24},{24,16},{1,9},{9,1},{17,25},{25,17},{2,10},{10... | collective-permute-start | bytes 4718600 | tf_op jit(solution)/shard_map/ppermute | solution.py:49
  370.5 160.6 %collective-permute-start.67 = (bf16[2,1,1,128,3072]{4,3,0,2,1:T(8,128)(2,1)}, bf16[2,1,1,128,3072]{4,3,0,2,1:T(8,128)(2,1)}, u32[]{:S(2)}, u32[]{:S(2)}) collective-permute-start(bf16[2,1,1,128,3072]{4,3,0,2,1:T(8,128)(2,1)} %bitcast.109), channel_id=1, source_target_pairs={{0,2},{1,3},{2,4},{3,5},{4,6},{5,7},{6,0},{7,1},{8,10},{9,11},{10,... | collective-permute-start | bytes 4718600 | tf_op jit(solution)/shard_map/ppermute | solution.py:49
  427.3 45.2 %collective-permute-start.77 = (bf16[2,1,1,128,1536]{4,3,2,1,0:T(8,128)(2,1)}, bf16[2,1,1,128,1536]{4,3,2,1,0:T(8,128)(2,1)S(1)}, u32[]{:S(2)}, u32[]{:S(2)}) collective-permute-start(bf16[2,1,1,128,1536]{4,3,2,1,0:T(8,128)(2,1)} %collective-permute-done.76), channel_id=1, source_target_pairs={{0,8},{8,0},{16,24},{24,16},{1,9},{9,1},{17,25},{25,17},{2,10},{10... | collective-permute-start | bytes 2359304 | tf_op jit(solution)/shard_map/ppermute | solution.py:49
  442.3 31.4 %collective-permute-start.57 = (bf16[96,2048]{1,0:T(8,128)(2,1)S(1)}, bf16[96,2048]{1,0:T(8,128)(2,1)S(1)}, u32[]{:S(2)}, u32[]{:S(2)}) collective-permute-start(bf16[96,2048]{1,0:T(8,128)(2,1)S(1)} %get-tuple-element.107), channel_id=1, source_target_pairs={{0,1},{1,0},{2,3},{3,2},{4,5},{5,4},{6,7},{7,6},{8,9},{9,8},{10,11... | collective-permute-start | bytes 1179656 | tf_op jit(solution)/shard_map/ppermute | solution.py:49
  511.7 24.7 %collective-permute-start.79 = (bf16[2,1,1,128,1536]{4,3,2,1,0:T(8,128)(2,1)}, bf16[2,1,1,128,1536]{4,3,2,1,0:T(8,128)(2,1)}, u32[]{:S(2)}, u32[]{:S(2)}) collective-permute-start(bf16[2,1,1,128,1536]{4,3,2,1,0:T(8,128)(2,1)} %copy-done.73), channel_id=1, source_target_pairs={{0,8},{8,0},{16,24},{24,16},{1,9},{9,1},{17,25},{25,17},{2,10},{10... | collective-permute-start | bytes 2359304 | tf_op jit(solution)/shard_map/ppermute | solution.py:49
  531.1 40.6 %collective-permute-start.69 = (bf16[2,1,1,128,3072]{4,3,0,2,1:T(8,128)(2,1)}, bf16[2,1,1,128,3072]{4,3,0,2,1:T(8,128)(2,1)}, u32[]{:S(2)}, u32[]{:S(2)}) collective-permute-start(bf16[2,1,1,128,3072]{4,3,0,2,1:T(8,128)(2,1)} %collective-permute-done.67), channel_id=1, source_target_pairs={{0,2},{1,3},{2,4},{3,5},{4,6},{5,7},{6,0},{7,1},{8,10},{9,11},{10,... | collective-permute-start | bytes 4718600 | tf_op jit(solution)/shard_map/ppermute | solution.py:49
  536.4 42.8 %collective-permute-start.68 = (bf16[2,1,1,128,3072]{4,3,0,2,1:T(8,128)(2,1)}, bf16[2,1,1,128,3072]{4,3,0,2,1:T(8,128)(2,1)}, u32[]{:S(2)}, u32[]{:S(2)}) collective-permute-start(bf16[2,1,1,128,3072]{4,3,0,2,1:T(8,128)(2,1)} %collective-permute-done.67), channel_id=1, source_target_pairs={{0,8},{8,0},{16,24},{24,16},{1,9},{9,1},{17,25},{25,17},{2,10},{10... | collective-permute-start | bytes 4718600 | tf_op jit(solution)/shard_map/ppermute | solution.py:49
  538.3 38.7 %collective-permute-start.81 = (bf16[2,1,1,128,1536]{4,3,2,1,0:T(8,128)(2,1)}, bf16[2,1,1,128,1536]{4,3,2,1,0:T(8,128)(2,1)}, u32[]{:S(2)}, u32[]{:S(2)}) collective-permute-start(bf16[2,1,1,128,1536]{4,3,2,1,0:T(8,128)(2,1)} %collective-permute-done.80), channel_id=1, source_target_pairs={{0,8},{8,0},{16,24},{24,16},{1,9},{9,1},{17,25},{25,17},{2,10},{10... | collective-permute-start | bytes 2359304 | tf_op jit(solution)/shard_map/ppermute | solution.py:49
  571.6 38.0 %collective-permute-start.71 = (bf16[2,1,1,128,3072]{4,3,0,2,1:T(8,128)(2,1)}, bf16[2,1,1,128,3072]{4,3,0,2,1:T(8,128)(2,1)S(1)}, u32[]{:S(2)}, u32[]{:S(2)}) collective-permute-start(bf16[2,1,1,128,3072]{4,3,0,2,1:T(8,128)(2,1)} %collective-permute-done.69), channel_id=1, source_target_pairs={{0,2},{1,3},{2,4},{3,5},{4,6},{5,7},{6,0},{7,1},{8,10},{9,11},{10,... | collective-permute-start | bytes 4718600 | tf_op jit(solution)/shard_map/ppermute | solution.py:49
  577.0 35.4 %collective-permute-start.70 = (bf16[2,1,1,128,3072]{4,3,0,2,1:T(8,128)(2,1)}, bf16[2,1,1,128,3072]{4,3,0,2,1:T(8,128)(2,1)S(1)}, u32[]{:S(2)}, u32[]{:S(2)}) collective-permute-start(bf16[2,1,1,128,3072]{4,3,0,2,1:T(8,128)(2,1)} %collective-permute-done.69), channel_id=1, source_target_pairs={{0,8},{8,0},{16,24},{24,16},{1,9},{9,1},{17,25},{25,17},{2,10},{10... | collective-permute-start | bytes 4718600 | tf_op jit(solution)/shard_map/ppermute | solution.py:49
  656.5 50.1 %collective-permute-start.99 = (bf16[96,2048]{1,0:T(8,128)(2,1)S(1)}, bf16[96,2048]{1,0:T(8,128)(2,1)S(1)}, u32[]{:S(2)}, u32[]{:S(2)}) collective-permute-start(bf16[96,2048]{1,0:T(8,128)(2,1)S(1)} %get-tuple-element.97), channel_id=1, source_target_pairs={{0,1},{1,0},{2,3},{3,2},{4,5},{5,4},{6,7},{7,6},{8,9},{9,8},{10,11... | collective-permute-start | bytes 1179656 | tf_op jit(solution)/shard_map/ppermute | solution.py:49
  657.2 27.4 %collective-permute-start.97 = (bf16[96,2048]{1,0:T(8,128)(2,1)S(1)}, bf16[96,2048]{1,0:T(8,128)(2,1)S(1)}, u32[]{:S(2)}, u32[]{:S(2)}) collective-permute-start(bf16[96,2048]{1,0:T(8,128)(2,1)S(1)} %get-tuple-element.96), channel_id=1, source_target_pairs={{0,1},{1,0},{2,3},{3,2},{4,5},{5,4},{6,7},{7,6},{8,9},{9,8},{10,11... | collective-permute-start | bytes 1179656 | tf_op jit(solution)/shard_map/ppermute | solution.py:49
  658.7 56.1 %collective-permute-start.96 = (bf16[96,2048]{1,0:T(8,128)(2,1)S(1)}, bf16[96,2048]{1,0:T(8,128)(2,1)S(1)}, u32[]{:S(2)}, u32[]{:S(2)}) collective-permute-start(bf16[96,2048]{1,0:T(8,128)(2,1)S(1)} %get-tuple-element.95), channel_id=1, source_target_pairs={{0,16},{8,24},{16,0},{24,8},{1,17},{9,25},{17,1},{25,9},{2,18},{10... | collective-permute-start | bytes 1179656 | tf_op jit(solution)/shard_map/ppermute | solution.py:49
  659.5 25.9 %collective-permute-start.94 = (bf16[96,2048]{1,0:T(8,128)(2,1)S(1)}, bf16[96,2048]{1,0:T(8,128)(2,1)S(1)}, u32[]{:S(2)}, u32[]{:S(2)}) collective-permute-start(bf16[96,2048]{1,0:T(8,128)(2,1)S(1)} %get-tuple-element.94), channel_id=1, source_target_pairs={{0,16},{8,24},{16,0},{24,8},{1,17},{9,25},{17,1},{25,9},{2,18},{10... | collective-permute-start | bytes 1179656 | tf_op jit(solution)/shard_map/ppermute | solution.py:49
  669.4 60.6 %collective-permute-start.87 = (bf16[96,2048]{1,0:T(8,128)(2,1)S(1)}, bf16[96,2048]{1,0:T(8,128)(2,1)}, u32[]{:S(2)}, u32[]{:S(2)}) collective-permute-start(bf16[96,2048]{1,0:T(8,128)(2,1)S(1)} %get-tuple-element.101), channel_id=1, source_target_pairs={{0,1},{1,0},{2,3},{3,2},{4,5},{5,4},{6,7},{7,6},{8,9},{9,8},{10,11... | collective-permute-start | bytes 1179656 | tf_op jit(solution)/shard_map/ppermute | solution.py:49
  685.4 49.2 %collective-permute-start.84 = (bf16[96,2048]{1,0:T(8,128)(2,1)}, bf16[96,2048]{1,0:T(8,128)(2,1)}, u32[]{:S(2)}, u32[]{:S(2)}) collective-permute-start(bf16[96,2048]{1,0:T(8,128)(2,1)} %get-tuple-element.99), channel_id=1, source_target_pairs={{0,16},{8,24},{16,0},{24,8},{1,17},{9,25},{17,1},{25,9},{2,18},{10... | collective-permute-start | bytes 1179656 | tf_op jit(solution)/shard_map/ppermute | solution.py:49
  706.6 267.0 %collective-permute-start.152 = (bf16[1024,1536]{1,0:T(8,128)(2,1)}, bf16[1024,1536]{1,0:T(8,128)(2,1)}, u32[]{:S(2)}, u32[]{:S(2)}) collective-permute-start(bf16[1024,1536]{1,0:T(8,128)(2,1)} %convolution_convert_fusion.1), channel_id=1, source_target_pairs={{0,8},{8,0},{16,24},{24,16},{1,9},{9,1},{17,25},{25,17},{2,10},{10... | collective-permute-start | bytes 9437192 | tf_op jit(solution)/shard_map/ppermute | solution.py:49
  788.1 24.4 %collective-permute-start.107 = (f32[4,2,640]{2,1,0:T(2,128)S(1)}, f32[4,2,640]{2,1,0:T(2,128)S(1)}, u32[]{:S(2)}, u32[]{:S(2)}) collective-permute-start(f32[4,2,640]{2,1,0:T(2,128)S(1)} %slice.451), channel_id=1, source_target_pairs={{4,0},{5,1},{6,2},{7,3},{12,8},{13,9},{14,10},{15,11},{20,16},{21,... | collective-permute-start | bytes 61448 | tf_op jit(solution)/shard_map/ppermute | solution.py:49
  812.5 146.6 %collective-permute-start.140 = (bf16[1024,640]{1,0:T(8,128)(2,1)}, bf16[1024,640]{1,0:T(8,128)(2,1)}, u32[]{:S(2)}, u32[]{:S(2)}) collective-permute-start(bf16[1024,640]{1,0:T(8,128)(2,1)} %convolution_convert_fusion.6), channel_id=1, source_target_pairs={{0,8},{8,0},{16,24},{24,16},{1,9},{9,1},{17,25},{25,17},{2,10},{10... | collective-permute-start | bytes 3932168 | tf_op jit(solution)/shard_map/ppermute | solution.py:49
  853.9 29.1 %collective-permute-start.115 = (bf16[96,2048]{1,0:T(8,128)(2,1)S(1)}, bf16[96,2048]{1,0:T(8,128)(2,1)S(1)}, u32[]{:S(2)}, u32[]{:S(2)}) collective-permute-start(bf16[96,2048]{1,0:T(8,128)(2,1)S(1)} %get-tuple-element.93), channel_id=1, source_target_pairs={{0,1},{1,0},{2,3},{3,2},{4,5},{5,4},{6,7},{7,6},{8,9},{9,8},{10,11... | collective-permute-start | bytes 1179656 | tf_op jit(solution)/shard_map/ppermute | solution.py:49
  862.0 28.4 %collective-permute-start.112 = (bf16[96,2048]{1,0:T(8,128)(2,1)S(1)}, bf16[96,2048]{1,0:T(8,128)(2,1)S(1)}, u32[]{:S(2)}, u32[]{:S(2)}) collective-permute-start(bf16[96,2048]{1,0:T(8,128)(2,1)S(1)} %get-tuple-element.91), channel_id=1, source_target_pairs={{0,16},{8,24},{16,0},{24,8},{1,17},{9,25},{17,1},{25,9},{2,18},{10... | collective-permute-start | bytes 1179656 | tf_op jit(solution)/shard_map/ppermute | solution.py:49
  890.5 50.1 %collective-permute-start.136 = (bf16[2,2,2,160,160]{4,3,2,1,0:T(8,128)(2,1)S(1)}, bf16[2,2,2,160,160]{4,3,2,1,0:T(8,128)(2,1)}, u32[]{:S(2)}, u32[]{:S(2)}) collective-permute-start(bf16[2,2,2,160,160]{4,3,2,1,0:T(8,128)(2,1)S(1)} %add_convert_fusion.4), channel_id=1, source_target_pairs={{0,4},{1,5},{2,6},{3,7},{4,0},{5,1},{6,2},{7,3},{8,12},{9,13},{10,... | collective-permute-start | bytes 1228808 | tf_op jit(solution)/shard_map/ppermute | solution.py:49
  897.0 43.5 %collective-permute-start.135 = (bf16[2,2,2,160,160]{4,3,2,1,0:T(8,128)(2,1)S(1)}, bf16[2,2,2,160,160]{4,3,2,1,0:T(8,128)(2,1)}, u32[]{:S(2)}, u32[]{:S(2)}) collective-permute-start(bf16[2,2,2,160,160]{4,3,2,1,0:T(8,128)(2,1)S(1)} %add_convert_fusion.4), channel_id=1, source_target_pairs={{0,2},{1,3},{2,4},{3,5},{4,6},{5,7},{6,0},{7,1},{8,10},{9,11},{10,... | collective-permute-start | bytes 1228808 | tf_op jit(solution)/shard_map/ppermute | solution.py:49
  901.0 41.4 %collective-permute-start.116 = (f32[2,2,4,2,64]{4,3,2,1,0:T(2,128)S(1)}, f32[2,2,4,2,64]{4,3,2,1,0:T(2,128)S(1)}, u32[]{:S(2)}, u32[]{:S(2)}) collective-permute-start(f32[2,2,4,2,64]{4,3,2,1,0:T(2,128)S(1)} %fusion.106), channel_id=1, source_target_pairs={{0,8},{8,0},{16,24},{24,16},{1,9},{9,1},{17,25},{25,17},{2,10},{10... | collective-permute-start | bytes 24584 | tf_op jit(solution)/shard_map/ppermute | solution.py:49
  950.8 111.2 %collective-permute-start.146 = (bf16[1024,3072]{1,0:T(8,128)(2,1)}, bf16[1024,3072]{1,0:T(8,128)(2,1)S(1)}, u32[]{:S(2)}, u32[]{:S(2)}) collective-permute-start(bf16[1024,3072]{1,0:T(8,128)(2,1)} %convolution_convert_fusion), channel_id=1, source_target_pairs={{0,8},{8,0},{16,24},{24,16},{1,9},{9,1},{17,25},{25,17},{2,10},{10... | collective-permute-start | bytes 18874376 | tf_op jit(solution)/shard_map/ppermute | solution.py:49
  950.8 66.2 %collective-permute-start.122 = (bf16[1024,1280]{1,0:T(8,128)(2,1)}, bf16[1024,1280]{1,0:T(8,128)(2,1)S(1)}, u32[]{:S(2)}, u32[]{:S(2)}) collective-permute-start(bf16[1024,1280]{1,0:T(8,128)(2,1)} %convolution_convert_fusion.2), channel_id=1, source_target_pairs={{0,8},{8,0},{16,24},{24,16},{1,9},{9,1},{17,25},{25,17},{2,10},{10... | collective-permute-start | bytes 7864328 | tf_op jit(solution)/shard_map/ppermute | solution.py:49
  971.1 26.3 %collective-permute-start.139 = (bf16[2,2,2,2,160,160]{5,4,2,3,1,0:T(8,128)(2,1)S(1)}, bf16[2,2,2,2,160,160]{5,4,2,3,1,0:T(8,128)(2,1)S(1)}, u32[]{:S(2)}, u32[]{:S(2)}) collective-permute-start(bf16[2,2,2,2,160,160]{5,4,2,3,1,0:T(8,128)(2,1)S(1)} %copy_dynamic-update-slice_fusion), channel_id=1, source_target_pairs={{0,16},{8,24},{16,0},{24,8},{1,17},{9,25},{17,1},{25,9},{2,18},{10... | collective-permute-start | bytes 2457608 | tf_op jit(solution)/shard_map/ppermute | solution.py:49
  978.5 28.9 %collective-permute-start.153 = (bf16[256,1536]{1,0:T(8,128)(2,1)S(1)}, bf16[256,1536]{1,0:T(8,128)(2,1)S(1)}, u32[]{:S(2)}, u32[]{:S(2)}) collective-permute-start(bf16[256,1536]{1,0:T(8,128)(2,1)S(1)} %fusion.42), channel_id=1, source_target_pairs={{0,2},{1,3},{2,4},{3,5},{4,6},{5,7},{6,0},{7,1},{8,10},{9,11},{10,... | collective-permute-start | bytes 2359304 | tf_op jit(solution)/shard_map/ppermute | solution.py:49
  1019.3 24.8 %collective-permute-start.123 = (bf16[256,1280]{1,0:T(8,128)(2,1)S(1)}, bf16[256,1280]{1,0:T(8,128)(2,1)S(1)}, u32[]{:S(2)}, u32[]{:S(2)}) collective-permute-start(bf16[256,1280]{1,0:T(8,128)(2,1)S(1)} %fusion.68), channel_id=1, source_target_pairs={{0,2},{1,3},{2,4},{3,5},{4,6},{5,7},{6,0},{7,1},{8,10},{9,11},{10,... | collective-permute-start | bytes 1966088 | tf_op jit(solution)/shard_map/ppermute | solution.py:49
  1030.3 30.7 %collective-permute-start.155 = (bf16[256,1536]{1,0:T(8,128)(2,1)S(1)}, bf16[256,1536]{1,0:T(8,128)(2,1)S(1)}, u32[]{:S(2)}, u32[]{:S(2)}) collective-permute-start(bf16[256,1536]{1,0:T(8,128)(2,1)S(1)} %fusion.32), channel_id=1, source_target_pairs={{0,2},{1,3},{2,4},{3,5},{4,6},{5,7},{6,0},{7,1},{8,10},{9,11},{10,... | collective-permute-start | bytes 2359304 | tf_op jit(solution)/shard_map/ppermute | solution.py:49
  1044.3 29.3 %collective-permute-start.124 = (bf16[256,1280]{1,0:T(8,128)(2,1)S(1)}, bf16[256,1280]{1,0:T(8,128)(2,1)S(1)}, u32[]{:S(2)}, u32[]{:S(2)}) collective-permute-start(bf16[256,1280]{1,0:T(8,128)(2,1)S(1)} %fusion.35), channel_id=1, source_target_pairs={{0,2},{1,3},{2,4},{3,5},{4,6},{5,7},{6,0},{7,1},{8,10},{9,11},{10,... | collective-permute-start | bytes 1966088 | tf_op jit(solution)/shard_map/ppermute | solution.py:49
  1073.5 39.2 %collective-permute-start.147 = (bf16[256,3072]{1,0:T(8,128)(2,1)S(1)}, bf16[256,3072]{1,0:T(8,128)(2,1)S(1)}, u32[]{:S(2)}, u32[]{:S(2)}) collective-permute-start(bf16[256,3072]{1,0:T(8,128)(2,1)S(1)} %fusion.29), channel_id=1, source_target_pairs={{0,2},{1,3},{2,4},{3,5},{4,6},{5,7},{6,0},{7,1},{8,10},{9,11},{10,... | collective-permute-start | bytes 4718600 | tf_op jit(solution)/shard_map/ppermute | solution.py:49
  1073.8 53.0 %collective-permute-start.125 = (bf16[256,1280]{1,0:T(8,128)(2,1)S(1)}, bf16[256,1280]{1,0:T(8,128)(2,1)S(1)}, u32[]{:S(2)}, u32[]{:S(2)}) collective-permute-start(bf16[256,1280]{1,0:T(8,128)(2,1)S(1)} %fusion.36), channel_id=1, source_target_pairs={{0,2},{1,3},{2,4},{3,5},{4,6},{5,7},{6,0},{7,1},{8,10},{9,11},{10,... | collective-permute-start | bytes 1966088 | tf_op jit(solution)/shard_map/ppermute | solution.py:49
  1113.2 42.1 %collective-permute-start.148 = (bf16[256,3072]{1,0:T(8,128)(2,1)S(1)}, bf16[256,3072]{1,0:T(8,128)(2,1)S(1)}, u32[]{:S(2)}, u32[]{:S(2)}) collective-permute-start(bf16[256,3072]{1,0:T(8,128)(2,1)S(1)} %fusion.10), channel_id=1, source_target_pairs={{0,2},{1,3},{2,4},{3,5},{4,6},{5,7},{6,0},{7,1},{8,10},{9,11},{10,... | collective-permute-start | bytes 4718600 | tf_op jit(solution)/shard_map/ppermute | solution.py:49
  1127.0 29.0 %collective-permute-start.126 = (bf16[2,64,1280]{2,1,0:T(8,128)(2,1)S(1)}, bf16[2,64,1280]{2,1,0:T(8,128)(2,1)S(1)}, u32[]{:S(2)}, u32[]{:S(2)}) collective-permute-start(bf16[2,64,1280]{2,1,0:T(8,128)(2,1)S(1)} %dynamic-slice_bitcast_fusion.8), channel_id=1, source_target_pairs={{0,16},{8,24},{16,0},{24,8},{1,17},{9,25},{17,1},{25,9},{2,18},{10... | collective-permute-start | bytes 983048 | tf_op jit(solution)/shard_map/ppermute | solution.py:49
  1155.9 30.7 %collective-permute-start.149 = (bf16[256,3072]{1,0:T(8,128)(2,1)S(1)}, bf16[256,3072]{1,0:T(8,128)(2,1)S(1)}, u32[]{:S(2)}, u32[]{:S(2)}) collective-permute-start(bf16[256,3072]{1,0:T(8,128)(2,1)S(1)} %fusion.11), channel_id=1, source_target_pairs={{0,2},{1,3},{2,4},{3,5},{4,6},{5,7},{6,0},{7,1},{8,10},{9,11},{10,... | collective-permute-start | bytes 4718600 | tf_op jit(solution)/shard_map/ppermute | solution.py:49
  1156.1 32.2 %collective-permute-start.127 = (bf16[2,64,1280]{2,1,0:T(8,128)(2,1)S(1)}, bf16[2,64,1280]{2,1,0:T(8,128)(2,1)S(1)}, u32[]{:S(2)}, u32[]{:S(2)}) collective-permute-start(bf16[2,64,1280]{2,1,0:T(8,128)(2,1)S(1)} %get-tuple-element.159), channel_id=1, source_target_pairs={{0,1},{1,0},{2,3},{3,2},{4,5},{5,4},{6,7},{7,6},{8,9},{9,8},{10,11... | collective-permute-start | bytes 983048 | tf_op jit(solution)/shard_map/ppermute | solution.py:49
  (204 other events, 3115.0 us)

commit v2 on v1

v2 whole, which is shorter than its diff:
```python
import functools

import jax
import jax.numpy as jnp
from jax import lax
from jax.experimental import pallas as pl
from jax.experimental.pallas import tpu as pltpu
from jax.sharding import PartitionSpec as P

NORM_EPS = 1e-06
F32 = jnp.float32
BF16 = jnp.bfloat16
TAPS = 4
HALO = 8


class Grid:
    def __init__(self, n_seq, n_blk):
        core = 2 if n_seq % 2 == 0 else 1
        nx = max(d for d in range(1, n_blk + 1) if d * d <= n_blk and n_blk % d == 0)
        self.n = {"y": n_seq // core, "c": core, "z": n_blk // nx, "x": nx}
        self.n_blk = n_blk

    def index(self, part):
        seq, blk = lax.axis_index("seq"), lax.axis_index("blk")
        return {
            "y": seq // self.n["c"],
            "c": seq % self.n["c"],
            "z": blk // self.n["x"],
            "x": blk % self.n["x"],
        }[part]

    def shift(self, value, part, by, wrap=True):
        outer, inner, axis = {
            "y": ("y", "c", "seq"),
            "c": ("y", "c", "seq"),
            "z": ("z", "x", "blk"),
            "x": ("z", "x", "blk"),
        }[part]
        pairs = []
        for o in range(self.n[outer]):
            for i in range(self.n[inner]):
                p = (o if part == outer else i) + by
                if not wrap and not 0 <= p < self.n[part]:
                    continue
                p = p % self.n[part]
                to = (p, i) if part == outer else (o, p)
                pairs.append((o * self.n[inner] + i, to[0] * self.n[inner] + to[1]))
        return lax.ppermute(value, axis, pairs)

    def shift_plane(self, value, by_y, by_x):
        ny, nc, nz, nx = (self.n[p] for p in "yczx")
        pairs = []
        for y in range(ny):
            for c in range(nc):
                for z in range(nz):
                    for x in range(nx):
                        to = (((y + by_y) % ny * nc + c) * nz + z) * nx + (x + by_x) % nx
                        pairs.append((((y * nc + c) * nz + z) * nx + x, to))
        return lax.ppermute(value, ("seq", "blk"), pairs)

    def place(self, by_shift, part):
        n, me = self.n[part], self.index(part)
        if n == 1:
            return by_shift[0][None]
        if n == 2:
            here, there = by_shift
            low = me == 0
            return jnp.stack([jnp.where(low, here, there), jnp.where(low, there, here)])
        out = jnp.zeros((n, *by_shift[0].shape), by_shift[0].dtype)
        for r, value in enumerate(by_shift):
            out = lax.dynamic_update_index_in_dim(out, value, (me - r) % n, 0)
        return out

    def gather(self, value, part):
        n = self.n[part]
        return self.place([value] + [self.shift(value, part, r) for r in range(1, n)], part)

    def exchange(self, value, part, dim):
        n, me = self.n[part], self.index(part)
        got = []
        for r in range(n):
            piece = lax.dynamic_index_in_dim(value, (me + r) % n, dim, keepdims=False)
            got.append(self.shift(piece, part, r) if r else piece)
        return self.place(got, part)

    def total(self, value, part, *late):
        out = value.astype(F32)
        for r in range(1, self.n[part]):
            out = out + after(self.shift(value, part, r), *late).astype(F32)
        return out.astype(value.dtype)

    def turn(self, value, back=False):
        ny, nc, nz = self.n["y"], self.n["c"], self.n["z"]
        places = [
            (y * nc + c) * nz + z for c in range(nc) for z in range(nz) for y in range(ny)
        ]
        width = value.shape[-1] // len(places)
        if width % 128:
            cut = value.reshape(*value.shape[:-1], *((nc, nz, ny) if back else (ny, nc, nz)), width)
            k = value.ndim - 1
            order = (k + 2, k, k + 1) if back else (k + 1, k + 2, k)
            return cut.transpose(tuple(range(k)) + order + (k + 3,)).reshape(value.shape)

        def kernel(src, dst):
            for k, place in enumerate(places):
                here, there = pl.ds(k * width, width), pl.ds(place * width, width)
                if back:
                    dst[:, :, there] = src[:, :, here]
                else:
                    dst[:, :, here] = src[:, :, there]

        return pl.pallas_call(
            kernel,
            out_shape=jax.ShapeDtypeStruct(value.shape, value.dtype),
            cost_estimate=pl.CostEstimate(flops=0, bytes_accessed=4 * value.size, transcendentals=0),
        )(value)

    def spread(self, shard, *late, normed=False):
        nx, ny = self.n["x"], self.n["y"]
        micro, step, width = shard.shape
        got = {(0, 0): shard}
        for r in range(1, nx):
            got[0, r] = after(self.shift(shard, "x", r), *late)
        for r in range(1, ny):
            got[r, 0] = after(self.shift(shard, "y", r), *late)
        hop = [v for k, v in got.items() if k != (0, 0)]
        out = []
        for m in range(micro):
            for ry in range(ny):
                for rx in range(nx):
                    if ry == 0 or rx == 0:
                        out.append((got[ry, rx], m))
                    elif m % 2 == 0:
                        out.append((self.shift(got[0, rx][m], "y", ry), None))
                    else:
                        out.append((self.shift(got[ry, 0][m], "x", rx), None))
        rows = assemble_rows(out, step, width, normed)
        return rows.reshape(len(out) * step, width), hop

    def collect(self, partial, micro):
        nx, ny = self.n["x"], self.n["y"]
        part = partial.reshape(micro, ny, nx, -1, partial.shape[1])
        out = []
        for m in range(micro):
            if m % 2 == 0:
                held = part[m, 0].astype(F32)
                for r in range(1, ny):
                    held = held + self.shift(part[m, r], "y", -r).astype(F32)
                last, n = "x", nx
            else:
                held = part[m, :, 0].astype(F32)
                for r in range(1, nx):
                    held = held + self.shift(part[m, :, r], "x", -r).astype(F32)
                last, n = "y", ny
            total = held[0]
            for r in range(1, n):
                total = total + self.shift(held[r].astype(BF16), last, -r).astype(F32)
            out.append(total)
        return jnp.stack(out)

    def columns_of(self, pieces, *late):
        nx, ny = self.n["x"], self.n["y"]
        x, y = self.index("x"), self.index("y")

        def take(yy, xx):
            out = []
            for w in pieces:
                width = w.shape[1] // (nx * ny)
                out.append(lax.dynamic_slice_in_dim(w, (yy * nx + xx) * width, width, 1))
            return out[0] if len(out) == 1 else jnp.concatenate(out, axis=1)

        rows = []
        for ry in range(ny):
            got = []
            for rx in range(nx):
                piece = take((y + ry) % ny, (x + rx) % nx)
                got.append(after(self.shift_plane(piece, ry, rx), *late) if ry or rx else piece)
            rows.append(self.place(got, "x"))
        return self.place(rows, "y")

    def ring_first(self, block):
        if self.n["z"] != 4:
            return (self.shift(block, "z", -1),)
        return self.shift(block, "z", -1), self.shift(block, "z", 1)

    def ring_rest(self, block, first, *late):
        nz = self.n["z"]
        first = [after(v, *late) for v in first]
        if nz != 4:
            out = [block, first[0]]
            for _ in range(2, nz):
                out.append(self.shift(out[-1], "z", -1))
            return out[:nz]
        half = block.shape[0] // 2
        above, below = first
        far = [self.shift(above[:half], "z", -1), self.shift(below[half:], "z", 1)]
        return [block, above, *far, below]

    def whole_rows(self, pieces, *cuts):
        nc, nz = self.n["c"], self.n["z"]
        c, z = self.index("c"), self.index("z")
        block = sum(p.shape[0] for p in pieces) // nz
        starts = [sum(p.shape[0] for p in pieces[:i]) for i in range(len(pieces))]
        parts, places = [], []
        for s in range(nc):
            parts += [self.shift(p, "c", -s) if s else p for p in pieces]
            for at in starts:
                where = ((c + s) % nc * nz + (z + at // block) % nz) * block + at % block
                places.append(where)
        places = jnp.stack(places).astype(jnp.int32)
        return [assemble_tall(parts, places, i, len(cuts)) for i in cuts]

    def z_groups(self):
        nz, nx = self.n["z"], self.n["x"]
        return [[z * nx + x for z in range(nz)] for x in range(nx)]

    def all_rows(self, block):
        ny, nc, nz, nx = (self.n[p] for p in "yczx")
        groups = [
            [((y * nc + c) * nz + z) * nx + x for c in range(nc) for z in range(nz)]
            for y in range(ny)
            for x in range(nx)
        ]
        return lax.all_gather(
            block, ("seq", "blk"), axis=0, tiled=True, axis_index_groups=groups
        )

    def to_owners(self, done, *late):
        nx, ny = self.n["x"], self.n["y"]
        x, y = self.index("x"), self.index("y")
        rows = []
        for ry in range(ny):
            got = []
            for rx in range(nx):
                piece = lax.dynamic_slice(
                    done, ((y + ry) % ny, (x + rx) % nx, 0, 0), (1, 1, *done.shape[2:])
                )[0, 0]
                got.append(after(self.shift_plane(piece, ry, rx), *late) if ry or rx else piece)
            rows.append(self.place(got, "x"))
        return self.place(rows, "y")


class WeightSum:
    def __init__(self, grid, left, right):
        self.grid, self.left, self.right = grid, left, right
        self.share = left.shape[1] // grid.n["c"]

    def product(self, core):
        cut = lax.dynamic_slice_in_dim(self.left, core * self.share, self.share, 1)
        return lax.dot_general(
            cut, self.right, (((0,), (0,)), ((), ())), preferred_element_type=F32
        )

    def meet(self):
        grid, nc = self.grid, self.grid.n["c"]
        c = grid.index("c")
        others = [
            grid.shift(self.product((c + s) % nc).astype(BF16), "c", s) for s in range(1, nc)
        ]
        mine = self.product(c)
        for other in others:
            mine = mine + other.astype(F32)
        self.mine = mine

    def along_z(self, *late):
        self.done = lax.psum_scatter(
            after(self.mine.astype(BF16), *late),
            "blk",
            scatter_dimension=0,
            tiled=True,
            axis_index_groups=self.grid.z_groups(),
        )

    def slab(self, r):
        nz = self.grid.n["z"]
        rows = self.share // nz
        at = (self.grid.index("z") + r) % nz * rows
        return lax.dynamic_slice_in_dim(self.mine, at, rows, 0)

    def step_one(self, *late):
        low = after(self.slab(2).astype(BF16), *late)
        half = low.shape[0] // 2
        self.first = [
            self.grid.shift(low[:half], "z", 1),
            self.grid.shift(low[half:], "z", -1),
        ]

    def step_two(self, *late):
        grid = self.grid
        up, down = [after(v, *late).astype(F32) for v in self.first]
        half = up.shape[0]
        above, below = self.slab(1), self.slab(3)
        to_up = jnp.concatenate([above[:half] + up, above[half:]], axis=0).astype(BF16)
        to_down = jnp.concatenate([below[:half], below[half:] + down], axis=0).astype(BF16)
        self.second = [grid.shift(to_up, "z", 1), grid.shift(to_down, "z", -1)]

    def join(self, *late):
        second = [after(v, *late).astype(F32) for v in self.second]
        self.done = (self.slab(0) + (second[0] + second[1])).astype(BF16)

    def finish(self, count, *late):
        grid = self.grid
        ny, nx = grid.n["y"], grid.n["x"]
        width = self.done.shape[1] // count
        done = after(self.done, *late).reshape(ny, nx, -1, self.done.shape[1])
        side = grid.to_owners(done)
        return [
            jnp.concatenate(
                [
                    side[yy, xx, :, i * width : (i + 1) * width].astype(F32)
                    for yy in range(ny)
                    for xx in range(nx)
                ],
                axis=1,
            )
            for i in range(count)
        ]


def after(value, *others):
    return lax.optimization_barrier((value, *others))[0]


def assemble_rows(pieces, step, width, normed):
    arrays = []
    for value, _ in pieces:
        if not any(value is a for a in arrays):
            arrays.append(value)
    which = [next(i for i, a in enumerate(arrays) if a is value) for value, _ in pieces]
    cut = 32 if step % 32 == 0 else step

    def kernel(*refs):
        out = refs[-1]
        for k, (_, lead) in enumerate(pieces):
            ref = refs[which[k]]
            block = ref[...] if lead is None else ref[lead]
            if normed:
                block = block.astype(F32)
                square = jnp.mean(block * block, axis=-1, keepdims=True)
                block = (block * lax.rsqrt(square + NORM_EPS)).astype(out.dtype)
            out[k] = block

    specs = []
    for a in arrays:
        if a.ndim == 2:
            specs.append(pl.BlockSpec((cut, width), lambda i: (i, 0)))
        else:
            specs.append(pl.BlockSpec((a.shape[0], cut, width), lambda i: (0, i, 0)))
    count = len(pieces)
    return pl.pallas_call(
        kernel,
        grid=(step // cut,),
        in_specs=specs,
        out_specs=pl.BlockSpec((count, cut, width), lambda i: (0, i, 0)),
        out_shape=jax.ShapeDtypeStruct((count, step, width), BF16),
        compiler_params=pltpu.CompilerParams(vmem_limit_bytes=32 * 1024 * 1024),
        cost_estimate=pl.CostEstimate(
            flops=0, bytes_accessed=4 * count * step * width, transcendentals=0
        ),
    )(*arrays)


def assemble_tall(pieces, places, part, parts):
    width = pieces[0].shape[1] // parts
    total = sum(p.shape[0] for p in pieces)
    cut = next((t for t in (512, 640, 128) if width % t == 0), width)
    steps = width // cut

    def kernel(where, *refs):
        out = refs[-1]
        for i, ref in enumerate(refs[:-1]):
            out[pl.ds(pl.multiple_of(where[i], 64), ref.shape[0])] = ref[...]

    if cut % 128 and parts > 1:
        pieces = [p[:, part * width : (part + 1) * width] for p in pieces]
        part = 0
    return pl.pallas_call(
        kernel,
        grid_spec=pltpu.PrefetchScalarGridSpec(
            num_scalar_prefetch=1,
            grid=(steps,),
            in_specs=[
                pl.BlockSpec((p.shape[0], cut), lambda i, where: (0, i + part * steps))
                for p in pieces
            ],
            out_specs=pl.BlockSpec((total, cut), lambda i, where: (0, i)),
        ),
        out_shape=jax.ShapeDtypeStruct((total, width), BF16),
        compiler_params=pltpu.CompilerParams(vmem_limit_bytes=32 * 1024 * 1024),
        cost_estimate=pl.CostEstimate(flops=0, bytes_accessed=4 * total * width, transcendentals=0),
    )(places, *pieces)


def pack_small(rate_weight, input_weight, small):
    heads, block, _ = rate_weight.shape
    rows = heads * block
    by_head = jnp.moveaxis(small.reshape(8, heads, block), 1, 0)
    by_head = jnp.pad(by_head, ((0, 0), (0, 8), (0, 0))).reshape(heads * 16, block)

    def kernel(rate, gate_in, values, out):
        for h in range(heads):
            out[0, h * block : (h + 1) * block] = rate[h]
            out[1, h * block : (h + 1) * block] = gate_in[h]
        rest = values[...]
        for t in range(3):
            high = rest.astype(BF16)
            at = rows + t * heads * 16
            out[0, at : at + heads * 16] = high
            out[1, at : at + heads * 16] = high
            rest = rest - high.astype(F32)

    return pl.pallas_call(
        kernel,
        out_shape=jax.ShapeDtypeStruct((2, rows + 48 * heads, block), BF16),
        cost_estimate=pl.CostEstimate(flops=0, bytes_accessed=8 * rows * block, transcendentals=0),
    )(rate_weight, input_weight, by_head)


def unpack_small(halves, place, per, heads):
    _, _, depth, block = halves.shape
    rows = heads * block
    width = per * rows

    def kernel(which, share, gates, vec):
        row = lax.broadcasted_iota(jnp.int32, (block, width), 0)
        column = lax.broadcasted_iota(jnp.int32, (block, width), 1)
        total = jnp.zeros((16, width), F32)
        for p in range(per):
            for h in range(heads):
                head = p * heads + h
                pick = jnp.where(column == row + head * block, 1.0, 0.0).astype(BF16)
                for g in range(2):
                    part = share[g, p, h * block : (h + 1) * block]
                    gates[g, head * block : (head + 1) * block] = jnp.dot(
                        part, pick, preferred_element_type=F32
                    ).astype(BF16)
                for t in range(3):
                    at = rows + (t * heads + h) * 16
                    total = total + jnp.dot(
                        share[0, p, at : at + 16], pick, preferred_element_type=F32
                    )
        vec[...] = total[0:8]

    return pl.pallas_call(
        kernel,
        grid_spec=pltpu.PrefetchScalarGridSpec(
            num_scalar_prefetch=1,
            grid=(1,),
            in_specs=[pl.BlockSpec((2, per, depth, block), lambda i, which: (0, which[0], 0, 0))],
            out_specs=[
                pl.BlockSpec((2, width, width), lambda i, which: (0, 0, 0)),
                pl.BlockSpec((8, width), lambda i, which: (0, 0)),
            ],
        ),
        out_shape=[
            jax.ShapeDtypeStruct((2, width, width), BF16),
            jax.ShapeDtypeStruct((8, width), F32),
        ],
        compiler_params=pltpu.CompilerParams(vmem_limit_bytes=32 * 1024 * 1024),
        cost_estimate=pl.CostEstimate(
            flops=0, bytes_accessed=4 * width * width, transcendentals=0
        ),
    )(place.astype(jnp.int32)[None], halves)


def decay_terms(rate, slope):
    log_decay = rate * slope
    small = 1.0 / 40320.0
    for div in (5040.0, 720.0, 120.0, 24.0, 6.0, 2.0, 1.0):
        small = small * log_decay + 1.0 / div
    less = jnp.where(log_decay < -0.4, jnp.exp(log_decay) - 1.0, log_decay * small)
    decay = 1.0 + less
    square = -less * (1.0 + decay)
    return decay, square


def split_dot(value, weight):
    high = value.astype(BF16)
    rest = (value - high.astype(F32)).astype(BF16)
    return jnp.dot(high, weight, preferred_element_type=F32) + jnp.dot(
        rest, weight, preferred_element_type=F32
    )


def forward_kernel(order, u, halo, same, vec, gates, conv, rate, gate_in, state, prods, ends, rows, keep_a, keep_b):
    nx, step = u.shape[1], u.shape[2]
    length = nx * step
    rows[0:HALO] = halo[0]
    for i in range(nx):
        rows[HALO + i * step : HALO + (i + 1) * step] = u[0, order[i]].astype(F32)
    filtered = vec[4:5] + rows[HALO : HALO + length] * vec[0:1]
    for k in range(1, TAPS):
        filtered = filtered + rows[HALO - k : HALO - k + length] * same[0, :, k : k + 1] * vec[k : k + 1]
    conv[0] = filtered
    r_gate = jax.nn.sigmoid(split_dot(filtered, gates[0]) + vec[5:6])
    i_gate = jax.nn.sigmoid(split_dot(filtered, gates[1]) + vec[6:7])
    rate[0] = r_gate
    gate_in[0] = i_gate
    decay, square = decay_terms(r_gate, vec[7:8])
    a = decay * same[0, :, 1:2]
    b = jnp.sqrt(square) * i_gate * filtered
    width = a.shape[1]
    tiles = length // 8
    a = a.reshape(tiles, 8, width)
    b = b.reshape(tiles, 8, width)
    row = lax.broadcasted_iota(jnp.int32, (tiles, 8, width), 1)
    for d in (1, 2, 4):
        a_back = jnp.where(row >= d, pltpu.roll(a, d, 1), 1.0)
        b_back = jnp.where(row >= d, pltpu.roll(b, d, 1), 0.0)
        b = b + a * b_back
        a = a * a_back
    keep_a[...] = a.reshape(length, width)
    keep_b[...] = b.reshape(length, width)
    carry_s = jnp.zeros((1, width), F32)
    carry_a = jnp.ones((1, width), F32)
    for t in range(tiles):
        at = keep_a[t * 8 : t * 8 + 8]
        bt = keep_b[t * 8 : t * 8 + 8]
        s = bt + at * carry_s
        p = at * carry_a
        at_row = (t * 8) % step
        state[0, order[t * 8 // step], at_row : at_row + 8] = s
        prods[0, order[t * 8 // step], at_row : at_row + 8] = p
        carry_s = s[7:8]
        carry_a = p[7:8]
    ends[0, 0:1] = carry_a
    ends[0, 1:2] = carry_s
    ends[0, 2:8] = jnp.zeros((6, width), F32)


def reverse_kernel(order, d_state, same, vec, rate, grads, prods, ends, keep_g, keep_a):
    nx, step = d_state.shape[1], d_state.shape[2]
    length = nx * step
    width = rate.shape[2]
    decay, _ = decay_terms(rate[0], vec[7:8])
    a = decay * same[0, :, 1:2]
    keep_a[0:length] = a
    keep_a[length : length + 8] = jnp.ones((8, width), F32)
    for i in range(nx):
        keep_g[i * step : (i + 1) * step] = d_state[0, order[i]].astype(F32)
    first = a[0:1]
    tiles = length // 8
    nxt = keep_a[1 : length + 1].reshape(tiles, 8, width)
    g = keep_g[...].reshape(tiles, 8, width)
    row = lax.broadcasted_iota(jnp.int32, (tiles, 8, width), 1)
    p = nxt
    for d in (1, 2, 4):
        g_ahead = jnp.where(row < 8 - d, pltpu.roll(g, 8 - d, 1), 0.0)
        p_ahead = jnp.where(row < 8 - d, pltpu.roll(p, 8 - d, 1), 1.0)
        g = g + p * g_ahead
        p = p * p_ahead
    keep_g[...] = g.reshape(length, width)
    keep_a[0:length] = p.reshape(length, width)
    carry_g = jnp.zeros((1, width), F32)
    carry_p = jnp.ones((1, width), F32)
    for t in reversed(range(tiles)):
        pt = keep_a[t * 8 : t * 8 + 8]
        gt = keep_g[t * 8 : t * 8 + 8] + pt * carry_g
        pt = pt * carry_p
        grads[0, t * 8 : t * 8 + 8] = gt
        prods[0, t * 8 : t * 8 + 8] = pt
        carry_g = gt[0:1]
        carry_p = pt[0:1]
    ends[0, 0:1] = first * carry_p
    ends[0, 1:2] = first * carry_g
    ends[0, 2:8] = jnp.zeros((6, width), F32)


def final_kernel(
    order, u, halo, same, vec, gates, conv, rate, gate_in, state, prods, start, grads, back, carry,
    d_u, head, d_rate, d_input, sums, rows, tail,
):
    nx, step = u.shape[1], u.shape[2]
    length = nx * step
    width = conv.shape[2]
    d_s = grads[0] + back[0] * carry[0, 0:1]
    for i in range(nx):
        rows[HALO + i * step : HALO + (i + 1) * step] = (
            state[0, order[i]] + prods[0, order[i]] * start[0, 0:1]
        )
    rows[HALO - 1 : HALO] = start[0, 0:1]
    s_prev = rows[HALO - 1 : HALO - 1 + length]
    r_gate, i_gate, filtered = rate[0], gate_in[0], conv[0]
    decay, square = decay_terms(r_gate, vec[7:8])
    inverse = lax.rsqrt(jnp.maximum(square, 1e-37))
    scale = square * inverse
    a = decay * same[0, :, 1:2]
    d_scaled = d_s * i_gate * filtered
    d_log = d_s * s_prev * a - d_scaled * (decay * decay) * inverse
    d_i = d_s * scale * filtered * i_gate * (1.0 - i_gate)
    d_r = d_log * vec[7:8] * r_gate * (1.0 - r_gate)
    d_r_low = d_r.astype(BF16)
    d_i_low = d_i.astype(BF16)
    d_rate[0] = d_r_low
    d_input[0] = d_i_low
    back_dims = (((1,), (1,)), ((), ()))
    d_c = (
        d_s * scale * i_gate
        + lax.dot_general(d_r_low, gates[0], back_dims, preferred_element_type=F32)
        + lax.dot_general(d_i_low, gates[1], back_dims, preferred_element_type=F32)
    )
    rows[0:HALO] = halo[0]
    for i in range(nx):
        rows[HALO + i * step : HALO + (i + 1) * step] = u[0, order[i]].astype(F32)

    def column(value):
        return jnp.sum(value, axis=0, keepdims=True)

    parts = [column(d_c * rows[HALO : HALO + length])]
    tail[0:HALO] = jnp.zeros((HALO, width), F32)
    tail[HALO + length : 2 * HALO + length] = jnp.zeros((HALO, width), F32)
    d_rows = d_c * vec[0:1]
    d_head = jnp.zeros((HALO, width), F32)
    for k in range(1, TAPS):
        masked = d_c * same[0, :, k : k + 1]
        parts.append(column(masked * rows[HALO - k : HALO - k + length]))
        tail[HALO : HALO + length] = masked * vec[k : k + 1]
        d_rows = d_rows + tail[HALO + k : HALO + k + length]
        d_head = d_head + tail[k : k + HALO]
    for i in range(nx):
        d_u[0, order[i]] = d_rows[i * step : (i + 1) * step]
    head[0] = d_head
    parts += [column(d_c), column(d_r), column(d_i), column(d_log * r_gate)]

    @pl.when(pl.program_id(0) == 0)
    def _():
        sums[...] = jnp.zeros_like(sums)

    for i, value in enumerate(parts):
        sums[i : i + 1] += value


def chain_spec(*dims):
    return pl.BlockSpec((1, *dims), lambda i: (i,) + (0,) * len(dims))


def whole_spec(*dims):
    return pl.BlockSpec(dims, lambda i: (0,) * len(dims))


def scan_call(kernel, chains, operands, outs, scratch, flops):
    specs = [pl.BlockSpec(memory_space=pltpu.SMEM)]
    for value, chained in operands[1:]:
        specs.append(chain_spec(*value.shape[1:]) if chained else whole_spec(*value.shape))
    shapes, out_specs = [], []
    for shape, dtype, chained in outs:
        shapes.append(jax.ShapeDtypeStruct(shape, dtype))
        out_specs.append(chain_spec(*shape[1:]) if chained else whole_spec(*shape))
    moved = sum(v.size * v.dtype.itemsize for v, _ in operands)
    moved += sum(s.size * s.dtype.itemsize for s in shapes)
    return pl.pallas_call(
        kernel,
        grid=(chains,),
        in_specs=specs,
        out_specs=out_specs,
        out_shape=shapes,
        scratch_shapes=[pltpu.VMEM(s, F32) for s in scratch],
        compiler_params=pltpu.CompilerParams(vmem_limit_bytes=48 * 1024 * 1024),
        cost_estimate=pl.CostEstimate(flops=flops, bytes_accessed=moved, transcendentals=0),
    )(*[v for v, _ in operands])


def norm_back(weighted, rows_in, scale_vec):
    return scale_vec * weighted - rows_in * scale_vec**3 * jnp.mean(
        weighted * rows_in, axis=-1, keepdims=True
    )


def mix(left, right):
    return jnp.dot(left, right, preferred_element_type=F32)


def mix_back(left, right):
    return lax.dot_general(left, right, (((1,), (1,)), ((), ())), preferred_element_type=F32)


def on_device(
    grid,
    inputs,
    seg_ids,
    norm_in,
    proj_y,
    proj_x,
    conv_weight,
    conv_bias,
    rate_weight,
    rate_bias,
    input_weight,
    input_bias,
    decay_param,
    proj_out,
    norm_mlp,
    mlp_gate,
    mlp_up,
    mlp_down,
    cotangent,
):
    nx, ny, nz, nc = (grid.n[p] for p in "xyzc")
    x, y, z, c = (grid.index(p) for p in "xyzc")
    micro, step, depth = inputs.shape
    chains = micro * ny
    length = nx * step
    shard = proj_x.shape[0]

    gain_in = norm_in.astype(F32)[:, None]
    gain_mlp = norm_mlp.astype(F32)[:, None]

    def gained(matrix, gain):
        return (matrix.astype(F32) * gain).astype(BF16)

    width = proj_x.shape[1] // (nx * ny)
    ff_width = mlp_down.shape[1] // (nx * ny)
    plane = nx * ny * shard
    width = proj_x.shape[1] // (nx * ny)
    ff_width = mlp_down.shape[1] // (nx * ny)
    plane = nx * ny * shard
    slope = -8.0 * jax.nn.softplus(-decay_param)
    slope_back = 8.0 * jax.nn.sigmoid(-decay_param)
    small = jnp.concatenate(
        [conv_weight, conv_bias[None], rate_bias[None], input_bias[None], slope[None]], axis=0
    )
    share = small.shape[1]
    heads, block = rate_weight.shape[0], rate_weight.shape[1]
    per = nz // ny
    packed = pack_small(rate_weight, input_weight, small)
    beside = [grid.shift(seg_ids, "y", r) for r in range(1, ny)]
    weights_in = grid.columns_of(
        [gained(proj_x, gain_in), gained(proj_y, gain_in), proj_out]
    ).reshape(plane, 3 * width)
    own_rows = grid.turn(after(inputs, weights_in))
    source = own_rows.astype(F32)
    normed, in_hop = grid.spread(own_rows, normed=True)
    own_x, own_yo = weights_in[:, :width], weights_in[:, width:]
    first_x = grid.ring_first(own_x)
    half = lax.dynamic_index_in_dim(after(packed, weights_in), c, 0, keepdims=False)
    by_z = grid.place([half] + [grid.shift(half, "z", r) for r in range(1, nz)], "z")
    by_z = lax.dynamic_slice_in_dim(by_z, y * per, per, 0)
    blocks_x = grid.ring_rest(own_x, first_x, by_z, *in_hop)
    (mix_x,) = grid.whole_rows(blocks_x, 0)
    first_yo = grid.ring_first(after(own_yo, *blocks_x))
    by_x = grid.place([by_z] + [grid.shift(by_z, "x", r) for r in range(1, nx)], "x")
    by_x = jnp.moveaxis(by_x, 0, 1).reshape(per * nx, *half.shape)
    halves = grid.place([by_x] + [grid.shift(by_x, "c", r) for r in range(1, nc)], "c")
    pieces = [gained(mlp_gate, gain_mlp), gained(mlp_up, gain_mlp), mlp_down]
    weights_ff = grid.columns_of([after(p, weights_in) for p in pieces]).reshape(plane, -1)

    drive = mix(normed, mix_x).astype(BF16).reshape(chains, nx, step, width)
    own_cot = grid.turn(after(cotangent, drive))
    gates, vec = unpack_small(after(halves, drive), x, per, heads)
    segments = after(jnp.stack([seg_ids, *beside], axis=1), drive)
    padded = jnp.pad(segments, ((0, 0), (0, 0), (HALO, 0)), constant_values=-1)
    near = lax.dynamic_slice_in_dim(padded, z * length, length + HALO, 2)
    here = near[:, :, HALO:]
    same = [jnp.ones_like(here, dtype=F32)]
    for k in range(1, TAPS):
        same.append((near[:, :, HALO - k : HALO - k + length] == here).astype(F32))
    same = jnp.stack(same + [jnp.zeros_like(same[0])] * (8 - TAPS), axis=-1)
    same = same.reshape(chains, length, 8)
    order = ((x - jnp.arange(nx, dtype=jnp.int32)) % nx).astype(jnp.int32)

    blocks_yo = grid.ring_rest(own_yo, first_yo, drive)
    ff_all = grid.all_rows(after(weights_ff, *blocks_yo))
    mix_y, mix_out = grid.whole_rows(blocks_yo, 0, 1)
    pre_y = mix(normed, mix_y)
    branch_y, gelu_y_back = jax.vjp(jax.nn.gelu, pre_y)
    last = lax.dynamic_index_in_dim(drive, (x - (nx - 1)) % nx, 1, keepdims=False)
    halo = grid.shift(last[:, step - HALO :].astype(F32), "z", 1, wrap=False)
    shape = (chains, length, width)
    turned = (chains, nx, step, width)
    conv, rate, gate_in, state, prods, ends = scan_call(
        forward_kernel,
        chains,
        [(order, False), (drive, True), (halo, True), (same, True), (vec, False), (gates, False)],
        [(shape, F32, True)] * 3 + [(turned, F32, True)] * 2 + [((chains, 8, width), F32, True)],
        [(length + HALO, width), (length, width), (length, width)],
        flops=8 * chains * length * width * width,
    )

    def carry_from(summary, sign):
        carry = jnp.zeros((chains, 1, width), F32)
        for r in reversed(range(1, nz)):
            got = grid.shift(summary, "z", sign * r, wrap=False)
            carry = got[:, 1:2] + got[:, 0:1] * carry
        return carry

    rows_cot, cot_hop = grid.spread(own_cot, ends)
    start = carry_from(after(ends, *cot_hop)[:, 0:2], 1)
    hidden = (state + prods * start[:, None]).astype(BF16)
    hidden_f = hidden.reshape(chains * length, width).astype(F32)
    mixed = (branch_y * hidden_f).astype(BF16)
    resid = source + grid.collect(mix_back(mixed, mix_out).astype(BF16), micro)

    scale_mlp = lax.rsqrt(jnp.mean(resid * resid, axis=-1, keepdims=True) + NORM_EPS)
    normed_mlp, _ = grid.spread((resid * scale_mlp).astype(BF16))
    ff_all = after(ff_all, normed_mlp)
    ff_gate = ff_all[:, :ff_width]
    ff_up = ff_all[:, ff_width : 2 * ff_width]
    ff_down = ff_all[:, 2 * ff_width :]
    pre_gate = mix(normed_mlp, ff_gate)
    pre_up = mix(normed_mlp, ff_up)
    activated, gelu_gate_back = jax.vjp(jax.nn.gelu, pre_gate)
    product = (activated * pre_up).astype(BF16)
    grad_prod = mix(rows_cot, ff_down)
    grad_gate = gelu_gate_back(grad_prod * pre_up)[0].astype(BF16)
    grad_up = (grad_prod * activated).astype(BF16)
    part_mlp = (mix_back(grad_gate, ff_gate) + mix_back(grad_up, ff_up)).astype(BF16)
    weighted_mlp = grid.collect(part_mlp, micro)
    grad_ff = jnp.concatenate([grad_gate, grad_up], axis=1)
    sum_down = WeightSum(grid, rows_cot, after(product, part_mlp))
    sum_ff = WeightSum(grid, normed_mlp, after(grad_ff, part_mlp))
    sum_down.meet()
    sum_ff.meet()
    sum_ff.mine = jnp.concatenate([sum_ff.mine.astype(BF16), sum_down.mine.astype(BF16)], axis=1)
    sum_ff.along_z()
    grad_resid = own_cot.astype(F32) + norm_back(weighted_mlp, resid, scale_mlp)
    grad_branch, _ = grid.spread(grad_resid.astype(BF16), sum_ff.mine)

    grad_mixed = mix(grad_branch, mix_out)
    grad_pre_y = gelu_y_back(grad_mixed * hidden_f)[0].astype(BF16)
    grad_state = (grad_mixed * branch_y).astype(BF16).reshape(turned)
    d_local, d_prods, d_ends = scan_call(
        reverse_kernel,
        chains,
        [(order, False), (grad_state, True), (same, True), (vec, False), (rate, True)],
        [(shape, F32, True)] * 2 + [((chains, 8, width), F32, True)],
        [(length, width), (length + HALO, width)],
        flops=40 * chains * length * width,
    )
    d_carry = carry_from(d_ends[:, 0:2], -1)
    d_drive, head, *d_pre, sums = scan_call(
        final_kernel,
        chains,
        [
            (order, False),
            (drive, True),
            (halo, True),
            (same, True),
            (vec, False),
            (gates, False),
            (conv, True),
            (rate, True),
            (gate_in, True),
            (state, True),
            (prods, True),
            (start, True),
            (d_local, True),
            (d_prods, True),
            (d_carry, True),
        ],
        [
            (turned, F32, True),
            ((chains, HALO, width), F32, True),
            (shape, BF16, True),
            (shape, BF16, True),
            ((8, width), F32, False),
        ],
        [(length + HALO, width), (length + 2 * HALO, width)],
        flops=8 * chains * length * width * width,
    )
    behind = grid.shift(head, "z", -1, wrap=False)
    chunk = lax.broadcasted_iota(jnp.int32, (1, nx, 1, 1), 1)
    tail = jnp.pad(behind, ((0, 0), (step - HALO, 0), (0, 0)))[:, None]
    d_drive = d_drive + jnp.where(chunk == (x - (nx - 1)) % nx, tail, 0.0)
    grad_drive = d_drive.astype(BF16).reshape(chains * length, width)
    part_in = (mix_back(grad_pre_y, mix_y) + mix_back(grad_drive, mix_x)).astype(BF16)
    weighted_in = grid.collect(part_in, micro)
    both = jnp.concatenate([grad_pre_y, grad_drive], axis=1)
    sum_in = WeightSum(grid, normed, after(both, weighted_in))
    sum_out = WeightSum(grid, grad_branch, after(mixed, weighted_in))
    sum_in.meet()
    sum_out.meet()
    sum_in.mine = jnp.concatenate([sum_in.mine.astype(BF16), sum_out.mine.astype(BF16)], axis=1)
    sum_in.along_z(sum_ff.done)
    part_out = mix_back(after(product, weighted_in), ff_down).astype(BF16)
    block_out = resid + grid.collect(part_out, micro)
    block_out = grid.turn(block_out.astype(BF16), back=True)
    grad_gate_w, grad_up_w, grad_down_w = sum_ff.finish(3)
    grad_y_w, grad_x_w, grad_out_w = sum_in.finish(3)
    scale_in = lax.rsqrt(jnp.mean(source * source, axis=-1, keepdims=True) + NORM_EPS)
    grad_source = grad_resid + norm_back(weighted_in, source, scale_in)
    grad_source = grid.turn(grad_source.astype(BF16), back=True)

    def gain_grad(*pairs):
        return sum(jnp.sum(w.astype(F32) * g, axis=1) for w, g in pairs)

    grad_norm_in = gain_grad((proj_y, grad_y_w), (proj_x, grad_x_w))
    grad_norm_mlp = gain_grad((mlp_gate, grad_gate_w), (mlp_up, grad_up_w))

    d_pre = [after(v, weighted_in) for v in d_pre]
    conv_low = conv.reshape(chains * length, width).astype(BF16)
    gate_dense = [
        lax.dot_general(
            conv_low,
            d.reshape(chains * length, width),
            (((0,), (0,)), ((), ())),
            preferred_element_type=F32,
        )
        for d in d_pre
    ]
    blocks = jnp.stack(
        [
            jnp.concatenate(
                [d[h * block : (h + 1) * block, h * block : (h + 1) * block] for d in gate_dense]
                + [sums[:, h * block : (h + 1) * block]],
                axis=0,
            )
            for h in range(per * heads)
        ]
    )
    blocks = blocks.astype(BF16).reshape(per, heads, 2 * block + 8, block)
    blocks = grid.total(blocks, "c")
    blocks = grid.total(blocks, "z")
    got = [
        [grid.shift_plane(blocks, ry, rx) if ry or rx else blocks for rx in range(nx)]
        for ry in range(ny)
    ]
    by_y = grid.place([grid.place(row, "x") for row in got], "y")
    mine = lax.dynamic_index_in_dim(
        by_y.reshape(ny * nx * per, *blocks.shape[1:]), z * nx + x, 0, keepdims=False
    ).astype(F32)
    mats = mine[:, : 2 * block].reshape(heads, 2, block, block)
    sums_own = jnp.moveaxis(mine[:, 2 * block :], 0, 1).reshape(8, share)
    return (
        block_out,
        grad_source,
        grad_norm_in,
        grad_y_w * gain_in,
        grad_x_w * gain_in,
        sums_own[0:4],
        sums_own[4],
        mats[:, 0],
        sums_own[5],
        mats[:, 1],
        sums_own[6],
        sums_own[7] * slope_back,
        grad_out_w,
        grad_norm_mlp,
        grad_gate_w * gain_mlp,
        grad_up_w * gain_mlp,
        grad_down_w,
    )


def solution(mesh):
    grid = Grid(mesh.shape["seq"], mesh.shape["blk"])
    every = ("seq", "blk")
    placed = (
        P(None, every, None),
        P(None, "seq"),
        P(every),
        P(every, None),
        P(every, None),
        P(None, "blk"),
        P("blk"),
        P("blk", None, None),
        P("blk"),
        P("blk", None, None),
        P("blk"),
        P("blk"),
        P(every, None),
        P(every),
        P(every, None),
        P(every, None),
        P(every, None),
        P(None, every, None),
    )
    return jax.shard_map(
        functools.partial(on_device, grid),
        mesh=mesh,
        in_specs=placed,
        out_specs=(
            P(None, every, None),
            P(None, every, None),
            P(every),
            P(every, None),
            P(every, None),
            P(None, "blk"),
            P("blk"),
            P("blk", None, None),
            P("blk"),
            P("blk", None, None),
            P("blk"),
            P("blk"),
            P(every, None),
            P(every),
            P(every, None),
            P(every, None),
            P(every, None),
        ),
        check_vma=False,
    )
```

time: 1230 us -> 757 us (0.62)
  local copies, waits for them, and re-layouts: 351 us -> 60.5 us
  waiting for transfers between devices: 526 us -> 346 us
  starting transfers between devices: 147 us -> 103 us
  Pallas kernels: 28.7 us -> 52.8 us
  other arithmetic: 41.6 us -> 56.4 us
  between operations: 3.83 us -> 16.2 us
    ppermute x158 -> x72, waiting for transfers between devices: 526 us -> 244 us  [shift(): return lax.ppermute(value, axis, pairs)]
    concatenate x72 -> x0, local copies, waits for them, and re-layouts: 140 us -> none  [spread(): jnp.concatenate([grid.spread(shard[m], firsts[m]) for m in range(micro)],...]
    dynamic_update_slice x110 -> x3, local copies, waits for them, and re-layouts: 94.4 us -> 2.84 us  [place(): out = lax.dynamic_update_index_in_dim(out, value, (me - r) % n, 0)]
    ppermute x0 -> x15, waiting for transfers between devices: none -> 76.4 us  [shift_plane(): return lax.ppermute(value, ('seq', 'blk'), pairs)]
    ppermute x158 -> x72, starting transfers between devices: 147 us -> 84.2 us  [shift(): return lax.ppermute(value, axis, pairs)]
    unnamed x250 -> x205, local copies, waits for them, and re-layouts: 48.4 us -> 18.9 us
    pallas_call x0 -> x13, Pallas kernels: none -> 24.1 us  [the longest x4 8.76 us: turn(): pl.pallas_call(kernel, out_shape=jax.ShapeDtypeStruct(value.shape, value....]
    ppermute x0 -> x15, starting transfers between devices: none -> 18.8 us  [shift_plane(): return lax.ppermute(value, ('seq', 'blk'), pairs)]
  transfers between devices with their start and end apart: 158 -> 90, of which waited for: 70 -> 51; matrix products, arithmetic and copies ran while one was open for 37% -> 18% of each run, Pallas kernels for 2% -> 7%
where the time goes in v2:
time: 757 us; the launch traced here: 747 us
  waiting for transfers between devices  346 us (46%)
  matrix products  113 us (15%)
  starting transfers between devices  103 us (14%)
  local copies, waits for them, and re-layouts  60.5 us (8%)
  other arithmetic  56.4 us (7%)
  Pallas kernels  52.8 us (7%)
  between operations  16.2 us (2%)
    ppermute x72, waiting for transfers between devices, shift(): return lax.ppermute(value, axis, pairs)  244 us
    ppermute x72, starting transfers between devices, shift(): return lax.ppermute(value, axis, pairs)  84.2 us
    ppermute x15, waiting for transfers between devices, shift_plane(): return lax.ppermute(value, ('seq', 'blk'), pairs)  76.4 us
    dot_general x6, matrix products, mix(): return jnp.dot(left, right, preferred_element_type=F32)  40.6 us
    dot_general x6, matrix products, mix_back(): lax.dot_general(left, right, (((1,), (1,)), ((), ())), preferred_element_...  38.6 us
    dot_general x8, matrix products, product(): lax.dot_general(cut, self.right, (((0,), (0,)), ((), ())), preferred_elem...  31.6 us
    pallas_call x3, Pallas kernels, scan_call(): pl.pallas_call(kernel, grid=(chains,), in_specs=specs, out_specs=out_spec...  28.7 us
    unnamed x205, local copies, waits for them, and re-layouts  18.9 us
  transfers between devices with their start and end apart: 90, of which 51 were waited for; matrix products, arithmetic and copies ran while one was open for 18% of the time, Pallas kernels for 7%

profile of v2, /device:TPU:0, one launch (start us, length us, event | category | flops | bytes accessed | tf_op | source)
XLA Modules:
  0.0 747.4 jit_solution(1235601139726259152)
XLA Ops:
  9.5 3.0 collective-permute-start
  18.5 6.5 collective-permute-done.2
  29.4 2.6 collective-permute-start.9
  46.0 3.4 collective-permute-start.12
  51.2 27.0 %collective-permute-done.46 = bf16[64,4608]{1,0:T(8,128)(2,1)S(1)} collective-permute-done((bf16[64,4608]{1,0:T(8,128)(2,1)S(1)}, bf16[64,4608]{1,0:T(8,128)(2,1)S(1)}, u32[]{:S(2)}, u32[]{:S(2)}) %collective-permute-start.46) | collective-permute-done | bytes 589856 | tf_op jit(solution)/shard_map/ppermute | solution.py:60
  79.2 9.6 %collective-permute-done.45 = bf16[64,4608]{1,0:T(8,128)(2,1)S(1)} collective-permute-done((bf16[64,4608]{1,0:T(8,128)(2,1)S(1)}, bf16[64,4608]{1,0:T(8,128)(2,1)S(1)}, u32[]{:S(2)}, u32[]{:S(2)}) %collective-permute-start.45) | collective-permute-done | bytes 589856 | tf_op jit(solution)/shard_map/ppermute | solution.py:60
  93.7 5.0 collective-permute-done.13.refs_3_
  107.2 5.6 collective-permute-done.5.refs_3_
  114.6 3.5 convolution_convert_fusion.5
  118.1 3.7 collective-permute-done.21.refs_4_
  121.9 12.4 %collective-permute-done.14.refs_1_ = bf16[256,1280]{1,0:T(8,128)(2,1)S(1)} collective-permute-done((bf16[256,1280]{1,0:T(8,128)(2,1)S(1)}, bf16[256,1280]{1,0:T(8,128)(2,1)S(1)}, u32[]{:S(2)}, u32[]{:S(2)}) %collective-permute-start.14) | collective-permute-done | bytes 655392 | tf_op jit(solution)/shard_map/ppermute | solution.py:49
  134.3 3.0 collective-permute-start.20
  138.9 4.0 collective-permute-done.22.refs_3_
  143.6 5.3 collective-permute-done.20.refs_2_
  150.8 10.7 %collective-permute-done.30 = bf16[2,416,160]{2,1,0:T(8,128)(2,1)S(1)} collective-permute-done((bf16[2,416,160]{2,1,0:T(8,128)(2,1)S(1)}, bf16[2,416,160]{2,1,0:T(8,128)(2,1)S(1)}, u32[]{:S(2)}, u32[]{:S(2)}) %collective-permute-start.30) | collective-permute-done | bytes 266272 | tf_op jit(solution)/shard_map/ppermute | solution.py:49
  162.7 3.1 collective-permute-done.29
  174.7 3.4 collective-permute-start.28
  190.2 10.4 %shard_map.311 = (f32[4,192,640]{2,1,0:T(8,128)S(1)}, f32[4,192,640]{2,1,0:T(8,128)}, f32[4,192,640]{2,1,0:T(8,128)}, f32[4,2,96,640]{3,2,1,0:T(8,128)}, f32[4,2...) custom-call(s32[2]{0:T(128)S(1)} %and_select_fusion.order, bf16[4,2,96,640]{3,2,1,0:T(8,128)(2,1)S(1)} %bitcast.413, ...), custom_call_target="tpu_custom_call" | custom-call | flops 2516582400 | bytes 12660744 | tf_op jit(solution)/shard_map/pallas_call | solution.py:652
  202.6 5.5 collective-permute-start.35
  208.1 6.9 collective-permute-start.36
  221.1 3.1 shard_map.309
  224.2 4.3 fusion.24
  228.5 3.1 convolution_convert_fusion.3
  231.9 20.0 %collective-permute-done.37 = bf16[2,96,2048]{2,1,0:T(8,128)(2,1)S(1)} collective-permute-done((bf16[2,96,2048]{2,1,0:T(8,128)(2,1)S(1)}, bf16[2,96,2048]{2,1,0:T(8,128)(2,1)S(1)}, u32[]{:S(2)}, u32[]{:S(2)}) %collective-permute-start.37) | collective-permute-done | bytes 786464 | tf_op jit(solution)/shard_map/ppermute | solution.py:49
  254.7 8.8 %collective-permute-done.38 = bf16[96,2048]{1,0:T(8,128)(2,1)S(1)} collective-permute-done((bf16[96,2048]{1,0:T(8,128)(2,1)S(1)}, bf16[96,2048]{1,0:T(8,128)(2,1)S(1)}, u32[]{:S(2)}, u32[]{:S(2)}) %collective-permute-start.38) | collective-permute-done | bytes 393248 | tf_op jit(solution)/shard_map/ppermute | solution.py:49
  272.8 12.9 %collective-permute-done.41.refs_1_ = bf16[2,96,2048]{2,1,0:T(8,128)(2,1)S(1)} collective-permute-done((bf16[2,96,2048]{2,1,0:T(8,128)(2,1)S(1)}, bf16[2,96,2048]{2,1,0:T(8,128)(2,1)S(1)}, u32[]{:S(2)}, u32[]{:S(2)}) %collective-permute-start.41) | collective-permute-done | bytes 786464 | tf_op jit(solution)/shard_map/ppermute | solution.py:49
  294.2 3.8 collective-permute-done.48.refs_3_
  308.0 8.4 %all-gather.2.cloned.1.call-done = bf16[2048,4608]{1,0:T(8,128)(2,1)} async-done(((bf16[256,4608]{1,0:T(8,128)(2,1)}), bf16[2048,4608]{1,0:T(8,128)(2,1)}) %all-gather.2.cloned.1.call-update) | async-done | bytes 18874384 | tf_op jit(solution)/shard_map/all_gather | solution.py:225
  316.5 8.2 %fusion.6 = f32[768,1536]{1,0:T(8,128)S(1)} fusion(bf16[768,2048]{1,0:T(8,128)(2,1)} %bitcast.408, bf16[2048,4608]{1,0:T(8,128)(2,1)} %all-gather.2.cloned.1.call-done), kind=kOutput, calls=%fused_computation.14 | convolution fusion | flops 4831838208 | bytes 14155776 | tf_op jit(solution)/shard_map/dot_general | solution.py:671
  324.7 9.7 %fusion.2 = f32[768,1536]{1,0:T(8,128)} fusion(bf16[768,2048]{1,0:T(8,128)(2,1)S(1)} %bitcast.405, bf16[2048,4608]{1,0:T(8,128)(2,1)} %all-gather.2.cloned.1.call-done), kind=kOutput, calls=%fused_computation.10 | convolution fusion | flops 4831838208 | bytes 14155776 | tf_op jit(solution)/shard_map/dot_general | solution.py:671
  334.4 11.1 %fusion.18 = (bf16[768,1536]{1,0:T(8,128)(2,1)S(1)}, bf16[768,1536]{1,0:T(8,128)(2,1)S(1)}, bf16[768,1536]{1,0:T(8,128)(2,1)S(1)}) fusion(f32[768,1536]{1,0:T(8,128)} %fusion.2, f32[768,1536]{1,0:T(8,128)S(1)} %fusion.6, bf16[768,2048]{1,0:T(8,128)(2,1)S(1)} %bitcast.409, bf16[2048,4608]{1,0:T(8,128)(2,1)} %all-gather.2.cloned.1.call-done), kind=kOutput, calls=%fused_computation.27 | convolution fusion | flops 4862509056 | bytes 25952256 | tf_op jit(solution)/shard_map/dot_general | solution.py:671
  345.5 10.6 %fusion.4 = f32[768,2048]{1,0:T(8,128)} fusion(bf16[768,1536]{1,0:T(8,128)(2,1)S(1)} %get-tuple-element.176, bf16[2048,4608]{1,0:T(8,128)(2,1)} %all-gather.2.cloned.1.call-done), kind=kOutput, calls=%fused_computation.12 | convolution fusion | flops 4831838208 | bytes 14942208 | tf_op jit(solution)/shard_map/dot_general | solution.py:675
  356.8 10.9 %add_convert_fusion.3 = bf16[768,2048]{1,0:T(8,128)(2,1)S(1)} fusion(f32[768,2048]{1,0:T(8,128)} %fusion.4, bf16[768,1536]{1,0:T(8,128)(2,1)S(1)} %get-tuple-element.175, bf16[2048,4608]{1,0:T(8,128)(2,1)} %all-gather.2.cloned.1.call-done), kind=kOutput, calls=%fused_computation.6 | convolution fusion | flops 4834983936 | bytes 18087936 | tf_op jit(solution)/shard_map/dot_general | solution.py:675
  367.7 7.2 convolution_convert_fusion
  380.0 4.0 convolution_convert_fusion.2
  384.0 12.9 %collective-permute-done.50 = bf16[2,96,2048]{2,1,0:T(8,128)(2,1)S(1)} collective-permute-done((bf16[2,96,2048]{2,1,0:T(8,128)(2,1)}, bf16[2,96,2048]{2,1,0:T(8,128)(2,1)S(1)}, u32[]{:S(2)}, u32[]{:S(2)}) %collective-permute-start.50) | collective-permute-done | bytes 786464 | tf_op jit(solution)/shard_map/ppermute | solution.py:49
  402.4 8.0 %collective-permute-done.51 = bf16[96,2048]{1,0:T(8,128)(2,1)S(1)} collective-permute-done((bf16[96,2048]{1,0:T(8,128)(2,1)S(1)}, bf16[96,2048]{1,0:T(8,128)(2,1)S(1)}, u32[]{:S(2)}, u32[]{:S(2)}) %collective-permute-start.51) | collective-permute-done | bytes 393248 | tf_op jit(solution)/shard_map/ppermute | solution.py:49
  414.6 5.1 add_convert_fusion.2
  419.8 7.7 %add_convert_fusion = bf16[1024,3072]{1,0:T(8,128)(2,1)S(1)} fusion(bf16[1024,3072]{1,0:T(8,128)(2,1)} %collective-permute-done.55, bf16[768,3072]{1,0:T(8,128)(2,1)S(1)} %bitcast.419, bf16[768,2048]{1,0:T(8,128)(2,1)S(1)} %bitcast.411, s32[]{:T(128)S(6)} %select_n.683), kind=kOutput, calls=%fused_computation | convolution fusion | flops 4841275392 | bytes 18874372 | tf_op jit(solution)/shard_map/dot_general | solution.py:251
  427.5 4.6 pad_maximum_fusion
  435.2 16.2 %collective-permute-done.57.refs_2_ = bf16[2,96,2048]{2,1,0:T(8,128)(2,1)S(1)} collective-permute-done((bf16[2,96,2048]{2,1,0:T(8,128)(2,1)S(1)}, bf16[2,96,2048]{2,1,0:T(8,128)(2,1)S(1)}, u32[]{:S(2)}, u32[]{:S(2)}) %collective-permute-start.57) | collective-permute-done | bytes 786464 | tf_op jit(solution)/shard_map/ppermute | solution.py:49
  454.5 5.8 collective-permute-done.59.refs_4_
  461.3 3.8 fusion.31
  465.2 7.3 shard_map.317
  478.9 5.5 collective-permute-done.60
  486.9 11.1 %shard_map.318 = (f32[4,2,96,640]{3,2,1,0:T(8,128)}, f32[4,8,640]{2,1,0:T(8,128)S(1)}, bf16[4,192,640]{2,1,0:T(8,128)(2,1)S(1)}, bf16[4,192,640]{2,1,0:T(8,128)(2,1)S(1)}, f32[8,640]{1,0:T(8,128)S(1)}) custom-call(s32[2]{0:T(128)S(1)} %and_select_fusion.order, bf16[4,2,96,640]{3,2,1,0:T(8,128)(2,1)S(1)} %bitcast.414, f32[4,8,640]{2,1,0:T(8,128)S(1)} %copy-done.42, ...), custom_call_target="tpu_custom_call" | custom-call | flops 2516582400 | bytes 20566024 | tf_op jit(solution)/shard_map/pallas_call | solution.py:652
  499.3 8.6 %collective-permute-done.63 = f32[4,8,640]{2,1,0:T(8,128)S(1)} collective-permute-done((f32[4,8,640]{2,1,0:T(8,128)S(1)}, f32[4,8,640]{2,1,0:T(8,128)S(1)}, u32[]{:S(2)}, u32[]{:S(2)}) %collective-permute-start.63) | collective-permute-done | bytes 81952 | tf_op jit(solution)/shard_map/ppermute | solution.py:49
  510.3 2.6 fusion.109
  513.0 3.3 add_convert_fusion.1
  524.3 9.7 %collective-permute-done.64 = bf16[2,96,2048]{2,1,0:T(8,128)(2,1)} collective-permute-done((bf16[2,96,2048]{2,1,0:T(8,128)(2,1)}, bf16[2,96,2048]{2,1,0:T(8,128)(2,1)}, u32[]{:S(2)}, u32[]{:S(2)}) %collective-permute-start.64) | collective-permute-done | bytes 786464 | tf_op jit(solution)/shard_map/ppermute | solution.py:49
  534.0 2.6 collective-permute-done.66
  539.1 7.4 collective-permute-done.65
  553.2 8.1 %fusion.19 = bf16[768,2048]{1,0:T(8,128)(2,1)S(1)} fusion(bf16[768,1536]{1,0:T(8,128)(2,1)S(1)} %copy-done.98, bf16[2048,4608]{1,0:T(8,128)(2,1)} %all-gather.2.cloned.1.call-done), kind=kOutput, calls=%fused_computation.36 | convolution fusion | flops 4833411072 | bytes 11796480 | tf_op jit(solution)/shard_map/dot_general | solution.py:675
  567.1 14.5 %collective-permute-done.68 = bf16[2,96,2048]{2,1,0:T(8,128)(2,1)S(1)} collective-permute-done((bf16[2,96,2048]{2,1,0:T(8,128)(2,1)S(1)}, bf16[2,96,2048]{2,1,0:T(8,128)(2,1)S(1)}, u32[]{:S(2)}, u32[]{:S(2)}) %collective-permute-start.68) | collective-permute-done | bytes 786464 | tf_op jit(solution)/shard_map/ppermute | solution.py:49
  581.7 3.6 collective-permute-start.80
  585.9 6.3 collective-permute-done.78
  594.1 33.5 %collective-permute-done.79 = bf16[2,2,328,160]{2,3,1,0:T(8,128)(2,1)S(1)} collective-permute-done((bf16[2,2,328,160]{2,3,1,0:T(8,128)(2,1)S(1)}, bf16[2,2,328,160]{2,3,1,0:T(8,128)(2,1)S(1)}, u32[]{:S(2)}, u32[]{:S(2)}) %collective-permute-start.79) | collective-permute-done | bytes 419872 | tf_op jit(solution)/shard_map/ppermute | solution.py:49
  642.9 3.4 fusion.40
  652.0 7.8 %collective-permute-done.82 = bf16[2,2,328,160]{2,3,1,0:T(8,128)(2,1)} collective-permute-done((bf16[2,2,328,160]{2,3,1,0:T(8,128)(2,1)}, bf16[2,2,328,160]{2,3,1,0:T(8,128)(2,1)}, u32[]{:S(2)}, u32[]{:S(2)}) %collective-permute-start.82) | collective-permute-done | bytes 419872 | tf_op jit(solution)/shard_map/ppermute | solution.py:60
  661.9 5.6 copy.154
  684.1 4.5 collective-permute-done.84
  688.6 12.0 %collective-permute-done.85 = bf16[64,4608]{1,0:T(8,128)(2,1)S(1)} collective-permute-done((bf16[64,4608]{1,0:T(8,128)(2,1)}, bf16[64,4608]{1,0:T(8,128)(2,1)S(1)}, u32[]{:S(2)}, u32[]{:S(2)}) %collective-permute-start.85) | collective-permute-done | bytes 589856 | tf_op jit(solution)/shard_map/ppermute | solution.py:60
  703.5 17.1 %reduce-scatter.5.cloned.1.call-done = bf16[256,1920]{1,0:T(8,128)(2,1)} async-done(((bf16[1024,1920]{1,0:T(8,128)(2,1)}), bf16[256,1920]{1,0:T(8,128)(2,1)}) %reduce-scatter.5.cloned.1.call-update) | async-done | bytes 983056 | tf_op jit(solution)/shard_map/reduce_scatter | solution.py:267
  729.3 6.4 collective-permute-done.75
  (536 shorter events, 225.4 us)
Async XLA Ops:
  7.2 309.3 %all-gather.2.cloned.1.call-start = ((), (), s32[]{:S(2)}) async-start(), calls=%async_computation.2 | async-start | bytes 21233664 | tf_op jit(solution)/shard_map/all_gather | solution.py:225
  9.5 17.2 %collective-permute-start = (bf16[64,1920]{1,0:T(8,128)(2,1)S(1)}, bf16[64,1920]{1,0:T(8,128)(2,1)S(1)}, u32[]{:S(2)}, u32[]{:S(2)}) collective-permute-start(bf16[64,1920]{1,0:T(8,128)(2,1)S(1)} %pad_maximum_fusion.31), channel_id=1, source_target_pairs={{0,1},{1,0},{2,3},{3,2},{4,5},{5,4},{6,7},{7,6},{8,9},{9,8},{10,11... | collective-permute-start | bytes 737288 | tf_op jit(solution)/shard_map/ppermute | solution.py:60
  12.5 12.5 %collective-permute-start.2 = (bf16[64,1920]{1,0:T(8,128)(2,1)S(1)}, bf16[64,1920]{1,0:T(8,128)(2,1)S(1)}, u32[]{:S(2)}, u32[]{:S(2)}) collective-permute-start(bf16[64,1920]{1,0:T(8,128)(2,1)S(1)} %pad_maximum_fusion.33), channel_id=1, source_target_pairs={{0,17},{1,16},{2,19},{3,18},{4,21},{5,20},{6,23},{7,22},{8,25},{9,... | collective-permute-start | bytes 737288 | tf_op jit(solution)/shard_map/ppermute | solution.py:60
  14.1 12.5 %collective-permute-start.1 = (bf16[64,1920]{1,0:T(8,128)(2,1)S(1)}, bf16[64,1920]{1,0:T(8,128)(2,1)S(1)}, u32[]{:S(2)}, u32[]{:S(2)}) collective-permute-start(bf16[64,1920]{1,0:T(8,128)(2,1)S(1)} %pad_maximum_fusion.32), channel_id=1, source_target_pairs={{0,16},{1,17},{2,18},{3,19},{4,20},{5,21},{6,22},{7,23},{8,24},{9,... | collective-permute-start | bytes 737288 | tf_op jit(solution)/shard_map/ppermute | solution.py:60
  27.8 11.4 %collective-permute-start.8 = (bf16[416,160]{1,0:T(8,128)(2,1)S(1)}, bf16[416,160]{1,0:T(8,128)(2,1)}, u32[]{:S(2)}, u32[]{:S(2)}) collective-permute-start(bf16[416,160]{1,0:T(8,128)(2,1)S(1)} %get-tuple-element.280), channel_id=1, source_target_pairs={{0,2},{1,3},{2,4},{3,5},{4,6},{5,7},{6,0},{7,1},{8,10},{9,11},{10,... | collective-permute-start | bytes 399368 | tf_op jit(solution)/shard_map/ppermute | solution.py:49
  29.4 14.2 %collective-permute-start.9 = (bf16[416,160]{1,0:T(8,128)(2,1)S(1)}, bf16[416,160]{1,0:T(8,128)(2,1)}, u32[]{:S(2)}, u32[]{:S(2)}) collective-permute-start(bf16[416,160]{1,0:T(8,128)(2,1)S(1)} %get-tuple-element.280), channel_id=1, source_target_pairs={{0,4},{1,5},{2,6},{3,7},{4,0},{5,1},{6,2},{7,3},{8,12},{9,13},{10,... | collective-permute-start | bytes 399368 | tf_op jit(solution)/shard_map/ppermute | solution.py:49
  32.0 13.9 %collective-permute-start.10 = (bf16[416,160]{1,0:T(8,128)(2,1)S(1)}, bf16[416,160]{1,0:T(8,128)(2,1)}, u32[]{:S(2)}, u32[]{:S(2)}) collective-permute-start(bf16[416,160]{1,0:T(8,128)(2,1)S(1)} %get-tuple-element.280), channel_id=1, source_target_pairs={{0,6},{1,7},{2,0},{3,1},{4,2},{5,3},{6,4},{7,5},{8,14},{9,15},{10,... | collective-permute-start | bytes 399368 | tf_op jit(solution)/shard_map/ppermute | solution.py:49
  35.5 53.5 %collective-permute-start.3 = (bf16[2,96,2048]{2,1,0:T(8,128)(2,1)}, bf16[2,96,2048]{2,1,0:T(8,128)(2,1)S(1)}, u32[]{:S(2)}, u32[]{:S(2)}) collective-permute-start(bf16[2,96,2048]{2,1,0:T(8,128)(2,1)} %shard_map.305.refs_0_), channel_id=1, source_target_pairs={{0,1},{1,0},{2,3},{3,2},{4,5},{5,4},{6,7},{7,6},{8,9},{9,8},{10,11... | collective-permute-start | bytes 2359304 | tf_op jit(solution)/shard_map/ppermute | solution.py:49
  37.0 52.1 %collective-permute-start.4 = (bf16[2,96,2048]{2,1,0:T(8,128)(2,1)}, bf16[2,96,2048]{2,1,0:T(8,128)(2,1)S(1)}, u32[]{:S(2)}, u32[]{:S(2)}) collective-permute-start(bf16[2,96,2048]{2,1,0:T(8,128)(2,1)} %shard_map.305.refs_0_), channel_id=1, source_target_pairs={{0,16},{8,24},{16,0},{24,8},{1,17},{9,25},{17,1},{25,9},{2,18},{10... | collective-permute-start | bytes 2359304 | tf_op jit(solution)/shard_map/ppermute | solution.py:49
  39.2 39.0 %collective-permute-start.46 = (bf16[64,4608]{1,0:T(8,128)(2,1)S(1)}, bf16[64,4608]{1,0:T(8,128)(2,1)S(1)}, u32[]{:S(2)}, u32[]{:S(2)}) collective-permute-start(bf16[64,4608]{1,0:T(8,128)(2,1)S(1)} %pad_maximum_fusion.21), channel_id=1, source_target_pairs={{0,16},{1,17},{2,18},{3,19},{4,20},{5,21},{6,22},{7,23},{8,24},{9,... | collective-permute-start | bytes 1769480 | tf_op jit(solution)/shard_map/ppermute | solution.py:60
  43.6 35.1 %collective-permute-start.47 = (bf16[64,4608]{1,0:T(8,128)(2,1)S(1)}, bf16[64,4608]{1,0:T(8,128)(2,1)S(1)}, u32[]{:S(2)}, u32[]{:S(2)}) collective-permute-start(bf16[64,4608]{1,0:T(8,128)(2,1)S(1)} %pad_maximum_fusion.22), channel_id=1, source_target_pairs={{0,17},{1,16},{2,19},{3,18},{4,21},{5,20},{6,23},{7,22},{8,25},{9,... | collective-permute-start | bytes 1769480 | tf_op jit(solution)/shard_map/ppermute | solution.py:60
  46.0 43.1 %collective-permute-start.12 = (bf16[256,640]{1,0:T(8,128)(2,1)S(1)}, bf16[256,640]{1,0:T(8,128)(2,1)S(1)}, u32[]{:S(2)}, u32[]{:S(2)}) collective-permute-start(bf16[256,640]{1,0:T(8,128)(2,1)S(1)} %slice.483.refs_0_), channel_id=1, source_target_pairs={{0,2},{1,3},{2,4},{3,5},{4,6},{5,7},{6,0},{7,1},{8,10},{9,11},{10,... | collective-permute-start | bytes 983048 | tf_op jit(solution)/shard_map/ppermute | solution.py:49
  78.2 11.5 %collective-permute-start.7 = (bf16[256,640]{1,0:T(8,128)(2,1)S(1)}, bf16[256,640]{1,0:T(8,128)(2,1)S(1)}, u32[]{:S(2)}, u32[]{:S(2)}) collective-permute-start(bf16[256,640]{1,0:T(8,128)(2,1)S(1)} %slice.483.refs_0_), channel_id=1, source_target_pairs={{0,6},{1,7},{2,0},{3,1},{4,2},{5,3},{6,4},{7,5},{8,14},{9,15},{10,... | collective-permute-start | bytes 983048 | tf_op jit(solution)/shard_map/ppermute | solution.py:49
  88.9 12.4 %collective-permute-start.15 = (bf16[256,640]{1,0:T(8,128)(2,1)S(1)}, bf16[256,640]{1,0:T(8,128)(2,1)S(1)}, u32[]{:S(2)}, u32[]{:S(2)}) collective-permute-start(bf16[256,640]{1,0:T(8,128)(2,1)S(1)} %slice.483.refs_0_), channel_id=1, source_target_pairs={{0,8},{8,0},{16,24},{24,16},{1,9},{9,1},{17,25},{25,17},{2,10},{10... | collective-permute-start | bytes 983048 | tf_op jit(solution)/shard_map/ppermute | solution.py:49
  89.1 13.2 %collective-permute-start.19 = (bf16[256,640]{1,0:T(8,128)(2,1)S(1)}, bf16[256,640]{1,0:T(8,128)(2,1)S(1)}, u32[]{:S(2)}, u32[]{:S(2)}) collective-permute-start(bf16[256,640]{1,0:T(8,128)(2,1)S(1)} %collective-permute-done.12.refs_4_), channel_id=1, source_target_pairs={{0,8},{8,0},{16,24},{24,16},{1,9},{9,1},{17,25},{25,17},{2,10},{10... | collective-permute-start | bytes 983048 | tf_op jit(solution)/shard_map/ppermute | solution.py:49
  89.7 16.7 %collective-permute-start.16 = (bf16[256,640]{1,0:T(8,128)(2,1)S(1)}, bf16[256,640]{1,0:T(8,128)(2,1)S(1)}, u32[]{:S(2)}, u32[]{:S(2)}) collective-permute-start(bf16[256,640]{1,0:T(8,128)(2,1)S(1)} %collective-permute-done.7.refs_1_), channel_id=1, source_target_pairs={{0,8},{8,0},{16,24},{24,16},{1,9},{9,1},{17,25},{25,17},{2,10},{10... | collective-permute-start | bytes 983048 | tf_op jit(solution)/shard_map/ppermute | solution.py:49
  101.3 11.6 %collective-permute-start.5 = (bf16[96,2048]{1,0:T(8,128)(2,1)S(1)}, bf16[96,2048]{1,0:T(8,128)(2,1)S(1)}, u32[]{:S(2)}, u32[]{:S(2)}) collective-permute-start(bf16[96,2048]{1,0:T(8,128)(2,1)S(1)} %slice_bitcast_fusion.27), channel_id=1, source_target_pairs={{0,16},{8,24},{16,0},{24,8},{1,17},{9,25},{17,1},{25,9},{2,18},{10... | collective-permute-start | bytes 1179656 | tf_op jit(solution)/shard_map/ppermute | solution.py:49
  102.4 19.4 %collective-permute-start.21 = (bf16[256,1280]{1,0:T(8,128)(2,1)S(1)}, bf16[256,1280]{1,0:T(8,128)(2,1)S(1)}, u32[]{:S(2)}, u32[]{:S(2)}) collective-permute-start(bf16[256,1280]{1,0:T(8,128)(2,1)S(1)} %slice.482.refs_0_), channel_id=1, source_target_pairs={{0,2},{1,3},{2,4},{3,5},{4,6},{5,7},{6,0},{7,1},{8,10},{9,11},{10,... | collective-permute-start | bytes 1966088 | tf_op jit(solution)/shard_map/ppermute | solution.py:49
  103.7 30.5 %collective-permute-start.14 = (bf16[256,1280]{1,0:T(8,128)(2,1)S(1)}, bf16[256,1280]{1,0:T(8,128)(2,1)S(1)}, u32[]{:S(2)}, u32[]{:S(2)}) collective-permute-start(bf16[256,1280]{1,0:T(8,128)(2,1)S(1)} %slice.482.refs_0_), channel_id=1, source_target_pairs={{0,6},{1,7},{2,0},{3,1},{4,2},{5,3},{6,4},{7,5},{8,14},{9,15},{10,... | collective-permute-start | bytes 1966088 | tf_op jit(solution)/shard_map/ppermute | solution.py:49
  121.8 21.1 %collective-permute-start.22 = (bf16[128,1280]{1,0:T(8,128)(2,1)S(1)}, bf16[128,1280]{1,0:T(8,128)(2,1)S(1)}, u32[]{:S(2)}, u32[]{:S(2)}) collective-permute-start(bf16[128,1280]{1,0:T(8,128)(2,1)S(1)} %slice.373), channel_id=1, source_target_pairs={{0,2},{1,3},{2,4},{3,5},{4,6},{5,7},{6,0},{7,1},{8,10},{9,11},{10,... | collective-permute-start | bytes 983048 | tf_op jit(solution)/shard_map/ppermute | solution.py:49
  134.3 14.6 %collective-permute-start.20 = (bf16[128,1280]{1,0:T(8,128)(2,1)S(1)}, bf16[128,1280]{1,0:T(8,128)(2,1)S(1)}, u32[]{:S(2)}, u32[]{:S(2)}) collective-permute-start(bf16[128,1280]{1,0:T(8,128)(2,1)S(1)} %slice.372), channel_id=1, source_target_pairs={{0,6},{1,7},{2,0},{3,1},{4,2},{5,3},{6,4},{7,5},{8,14},{9,15},{10,... | collective-permute-start | bytes 983048 | tf_op jit(solution)/shard_map/ppermute | solution.py:49
  149.6 491.1 %reduce-scatter.3.cloned.1.call-start = ((), (), s32[]{:S(2)}) async-start(), calls=%async_computation.3 | async-start | bytes 11796480 | tf_op jit(solution)/shard_map/reduce_scatter | solution.py:267
  149.7 11.7 %collective-permute-start.30 = (bf16[2,416,160]{2,1,0:T(8,128)(2,1)S(1)}, bf16[2,416,160]{2,1,0:T(8,128)(2,1)S(1)}, u32[]{:S(2)}, u32[]{:S(2)}) collective-permute-start(bf16[2,416,160]{2,1,0:T(8,128)(2,1)S(1)} %copy-done.75), channel_id=1, source_target_pairs={{0,1},{1,0},{2,3},{3,2},{4,5},{5,4},{6,7},{7,6},{8,9},{9,8},{10,11... | collective-permute-start | bytes 798728 | tf_op jit(solution)/shard_map/ppermute | solution.py:49
  165.9 53.3 %collective-permute-start.23 = (bf16[256,1280]{1,0:T(8,128)(2,1)S(1)}, bf16[256,1280]{1,0:T(8,128)(2,1)}, u32[]{:S(2)}, u32[]{:S(2)}) collective-permute-start(bf16[256,1280]{1,0:T(8,128)(2,1)S(1)} %slice.482.refs_0_), channel_id=1, source_target_pairs={{0,8},{8,0},{16,24},{24,16},{1,9},{9,1},{17,25},{25,17},{2,10},{10... | collective-permute-start | bytes 1966088 | tf_op jit(solution)/shard_map/ppermute | solution.py:49
  170.8 29.8 %collective-permute-start.33 = (bf16[2,96,2048]{2,1,0:T(8,128)(2,1)}, bf16[2,96,2048]{2,1,0:T(8,128)(2,1)}, u32[]{:S(2)}, u32[]{:S(2)}) collective-permute-start(bf16[2,96,2048]{2,1,0:T(8,128)(2,1)} %shard_map.312.refs_0_), channel_id=1, source_target_pairs={{0,16},{8,24},{16,0},{24,8},{1,17},{9,25},{17,1},{25,9},{2,18},{10... | collective-permute-start | bytes 2359304 | tf_op jit(solution)/shard_map/ppermute | solution.py:49
  171.4 29.2 %collective-permute-start.32 = (bf16[2,96,2048]{2,1,0:T(8,128)(2,1)}, bf16[2,96,2048]{2,1,0:T(8,128)(2,1)}, u32[]{:S(2)}, u32[]{:S(2)}) collective-permute-start(bf16[2,96,2048]{2,1,0:T(8,128)(2,1)} %shard_map.312.refs_0_), channel_id=1, source_target_pairs={{0,1},{1,0},{2,3},{3,2},{4,5},{5,4},{6,7},{7,6},{8,9},{9,8},{10,11... | collective-permute-start | bytes 2359304 | tf_op jit(solution)/shard_map/ppermute | solution.py:49
  174.7 12.3 %collective-permute-start.28 = (f32[4,8,640]{2,1,0:T(8,128)S(1)}, f32[4,8,640]{2,1,0:T(8,128)S(1)}, u32[]{:S(2)}, u32[]{:S(2)}) collective-permute-start(f32[4,8,640]{2,1,0:T(8,128)S(1)} %slice_convert_fusion.8), channel_id=1, source_target_pairs={{0,2},{1,3},{2,4},{3,5},{4,6},{5,7},{8,10},{9,11},{10,12},{11,13},... | collective-permute-start | bytes 245768 | tf_op jit(solution)/shard_map/ppermute | solution.py:49
  186.9 32.3 %collective-permute-start.27 = (bf16[256,1280]{1,0:T(8,128)(2,1)S(1)}, bf16[256,1280]{1,0:T(8,128)(2,1)S(1)}, u32[]{:S(2)}, u32[]{:S(2)}) collective-permute-start(bf16[256,1280]{1,0:T(8,128)(2,1)S(1)} %copy-done.3), channel_id=1, source_target_pairs={{0,8},{8,0},{16,24},{24,16},{1,9},{9,1},{17,25},{25,17},{2,10},{10... | collective-permute-start | bytes 1966088 | tf_op jit(solution)/shard_map/ppermute | solution.py:49
  187.0 32.2 %collective-permute-start.24 = (bf16[256,1280]{1,0:T(8,128)(2,1)S(1)}, bf16[256,1280]{1,0:T(8,128)(2,1)S(1)}, u32[]{:S(2)}, u32[]{:S(2)}) collective-permute-start(bf16[256,1280]{1,0:T(8,128)(2,1)S(1)} %copy-done.5), channel_id=1, source_target_pairs={{0,8},{8,0},{16,24},{24,16},{1,9},{9,1},{17,25},{25,17},{2,10},{10... | collective-permute-start | bytes 1966088 | tf_op jit(solution)/shard_map/ppermute | solution.py:49
  202.6 12.4 %collective-permute-start.35 = (f32[4,2,640]{2,1,0:T(2,128)S(1)}, f32[4,2,640]{2,1,0:T(2,128)S(1)}, u32[]{:S(2)}, u32[]{:S(2)}) collective-permute-start(f32[4,2,640]{2,1,0:T(2,128)S(1)} %slice.379), channel_id=1, source_target_pairs={{0,4},{1,5},{2,6},{3,7},{8,12},{9,13},{10,14},{11,15},{16,20},{17,... | collective-permute-start | bytes 61448 | tf_op jit(solution)/shard_map/ppermute | solution.py:49
  231.7 20.1 %collective-permute-start.37 = (bf16[2,96,2048]{2,1,0:T(8,128)(2,1)S(1)}, bf16[2,96,2048]{2,1,0:T(8,128)(2,1)S(1)}, u32[]{:S(2)}, u32[]{:S(2)}) collective-permute-start(bf16[2,96,2048]{2,1,0:T(8,128)(2,1)S(1)} %slice_bitcast_fusion.22), channel_id=1, source_target_pairs={{0,16},{8,24},{16,0},{24,8},{1,17},{9,25},{17,1},{25,9},{2,18},{10... | collective-permute-start | bytes 2359304 | tf_op jit(solution)/shard_map/ppermute | solution.py:49
  231.8 20.1 %collective-permute-start.39 = (bf16[2,96,2048]{2,1,0:T(8,128)(2,1)S(1)}, bf16[2,96,2048]{2,1,0:T(8,128)(2,1)S(1)}, u32[]{:S(2)}, u32[]{:S(2)}) collective-permute-start(bf16[2,96,2048]{2,1,0:T(8,128)(2,1)S(1)} %slice_bitcast_fusion.19), channel_id=1, source_target_pairs={{0,1},{1,0},{2,3},{3,2},{4,5},{5,4},{6,7},{7,6},{8,9},{9,8},{10,11... | collective-permute-start | bytes 2359304 | tf_op jit(solution)/shard_map/ppermute | solution.py:49
  265.2 20.5 %collective-permute-start.41 = (bf16[2,96,2048]{2,1,0:T(8,128)(2,1)S(1)}, bf16[2,96,2048]{2,1,0:T(8,128)(2,1)S(1)}, u32[]{:S(2)}, u32[]{:S(2)}) collective-permute-start(bf16[2,96,2048]{2,1,0:T(8,128)(2,1)S(1)} %multiply_convert_fusion.3.refs_0_), channel_id=1, source_target_pairs={{0,1},{1,0},{2,3},{3,2},{4,5},{5,4},{6,7},{7,6},{8,9},{9,8},{10,11... | collective-permute-start | bytes 2359304 | tf_op jit(solution)/shard_map/ppermute | solution.py:49
  268.5 25.8 %collective-permute-start.49 = (bf16[96,2048]{1,0:T(8,128)(2,1)}, bf16[96,2048]{1,0:T(8,128)(2,1)}, u32[]{:S(2)}, u32[]{:S(2)}) collective-permute-start(bf16[96,2048]{1,0:T(8,128)(2,1)} %slice_bitcast_fusion.30), channel_id=1, source_target_pairs={{0,1},{1,0},{2,3},{3,2},{4,5},{5,4},{6,7},{7,6},{8,9},{9,8},{10,11... | collective-permute-start | bytes 1179656 | tf_op jit(solution)/shard_map/ppermute | solution.py:49
  269.0 20.5 %collective-permute-start.42 = (bf16[2,96,2048]{2,1,0:T(8,128)(2,1)S(1)}, bf16[2,96,2048]{2,1,0:T(8,128)(2,1)S(1)}, u32[]{:S(2)}, u32[]{:S(2)}) collective-permute-start(bf16[2,96,2048]{2,1,0:T(8,128)(2,1)S(1)} %multiply_convert_fusion.3.refs_0_), channel_id=1, source_target_pairs={{0,16},{8,24},{16,0},{24,8},{1,17},{9,25},{17,1},{25,9},{2,18},{10... | collective-permute-start | bytes 2359304 | tf_op jit(solution)/shard_map/ppermute | solution.py:49
  272.2 25.9 %collective-permute-start.48 = (bf16[96,2048]{1,0:T(8,128)(2,1)}, bf16[96,2048]{1,0:T(8,128)(2,1)}, u32[]{:S(2)}, u32[]{:S(2)}) collective-permute-start(bf16[96,2048]{1,0:T(8,128)(2,1)} %slice_bitcast_fusion.31), channel_id=1, source_target_pairs={{0,16},{8,24},{16,0},{24,8},{1,17},{9,25},{17,1},{25,9},{2,18},{10... | collective-permute-start | bytes 1179656 | tf_op jit(solution)/shard_map/ppermute | solution.py:49
  286.5 17.5 %collective-permute-start.43 = (bf16[96,2048]{1,0:T(8,128)(2,1)}, bf16[96,2048]{1,0:T(8,128)(2,1)}, u32[]{:S(2)}, u32[]{:S(2)}) collective-permute-start(bf16[96,2048]{1,0:T(8,128)(2,1)} %slice_bitcast_fusion.25), channel_id=1, source_target_pairs={{0,16},{8,24},{16,0},{24,8},{1,17},{9,25},{17,1},{25,9},{2,18},{10... | collective-permute-start | bytes 1179656 | tf_op jit(solution)/shard_map/ppermute | solution.py:49
  291.2 12.8 %collective-permute-start.44 = (bf16[96,2048]{1,0:T(8,128)(2,1)}, bf16[96,2048]{1,0:T(8,128)(2,1)}, u32[]{:S(2)}, u32[]{:S(2)}) collective-permute-start(bf16[96,2048]{1,0:T(8,128)(2,1)} %slice_bitcast_fusion.24), channel_id=1, source_target_pairs={{0,1},{1,0},{2,3},{3,2},{4,5},{5,4},{6,7},{7,6},{8,9},{9,8},{10,11... | collective-permute-start | bytes 1179656 | tf_op jit(solution)/shard_map/ppermute | solution.py:49
  374.9 44.9 %collective-permute-start.55 = (bf16[1024,3072]{1,0:T(8,128)(2,1)}, bf16[1024,3072]{1,0:T(8,128)(2,1)}, u32[]{:S(2)}, u32[]{:S(2)}) collective-permute-start(bf16[1024,3072]{1,0:T(8,128)(2,1)} %convolution_convert_fusion), channel_id=1, source_target_pairs={{0,8},{8,0},{16,24},{24,16},{1,9},{9,1},{17,25},{25,17},{2,10},{10... | collective-permute-start | bytes 18874376 | tf_op jit(solution)/shard_map/ppermute | solution.py:49
  377.1 19.9 %collective-permute-start.50 = (bf16[2,96,2048]{2,1,0:T(8,128)(2,1)}, bf16[2,96,2048]{2,1,0:T(8,128)(2,1)S(1)}, u32[]{:S(2)}, u32[]{:S(2)}) collective-permute-start(bf16[2,96,2048]{2,1,0:T(8,128)(2,1)} %slice_bitcast_fusion.16), channel_id=1, source_target_pairs={{0,16},{8,24},{16,0},{24,8},{1,17},{9,25},{17,1},{25,9},{2,18},{10... | collective-permute-start | bytes 2359304 | tf_op jit(solution)/shard_map/ppermute | solution.py:49
  378.5 19.6 %collective-permute-start.52 = (bf16[2,96,2048]{2,1,0:T(8,128)(2,1)}, bf16[2,96,2048]{2,1,0:T(8,128)(2,1)S(1)}, u32[]{:S(2)}, u32[]{:S(2)}) collective-permute-start(bf16[2,96,2048]{2,1,0:T(8,128)(2,1)} %slice_bitcast_fusion.13), channel_id=1, source_target_pairs={{0,1},{1,0},{2,3},{3,2},{4,5},{5,4},{6,7},{7,6},{8,9},{9,8},{10,11... | collective-permute-start | bytes 2359304 | tf_op jit(solution)/shard_map/ppermute | solution.py:49
  384.0 29.4 %collective-permute-start.56 = (bf16[1024,1536]{1,0:T(8,128)(2,1)}, bf16[1024,1536]{1,0:T(8,128)(2,1)}, u32[]{:S(2)}, u32[]{:S(2)}) collective-permute-start(bf16[1024,1536]{1,0:T(8,128)(2,1)} %convolution_convert_fusion.2), channel_id=1, source_target_pairs={{0,8},{8,0},{16,24},{24,16},{1,9},{9,1},{17,25},{25,17},{2,10},{10... | collective-permute-start | bytes 9437192 | tf_op jit(solution)/shard_map/ppermute | solution.py:49
  432.1 288.6 %reduce-scatter.5.cloned.1.call-start = ((), (), s32[]{:S(2)}) async-start(), calls=%async_computation.4 | async-start | bytes 4915200 | tf_op jit(solution)/shard_map/reduce_scatter | solution.py:267
  434.0 17.4 %collective-permute-start.57 = (bf16[2,96,2048]{2,1,0:T(8,128)(2,1)S(1)}, bf16[2,96,2048]{2,1,0:T(8,128)(2,1)S(1)}, u32[]{:S(2)}, u32[]{:S(2)}) collective-permute-start(bf16[2,96,2048]{2,1,0:T(8,128)(2,1)S(1)} %fusion.103.refs_0_), channel_id=1, source_target_pairs={{0,16},{8,24},{16,0},{24,8},{1,17},{9,25},{17,1},{25,9},{2,18},{10... | collective-permute-start | bytes 2359304 | tf_op jit(solution)/shard_map/ppermute | solution.py:49
  434.7 17.7 %collective-permute-start.54 = (bf16[2,96,2048]{2,1,0:T(8,128)(2,1)S(1)}, bf16[2,96,2048]{2,1,0:T(8,128)(2,1)S(1)}, u32[]{:S(2)}, u32[]{:S(2)}) collective-permute-start(bf16[2,96,2048]{2,1,0:T(8,128)(2,1)S(1)} %fusion.103.refs_0_), channel_id=1, source_target_pairs={{0,1},{1,0},{2,3},{3,2},{4,5},{5,4},{6,7},{7,6},{8,9},{9,8},{10,11... | collective-permute-start | bytes 2359304 | tf_op jit(solution)/shard_map/ppermute | solution.py:49
  519.2 14.8 %collective-permute-start.64 = (bf16[2,96,2048]{2,1,0:T(8,128)(2,1)}, bf16[2,96,2048]{2,1,0:T(8,128)(2,1)}, u32[]{:S(2)}, u32[]{:S(2)}) collective-permute-start(bf16[2,96,2048]{2,1,0:T(8,128)(2,1)} %slice_bitcast_fusion.10), channel_id=1, source_target_pairs={{0,16},{8,24},{16,0},{24,8},{1,17},{9,25},{17,1},{25,9},{2,18},{10... | collective-permute-start | bytes 2359304 | tf_op jit(solution)/shard_map/ppermute | solution.py:49
  520.7 15.9 %collective-permute-start.66 = (bf16[2,96,2048]{2,1,0:T(8,128)(2,1)}, bf16[2,96,2048]{2,1,0:T(8,128)(2,1)}, u32[]{:S(2)}, u32[]{:S(2)}) collective-permute-start(bf16[2,96,2048]{2,1,0:T(8,128)(2,1)} %slice_bitcast_fusion.7), channel_id=1, source_target_pairs={{0,1},{1,0},{2,3},{3,2},{4,5},{5,4},{6,7},{7,6},{8,9},{9,8},{10,11... | collective-permute-start | bytes 2359304 | tf_op jit(solution)/shard_map/ppermute | solution.py:49
  549.3 86.8 %collective-permute-start.72 = (bf16[1024,1280]{1,0:T(8,128)(2,1)S(1)}, bf16[1024,1280]{1,0:T(8,128)(2,1)S(1)}, u32[]{:S(2)}, u32[]{:S(2)}) collective-permute-start(bf16[1024,1280]{1,0:T(8,128)(2,1)S(1)} %convolution_convert_fusion.1), channel_id=1, source_target_pairs={{0,8},{8,0},{16,24},{24,16},{1,9},{9,1},{17,25},{25,17},{2,10},{10... | collective-permute-start | bytes 7864328 | tf_op jit(solution)/shard_map/ppermute | solution.py:49
  552.3 13.4 %collective-permute-start.77 = (bf16[2,2,328,160]{2,3,1,0:T(8,128)(2,1)S(1)}, bf16[2,2,328,160]{2,3,1,0:T(8,128)(2,1)S(1)}, u32[]{:S(2)}, u32[]{:S(2)}) collective-permute-start(bf16[2,2,328,160]{2,3,1,0:T(8,128)(2,1)S(1)} %bitcast.440), channel_id=1, source_target_pairs={{0,8},{8,0},{16,24},{24,16},{1,9},{9,1},{17,25},{25,17},{2,10},{10... | collective-permute-start | bytes 1259528 | tf_op jit(solution)/shard_map/ppermute | solution.py:49
  561.5 20.1 %collective-permute-start.68 = (bf16[2,96,2048]{2,1,0:T(8,128)(2,1)S(1)}, bf16[2,96,2048]{2,1,0:T(8,128)(2,1)S(1)}, u32[]{:S(2)}, u32[]{:S(2)}) collective-permute-start(bf16[2,96,2048]{2,1,0:T(8,128)(2,1)S(1)} %slice_bitcast_fusion.4), channel_id=1, source_target_pairs={{0,16},{8,24},{16,0},{24,8},{1,17},{9,25},{17,1},{25,9},{2,18},{10... | collective-permute-start | bytes 2359304 | tf_op jit(solution)/shard_map/ppermute | solution.py:49
  561.7 20.0 %collective-permute-start.70 = (bf16[2,96,2048]{2,1,0:T(8,128)(2,1)S(1)}, bf16[2,96,2048]{2,1,0:T(8,128)(2,1)S(1)}, u32[]{:S(2)}, u32[]{:S(2)}) collective-permute-start(bf16[2,96,2048]{2,1,0:T(8,128)(2,1)S(1)} %slice_bitcast_fusion.1), channel_id=1, source_target_pairs={{0,1},{1,0},{2,3},{3,2},{4,5},{5,4},{6,7},{7,6},{8,9},{9,8},{10,11... | collective-permute-start | bytes 2359304 | tf_op jit(solution)/shard_map/ppermute | solution.py:49
  565.0 68.1 %collective-permute-start.73 = (bf16[1024,640]{1,0:T(8,128)(2,1)S(1)}, bf16[1024,640]{1,0:T(8,128)(2,1)S(1)}, u32[]{:S(2)}, u32[]{:S(2)}) collective-permute-start(bf16[1024,640]{1,0:T(8,128)(2,1)S(1)} %convolution_convert_fusion.4), channel_id=1, source_target_pairs={{0,8},{8,0},{16,24},{24,16},{1,9},{9,1},{17,25},{25,17},{2,10},{10... | collective-permute-start | bytes 3932168 | tf_op jit(solution)/shard_map/ppermute | solution.py:49
  565.8 26.5 %collective-permute-start.78 = (bf16[2,2,328,160]{2,3,1,0:T(8,128)(2,1)S(1)}, bf16[2,2,328,160]{2,3,1,0:T(8,128)(2,1)S(1)}, u32[]{:S(2)}, u32[]{:S(2)}) collective-permute-start(bf16[2,2,328,160]{2,3,1,0:T(8,128)(2,1)S(1)} %add_convert_fusion.9), channel_id=1, source_target_pairs={{0,2},{1,3},{2,4},{3,5},{4,6},{5,7},{6,0},{7,1},{8,10},{9,11},{10,... | collective-permute-start | bytes 1259528 | tf_op jit(solution)/shard_map/ppermute | solution.py:49
  581.5 46.1 %collective-permute-start.79 = (bf16[2,2,328,160]{2,3,1,0:T(8,128)(2,1)S(1)}, bf16[2,2,328,160]{2,3,1,0:T(8,128)(2,1)S(1)}, u32[]{:S(2)}, u32[]{:S(2)}) collective-permute-start(bf16[2,2,328,160]{2,3,1,0:T(8,128)(2,1)S(1)} %add_convert_fusion.9), channel_id=1, source_target_pairs={{0,4},{1,5},{2,6},{3,7},{4,0},{5,1},{6,2},{7,3},{8,12},{9,13},{10,... | collective-permute-start | bytes 1259528 | tf_op jit(solution)/shard_map/ppermute | solution.py:49
  581.7 47.5 %collective-permute-start.80 = (bf16[2,2,328,160]{2,3,1,0:T(8,128)(2,1)S(1)}, bf16[2,2,328,160]{2,3,1,0:T(8,128)(2,1)S(1)}, u32[]{:S(2)}, u32[]{:S(2)}) collective-permute-start(bf16[2,2,328,160]{2,3,1,0:T(8,128)(2,1)S(1)} %add_convert_fusion.9), channel_id=1, source_target_pairs={{0,6},{1,7},{2,0},{3,1},{4,2},{5,3},{6,4},{7,5},{8,14},{9,15},{10,... | collective-permute-start | bytes 1259528 | tf_op jit(solution)/shard_map/ppermute | solution.py:49
  592.3 39.4 %collective-permute-start.69 = (bf16[96,2048]{1,0:T(8,128)(2,1)S(1)}, bf16[96,2048]{1,0:T(8,128)(2,1)S(1)}, u32[]{:S(2)}, u32[]{:S(2)}) collective-permute-start(bf16[96,2048]{1,0:T(8,128)(2,1)S(1)} %fusion.81), channel_id=1, source_target_pairs={{0,1},{1,0},{2,3},{3,2},{4,5},{5,4},{6,7},{7,6},{8,9},{9,8},{10,11... | collective-permute-start | bytes 1179656 | tf_op jit(solution)/shard_map/ppermute | solution.py:49
  627.6 13.2 %collective-permute-start.71 = (bf16[96,2048]{1,0:T(8,128)(2,1)S(1)}, bf16[96,2048]{1,0:T(8,128)(2,1)}, u32[]{:S(2)}, u32[]{:S(2)}) collective-permute-start(bf16[96,2048]{1,0:T(8,128)(2,1)S(1)} %fusion.82), channel_id=1, source_target_pairs={{0,16},{8,24},{16,0},{24,8},{1,17},{9,25},{17,1},{25,9},{2,18},{10... | collective-permute-start | bytes 1179656 | tf_op jit(solution)/shard_map/ppermute | solution.py:49
  630.2 20.5 %collective-permute-start.81 = (bf16[2,2,328,160]{2,3,1,0:T(8,128)(2,1)}, bf16[2,2,328,160]{2,3,1,0:T(8,128)(2,1)}, u32[]{:S(2)}, u32[]{:S(2)}) collective-permute-start(bf16[2,2,328,160]{2,3,1,0:T(8,128)(2,1)} %add_convert_fusion.8), channel_id=1, source_target_pairs={{0,1},{1,0},{2,3},{3,2},{4,5},{5,4},{6,7},{7,6},{8,9},{9,8},{10,11... | collective-permute-start | bytes 1259528 | tf_op jit(solution)/shard_map/ppermute | solution.py:60
  631.7 28.1 %collective-permute-start.82 = (bf16[2,2,328,160]{2,3,1,0:T(8,128)(2,1)}, bf16[2,2,328,160]{2,3,1,0:T(8,128)(2,1)}, u32[]{:S(2)}, u32[]{:S(2)}) collective-permute-start(bf16[2,2,328,160]{2,3,1,0:T(8,128)(2,1)} %add_convert_fusion.8), channel_id=1, source_target_pairs={{0,16},{1,17},{2,18},{3,19},{4,20},{5,21},{6,22},{7,23},{8,24},{9,... | collective-permute-start | bytes 1259528 | tf_op jit(solution)/shard_map/ppermute | solution.py:60
  633.1 26.7 %collective-permute-start.83 = (bf16[2,2,328,160]{2,3,1,0:T(8,128)(2,1)}, bf16[2,2,328,160]{2,3,1,0:T(8,128)(2,1)}, u32[]{:S(2)}, u32[]{:S(2)}) collective-permute-start(bf16[2,2,328,160]{2,3,1,0:T(8,128)(2,1)} %add_convert_fusion.8), channel_id=1, source_target_pairs={{0,17},{1,16},{2,19},{3,18},{4,21},{5,20},{6,23},{7,22},{8,25},{9,... | collective-permute-start | bytes 1259528 | tf_op jit(solution)/shard_map/ppermute | solution.py:60
  672.0 16.6 %collective-permute-start.84 = (bf16[64,4608]{1,0:T(8,128)(2,1)}, bf16[64,4608]{1,0:T(8,128)(2,1)}, u32[]{:S(2)}, u32[]{:S(2)}) collective-permute-start(bf16[64,4608]{1,0:T(8,128)(2,1)} %get-tuple-element.192), channel_id=1, source_target_pairs={{0,1},{1,0},{2,3},{3,2},{4,5},{5,4},{6,7},{7,6},{8,9},{9,8},{10,11... | collective-permute-start | bytes 1769480 | tf_op jit(solution)/shard_map/ppermute | solution.py:60
  673.5 27.1 %collective-permute-start.85 = (bf16[64,4608]{1,0:T(8,128)(2,1)}, bf16[64,4608]{1,0:T(8,128)(2,1)S(1)}, u32[]{:S(2)}, u32[]{:S(2)}) collective-permute-start(bf16[64,4608]{1,0:T(8,128)(2,1)} %get-tuple-element.194), channel_id=1, source_target_pairs={{0,16},{1,17},{2,18},{3,19},{4,20},{5,21},{6,22},{7,23},{8,24},{9,... | collective-permute-start | bytes 1769480 | tf_op jit(solution)/shard_map/ppermute | solution.py:60
  674.9 25.7 %collective-permute-start.86 = (bf16[64,4608]{1,0:T(8,128)(2,1)}, bf16[64,4608]{1,0:T(8,128)(2,1)S(1)}, u32[]{:S(2)}, u32[]{:S(2)}) collective-permute-start(bf16[64,4608]{1,0:T(8,128)(2,1)} %get-tuple-element.193), channel_id=1, source_target_pairs={{0,17},{1,16},{2,19},{3,18},{4,21},{5,20},{6,23},{7,22},{8,25},{9,... | collective-permute-start | bytes 1769480 | tf_op jit(solution)/shard_map/ppermute | solution.py:60
  723.4 12.3 %collective-permute-start.75 = (bf16[64,1920]{1,0:T(8,128)(2,1)S(1)}, bf16[64,1920]{1,0:T(8,128)(2,1)S(1)}, u32[]{:S(2)}, u32[]{:S(2)}) collective-permute-start(bf16[64,1920]{1,0:T(8,128)(2,1)S(1)} %get-tuple-element.231), channel_id=1, source_target_pairs={{0,16},{1,17},{2,18},{3,19},{4,20},{5,21},{6,22},{7,23},{8,24},{9,... | collective-permute-start | bytes 737288 | tf_op jit(solution)/shard_map/ppermute | solution.py:60
  (127 other events, 988.3 us)
Sparse Core Ops, SparseCore 0:
  149.8 166.6 all-gather.1
  432.2 186.9 reduce-scatter.2
  640.8 79.7 reduce-scatter.4

commit v3 on v2

--- a/solution.py
+++ b/solution.py
@@ -58,6 +58,18 @@
                         to = (((y + by_y) % ny * nc + c) * nz + z) * nx + (x + by_x) % nx
                         pairs.append((((y * nc + c) * nz + z) * nx + x, to))
         return lax.ppermute(value, ("seq", "blk"), pairs)
+
+    def rows_ahead(self, rows):
+        ny, nc, nz, nx = (self.n[p] for p in "yczx")
+        out = None
+        for x in range(nx):
+            pairs = []
+            for s in range(ny * nc):
+                for z in range(nz - 1):
+                    pairs.append(((s * nz + z) * nx + nx - 1, (s * nz + z + 1) * nx + x))
+            got = lax.ppermute(rows, ("seq", "blk"), pairs)
+            out = got if out is None else out + got
+        return out
 
     def place(self, by_shift, part):
         n, me = self.n[part], self.index(part)
@@ -138,7 +150,7 @@
         rows = assemble_rows(out, step, width, normed)
         return rows.reshape(len(out) * step, width), hop
 
-    def collect(self, partial, micro):
+    def collect(self, partial, micro, *late):
         nx, ny = self.n["x"], self.n["y"]
         part = partial.reshape(micro, ny, nx, -1, partial.shape[1])
         out = []
@@ -146,12 +158,12 @@
             if m % 2 == 0:
                 held = part[m, 0].astype(F32)
                 for r in range(1, ny):
-                    held = held + self.shift(part[m, r], "y", -r).astype(F32)
+                    held = held + after(self.shift(part[m, r], "y", -r), *late).astype(F32)
                 last, n = "x", nx
             else:
                 held = part[m, :, 0].astype(F32)
                 for r in range(1, nx):
-                    held = held + self.shift(part[m, :, r], "x", -r).astype(F32)
+                    held = held + after(self.shift(part[m, :, r], "x", -r), *late).astype(F32)
                 last, n = "y", ny
             total = held[0]
             for r in range(1, n):
@@ -178,38 +190,6 @@
                 got.append(after(self.shift_plane(piece, ry, rx), *late) if ry or rx else piece)
             rows.append(self.place(got, "x"))
         return self.place(rows, "y")
-
-    def ring_first(self, block):
-        if self.n["z"] != 4:
-            return (self.shift(block, "z", -1),)
-        return self.shift(block, "z", -1), self.shift(block, "z", 1)
-
-    def ring_rest(self, block, first, *late):
-        nz = self.n["z"]
-        first = [after(v, *late) for v in first]
-        if nz != 4:
-            out = [block, first[0]]
-            for _ in range(2, nz):
-                out.append(self.shift(out[-1], "z", -1))
-            return out[:nz]
-        half = block.shape[0] // 2
-        above, below = first
-        far = [self.shift(above[:half], "z", -1), self.shift(below[half:], "z", 1)]
-        return [block, above, *far, below]
-
-    def whole_rows(self, pieces, *cuts):
-        nc, nz = self.n["c"], self.n["z"]
-        c, z = self.index("c"), self.index("z")
-        block = sum(p.shape[0] for p in pieces) // nz
-        starts = [sum(p.shape[0] for p in pieces[:i]) for i in range(len(pieces))]
-        parts, places = [], []
-        for s in range(nc):
-            parts += [self.shift(p, "c", -s) if s else p for p in pieces]
-            for at in starts:
-                where = ((c + s) % nc * nz + (z + at // block) % nz) * block + at % block
-                places.append(where)
-        places = jnp.stack(places).astype(jnp.int32)
-        return [assemble_tall(parts, places, i, len(cuts)) for i in cuts]
 
     def z_groups(self):
         nz, nx = self.n["z"], self.n["x"]
@@ -252,15 +232,14 @@
             cut, self.right, (((0,), (0,)), ((), ())), preferred_element_type=F32
         )
 
+    def lend(self):
+        nc, c = self.grid.n["c"], self.grid.index("c")
+        self.lent = [self.product((c + s) % nc).astype(BF16) for s in range(1, nc)]
+
     def meet(self):
-        grid, nc = self.grid, self.grid.n["c"]
-        c = grid.index("c")
-        others = [
-            grid.shift(self.product((c + s) % nc).astype(BF16), "c", s) for s in range(1, nc)
-        ]
-        mine = self.product(c)
-        for other in others:
-            mine = mine + other.astype(F32)
+        mine = self.product(self.grid.index("c"))
+        for s, lent in enumerate(self.lent):
+            mine = mine + self.grid.shift(lent, "c", s + 1).astype(F32)
         self.mine = mine
 
     def along_z(self, *late):
@@ -271,33 +250,6 @@
             tiled=True,
             axis_index_groups=self.grid.z_groups(),
         )
-
-    def slab(self, r):
-        nz = self.grid.n["z"]
-        rows = self.share // nz
-        at = (self.grid.index("z") + r) % nz * rows
-        return lax.dynamic_slice_in_dim(self.mine, at, rows, 0)
-
-    def step_one(self, *late):
-        low = after(self.slab(2).astype(BF16), *late)
-        half = low.shape[0] // 2
-        self.first = [
-            self.grid.shift(low[:half], "z", 1),
-            self.grid.shift(low[half:], "z", -1),
-        ]
-
-    def step_two(self, *late):
-        grid = self.grid
-        up, down = [after(v, *late).astype(F32) for v in self.first]
-        half = up.shape[0]
-        above, below = self.slab(1), self.slab(3)
-        to_up = jnp.concatenate([above[:half] + up, above[half:]], axis=0).astype(BF16)
-        to_down = jnp.concatenate([below[:half], below[half:] + down], axis=0).astype(BF16)
-        self.second = [grid.shift(to_up, "z", 1), grid.shift(to_down, "z", -1)]
-
-    def join(self, *late):
-        second = [after(v, *late).astype(F32) for v in self.second]
-        self.done = (self.slab(0) + (second[0] + second[1])).astype(BF16)
 
     def finish(self, count, *late):
         grid = self.grid
@@ -359,37 +311,6 @@
             flops=0, bytes_accessed=4 * count * step * width, transcendentals=0
         ),
     )(*arrays)
-
-
-def assemble_tall(pieces, places, part, parts):
-    width = pieces[0].shape[1] // parts
-    total = sum(p.shape[0] for p in pieces)
-    cut = next((t for t in (512, 640, 128) if width % t == 0), width)
-    steps = width // cut
-
-    def kernel(where, *refs):
-        out = refs[-1]
-        for i, ref in enumerate(refs[:-1]):
-            out[pl.ds(pl.multiple_of(where[i], 64), ref.shape[0])] = ref[...]
-
-    if cut % 128 and parts > 1:
-        pieces = [p[:, part * width : (part + 1) * width] for p in pieces]
-        part = 0
-    return pl.pallas_call(
-        kernel,
-        grid_spec=pltpu.PrefetchScalarGridSpec(
-            num_scalar_prefetch=1,
-            grid=(steps,),
-            in_specs=[
-                pl.BlockSpec((p.shape[0], cut), lambda i, where: (0, i + part * steps))
-                for p in pieces
-            ],
-            out_specs=pl.BlockSpec((total, cut), lambda i, where: (0, i)),
-        ),
-        out_shape=jax.ShapeDtypeStruct((total, width), BF16),
-        compiler_params=pltpu.CompilerParams(vmem_limit_bytes=32 * 1024 * 1024),
-        cost_estimate=pl.CostEstimate(flops=0, bytes_accessed=4 * total * width, transcendentals=0),
-    )(places, *pieces)
 
 
 def pack_small(rate_weight, input_weight, small):
@@ -728,27 +649,27 @@
     weights_in = grid.columns_of(
         [gained(proj_x, gain_in), gained(proj_y, gain_in), proj_out]
     ).reshape(plane, 3 * width)
-    own_rows = grid.turn(after(inputs, weights_in))
-    source = own_rows.astype(F32)
-    normed, in_hop = grid.spread(own_rows, normed=True)
-    own_x, own_yo = weights_in[:, :width], weights_in[:, width:]
-    first_x = grid.ring_first(own_x)
+    mix_all = grid.all_rows(weights_in)
     half = lax.dynamic_index_in_dim(after(packed, weights_in), c, 0, keepdims=False)
-    by_z = grid.place([half] + [grid.shift(half, "z", r) for r in range(1, nz)], "z")
-    by_z = lax.dynamic_slice_in_dim(by_z, y * per, per, 0)
-    blocks_x = grid.ring_rest(own_x, first_x, by_z, *in_hop)
-    (mix_x,) = grid.whole_rows(blocks_x, 0)
-    first_yo = grid.ring_first(after(own_yo, *blocks_x))
+    others = lax.optimization_barrier([grid.shift(half, "z", r) for r in range(1, nz)])
+    by_z = lax.dynamic_slice_in_dim(grid.place([half, *others], "z"), y * per, per, 0)
     by_x = grid.place([by_z] + [grid.shift(by_z, "x", r) for r in range(1, nx)], "x")
     by_x = jnp.moveaxis(by_x, 0, 1).reshape(per * nx, *half.shape)
     halves = grid.place([by_x] + [grid.shift(by_x, "c", r) for r in range(1, nc)], "c")
+    gates, vec = unpack_small(halves, x, per, heads)
+    own_rows = grid.turn(after(inputs, *others, *beside))
+    source = own_rows.astype(F32)
+    normed, in_hop = grid.spread(own_rows, halves, normed=True)
+    ahead = grid.rows_ahead(own_rows[:, step - 2 * HALO :])
+    ahead = jnp.stack([ahead] + [grid.shift(ahead, "y", r) for r in range(1, ny)], axis=1)
+    ahead = ahead.reshape(chains * 2 * HALO, depth)
     pieces = [gained(mlp_gate, gain_mlp), gained(mlp_up, gain_mlp), mlp_down]
-    weights_ff = grid.columns_of([after(p, weights_in) for p in pieces]).reshape(plane, -1)
-
-    drive = mix(normed, mix_x).astype(BF16).reshape(chains, nx, step, width)
-    own_cot = grid.turn(after(cotangent, drive))
-    gates, vec = unpack_small(after(halves, drive), x, per, heads)
-    segments = after(jnp.stack([seg_ids, *beside], axis=1), drive)
+    pieces = [after(p, weights_in) for p in pieces]
+    weights_ff = grid.columns_of(pieces, *in_hop).reshape(plane, -1)
+    ff_in = grid.all_rows(weights_ff[:, : 2 * ff_width])
+    ff_down = grid.all_rows(weights_ff[:, 2 * ff_width :])
+
+    segments = jnp.stack([seg_ids, *beside], axis=1)
     padded = jnp.pad(segments, ((0, 0), (0, 0), (HALO, 0)), constant_values=-1)
     near = lax.dynamic_slice_in_dim(padded, z * length, length + HALO, 2)
     here = near[:, :, HALO:]
@@ -759,13 +680,16 @@
     same = same.reshape(chains, length, 8)
     order = ((x - jnp.arange(nx, dtype=jnp.int32)) % nx).astype(jnp.int32)
 
-    blocks_yo = grid.ring_rest(own_yo, first_yo, drive)
-    ff_all = grid.all_rows(after(weights_ff, *blocks_yo))
-    mix_y, mix_out = grid.whole_rows(blocks_yo, 0, 1)
+    mix_all = after(mix_all, vec, same)
+    mix_x, mix_y, mix_out = (mix_all[:, i * width : (i + 1) * width] for i in range(3))
+    drive = mix(normed, mix_x).astype(BF16).reshape(chains, nx, step, width)
+    ahead = ahead.astype(F32)
+    ahead = ahead * lax.rsqrt(jnp.mean(ahead * ahead, axis=-1, keepdims=True) + NORM_EPS)
+    halo = mix(ahead.astype(BF16), mix_x).astype(BF16).reshape(chains, 2 * HALO, width)
+    halo = halo[:, HALO:].astype(F32)
+    own_cot = grid.turn(after(cotangent, drive))
     pre_y = mix(normed, mix_y)
     branch_y, gelu_y_back = jax.vjp(jax.nn.gelu, pre_y)
-    last = lax.dynamic_index_in_dim(drive, (x - (nx - 1)) % nx, 1, keepdims=False)
-    halo = grid.shift(last[:, step - HALO :].astype(F32), "z", 1, wrap=False)
     shape = (chains, length, width)
     turned = (chains, nx, step, width)
     conv, rate, gate_in, state, prods, ends = scan_call(
@@ -785,36 +709,38 @@
         return carry
 
     rows_cot, cot_hop = grid.spread(own_cot, ends)
-    start = carry_from(after(ends, *cot_hop)[:, 0:2], 1)
+    start = carry_from(ends[:, 0:2], 1)
     hidden = (state + prods * start[:, None]).astype(BF16)
     hidden_f = hidden.reshape(chains * length, width).astype(F32)
-    mixed = (branch_y * hidden_f).astype(BF16)
+    mixed = after((branch_y * hidden_f).astype(BF16), *cot_hop)
     resid = source + grid.collect(mix_back(mixed, mix_out).astype(BF16), micro)
 
     scale_mlp = lax.rsqrt(jnp.mean(resid * resid, axis=-1, keepdims=True) + NORM_EPS)
     normed_mlp, _ = grid.spread((resid * scale_mlp).astype(BF16))
-    ff_all = after(ff_all, normed_mlp)
-    ff_gate = ff_all[:, :ff_width]
-    ff_up = ff_all[:, ff_width : 2 * ff_width]
-    ff_down = ff_all[:, 2 * ff_width :]
-    pre_gate = mix(normed_mlp, ff_gate)
-    pre_up = mix(normed_mlp, ff_up)
+    pre_ff = mix(normed_mlp, after(ff_in, normed_mlp))
+    pre_gate, pre_up = pre_ff[:, :ff_width], pre_ff[:, ff_width:]
     activated, gelu_gate_back = jax.vjp(jax.nn.gelu, pre_gate)
     product = (activated * pre_up).astype(BF16)
+    sum_down = WeightSum(grid, rows_cot, product)
+    sum_down.lend()
+    sum_down.meet()
+    ff_down = after(ff_down, sum_down.mine)
     grad_prod = mix(rows_cot, ff_down)
     grad_gate = gelu_gate_back(grad_prod * pre_up)[0].astype(BF16)
     grad_up = (grad_prod * activated).astype(BF16)
-    part_mlp = (mix_back(grad_gate, ff_gate) + mix_back(grad_up, ff_up)).astype(BF16)
-    weighted_mlp = grid.collect(part_mlp, micro)
     grad_ff = jnp.concatenate([grad_gate, grad_up], axis=1)
-    sum_down = WeightSum(grid, rows_cot, after(product, part_mlp))
-    sum_ff = WeightSum(grid, normed_mlp, after(grad_ff, part_mlp))
-    sum_down.meet()
+    sum_ff = WeightSum(grid, normed_mlp, grad_ff)
+    sum_ff.lend()
+    part_mlp = mix_back(after(grad_ff, *sum_ff.lent), ff_in).astype(BF16)
+    sum_ff.right = after(grad_ff, part_mlp)
     sum_ff.meet()
     sum_ff.mine = jnp.concatenate([sum_ff.mine.astype(BF16), sum_down.mine.astype(BF16)], axis=1)
     sum_ff.along_z()
+    weighted_mlp = grid.collect(part_mlp, micro, sum_ff.mine)
     grad_resid = own_cot.astype(F32) + norm_back(weighted_mlp, resid, scale_mlp)
-    grad_branch, _ = grid.spread(grad_resid.astype(BF16), sum_ff.mine)
+    part_out = mix_back(after(product, weighted_mlp), ff_down).astype(BF16)
+    grad_branch, _ = grid.spread(grad_resid.astype(BF16), part_out)
+    block_out = resid + grid.collect(after(part_out, grad_branch), micro)
 
     grad_mixed = mix(grad_branch, mix_out)
     grad_pre_y = gelu_y_back(grad_mixed * hidden_f)[0].astype(BF16)
@@ -864,31 +790,16 @@
     d_drive = d_drive + jnp.where(chunk == (x - (nx - 1)) % nx, tail, 0.0)
     grad_drive = d_drive.astype(BF16).reshape(chains * length, width)
     part_in = (mix_back(grad_pre_y, mix_y) + mix_back(grad_drive, mix_x)).astype(BF16)
-    weighted_in = grid.collect(part_in, micro)
+    part_in = after(part_in, block_out)
     both = jnp.concatenate([grad_pre_y, grad_drive], axis=1)
-    sum_in = WeightSum(grid, normed, after(both, weighted_in))
-    sum_out = WeightSum(grid, grad_branch, after(mixed, weighted_in))
+    sum_in = WeightSum(grid, normed, after(both, part_in))
+    sum_out = WeightSum(grid, grad_branch, after(mixed, part_in))
+    sum_in.lend()
+    sum_out.lend()
     sum_in.meet()
     sum_out.meet()
     sum_in.mine = jnp.concatenate([sum_in.mine.astype(BF16), sum_out.mine.astype(BF16)], axis=1)
-    sum_in.along_z(sum_ff.done)
-    part_out = mix_back(after(product, weighted_in), ff_down).astype(BF16)
-    block_out = resid + grid.collect(part_out, micro)
-    block_out = grid.turn(block_out.astype(BF16), back=True)
-    grad_gate_w, grad_up_w, grad_down_w = sum_ff.finish(3)
-    grad_y_w, grad_x_w, grad_out_w = sum_in.finish(3)
-    scale_in = lax.rsqrt(jnp.mean(source * source, axis=-1, keepdims=True) + NORM_EPS)
-    grad_source = grad_resid + norm_back(weighted_in, source, scale_in)
-    grad_source = grid.turn(grad_source.astype(BF16), back=True)
-
-    def gain_grad(*pairs):
-        return sum(jnp.sum(w.astype(F32) * g, axis=1) for w, g in pairs)
-
-    grad_norm_in = gain_grad((proj_y, grad_y_w), (proj_x, grad_x_w))
-    grad_norm_mlp = gain_grad((mlp_gate, grad_gate_w), (mlp_up, grad_up_w))
-
-    d_pre = [after(v, weighted_in) for v in d_pre]
-    conv_low = conv.reshape(chains * length, width).astype(BF16)
+    conv_low = after(conv, part_in).reshape(chains * length, width).astype(BF16)
     gate_dense = [
         lax.dot_general(
             conv_low,
@@ -898,19 +809,35 @@
         )
         for d in d_pre
     ]
-    blocks = jnp.stack(
-        [
-            jnp.concatenate(
-                [d[h * block : (h + 1) * block, h * block : (h + 1) * block] for d in gate_dense]
-                + [sums[:, h * block : (h + 1) * block]],
-                axis=0,
-            )
-            for h in range(per * heads)
-        ]
-    )
-    blocks = blocks.astype(BF16).reshape(per, heads, 2 * block + 8, block)
-    blocks = grid.total(blocks, "c")
-    blocks = grid.total(blocks, "z")
+    rest = jnp.zeros((8, block), F32)
+    blocks = []
+    for h in range(per * heads):
+        at = slice(h * block, (h + 1) * block)
+        blocks.append(jnp.concatenate([gate_dense[0][at, at], sums[:, at], rest], axis=0))
+        blocks.append(jnp.concatenate([gate_dense[1][at, at], rest, rest], axis=0))
+    blocks = jnp.stack(blocks).astype(BF16).reshape(per, heads, 2, block + 16, block)
+    kept = lax.dynamic_index_in_dim(blocks, c, 2, keepdims=False).astype(F32)
+    for r in range(1, nc):
+        given = lax.dynamic_index_in_dim(blocks, (c + r) % nc, 2, keepdims=False)
+        kept = kept + grid.shift(given, "c", r).astype(F32)
+    blocks = kept.astype(BF16)
+    weighted_in = grid.collect(part_in, micro, sum_in.mine, blocks)
+    weighted_in = after(weighted_in, sum_ff.done)
+    sum_in.along_z(sum_ff.done)
+    grad_gate_w, grad_up_w, grad_down_w = sum_ff.finish(3)
+    block_out = grid.turn(block_out.astype(BF16), back=True)
+    grad_y_w, grad_x_w, grad_out_w = sum_in.finish(3)
+    scale_in = lax.rsqrt(jnp.mean(source * source, axis=-1, keepdims=True) + NORM_EPS)
+    grad_source = grad_resid + norm_back(weighted_in, source, scale_in)
+    grad_source = grid.turn(grad_source.astype(BF16), back=True)
+
+    def gain_grad(*pairs):
+        return sum(jnp.sum(w.astype(F32) * g, axis=1) for w, g in pairs)
+
+    grad_norm_in = gain_grad((proj_y, grad_y_w), (proj_x, grad_x_w))
+    grad_norm_mlp = gain_grad((mlp_gate, grad_gate_w), (mlp_up, grad_up_w))
+
+    blocks = grid.total(blocks, "z", grad_gate_w)
     got = [
         [grid.shift_plane(blocks, ry, rx) if ry or rx else blocks for rx in range(nx)]
         for ry in range(ny)
@@ -918,9 +845,10 @@
     by_y = grid.place([grid.place(row, "x") for row in got], "y")
     mine = lax.dynamic_index_in_dim(
         by_y.reshape(ny * nx * per, *blocks.shape[1:]), z * nx + x, 0, keepdims=False
-    ).astype(F32)
-    mats = mine[:, : 2 * block].reshape(heads, 2, block, block)
-    sums_own = jnp.moveaxis(mine[:, 2 * block :], 0, 1).reshape(8, share)
+    )
+    mats = grid.gather(mine, "c").astype(F32)
+    sums_own = jnp.moveaxis(mats[0, :, block : block + 8], 0, 1).reshape(8, share)
+    mats = mats[:, :, :block]
     return (
         block_out,
         grad_source,
@@ -929,9 +857,9 @@
         grad_x_w * gain_in,
         sums_own[0:4],
         sums_own[4],
-        mats[:, 0],
+        mats[0],
         sums_own[5],
-        mats[:, 1],
+        mats[1],
         sums_own[6],
         sums_own[7] * slope_back,
         grad_out_w,

time: 757 us -> 668 us (0.88)
  waiting for transfers between devices: 346 us -> 241 us
  matrix products: 113 us -> 125 us
    ppermute x72 -> x55, waiting for transfers between devices: 244 us -> 170 us  [shift(): return lax.ppermute(value, axis, pairs)]
    ppermute x15, waiting for transfers between devices: 76.4 us -> 47.4 us  [shift_plane(): return lax.ppermute(value, ('seq', 'blk'), pairs)]
    dot_general x8, matrix products: 31.6 us -> 40.6 us  [product(): lax.dot_general(cut, self.right, (((0,), (0,)), ((), ())), preferred_elem...]
    all_gather x1 -> x3, waiting for transfers between devices: 8.41 us -> 0.01 us  [all_rows(): lax.all_gather(block, ('seq', 'blk'), axis=0, tiled=True, axis_index_grou...]
    unnamed x205 -> x209, local copies, waits for them, and re-layouts: 18.9 us -> 26.6 us
    ppermute x72 -> x55, starting transfers between devices: 84.2 us -> 81.8 us  [shift(): return lax.ppermute(value, axis, pairs)]
    dot_general x6 -> x5, matrix products: 38.6 us -> 36.4 us  [mix_back(): lax.dot_general(left, right, (((1,), (1,)), ((), ())), preferred_element_...]
  transfers between devices with their start and end apart: 90 -> 77, of which waited for: 51 -> 45; matrix products, arithmetic and copies ran while one was open for 18% -> 30% of each run, Pallas kernels for 7% -> 7%
where the time goes in v3:
time: 668 us; the launch traced here: 661 us
  waiting for transfers between devices  241 us (36%)
  matrix products  125 us (19%)
  starting transfers between devices  102 us (15%)
  local copies, waits for them, and re-layouts  63.9 us (10%)
  other arithmetic  63.4 us (9%)
  Pallas kernels  48.9 us (7%)
  between operations  16.2 us (2%)
    ppermute x55, waiting for transfers between devices, shift(): return lax.ppermute(value, axis, pairs)  170 us
    ppermute x55, starting transfers between devices, shift(): return lax.ppermute(value, axis, pairs)  81.8 us
    ppermute x15, waiting for transfers between devices, shift_plane(): return lax.ppermute(value, ('seq', 'blk'), pairs)  47.4 us
    dot_general x6, matrix products, mix(): return jnp.dot(left, right, preferred_element_type=F32)  46.3 us
    dot_general x8, matrix products, product(): lax.dot_general(cut, self.right, (((0,), (0,)), ((), ())), preferred_elem...  40.6 us
    dot_general x5, matrix products, mix_back(): lax.dot_general(left, right, (((1,), (1,)), ((), ())), preferred_element_...  36.4 us
    pallas_call x3, Pallas kernels, scan_call(): pl.pallas_call(kernel, grid=(chains,), in_specs=specs, out_specs=out_spec...  28.9 us
    unnamed x209, local copies, waits for them, and re-layouts  26.6 us
  transfers between devices with their start and end apart: 77, of which 45 were waited for; matrix products, arithmetic and copies ran while one was open for 30% of the time, Pallas kernels for 7%

profile of v3, /device:TPU:0, one launch (start us, length us, event | category | flops | bytes accessed | tf_op | source)
XLA Modules:
  0.0 661.2 jit_solution(4036091356884981095)
XLA Ops:
  9.4 4.0 collective-permute-start.2
  14.2 6.1 collective-permute-done.2
  20.2 4.4 collective-permute-done.1
  33.5 2.6 collective-permute-start.4
  41.5 2.5 collective-permute-done.3
  44.0 15.8 %collective-permute-done.4 = bf16[416,160]{1,0:T(8,128)(2,1)S(1)} collective-permute-done((bf16[416,160]{1,0:T(8,128)(2,1)S(1)}, bf16[416,160]{1,0:T(8,128)(2,1)S(1)}, u32[]{:S(2)}, u32[]{:S(2)}) %collective-permute-start.4) | collective-permute-done | bytes 133152 | tf_op jit(solution)/shard_map/ppermute | solution.py:49
  67.6 6.1 collective-permute-done.8
  81.2 17.8 %collective-permute-done.10.refs_2_ = bf16[2,96,2048]{2,1,0:T(8,128)(2,1)S(1)} collective-permute-done((bf16[2,96,2048]{2,1,0:T(8,128)(2,1)}, bf16[2,96,2048]{2,1,0:T(8,128)(2,1)S(1)}, u32[]{:S(2)}, u32[]{:S(2)}) %collective-permute-start.10) | collective-permute-done | bytes 786464 | tf_op jit(solution)/shard_map/ppermute | solution.py:49
  99.0 3.0 collective-permute-done.7.refs_1_
  102.0 8.0 %collective-permute-done.30 = bf16[64,4608]{1,0:T(8,128)(2,1)} collective-permute-done((bf16[64,4608]{1,0:T(8,128)(2,1)}, bf16[64,4608]{1,0:T(8,128)(2,1)}, u32[]{:S(2)}, u32[]{:S(2)}) %collective-permute-start.30) | collective-permute-done | bytes 589856 | tf_op jit(solution)/shard_map/ppermute | solution.py:60
  127.4 23.4 %collective-permute-start.12 = (bf16[96,2048]{1,0:T(8,128)(2,1)S(1)}, bf16[96,2048]{1,0:T(8,128)(2,1)S(1)}, u32[]{:S(2)}, u32[]{:S(2)}) collective-permute-start(bf16[96,2048]{1,0:T(8,128)(2,1)S(1)} %slice_bitcast_fusion.30), channel_id=1, source_target_pairs={{0,1},{1,0},{2,3},{3,2},{4,5},{5,4},{6,7},{7,6},{8,9},{9,8},{10,11... | collective-permute-start | bytes 1179656 | tf_op jit(solution)/shard_map/ppermute | solution.py:49
  154.2 3.0 collective-permute-done.12.refs_4_
  161.9 2.5 fusion.48
  164.6 4.5 fusion.45
  169.2 10.3 %shard_map.309 = (f32[4,192,640]{2,1,0:T(8,128)S(1)}, f32[4,192,640]{2,1,0:T(8,128)}, f32[4,192,640]{2,1,0:T(8,128)}, f32[4,2,96,640]{3,2,1,0:T(8,128)}, f32[4,2...) custom-call(s32[2]{0:T(128)S(1)} %and_select_fusion.order, bf16[4,2,96,640]{3,2,1,0:T(8,128)(2,1)S(1)} %bitcast.427, ...), custom_call_target="tpu_custom_call" | custom-call | flops 2516582400 | bytes 12660744 | tf_op jit(solution)/shard_map/pallas_call | solution.py:573
  180.8 4.2 collective-permute-start.16
  185.1 2.4 collective-permute-start.17
  192.0 2.5 add_convert_fusion.5
  195.0 6.3 fusion.19
  201.3 5.8 collective-permute-done.20.refs_2_
  207.1 5.2 convolution_convert_fusion.3
  218.7 10.1 %collective-permute-done.21 = bf16[2,96,2048]{2,1,0:T(8,128)(2,1)S(1)} collective-permute-done((bf16[2,96,2048]{2,1,0:T(8,128)(2,1)}, bf16[2,96,2048]{2,1,0:T(8,128)(2,1)S(1)}, u32[]{:S(2)}, u32[]{:S(2)}) %collective-permute-start.21) | collective-permute-done | bytes 786464 | tf_op jit(solution)/shard_map/ppermute | solution.py:49
  228.8 2.8 collective-permute-done.23
  235.1 8.7 %collective-permute-done.22 = bf16[96,2048]{1,0:T(8,128)(2,1)S(1)} collective-permute-done((bf16[96,2048]{1,0:T(8,128)(2,1)S(1)}, bf16[96,2048]{1,0:T(8,128)(2,1)S(1)}, u32[]{:S(2)}, u32[]{:S(2)}) %collective-permute-start.22) | collective-permute-done | bytes 393248 | tf_op jit(solution)/shard_map/ppermute | solution.py:49
  250.7 14.8 %collective-permute-done.25.refs_1_ = bf16[2,96,2048]{2,1,0:T(8,128)(2,1)S(1)} collective-permute-done((bf16[2,96,2048]{2,1,0:T(8,128)(2,1)S(1)}, bf16[2,96,2048]{2,1,0:T(8,128)(2,1)S(1)}, u32[]{:S(2)}, u32[]{:S(2)}) %collective-permute-start.25) | collective-permute-done | bytes 786464 | tf_op jit(solution)/shard_map/ppermute | solution.py:49
  282.0 13.6 %fusion.113 = f32[768,3072]{1,0:T(8,128)S(1)} fusion(bf16[768,2048]{1,0:T(8,128)(2,1)} %bitcast.420, bf16[2048,3072]{1,0:T(8,128)(2,1)} %all-gather.6.cloned.1.call-done), kind=kOutput, calls=%fused_computation.386 | convolution fusion | flops 9663676416 | bytes 25165824 | tf_op jit(solution)/shard_map/dot_general | solution.py:592
  297.2 2.6 copy-done.54
  299.9 4.0 convolution_convert_fusion.2
  303.9 6.0 collective-permute-done.34
  309.9 7.3 %convert_add_fusion = bf16[1024,1536]{1,0:T(8,128)(2,1)} fusion(bf16[1024,1536]{1,0:T(8,128)(2,1)} %collective-permute-done.34, bf16[768,1536]{1,0:T(8,128)(2,1)} %copy-done.66, bf16[768,2048]{1,0:T(8,128)(2,1)} %bitcast.423, s32[]{:T(128)S(6)} %select_n.605), kind=kOutput, calls=%fused_computation.5 | convolution fusion | flops 2420637696 | bytes 10223620 | tf_op jit(solution)/shard_map/dot_general | solution.py:231
  317.2 12.9 %fusion.6 = (bf16[768,1536]{1,0:T(8,128)(2,1)S(1)}, bf16[768,1536]{1,0:T(8,128)(2,1)S(1)}) fusion(f32[768,3072]{1,0:T(8,128)} %copy-done.54, bf16[768,2048]{1,0:T(8,128)(2,1)} %bitcast.424, bf16[2048,1536]{1,0:T(8,128)(2,1)} %all-gather.8.cloned.1.call-done), kind=kOutput, calls=%fused_computation.14 | convolution fusion | flops 4860149760 | bytes 23592960 | tf_op jit(solution)/shard_map/dot_general | solution.py:592
  330.2 7.8 %convolution_convert_fusion = bf16[1024,3072]{1,0:T(8,128)(2,1)} fusion(bf16[768,2048]{1,0:T(8,128)(2,1)S(1)} %bitcast.421, s32[]{:T(128)S(6)} %select_n.607, bf16[768,1536]{1,0:T(8,128)(2,1)S(1)} %get-tuple-element.134, bf16[768,1536]{1,0:T(8,128)(2,1)S(1)} %get-tuple-element.133), kind=kOutput, calls=%fused_computation.6 | convolution fusion | flops 4844421120 | bytes 12582916 | tf_op jit(solution)/shard_map/dot_general | solution.py:231
  338.7 13.0 %convolution_convert_fusion.5 = bf16[768,2048]{1,0:T(8,128)(2,1)S(1)} fusion(bf16[768,3072]{1,0:T(8,128)(2,1)S(1)} %pad_maximum_fusion.1, bf16[2048,3072]{1,0:T(8,128)(2,1)} %all-gather.6.cloned.1.call-done), kind=kOutput, calls=%fused_computation.24 | convolution fusion | flops 9665249280 | bytes 20447232 | tf_op jit(solution)/shard_map/dot_general | solution.py:596
  356.0 7.6 %add_convert_fusion = bf16[1024,3072]{1,0:T(8,128)(2,1)S(1)} fusion(bf16[1024,3072]{1,0:T(8,128)(2,1)} %collective-permute-done.36, bf16[768,3072]{1,0:T(8,128)(2,1)S(1)} %pad_maximum_fusion.1, bf16[768,2048]{1,0:T(8,128)(2,1)S(1)} %bitcast.422, s32[]{:T(128)S(6)} %select_n.605), kind=kOutput, calls=%fused_computation | convolution fusion | flops 4841275392 | bytes 18874372 | tf_op jit(solution)/shard_map/dot_general | solution.py:231
  363.7 4.7 pad_maximum_fusion
  368.6 4.1 collective-permute-done.38
  378.9 8.8 %collective-permute-done.37 = bf16[96,2048]{1,0:T(8,128)(2,1)S(1)} collective-permute-done((bf16[96,2048]{1,0:T(8,128)(2,1)S(1)}, bf16[96,2048]{1,0:T(8,128)(2,1)S(1)}, u32[]{:S(2)}, u32[]{:S(2)}) %collective-permute-start.37) | collective-permute-done | bytes 393248 | tf_op jit(solution)/shard_map/ppermute | solution.py:49
  392.1 6.5 convolution_convert_fusion.4
  398.6 8.9 %collective-permute-done.41.refs_2_ = bf16[2,96,2048]{2,1,0:T(8,128)(2,1)S(1)} collective-permute-done((bf16[2,96,2048]{2,1,0:T(8,128)(2,1)S(1)}, bf16[2,96,2048]{2,1,0:T(8,128)(2,1)S(1)}, u32[]{:S(2)}, u32[]{:S(2)}) %collective-permute-start.41) | collective-permute-done | bytes 786464 | tf_op jit(solution)/shard_map/ppermute | solution.py:49
  411.6 5.4 collective-permute-done.43.refs_4_
  421.3 2.4 shard_map.313
  423.7 6.6 multiply_convert_fusion.2
  430.3 7.3 %shard_map.315 = (f32[4,192,640]{2,1,0:T(8,128)S(1)}, f32[4,192,640]{2,1,0:T(8,128)S(1)}, f32[4,8,640]{2,1,0:T(8,128)S(1)}) custom-call(s32[2]{0:T(128)S(1)} %and_select_fusion.order, bf16[4,2,96,640]{3,2,1,0:T(8,128)(2,1)S(1)} %bitcast.426, f32[4,192,8]{2,1,0:T(8,128)S(1)} %stack.270.same, f32[8,640]{1,0:T(8,128)S(1)} %get-tuple-element.79.vec, ...), custom_call_target="tpu_custom_call" | custom-call | flops 19660800 | bytes 7008264 | tf_op jit(solution)/shard_map/pallas_call | solution.py:573
  442.5 6.4 fusion.10
  451.7 11.4 %shard_map.316 = (f32[4,2,96,640]{3,2,1,0:T(8,128)}, f32[4,8,640]{2,1,0:T(8,128)S(1)}, bf16[4,192,640]{2,1,0:T(8,128)(2,1)S(1)}, bf16[4,192,640]{2,1,0:T(8,128)(2,1)S(1)}, f32[8,640]{1,0:T(8,128)S(1)}) custom-call(s32[2]{0:T(128)S(1)} %and_select_fusion.order, bf16[4,2,96,640]{3,2,1,0:T(8,128)(2,1)S(1)} %bitcast.428, ...), custom_call_target="tpu_custom_call" | custom-call | flops 2516582400 | bytes 20566024 | tf_op jit(solution)/shard_map/pallas_call | solution.py:573
  467.0 6.6 collective-permute-done.51
  477.4 5.4 add_convert_fusion.1
  487.3 6.6 collective-permute-done.45
  497.2 3.8 convolution_convert_fusion.1
  501.1 2.5 convolution_convert_fusion.6
  515.2 4.2 collective-permute-start.62
  519.4 3.5 add_convert_fusion.3
  523.0 4.0 add_convert_fusion.2
  529.1 3.0 collective-permute-done.57
  532.8 2.4 convert_add_fusion.3
  537.8 8.0 %collective-permute-done.56 = bf16[96,2048]{1,0:T(8,128)(2,1)S(1)} collective-permute-done((bf16[96,2048]{1,0:T(8,128)(2,1)S(1)}, bf16[96,2048]{1,0:T(8,128)(2,1)S(1)}, u32[]{:S(2)}, u32[]{:S(2)}) %collective-permute-start.56) | collective-permute-done | bytes 393248 | tf_op jit(solution)/shard_map/ppermute | solution.py:49
  548.1 2.7 dynamic-slice_bitcast_fusion.2
  556.4 3.0 fusion.35.src
  561.5 5.8 collective-permute-done.63
  568.3 8.3 %collective-permute-done.64 = bf16[64,4608]{1,0:T(8,128)(2,1)} collective-permute-done((bf16[64,4608]{1,0:T(8,128)(2,1)}, bf16[64,4608]{1,0:T(8,128)(2,1)}, u32[]{:S(2)}, u32[]{:S(2)}) %collective-permute-start.64) | collective-permute-done | bytes 589856 | tf_op jit(solution)/shard_map/ppermute | solution.py:60
  581.0 11.6 %collective-permute-done.67 = bf16[2,2,176,160]{2,3,1,0:T(8,128)(2,1)S(1)} collective-permute-done((bf16[2,2,176,160]{2,3,1,0:T(8,128)(2,1)S(1)}, bf16[2,2,176,160]{2,3,1,0:T(8,128)(2,1)S(1)}, u32[]{:S(2)}, u32[]{:S(2)}) %collective-permute-start.67) | collective-permute-done | bytes 225312 | tf_op jit(solution)/shard_map/ppermute | solution.py:49
  601.1 4.6 collective-permute-done.69
  611.2 23.5 %reduce-scatter.5.cloned.1.call-done = bf16[256,1920]{1,0:T(8,128)(2,1)} async-done(((bf16[1024,1920]{1,0:T(8,128)(2,1)}), bf16[256,1920]{1,0:T(8,128)(2,1)}) %reduce-scatter.5.cloned.1.call-update) | async-done | bytes 983056 | tf_op jit(solution)/shard_map/reduce_scatter | solution.py:246
  643.5 5.5 collective-permute-done.60
  (521 shorter events, 206.0 us)
Async XLA Ops:
  7.2 154.7 %all-gather.4.cloned.1.call-start = ((), (), s32[]{:S(2)}) async-start(), calls=%async_computation.2 | async-start | bytes 8847360 | tf_op jit(solution)/shard_map/all_gather | solution.py:205
  9.4 10.8 %collective-permute-start.2 = (bf16[64,1920]{1,0:T(8,128)(2,1)S(1)}, bf16[64,1920]{1,0:T(8,128)(2,1)S(1)}, u32[]{:S(2)}, u32[]{:S(2)}) collective-permute-start(bf16[64,1920]{1,0:T(8,128)(2,1)S(1)} %pad_maximum_fusion.31), channel_id=1, source_target_pairs={{0,17},{1,16},{2,19},{3,18},{4,21},{5,20},{6,23},{7,22},{8,25},{9,... | collective-permute-start | bytes 737288 | tf_op jit(solution)/shard_map/ppermute | solution.py:60
  13.4 11.2 %collective-permute-start.1 = (bf16[64,1920]{1,0:T(8,128)(2,1)S(1)}, bf16[64,1920]{1,0:T(8,128)(2,1)S(1)}, u32[]{:S(2)}, u32[]{:S(2)}) collective-permute-start(bf16[64,1920]{1,0:T(8,128)(2,1)S(1)} %pad_maximum_fusion.30), channel_id=1, source_target_pairs={{0,16},{1,17},{2,18},{3,19},{4,20},{5,21},{6,22},{7,23},{8,24},{9,... | collective-permute-start | bytes 737288 | tf_op jit(solution)/shard_map/ppermute | solution.py:60
  14.0 10.9 %collective-permute-start = (bf16[64,1920]{1,0:T(8,128)(2,1)S(1)}, bf16[64,1920]{1,0:T(8,128)(2,1)S(1)}, u32[]{:S(2)}, u32[]{:S(2)}) collective-permute-start(bf16[64,1920]{1,0:T(8,128)(2,1)S(1)} %pad_maximum_fusion.29), channel_id=1, source_target_pairs={{0,1},{1,0},{2,3},{3,2},{4,5},{5,4},{6,7},{7,6},{8,9},{9,8},{10,11... | collective-permute-start | bytes 737288 | tf_op jit(solution)/shard_map/ppermute | solution.py:60
  26.3 255.6 %all-gather.6.cloned.1.call-start = ((), (), s32[]{:S(2)}) async-start(), calls=%async_computation.3 | async-start | bytes 14155776 | tf_op jit(solution)/shard_map/all_gather | solution.py:205
  26.4 37.1 %collective-permute-start.6 = (s32[2,768]{1,0:T(2,128)S(1)}, s32[2,768]{1,0:T(2,128)S(1)}, u32[]{:S(2)}, u32[]{:S(2)}) collective-permute-start(s32[2,768]{1,0:T(2,128)S(1)} %copy-done.87), channel_id=1, source_target_pairs={{0,16},{8,24},{16,0},{24,8},{1,17},{9,25},{17,1},{25,9},{2,18},{10... | collective-permute-start | bytes 18440 | tf_op jit(solution)/shard_map/ppermute | solution.py:49
  31.9 12.1 %collective-permute-start.3 = (bf16[416,160]{1,0:T(8,128)(2,1)S(1)}, bf16[416,160]{1,0:T(8,128)(2,1)S(1)}, u32[]{:S(2)}, u32[]{:S(2)}) collective-permute-start(bf16[416,160]{1,0:T(8,128)(2,1)S(1)} %get-tuple-element.234), channel_id=1, source_target_pairs={{0,2},{1,3},{2,4},{3,5},{4,6},{5,7},{6,0},{7,1},{8,10},{9,11},{10,... | collective-permute-start | bytes 399368 | tf_op jit(solution)/shard_map/ppermute | solution.py:49
  33.5 26.2 %collective-permute-start.4 = (bf16[416,160]{1,0:T(8,128)(2,1)S(1)}, bf16[416,160]{1,0:T(8,128)(2,1)S(1)}, u32[]{:S(2)}, u32[]{:S(2)}) collective-permute-start(bf16[416,160]{1,0:T(8,128)(2,1)S(1)} %get-tuple-element.234), channel_id=1, source_target_pairs={{0,4},{1,5},{2,6},{3,7},{4,0},{5,1},{6,2},{7,3},{8,12},{9,13},{10,... | collective-permute-start | bytes 399368 | tf_op jit(solution)/shard_map/ppermute | solution.py:49
  36.1 23.7 %collective-permute-start.5 = (bf16[416,160]{1,0:T(8,128)(2,1)S(1)}, bf16[416,160]{1,0:T(8,128)(2,1)S(1)}, u32[]{:S(2)}, u32[]{:S(2)}) collective-permute-start(bf16[416,160]{1,0:T(8,128)(2,1)S(1)} %get-tuple-element.234), channel_id=1, source_target_pairs={{0,6},{1,7},{2,0},{3,1},{4,2},{5,3},{6,4},{7,5},{8,14},{9,15},{10,... | collective-permute-start | bytes 399368 | tf_op jit(solution)/shard_map/ppermute | solution.py:49
  40.7 61.3 %collective-permute-start.29 = (bf16[64,4608]{1,0:T(8,128)(2,1)}, bf16[64,4608]{1,0:T(8,128)(2,1)}, u32[]{:S(2)}, u32[]{:S(2)}) collective-permute-start(bf16[64,4608]{1,0:T(8,128)(2,1)} %pad_maximum_fusion.19), channel_id=1, source_target_pairs={{0,1},{1,0},{2,3},{3,2},{4,5},{5,4},{6,7},{7,6},{8,9},{9,8},{10,11... | collective-permute-start | bytes 1769480 | tf_op jit(solution)/shard_map/ppermute | solution.py:60
  60.7 13.0 %collective-permute-start.8 = (bf16[2,416,160]{2,1,0:T(8,128)(2,1)}, bf16[2,416,160]{2,1,0:T(8,128)(2,1)}, u32[]{:S(2)}, u32[]{:S(2)}) collective-permute-start(bf16[2,416,160]{2,1,0:T(8,128)(2,1)} %constant_dynamic-slice_fusion.17), channel_id=1, source_target_pairs={{0,1},{1,0},{2,3},{3,2},{4,5},{5,4},{6,7},{7,6},{8,9},{9,8},{10,11... | collective-permute-start | bytes 798728 | tf_op jit(solution)/shard_map/ppermute | solution.py:49
  61.9 40.1 %collective-permute-start.31 = (bf16[64,4608]{1,0:T(8,128)(2,1)}, bf16[64,4608]{1,0:T(8,128)(2,1)}, u32[]{:S(2)}, u32[]{:S(2)}) collective-permute-start(bf16[64,4608]{1,0:T(8,128)(2,1)} %pad_maximum_fusion.21), channel_id=1, source_target_pairs={{0,17},{1,16},{2,19},{3,18},{4,21},{5,20},{6,23},{7,22},{8,25},{9,... | collective-permute-start | bytes 1769480 | tf_op jit(solution)/shard_map/ppermute | solution.py:60
  65.7 33.3 %collective-permute-start.10 = (bf16[2,96,2048]{2,1,0:T(8,128)(2,1)}, bf16[2,96,2048]{2,1,0:T(8,128)(2,1)S(1)}, u32[]{:S(2)}, u32[]{:S(2)}) collective-permute-start(bf16[2,96,2048]{2,1,0:T(8,128)(2,1)} %shard_map.306.refs_0_), channel_id=1, source_target_pairs={{0,16},{8,24},{16,0},{24,8},{1,17},{9,25},{17,1},{25,9},{2,18},{10... | collective-permute-start | bytes 2359304 | tf_op jit(solution)/shard_map/ppermute | solution.py:49
  67.2 34.8 %collective-permute-start.7 = (bf16[2,96,2048]{2,1,0:T(8,128)(2,1)}, bf16[2,96,2048]{2,1,0:T(8,128)(2,1)S(1)}, u32[]{:S(2)}, u32[]{:S(2)}) collective-permute-start(bf16[2,96,2048]{2,1,0:T(8,128)(2,1)} %shard_map.306.refs_0_), channel_id=1, source_target_pairs={{0,1},{1,0},{2,3},{3,2},{4,5},{5,4},{6,7},{7,6},{8,9},{9,8},{10,11... | collective-permute-start | bytes 2359304 | tf_op jit(solution)/shard_map/ppermute | solution.py:49
  78.4 31.6 %collective-permute-start.30 = (bf16[64,4608]{1,0:T(8,128)(2,1)}, bf16[64,4608]{1,0:T(8,128)(2,1)}, u32[]{:S(2)}, u32[]{:S(2)}) collective-permute-start(bf16[64,4608]{1,0:T(8,128)(2,1)} %pad_maximum_fusion.20), channel_id=1, source_target_pairs={{0,16},{1,17},{2,18},{3,19},{4,20},{5,21},{6,22},{7,23},{8,24},{9,... | collective-permute-start | bytes 1769480 | tf_op jit(solution)/shard_map/ppermute | solution.py:60
  115.9 201.4 %all-gather.8.cloned.1.call-start = ((), (), s32[]{:S(2)}) async-start(), calls=%async_computation.4 | async-start | bytes 7077888 | tf_op jit(solution)/shard_map/all_gather | solution.py:205
  127.4 29.8 %collective-permute-start.12 = (bf16[96,2048]{1,0:T(8,128)(2,1)S(1)}, bf16[96,2048]{1,0:T(8,128)(2,1)S(1)}, u32[]{:S(2)}, u32[]{:S(2)}) collective-permute-start(bf16[96,2048]{1,0:T(8,128)(2,1)S(1)} %slice_bitcast_fusion.30), channel_id=1, source_target_pairs={{0,1},{1,0},{2,3},{3,2},{4,5},{5,4},{6,7},{7,6},{8,9},{9,8},{10,11... | collective-permute-start | bytes 1179656 | tf_op jit(solution)/shard_map/ppermute | solution.py:49
  180.8 11.1 %collective-permute-start.16 = (f32[4,2,640]{2,1,0:T(2,128)S(1)}, f32[4,2,640]{2,1,0:T(2,128)S(1)}, u32[]{:S(2)}, u32[]{:S(2)}) collective-permute-start(f32[4,2,640]{2,1,0:T(2,128)S(1)} %slice.373), channel_id=1, source_target_pairs={{0,2},{1,3},{2,4},{3,5},{4,6},{5,7},{8,10},{9,11},{10,12},{11,13},... | collective-permute-start | bytes 61448 | tf_op jit(solution)/shard_map/ppermute | solution.py:49
  191.0 16.1 %collective-permute-start.20 = (bf16[2,96,2048]{2,1,0:T(8,128)(2,1)}, bf16[2,96,2048]{2,1,0:T(8,128)(2,1)S(1)}, u32[]{:S(2)}, u32[]{:S(2)}) collective-permute-start(bf16[2,96,2048]{2,1,0:T(8,128)(2,1)} %shard_map.310.refs_0_), channel_id=1, source_target_pairs={{0,16},{8,24},{16,0},{24,8},{1,17},{9,25},{17,1},{25,9},{2,18},{10... | collective-permute-start | bytes 2359304 | tf_op jit(solution)/shard_map/ppermute | solution.py:49
  191.4 15.7 %collective-permute-start.19 = (bf16[2,96,2048]{2,1,0:T(8,128)(2,1)}, bf16[2,96,2048]{2,1,0:T(8,128)(2,1)S(1)}, u32[]{:S(2)}, u32[]{:S(2)}) collective-permute-start(bf16[2,96,2048]{2,1,0:T(8,128)(2,1)} %shard_map.310.refs_0_), channel_id=1, source_target_pairs={{0,1},{1,0},{2,3},{3,2},{4,5},{5,4},{6,7},{7,6},{8,9},{9,8},{10,11... | collective-permute-start | bytes 2359304 | tf_op jit(solution)/shard_map/ppermute | solution.py:49
  213.4 15.4 %collective-permute-start.21 = (bf16[2,96,2048]{2,1,0:T(8,128)(2,1)}, bf16[2,96,2048]{2,1,0:T(8,128)(2,1)S(1)}, u32[]{:S(2)}, u32[]{:S(2)}) collective-permute-start(bf16[2,96,2048]{2,1,0:T(8,128)(2,1)} %slice_bitcast_fusion.22), channel_id=1, source_target_pairs={{0,16},{8,24},{16,0},{24,8},{1,17},{9,25},{17,1},{25,9},{2,18},{10... | collective-permute-start | bytes 2359304 | tf_op jit(solution)/shard_map/ppermute | solution.py:49
  215.8 15.8 %collective-permute-start.23 = (bf16[2,96,2048]{2,1,0:T(8,128)(2,1)}, bf16[2,96,2048]{2,1,0:T(8,128)(2,1)S(1)}, u32[]{:S(2)}, u32[]{:S(2)}) collective-permute-start(bf16[2,96,2048]{2,1,0:T(8,128)(2,1)} %slice_bitcast_fusion.19), channel_id=1, source_target_pairs={{0,1},{1,0},{2,3},{3,2},{4,5},{5,4},{6,7},{7,6},{8,9},{9,8},{10,11... | collective-permute-start | bytes 2359304 | tf_op jit(solution)/shard_map/ppermute | solution.py:49
  218.4 329.7 %reduce-scatter.3.cloned.1.call-start = ((), (), s32[]{:S(2)}) async-start(), calls=%async_computation.5 | async-start | bytes 11796480 | tf_op jit(solution)/shard_map/reduce_scatter | solution.py:246
  233.6 10.2 %collective-permute-start.22 = (bf16[96,2048]{1,0:T(8,128)(2,1)S(1)}, bf16[96,2048]{1,0:T(8,128)(2,1)S(1)}, u32[]{:S(2)}, u32[]{:S(2)}) collective-permute-start(bf16[96,2048]{1,0:T(8,128)(2,1)S(1)} %fusion.77), channel_id=1, source_target_pairs={{0,1},{1,0},{2,3},{3,2},{4,5},{5,4},{6,7},{7,6},{8,9},{9,8},{10,11... | collective-permute-start | bytes 1179656 | tf_op jit(solution)/shard_map/ppermute | solution.py:49
  234.2 9.7 %collective-permute-start.24 = (bf16[96,2048]{1,0:T(8,128)(2,1)S(1)}, bf16[96,2048]{1,0:T(8,128)(2,1)S(1)}, u32[]{:S(2)}, u32[]{:S(2)}) collective-permute-start(bf16[96,2048]{1,0:T(8,128)(2,1)S(1)} %fusion.78), channel_id=1, source_target_pairs={{0,16},{8,24},{16,0},{24,8},{1,17},{9,25},{17,1},{25,9},{2,18},{10... | collective-permute-start | bytes 1179656 | tf_op jit(solution)/shard_map/ppermute | solution.py:49
  245.1 20.5 %collective-permute-start.25 = (bf16[2,96,2048]{2,1,0:T(8,128)(2,1)S(1)}, bf16[2,96,2048]{2,1,0:T(8,128)(2,1)S(1)}, u32[]{:S(2)}, u32[]{:S(2)}) collective-permute-start(bf16[2,96,2048]{2,1,0:T(8,128)(2,1)S(1)} %multiply_convert_fusion.3.refs_0_), channel_id=1, source_target_pairs={{0,1},{1,0},{2,3},{3,2},{4,5},{5,4},{6,7},{7,6},{8,9},{9,8},{10,11... | collective-permute-start | bytes 2359304 | tf_op jit(solution)/shard_map/ppermute | solution.py:49
  246.9 24.1 %collective-permute-start.33 = (bf16[96,2048]{1,0:T(8,128)(2,1)}, bf16[96,2048]{1,0:T(8,128)(2,1)S(1)}, u32[]{:S(2)}, u32[]{:S(2)}) collective-permute-start(bf16[96,2048]{1,0:T(8,128)(2,1)} %slice_bitcast_fusion.28), channel_id=1, source_target_pairs={{0,1},{1,0},{2,3},{3,2},{4,5},{5,4},{6,7},{7,6},{8,9},{9,8},{10,11... | collective-permute-start | bytes 1179656 | tf_op jit(solution)/shard_map/ppermute | solution.py:49
  247.9 19.4 %collective-permute-start.26 = (bf16[2,96,2048]{2,1,0:T(8,128)(2,1)S(1)}, bf16[2,96,2048]{2,1,0:T(8,128)(2,1)S(1)}, u32[]{:S(2)}, u32[]{:S(2)}) collective-permute-start(bf16[2,96,2048]{2,1,0:T(8,128)(2,1)S(1)} %multiply_convert_fusion.3.refs_0_), channel_id=1, source_target_pairs={{0,16},{8,24},{16,0},{24,8},{1,17},{9,25},{17,1},{25,9},{2,18},{10... | collective-permute-start | bytes 2359304 | tf_op jit(solution)/shard_map/ppermute | solution.py:49
  249.5 22.2 %collective-permute-start.32 = (bf16[96,2048]{1,0:T(8,128)(2,1)}, bf16[96,2048]{1,0:T(8,128)(2,1)}, u32[]{:S(2)}, u32[]{:S(2)}) collective-permute-start(bf16[96,2048]{1,0:T(8,128)(2,1)} %slice_bitcast_fusion.29), channel_id=1, source_target_pairs={{0,16},{8,24},{16,0},{24,8},{1,17},{9,25},{17,1},{25,9},{2,18},{10... | collective-permute-start | bytes 1179656 | tf_op jit(solution)/shard_map/ppermute | solution.py:49
  266.4 11.6 %collective-permute-start.27 = (bf16[96,2048]{1,0:T(8,128)(2,1)}, bf16[96,2048]{1,0:T(8,128)(2,1)}, u32[]{:S(2)}, u32[]{:S(2)}) collective-permute-start(bf16[96,2048]{1,0:T(8,128)(2,1)} %slice_bitcast_fusion.25), channel_id=1, source_target_pairs={{0,16},{8,24},{16,0},{24,8},{1,17},{9,25},{17,1},{25,9},{2,18},{10... | collective-permute-start | bytes 1179656 | tf_op jit(solution)/shard_map/ppermute | solution.py:49
  268.3 9.6 %collective-permute-start.28 = (bf16[96,2048]{1,0:T(8,128)(2,1)}, bf16[96,2048]{1,0:T(8,128)(2,1)}, u32[]{:S(2)}, u32[]{:S(2)}) collective-permute-start(bf16[96,2048]{1,0:T(8,128)(2,1)} %slice_bitcast_fusion.24), channel_id=1, source_target_pairs={{0,1},{1,0},{2,3},{3,2},{4,5},{5,4},{6,7},{7,6},{8,9},{9,8},{10,11... | collective-permute-start | bytes 1179656 | tf_op jit(solution)/shard_map/ppermute | solution.py:49
  338.0 18.1 %collective-permute-start.36 = (bf16[1024,3072]{1,0:T(8,128)(2,1)}, bf16[1024,3072]{1,0:T(8,128)(2,1)}, u32[]{:S(2)}, u32[]{:S(2)}) collective-permute-start(bf16[1024,3072]{1,0:T(8,128)(2,1)} %convolution_convert_fusion), channel_id=1, source_target_pairs={{0,8},{8,0},{16,24},{24,16},{1,9},{9,1},{17,25},{25,17},{2,10},{10... | collective-permute-start | bytes 18874376 | tf_op jit(solution)/shard_map/ppermute | solution.py:49
  352.7 20.0 %collective-permute-start.38 = (bf16[2,96,2048]{2,1,0:T(8,128)(2,1)}, bf16[2,96,2048]{2,1,0:T(8,128)(2,1)S(1)}, u32[]{:S(2)}, u32[]{:S(2)}) collective-permute-start(bf16[2,96,2048]{2,1,0:T(8,128)(2,1)} %slice_bitcast_fusion.13), channel_id=1, source_target_pairs={{0,1},{1,0},{2,3},{3,2},{4,5},{5,4},{6,7},{7,6},{8,9},{9,8},{10,11... | collective-permute-start | bytes 2359304 | tf_op jit(solution)/shard_map/ppermute | solution.py:49
  355.2 19.8 %collective-permute-start.35 = (bf16[2,96,2048]{2,1,0:T(8,128)(2,1)}, bf16[2,96,2048]{2,1,0:T(8,128)(2,1)}, u32[]{:S(2)}, u32[]{:S(2)}) collective-permute-start(bf16[2,96,2048]{2,1,0:T(8,128)(2,1)} %slice_bitcast_fusion.16), channel_id=1, source_target_pairs={{0,16},{8,24},{16,0},{24,8},{1,17},{9,25},{17,1},{25,9},{2,18},{10... | collective-permute-start | bytes 2359304 | tf_op jit(solution)/shard_map/ppermute | solution.py:49
  368.4 266.3 %reduce-scatter.5.cloned.1.call-start = ((), (), s32[]{:S(2)}) async-start(), calls=%async_computation.6 | async-start | bytes 4915200 | tf_op jit(solution)/shard_map/reduce_scatter | solution.py:246
  377.4 10.3 %collective-permute-start.37 = (bf16[96,2048]{1,0:T(8,128)(2,1)S(1)}, bf16[96,2048]{1,0:T(8,128)(2,1)S(1)}, u32[]{:S(2)}, u32[]{:S(2)}) collective-permute-start(bf16[96,2048]{1,0:T(8,128)(2,1)S(1)} %fusion.79), channel_id=1, source_target_pairs={{0,1},{1,0},{2,3},{3,2},{4,5},{5,4},{6,7},{7,6},{8,9},{9,8},{10,11... | collective-permute-start | bytes 1179656 | tf_op jit(solution)/shard_map/ppermute | solution.py:49
  378.0 10.0 %collective-permute-start.39 = (bf16[96,2048]{1,0:T(8,128)(2,1)S(1)}, bf16[96,2048]{1,0:T(8,128)(2,1)S(1)}, u32[]{:S(2)}, u32[]{:S(2)}) collective-permute-start(bf16[96,2048]{1,0:T(8,128)(2,1)S(1)} %fusion.80), channel_id=1, source_target_pairs={{0,16},{8,24},{16,0},{24,8},{1,17},{9,25},{17,1},{25,9},{2,18},{10... | collective-permute-start | bytes 1179656 | tf_op jit(solution)/shard_map/ppermute | solution.py:49
  389.7 17.8 %collective-permute-start.41 = (bf16[2,96,2048]{2,1,0:T(8,128)(2,1)S(1)}, bf16[2,96,2048]{2,1,0:T(8,128)(2,1)S(1)}, u32[]{:S(2)}, u32[]{:S(2)}) collective-permute-start(bf16[2,96,2048]{2,1,0:T(8,128)(2,1)S(1)} %fusion.109.refs_0_), channel_id=1, source_target_pairs={{0,16},{8,24},{16,0},{24,8},{1,17},{9,25},{17,1},{25,9},{2,18},{10... | collective-permute-start | bytes 2359304 | tf_op jit(solution)/shard_map/ppermute | solution.py:49
  390.7 19.0 %collective-permute-start.40 = (bf16[2,96,2048]{2,1,0:T(8,128)(2,1)S(1)}, bf16[2,96,2048]{2,1,0:T(8,128)(2,1)S(1)}, u32[]{:S(2)}, u32[]{:S(2)}) collective-permute-start(bf16[2,96,2048]{2,1,0:T(8,128)(2,1)S(1)} %fusion.109.refs_0_), channel_id=1, source_target_pairs={{0,1},{1,0},{2,3},{3,2},{4,5},{5,4},{6,7},{7,6},{8,9},{9,8},{10,11... | collective-permute-start | bytes 2359304 | tf_op jit(solution)/shard_map/ppermute | solution.py:49
  408.3 8.7 %collective-permute-start.43 = (bf16[96,2048]{1,0:T(8,128)(2,1)}, bf16[96,2048]{1,0:T(8,128)(2,1)S(1)}, u32[]{:S(2)}, u32[]{:S(2)}) collective-permute-start(bf16[96,2048]{1,0:T(8,128)(2,1)} %slice_bitcast_fusion.26), channel_id=1, source_target_pairs={{0,1},{1,0},{2,3},{3,2},{4,5},{5,4},{6,7},{7,6},{8,9},{9,8},{10,11... | collective-permute-start | bytes 1179656 | tf_op jit(solution)/shard_map/ppermute | solution.py:49
  410.7 8.4 %collective-permute-start.42 = (bf16[96,2048]{1,0:T(8,128)(2,1)}, bf16[96,2048]{1,0:T(8,128)(2,1)}, u32[]{:S(2)}, u32[]{:S(2)}) collective-permute-start(bf16[96,2048]{1,0:T(8,128)(2,1)} %slice_bitcast_fusion.27), channel_id=1, source_target_pairs={{0,16},{8,24},{16,0},{24,8},{1,17},{9,25},{17,1},{25,9},{2,18},{10... | collective-permute-start | bytes 1179656 | tf_op jit(solution)/shard_map/ppermute | solution.py:49
  437.7 13.9 %collective-permute-start.48 = (f32[4,2,640]{2,1,0:T(2,128)S(1)}, f32[4,2,640]{2,1,0:T(2,128)S(1)}, u32[]{:S(2)}, u32[]{:S(2)}) collective-permute-start(f32[4,2,640]{2,1,0:T(2,128)S(1)} %slice.415), channel_id=1, source_target_pairs={{2,0},{3,1},{4,2},{5,3},{6,4},{7,5},{10,8},{11,9},{12,10},{13,11},... | collective-permute-start | bytes 61448 | tf_op jit(solution)/shard_map/ppermute | solution.py:49
  439.0 12.6 %collective-permute-start.49 = (f32[4,2,640]{2,1,0:T(2,128)S(1)}, f32[4,2,640]{2,1,0:T(2,128)S(1)}, u32[]{:S(2)}, u32[]{:S(2)}) collective-permute-start(f32[4,2,640]{2,1,0:T(2,128)S(1)} %slice.415), channel_id=1, source_target_pairs={{4,0},{5,1},{6,2},{7,3},{12,8},{13,9},{14,10},{15,11},{20,16},{21,... | collective-permute-start | bytes 61448 | tf_op jit(solution)/shard_map/ppermute | solution.py:49
  440.3 11.3 %collective-permute-start.50 = (f32[4,2,640]{2,1,0:T(2,128)S(1)}, f32[4,2,640]{2,1,0:T(2,128)S(1)}, u32[]{:S(2)}, u32[]{:S(2)}) collective-permute-start(f32[4,2,640]{2,1,0:T(2,128)S(1)} %slice.415), channel_id=1, source_target_pairs={{6,0},{7,1},{14,8},{15,9},{22,16},{23,17},{30,24},{31,25}} | collective-permute-start | bytes 61448 | tf_op jit(solution)/shard_map/ppermute | solution.py:49
  449.9 33.0 %collective-permute-start.44 = (bf16[2,96,2048]{2,1,0:T(8,128)(2,1)}, bf16[2,96,2048]{2,1,0:T(8,128)(2,1)S(1)}, u32[]{:S(2)}, u32[]{:S(2)}) collective-permute-start(bf16[2,96,2048]{2,1,0:T(8,128)(2,1)} %slice_bitcast_fusion.10), channel_id=1, source_target_pairs={{0,16},{8,24},{16,0},{24,8},{1,17},{9,25},{17,1},{25,9},{2,18},{10... | collective-permute-start | bytes 2359304 | tf_op jit(solution)/shard_map/ppermute | solution.py:49
  450.7 32.1 %collective-permute-start.46 = (bf16[2,96,2048]{2,1,0:T(8,128)(2,1)}, bf16[2,96,2048]{2,1,0:T(8,128)(2,1)}, u32[]{:S(2)}, u32[]{:S(2)}) collective-permute-start(bf16[2,96,2048]{2,1,0:T(8,128)(2,1)} %slice_bitcast_fusion.7), channel_id=1, source_target_pairs={{0,1},{1,0},{2,3},{3,2},{4,5},{5,4},{6,7},{7,6},{8,9},{9,8},{10,11... | collective-permute-start | bytes 2359304 | tf_op jit(solution)/shard_map/ppermute | solution.py:49
  464.9 8.7 %collective-permute-start.51 = (f32[4,8,640]{2,1,0:T(8,128)S(1)}, f32[4,8,640]{2,1,0:T(8,128)S(1)}, u32[]{:S(2)}, u32[]{:S(2)}) collective-permute-start(f32[4,8,640]{2,1,0:T(8,128)S(1)} %get-tuple-element.112), channel_id=1, source_target_pairs={{2,0},{3,1},{4,2},{5,3},{6,4},{7,5},{10,8},{11,9},{12,10},{13,11},... | collective-permute-start | bytes 245768 | tf_op jit(solution)/shard_map/ppermute | solution.py:49
  485.2 8.7 %collective-permute-start.45 = (bf16[96,2048]{1,0:T(8,128)(2,1)S(1)}, bf16[96,2048]{1,0:T(8,128)(2,1)S(1)}, u32[]{:S(2)}, u32[]{:S(2)}) collective-permute-start(bf16[96,2048]{1,0:T(8,128)(2,1)S(1)} %fusion.81), channel_id=1, source_target_pairs={{0,1},{1,0},{2,3},{3,2},{4,5},{5,4},{6,7},{7,6},{8,9},{9,8},{10,11... | collective-permute-start | bytes 1179656 | tf_op jit(solution)/shard_map/ppermute | solution.py:49
  486.1 8.8 %collective-permute-start.47 = (bf16[96,2048]{1,0:T(8,128)(2,1)S(1)}, bf16[96,2048]{1,0:T(8,128)(2,1)S(1)}, u32[]{:S(2)}, u32[]{:S(2)}) collective-permute-start(bf16[96,2048]{1,0:T(8,128)(2,1)S(1)} %fusion.82), channel_id=1, source_target_pairs={{0,16},{8,24},{16,0},{24,8},{1,17},{9,25},{17,1},{25,9},{2,18},{10... | collective-permute-start | bytes 1179656 | tf_op jit(solution)/shard_map/ppermute | solution.py:49
  501.1 21.9 %collective-permute-start.53 = (bf16[1024,1280]{1,0:T(8,128)(2,1)}, bf16[1024,1280]{1,0:T(8,128)(2,1)}, u32[]{:S(2)}, u32[]{:S(2)}) collective-permute-start(bf16[1024,1280]{1,0:T(8,128)(2,1)} %convolution_convert_fusion.1), channel_id=1, source_target_pairs={{0,8},{8,0},{16,24},{24,16},{1,9},{9,1},{17,25},{25,17},{2,10},{10... | collective-permute-start | bytes 7864328 | tf_op jit(solution)/shard_map/ppermute | solution.py:49
  503.6 15.8 %collective-permute-start.54 = (bf16[1024,640]{1,0:T(8,128)(2,1)}, bf16[1024,640]{1,0:T(8,128)(2,1)}, u32[]{:S(2)}, u32[]{:S(2)}) collective-permute-start(bf16[1024,640]{1,0:T(8,128)(2,1)} %convolution_convert_fusion.6), channel_id=1, source_target_pairs={{0,8},{8,0},{16,24},{24,16},{1,9},{9,1},{17,25},{25,17},{2,10},{10... | collective-permute-start | bytes 3932168 | tf_op jit(solution)/shard_map/ppermute | solution.py:49
  511.9 20.3 %collective-permute-start.57 = (bf16[2,96,2048]{2,1,0:T(8,128)(2,1)}, bf16[2,96,2048]{2,1,0:T(8,128)(2,1)}, u32[]{:S(2)}, u32[]{:S(2)}) collective-permute-start(bf16[2,96,2048]{2,1,0:T(8,128)(2,1)} %slice_bitcast_fusion.1), channel_id=1, source_target_pairs={{0,1},{1,0},{2,3},{3,2},{4,5},{5,4},{6,7},{7,6},{8,9},{9,8},{10,11... | collective-permute-start | bytes 2359304 | tf_op jit(solution)/shard_map/ppermute | solution.py:49
  512.8 20.0 %collective-permute-start.52 = (bf16[2,96,2048]{2,1,0:T(8,128)(2,1)}, bf16[2,96,2048]{2,1,0:T(8,128)(2,1)}, u32[]{:S(2)}, u32[]{:S(2)}) collective-permute-start(bf16[2,96,2048]{2,1,0:T(8,128)(2,1)} %slice_bitcast_fusion.4), channel_id=1, source_target_pairs={{0,16},{8,24},{16,0},{24,8},{1,17},{9,25},{17,1},{25,9},{2,18},{10... | collective-permute-start | bytes 2359304 | tf_op jit(solution)/shard_map/ppermute | solution.py:49
  515.2 65.8 %collective-permute-start.62 = (bf16[2,2,176,160]{2,3,1,0:T(8,128)(2,1)S(1)}, bf16[2,2,176,160]{2,3,1,0:T(8,128)(2,1)}, u32[]{:S(2)}, u32[]{:S(2)}) collective-permute-start(bf16[2,2,176,160]{2,3,1,0:T(8,128)(2,1)S(1)} %fusion.71), channel_id=1, source_target_pairs={{0,2},{1,3},{2,4},{3,5},{4,6},{5,7},{6,0},{7,1},{8,10},{9,11},{10,... | collective-permute-start | bytes 675848 | tf_op jit(solution)/shard_map/ppermute | solution.py:49
  519.4 61.6 %collective-permute-start.66 = (bf16[2,2,176,160]{2,3,1,0:T(8,128)(2,1)S(1)}, bf16[2,2,176,160]{2,3,1,0:T(8,128)(2,1)}, u32[]{:S(2)}, u32[]{:S(2)}) collective-permute-start(bf16[2,2,176,160]{2,3,1,0:T(8,128)(2,1)S(1)} %fusion.71), channel_id=1, source_target_pairs={{0,4},{1,5},{2,6},{3,7},{4,0},{5,1},{6,2},{7,3},{8,12},{9,13},{10,... | collective-permute-start | bytes 675848 | tf_op jit(solution)/shard_map/ppermute | solution.py:49
  535.3 10.5 %collective-permute-start.56 = (bf16[96,2048]{1,0:T(8,128)(2,1)S(1)}, bf16[96,2048]{1,0:T(8,128)(2,1)S(1)}, u32[]{:S(2)}, u32[]{:S(2)}) collective-permute-start(bf16[96,2048]{1,0:T(8,128)(2,1)S(1)} %fusion.83), channel_id=1, source_target_pairs={{0,1},{1,0},{2,3},{3,2},{4,5},{5,4},{6,7},{7,6},{8,9},{9,8},{10,11... | collective-permute-start | bytes 1179656 | tf_op jit(solution)/shard_map/ppermute | solution.py:49
  536.5 10.2 %collective-permute-start.58 = (bf16[96,2048]{1,0:T(8,128)(2,1)S(1)}, bf16[96,2048]{1,0:T(8,128)(2,1)S(1)}, u32[]{:S(2)}, u32[]{:S(2)}) collective-permute-start(bf16[96,2048]{1,0:T(8,128)(2,1)S(1)} %fusion.84), channel_id=1, source_target_pairs={{0,16},{8,24},{16,0},{24,8},{1,17},{9,25},{17,1},{25,9},{2,18},{10... | collective-permute-start | bytes 1179656 | tf_op jit(solution)/shard_map/ppermute | solution.py:49
  550.8 16.6 %collective-permute-start.63 = (bf16[64,4608]{1,0:T(8,128)(2,1)}, bf16[64,4608]{1,0:T(8,128)(2,1)}, u32[]{:S(2)}, u32[]{:S(2)}) collective-permute-start(bf16[64,4608]{1,0:T(8,128)(2,1)} %get-tuple-element.149), channel_id=1, source_target_pairs={{0,1},{1,0},{2,3},{3,2},{4,5},{5,4},{6,7},{7,6},{8,9},{9,8},{10,11... | collective-permute-start | bytes 1769480 | tf_op jit(solution)/shard_map/ppermute | solution.py:60
  551.7 25.0 %collective-permute-start.64 = (bf16[64,4608]{1,0:T(8,128)(2,1)}, bf16[64,4608]{1,0:T(8,128)(2,1)}, u32[]{:S(2)}, u32[]{:S(2)}) collective-permute-start(bf16[64,4608]{1,0:T(8,128)(2,1)} %get-tuple-element.151), channel_id=1, source_target_pairs={{0,16},{1,17},{2,18},{3,19},{4,20},{5,21},{6,22},{7,23},{8,24},{9,... | collective-permute-start | bytes 1769480 | tf_op jit(solution)/shard_map/ppermute | solution.py:60
  552.9 25.0 %collective-permute-start.65 = (bf16[64,4608]{1,0:T(8,128)(2,1)}, bf16[64,4608]{1,0:T(8,128)(2,1)}, u32[]{:S(2)}, u32[]{:S(2)}) collective-permute-start(bf16[64,4608]{1,0:T(8,128)(2,1)} %get-tuple-element.150), channel_id=1, source_target_pairs={{0,17},{1,16},{2,19},{3,18},{4,21},{5,20},{6,23},{7,22},{8,25},{9,... | collective-permute-start | bytes 1769480 | tf_op jit(solution)/shard_map/ppermute | solution.py:60
  567.4 25.3 %collective-permute-start.67 = (bf16[2,2,176,160]{2,3,1,0:T(8,128)(2,1)S(1)}, bf16[2,2,176,160]{2,3,1,0:T(8,128)(2,1)S(1)}, u32[]{:S(2)}, u32[]{:S(2)}) collective-permute-start(bf16[2,2,176,160]{2,3,1,0:T(8,128)(2,1)S(1)} %fusion.71), channel_id=1, source_target_pairs={{0,6},{1,7},{2,0},{3,1},{4,2},{5,3},{6,4},{7,5},{8,14},{9,15},{10,... | collective-permute-start | bytes 675848 | tf_op jit(solution)/shard_map/ppermute | solution.py:49
  595.0 10.6 %collective-permute-start.69 = (bf16[2,2,176,160]{2,3,1,0:T(8,128)(2,1)S(1)}, bf16[2,2,176,160]{2,3,1,0:T(8,128)(2,1)S(1)}, u32[]{:S(2)}, u32[]{:S(2)}) collective-permute-start(bf16[2,2,176,160]{2,3,1,0:T(8,128)(2,1)S(1)} %add_convert_fusion.6), channel_id=1, source_target_pairs={{0,16},{1,17},{2,18},{3,19},{4,20},{5,21},{6,22},{7,23},{8,24},{9,... | collective-permute-start | bytes 675848 | tf_op jit(solution)/shard_map/ppermute | solution.py:60
  596.4 9.2 %collective-permute-start.70 = (bf16[2,2,176,160]{2,3,1,0:T(8,128)(2,1)S(1)}, bf16[2,2,176,160]{2,3,1,0:T(8,128)(2,1)S(1)}, u32[]{:S(2)}, u32[]{:S(2)}) collective-permute-start(bf16[2,2,176,160]{2,3,1,0:T(8,128)(2,1)S(1)} %add_convert_fusion.6), channel_id=1, source_target_pairs={{0,17},{1,16},{2,19},{3,18},{4,21},{5,20},{6,23},{7,22},{8,25},{9,... | collective-permute-start | bytes 675848 | tf_op jit(solution)/shard_map/ppermute | solution.py:60
  637.4 11.6 %collective-permute-start.60 = (bf16[64,1920]{1,0:T(8,128)(2,1)S(1)}, bf16[64,1920]{1,0:T(8,128)(2,1)S(1)}, u32[]{:S(2)}, u32[]{:S(2)}) collective-permute-start(bf16[64,1920]{1,0:T(8,128)(2,1)S(1)} %get-tuple-element.182), channel_id=1, source_target_pairs={{0,16},{1,17},{2,18},{3,19},{4,20},{5,21},{6,22},{7,23},{8,24},{9,... | collective-permute-start | bytes 737288 | tf_op jit(solution)/shard_map/ppermute | solution.py:60
  (115 other events, 658.7 us)
Sparse Core Ops, SparseCore 0:
  26.4 92.9 all-gather.3
  121.6 125.4 all-gather.5
  248.7 64.5 all-gather.7
  368.5 169.9 reduce-scatter.2
  554.4 80.2 reduce-scatter.4

commit v4 on v3

--- a/solution.py
+++ b/solution.py
@@ -59,7 +59,7 @@
                         pairs.append((((y * nc + c) * nz + z) * nx + x, to))
         return lax.ppermute(value, ("seq", "blk"), pairs)
 
-    def rows_ahead(self, rows):
+    def rows_ahead(self, rows, *late):
         ny, nc, nz, nx = (self.n[p] for p in "yczx")
         out = None
         for x in range(nx):
@@ -67,7 +67,7 @@
             for s in range(ny * nc):
                 for z in range(nz - 1):
                     pairs.append(((s * nz + z) * nx + nx - 1, (s * nz + z + 1) * nx + x))
-            got = lax.ppermute(rows, ("seq", "blk"), pairs)
+            got = after(lax.ppermute(rows, ("seq", "blk"), pairs), *late)
             out = got if out is None else out + got
         return out
 
@@ -251,22 +251,22 @@
             axis_index_groups=self.grid.z_groups(),
         )
 
-    def finish(self, count, *late):
+    def finish(self, *cuts):
         grid = self.grid
         ny, nx = grid.n["y"], grid.n["x"]
-        width = self.done.shape[1] // count
-        done = after(self.done, *late).reshape(ny, nx, -1, self.done.shape[1])
+        done = self.done.reshape(ny, nx, -1, self.done.shape[1])
         side = grid.to_owners(done)
         return [
             jnp.concatenate(
                 [
-                    side[yy, xx, :, i * width : (i + 1) * width].astype(F32)
+                    side[yy, xx, :, at : at + width].astype(F32)
                     for yy in range(ny)
                     for xx in range(nx)
+                    for at, width in cut
                 ],
                 axis=1,
             )
-            for i in range(count)
+            for cut in cuts
         ]
 
 
@@ -652,22 +652,36 @@
     mix_all = grid.all_rows(weights_in)
     half = lax.dynamic_index_in_dim(after(packed, weights_in), c, 0, keepdims=False)
     others = lax.optimization_barrier([grid.shift(half, "z", r) for r in range(1, nz)])
-    by_z = lax.dynamic_slice_in_dim(grid.place([half, *others], "z"), y * per, per, 0)
+    own_rows = grid.turn(after(inputs, weights_in, *beside))
+    source = own_rows.astype(F32)
+    normed, in_hop = grid.spread(own_rows, *others, normed=True)
+    by_z = jnp.stack([half, *others])
+    by_z = jnp.stack(
+        [
+            lax.dynamic_index_in_dim(by_z, (z - y * per - i) % nz, 0, keepdims=False)
+            for i in range(per)
+        ]
+    )
+    by_z = after(by_z, *in_hop)
     by_x = grid.place([by_z] + [grid.shift(by_z, "x", r) for r in range(1, nx)], "x")
     by_x = jnp.moveaxis(by_x, 0, 1).reshape(per * nx, *half.shape)
     halves = grid.place([by_x] + [grid.shift(by_x, "c", r) for r in range(1, nc)], "c")
     gates, vec = unpack_small(halves, x, per, heads)
-    own_rows = grid.turn(after(inputs, *others, *beside))
-    source = own_rows.astype(F32)
-    normed, in_hop = grid.spread(own_rows, halves, normed=True)
-    ahead = grid.rows_ahead(own_rows[:, step - 2 * HALO :])
+    ahead = grid.rows_ahead(own_rows[:, step - HALO :], vec)
     ahead = jnp.stack([ahead] + [grid.shift(ahead, "y", r) for r in range(1, ny)], axis=1)
-    ahead = ahead.reshape(chains * 2 * HALO, depth)
+    ahead = ahead.reshape(chains * HALO, depth)
     pieces = [gained(mlp_gate, gain_mlp), gained(mlp_up, gain_mlp), mlp_down]
     pieces = [after(p, weights_in) for p in pieces]
     weights_ff = grid.columns_of(pieces, *in_hop).reshape(plane, -1)
-    ff_in = grid.all_rows(weights_ff[:, : 2 * ff_width])
-    ff_down = grid.all_rows(weights_ff[:, 2 * ff_width :])
+    wide = ff_width - ff_width // 3
+    ff_cuts = [
+        grid.all_rows(
+            jnp.concatenate(
+                [weights_ff[:, i * ff_width + lo : i * ff_width + hi] for i in range(3)], axis=1
+            )
+        )
+        for lo, hi in ((0, wide), (wide, ff_width))
+    ]
 
     segments = jnp.stack([seg_ids, *beside], axis=1)
     padded = jnp.pad(segments, ((0, 0), (0, 0), (HALO, 0)), constant_values=-1)
@@ -685,8 +699,7 @@
     drive = mix(normed, mix_x).astype(BF16).reshape(chains, nx, step, width)
     ahead = ahead.astype(F32)
     ahead = ahead * lax.rsqrt(jnp.mean(ahead * ahead, axis=-1, keepdims=True) + NORM_EPS)
-    halo = mix(ahead.astype(BF16), mix_x).astype(BF16).reshape(chains, 2 * HALO, width)
-    halo = halo[:, HALO:].astype(F32)
+    halo = mix(ahead.astype(BF16), mix_x).astype(BF16).reshape(chains, HALO, width).astype(F32)
     own_cot = grid.turn(after(cotangent, drive))
     pre_y = mix(normed, mix_y)
     branch_y, gelu_y_back = jax.vjp(jax.nn.gelu, pre_y)
@@ -717,28 +730,38 @@
 
     scale_mlp = lax.rsqrt(jnp.mean(resid * resid, axis=-1, keepdims=True) + NORM_EPS)
     normed_mlp, _ = grid.spread((resid * scale_mlp).astype(BF16))
-    pre_ff = mix(normed_mlp, after(ff_in, normed_mlp))
-    pre_gate, pre_up = pre_ff[:, :ff_width], pre_ff[:, ff_width:]
-    activated, gelu_gate_back = jax.vjp(jax.nn.gelu, pre_gate)
-    product = (activated * pre_up).astype(BF16)
-    sum_down = WeightSum(grid, rows_cot, product)
-    sum_down.lend()
-    sum_down.meet()
-    ff_down = after(ff_down, sum_down.mine)
-    grad_prod = mix(rows_cot, ff_down)
-    grad_gate = gelu_gate_back(grad_prod * pre_up)[0].astype(BF16)
-    grad_up = (grad_prod * activated).astype(BF16)
-    grad_ff = jnp.concatenate([grad_gate, grad_up], axis=1)
-    sum_ff = WeightSum(grid, normed_mlp, grad_ff)
-    sum_ff.lend()
-    part_mlp = mix_back(after(grad_ff, *sum_ff.lent), ff_in).astype(BF16)
-    sum_ff.right = after(grad_ff, part_mlp)
-    sum_ff.meet()
-    sum_ff.mine = jnp.concatenate([sum_ff.mine.astype(BF16), sum_down.mine.astype(BF16)], axis=1)
+    part_mlp, mines, outward, last = 0.0, [], [], ()
+    for ff in ff_cuts:
+        cut = ff.shape[1] // 3
+        ff = after(ff, normed_mlp, *last)
+        ff_in, ff_down = ff[:, : 2 * cut], ff[:, 2 * cut :]
+        pre_ff = mix(normed_mlp, ff_in).astype(BF16)
+        pre_gate, pre_up = pre_ff[:, :cut].astype(F32), pre_ff[:, cut:].astype(F32)
+        activated, gelu_gate_back = jax.vjp(jax.nn.gelu, pre_gate)
+        product = (activated * pre_up).astype(BF16)
+        sum_down = WeightSum(grid, rows_cot, product)
+        sum_down.lend()
+        grad_prod = mix(rows_cot, after(ff_down, *sum_down.lent))
+        grad_gate = gelu_gate_back(grad_prod * pre_up)[0].astype(BF16)
+        grad_up = (grad_prod * activated).astype(BF16)
+        grad_ff = jnp.concatenate([grad_gate, grad_up], axis=1)
+        sum_ff = WeightSum(grid, normed_mlp, grad_ff)
+        sum_ff.lend()
+        sum_down.right = after(product, *sum_ff.lent)
+        sum_down.meet()
+        part_mlp = part_mlp + mix_back(after(grad_ff, sum_down.mine), ff_in)
+        sum_ff.right = after(grad_ff, part_mlp)
+        sum_ff.meet()
+        mines += [sum_ff.mine.astype(BF16), sum_down.mine.astype(BF16)]
+        outward.append((product, ff_down))
+        last = (part_mlp, sum_ff.mine)
+    part_mlp = part_mlp.astype(BF16)
+    sum_ff.mine = jnp.concatenate(mines, axis=1)
     sum_ff.along_z()
     weighted_mlp = grid.collect(part_mlp, micro, sum_ff.mine)
     grad_resid = own_cot.astype(F32) + norm_back(weighted_mlp, resid, scale_mlp)
-    part_out = mix_back(after(product, weighted_mlp), ff_down).astype(BF16)
+    part_out = sum(mix_back(after(left, weighted_mlp), right) for left, right in outward)
+    part_out = part_out.astype(BF16)
     grad_branch, _ = grid.spread(grad_resid.astype(BF16), part_out)
     block_out = resid + grid.collect(after(part_out, grad_branch), micro)
 
@@ -824,9 +847,14 @@
     weighted_in = grid.collect(part_in, micro, sum_in.mine, blocks)
     weighted_in = after(weighted_in, sum_ff.done)
     sum_in.along_z(sum_ff.done)
-    grad_gate_w, grad_up_w, grad_down_w = sum_ff.finish(3)
+    grad_gate_w, grad_up_w, grad_down_w = sum_ff.finish(
+        *(
+            [(i * wide, wide), (3 * wide + i * (ff_width - wide), ff_width - wide)]
+            for i in range(3)
+        )
+    )
     block_out = grid.turn(block_out.astype(BF16), back=True)
-    grad_y_w, grad_x_w, grad_out_w = sum_in.finish(3)
+    grad_y_w, grad_x_w, grad_out_w = sum_in.finish(*([(i * width, width)] for i in range(3)))
     scale_in = lax.rsqrt(jnp.mean(source * source, axis=-1, keepdims=True) + NORM_EPS)
     grad_source = grad_resid + norm_back(weighted_in, source, scale_in)
     grad_source = grid.turn(grad_source.astype(BF16), back=True)

time: 668 us -> 657 us (0.984)
  starting transfers between devices: 102 us -> 88 us
  waiting for transfers between devices: 241 us -> 231 us
  local copies, waits for them, and re-layouts: 63.9 us -> 70.7 us
    ppermute x55 -> x57, waiting for transfers between devices: 170 us -> 141 us  [shift(): return lax.ppermute(value, axis, pairs)]
    ppermute x15, waiting for transfers between devices: 47.4 us -> 74 us  [shift_plane(): return lax.ppermute(value, ('seq', 'blk'), pairs)]
    ppermute x55 -> x57, starting transfers between devices: 81.8 us -> 68.7 us  [shift(): return lax.ppermute(value, axis, pairs)]
    reduce_scatter x2, waiting for transfers between devices: 23.5 us -> 16.5 us  [along_z(): lax.psum_scatter(after(self.mine.astype(BF16), *late), 'blk', scatter_dim...]
    dot_general x5 -> x7, matrix products: 36.4 us -> 42.3 us  [mix_back(): lax.dot_general(left, right, (((1,), (1,)), ((), ())), preferred_element_...]
    dot_general x6 -> x8, matrix products: 46.3 us -> 44.8 us  [mix(): return jnp.dot(left, right, preferred_element_type=F32)]
    dot_general x8 -> x12, matrix products: 40.6 us -> 40.2 us  [product(): lax.dot_general(cut, self.right, (((0,), (0,)), ((), ())), preferred_elem...]
    unnamed x209 -> x266, local copies, waits for them, and re-layouts: 26.6 us -> 26.9 us
  transfers between devices with their start and end apart: 77 -> 79, of which waited for: 45 -> 39; matrix products, arithmetic and copies ran while one was open for 30% -> 34% of each run, Pallas kernels for 7% -> 7%
where the time goes in v4:
time: 657 us; the launch traced here: 651 us
  waiting for transfers between devices  231 us (35%)
  matrix products  129 us (20%)
  starting transfers between devices  88 us (13%)
  local copies, waits for them, and re-layouts  70.7 us (11%)
  other arithmetic  66 us (10%)
  Pallas kernels  48.7 us (7%)
  between operations  16.6 us (3%)
    ppermute x57, waiting for transfers between devices, shift(): return lax.ppermute(value, axis, pairs)  141 us
    ppermute x15, waiting for transfers between devices, shift_plane(): return lax.ppermute(value, ('seq', 'blk'), pairs)  74 us
    ppermute x57, starting transfers between devices, shift(): return lax.ppermute(value, axis, pairs)  68.7 us
    dot_general x8, matrix products, mix(): return jnp.dot(left, right, preferred_element_type=F32)  44.8 us
    dot_general x7, matrix products, mix_back(): lax.dot_general(left, right, (((1,), (1,)), ((), ())), preferred_element_...  42.3 us
    dot_general x12, matrix products, product(): lax.dot_general(cut, self.right, (((0,), (0,)), ((), ())), preferred_elem...  40.2 us
    pallas_call x3, Pallas kernels, scan_call(): pl.pallas_call(kernel, grid=(chains,), in_specs=specs, out_specs=out_spec...  28.6 us
    unnamed x266, local copies, waits for them, and re-layouts  26.9 us
  transfers between devices with their start and end apart: 79, of which 39 were waited for; matrix products, arithmetic and copies ran while one was open for 34% of the time, Pallas kernels for 7%

profile of v4, /device:TPU:0, one launch (start us, length us, event | category | flops | bytes accessed | tf_op | source)
XLA Modules:
  0.0 650.6 jit_solution(1958769385906996877)
XLA Ops:
  9.4 4.0 collective-permute-start.2
  14.2 6.1 collective-permute-done.2
  20.2 4.4 collective-permute-done.1
  34.1 2.6 collective-permute-start.6
  42.7 2.9 collective-permute-done.5
  45.6 15.1 %collective-permute-done.6 = bf16[416,160]{1,0:T(8,128)(2,1)} collective-permute-done((bf16[416,160]{1,0:T(8,128)(2,1)}, bf16[416,160]{1,0:T(8,128)(2,1)}, u32[]{:S(2)}, u32[]{:S(2)}) %collective-permute-start.6) | collective-permute-done | bytes 133152 | tf_op jit(solution)/shard_map/ppermute | solution.py:49
  62.8 21.4 %collective-permute-done.30 = bf16[64,4608]{1,0:T(8,128)(2,1)S(1)} collective-permute-done((bf16[64,4608]{1,0:T(8,128)(2,1)S(1)}, bf16[64,4608]{1,0:T(8,128)(2,1)S(1)}, u32[]{:S(2)}, u32[]{:S(2)}) %collective-permute-start.30) | collective-permute-done | bytes 589856 | tf_op jit(solution)/shard_map/ppermute | solution.py:60
  84.2 4.1 collective-permute-done.29
  96.9 7.4 %collective-permute-done.11 = bf16[2,416,160]{2,1,0:T(8,128)(2,1)} collective-permute-done((bf16[2,416,160]{2,1,0:T(8,128)(2,1)S(1)}, bf16[2,416,160]{2,1,0:T(8,128)(2,1)}, u32[]{:S(2)}, u32[]{:S(2)}) %collective-permute-start.11) | collective-permute-done | bytes 266272 | tf_op jit(solution)/shard_map/ppermute | solution.py:49
  109.6 4.1 collective-permute-start.10
  114.5 2.4 collective-permute-start.9
  139.3 5.5 fusion.71
  144.8 10.3 %shard_map.309 = (f32[4,192,640]{2,1,0:T(8,128)S(1)}, f32[4,192,640]{2,1,0:T(8,128)}, f32[4,192,640]{2,1,0:T(8,128)}, f32[4,2,96,640]{3,2,1,0:T(8,128)}, f32[4,2...) custom-call(s32[2]{0:T(128)S(1)} %and_select_fusion.order, bf16[4,2,96,640]{3,2,1,0:T(8,128)(2,1)S(1)} %bitcast.509, ...), custom_call_target="tpu_custom_call" | custom-call | flops 2516582400 | bytes 12660744 | tf_op jit(solution)/shard_map/pallas_call | solution.py:573
  156.4 5.0 collective-permute-start.16
  161.5 4.0 collective-permute-start.17
  173.0 2.6 add_convert_fusion.6
  176.2 6.3 fusion.37
  182.5 5.7 collective-permute-done.20.refs_2_
  189.3 4.6 convolution_convert_fusion.2
  200.2 12.6 %collective-permute-done.21 = bf16[2,96,2048]{2,1,0:T(8,128)(2,1)S(1)} collective-permute-done((bf16[2,96,2048]{2,1,0:T(8,128)(2,1)}, bf16[2,96,2048]{2,1,0:T(8,128)(2,1)S(1)}, u32[]{:S(2)}, u32[]{:S(2)}) %collective-permute-start.21) | collective-permute-done | bytes 786464 | tf_op jit(solution)/shard_map/ppermute | solution.py:49
  219.2 5.0 collective-permute-done.22
  233.1 13.9 %collective-permute-done.25.refs_1_ = bf16[2,96,2048]{2,1,0:T(8,128)(2,1)S(1)} collective-permute-done((bf16[2,96,2048]{2,1,0:T(8,128)(2,1)S(1)}, bf16[2,96,2048]{2,1,0:T(8,128)(2,1)S(1)}, u32[]{:S(2)}, u32[]{:S(2)}) %collective-permute-start.25) | collective-permute-done | bytes 786464 | tf_op jit(solution)/shard_map/ppermute | solution.py:49
  250.9 3.7 collective-permute-done.33.refs_4_
  255.8 2.7 shard_map.312
  266.2 9.1 %fusion.12 = bf16[768,2048]{1,0:T(8,128)(2,1)S(1)} fusion(bf16[768,2048]{1,0:T(8,128)(2,1)S(1)} %bitcast.497, bf16[2048,3072]{1,0:T(8,128)(2,1)} %all-gather.6.cloned.1.call-done), kind=kOutput, calls=%fused_computation.28 | convolution fusion | flops 6444023808 | bytes 14680064 | tf_op jit(solution)/shard_map/dot_general | solution.py:592
  277.2 3.2 convolution_convert_fusion.4
  280.4 5.6 fusion.18
  286.0 5.6 convolution_convert_fusion.1
  295.0 4.7 convert_add_fusion.2
  299.8 11.1 %fusion = f32[768,2048]{1,0:T(8,128)} fusion(bf16[768,2048]{1,0:T(8,128)(2,1)S(1)} %pad_maximum_fusion.2, bf16[2048,3072]{1,0:T(8,128)(2,1)} %all-gather.6.cloned.1.call-done), kind=kOutput, calls=%fused_computation.2 | convolution fusion | flops 6442450944 | bytes 17825792 | tf_op jit(solution)/shard_map/dot_general | solution.py:596
  310.9 7.0 %convert_add_fusion = bf16[1024,2048]{1,0:T(8,128)(2,1)} fusion(bf16[1024,2048]{1,0:T(8,128)(2,1)} %collective-permute-done.35, bf16[768,2048]{1,0:T(8,128)(2,1)S(1)} %pad_maximum_fusion.2, bf16[768,2048]{1,0:T(8,128)(2,1)S(1)} %bitcast.499, s32[]{:T(128)S(6)} %select_n.600), kind=kOutput, calls=%fused_computation.1 | convolution fusion | flops 3227516928 | bytes 13107204 | tf_op jit(solution)/shard_map/dot_general | solution.py:231
  317.9 6.6 %fusion.45 = bf16[768,1024]{1,0:T(8,128)(2,1)S(1)} fusion(bf16[768,2048]{1,0:T(8,128)(2,1)} %bitcast.496, bf16[2048,1536]{1,0:T(8,128)(2,1)} %all-gather.8.cloned.1.call-done), kind=kOutput, calls=%fused_computation.92 | convolution fusion | flops 3222011904 | bytes 8912896 | tf_op jit(solution)/shard_map/dot_general | solution.py:592
  328.2 2.9 fusion.55
  336.0 5.6 fusion.9
  348.3 5.6 pad_maximum_fusion
  354.0 8.7 %collective-permute-done.40 = bf16[2,96,2048]{2,1,0:T(8,128)(2,1)S(1)} collective-permute-done((bf16[2,96,2048]{2,1,0:T(8,128)(2,1)}, bf16[2,96,2048]{2,1,0:T(8,128)(2,1)S(1)}, u32[]{:S(2)}, u32[]{:S(2)}) %collective-permute-start.40) | collective-permute-done | bytes 786464 | tf_op jit(solution)/shard_map/ppermute | solution.py:49
  369.3 8.1 %collective-permute-done.39 = bf16[96,2048]{1,0:T(8,128)(2,1)S(1)} collective-permute-done((bf16[96,2048]{1,0:T(8,128)(2,1)S(1)}, bf16[96,2048]{1,0:T(8,128)(2,1)S(1)}, u32[]{:S(2)}, u32[]{:S(2)}) %collective-permute-start.39) | collective-permute-done | bytes 393248 | tf_op jit(solution)/shard_map/ppermute | solution.py:49
  382.2 5.7 fusion.167
  387.9 3.5 add_convert_fusion.1
  391.3 6.0 collective-permute-done.43.refs_2_
  404.0 2.9 collective-permute-done.45.refs_4_
  406.9 2.7 collective-permute-done.44.refs_3_
  413.2 6.6 %multiply_convert_fusion.1 = (bf16[768,640]{1,0:T(8,128)(2,1)S(1)}, bf16[768,640]{1,0:T(8,128)(2,1)S(1)}) fusion(f32[768,640]{1,0:T(8,128)S(1)} %copy-done.122, bf16[4,2,96,640]{3,2,1,0:T(8,128)(2,1)S(1)} %copy-done.85, bf16[768,2048]{1,0:T(8,128)(2,1)S(1)} %bitcast.493, bf16[2048,1920]{1,0:T(8,128)(2,1)} %all-gather.4.cloned.1.call-done), kind=kOutput, calls=%fused_computation.81 | convolution fusion | flops 2025553920 | bytes 10682368 | tf_op jit(solution)/shard_map/dot_general | solution.py:592
  419.9 7.3 %shard_map.315 = (f32[4,192,640]{2,1,0:T(8,128)S(1)}, f32[4,192,640]{2,1,0:T(8,128)S(1)}, f32[4,8,640]{2,1,0:T(8,128)S(1)}) custom-call(s32[2]{0:T(128)S(1)} %and_select_fusion.order, bf16[4,2,96,640]{3,2,1,0:T(8,128)(2,1)S(1)} %bitcast.508, f32[4,192,8]{2,1,0:T(8,128)S(1)} %copy-done.3, f32[8,640]{1,0:T(8,128)S(1)} %copy-done.37, ...), custom_call_target="tpu_custom_call" | custom-call | flops 19660800 | bytes 7008264 | tf_op jit(solution)/shard_map/pallas_call | solution.py:573
  432.0 6.4 fusion.27
  441.6 11.0 %shard_map.316 = (f32[4,2,96,640]{3,2,1,0:T(8,128)}, f32[4,8,640]{2,1,0:T(8,128)}, bf16[4,192,640]{2,1,0:T(8,128)(2,1)S(1)}, bf16[4,192,640]{2,1,0:T(8,128)(2,1)S(1)}, f32[8,640]{1,0:T(8,128)S(1)}) custom-call(s32[2]{0:T(128)S(1)} %and_select_fusion.order, bf16[4,2,96,640]{3,2,1,0:T(8,128)(2,1)S(1)} %bitcast.510, f32[4,8,640]{2,1,0:T(8,128)S(1)} %copy-done.39, ...), custom_call_target="tpu_custom_call" | custom-call | flops 2516582400 | bytes 20566024 | tf_op jit(solution)/shard_map/pallas_call | solution.py:573
  457.1 7.1 %collective-permute-done.53 = f32[4,8,640]{2,1,0:T(8,128)} collective-permute-done((f32[4,8,640]{2,1,0:T(8,128)}, f32[4,8,640]{2,1,0:T(8,128)}, u32[]{:S(2)}, u32[]{:S(2)}) %collective-permute-start.53) | collective-permute-done | bytes 81952 | tf_op jit(solution)/shard_map/ppermute | solution.py:49
  469.0 5.4 add_convert_fusion
  474.4 3.0 convert_add_fusion.9
  479.6 5.8 collective-permute-done.47
  488.9 3.9 convolution_convert_fusion
  492.8 2.5 convolution_convert_fusion.5
  507.5 3.5 add_convert_fusion.4
  511.1 4.0 add_convert_fusion.2
  517.3 6.7 %collective-permute-done.59 = bf16[2,96,2048]{2,1,0:T(8,128)(2,1)} collective-permute-done((bf16[2,96,2048]{2,1,0:T(8,128)(2,1)}, bf16[2,96,2048]{2,1,0:T(8,128)(2,1)}, u32[]{:S(2)}, u32[]{:S(2)}) %collective-permute-start.59) | collective-permute-done | bytes 786464 | tf_op jit(solution)/shard_map/ppermute | solution.py:49
  524.6 2.4 convert_add_fusion.7
  529.2 8.4 %collective-permute-done.58 = bf16[96,2048]{1,0:T(8,128)(2,1)S(1)} collective-permute-done((bf16[96,2048]{1,0:T(8,128)(2,1)S(1)}, bf16[96,2048]{1,0:T(8,128)(2,1)S(1)}, u32[]{:S(2)}, u32[]{:S(2)}) %collective-permute-start.58) | collective-permute-done | bytes 393248 | tf_op jit(solution)/shard_map/ppermute | solution.py:49
  539.6 2.8 dynamic-slice_bitcast_fusion.2
  546.3 12.7 %collective-permute-done.65 = bf16[64,4608]{1,0:T(8,128)(2,1)} collective-permute-done((bf16[64,4608]{1,0:T(8,128)(2,1)}, bf16[64,4608]{1,0:T(8,128)(2,1)}, u32[]{:S(2)}, u32[]{:S(2)}) %collective-permute-start.65) | collective-permute-done | bytes 589856 | tf_op jit(solution)/shard_map/ppermute | solution.py:60
  558.9 11.1 %collective-permute-done.66 = bf16[64,4608]{1,0:T(8,128)(2,1)} collective-permute-done((bf16[64,4608]{1,0:T(8,128)(2,1)}, bf16[64,4608]{1,0:T(8,128)(2,1)}, u32[]{:S(2)}, u32[]{:S(2)}) %collective-permute-start.66) | collective-permute-done | bytes 589856 | tf_op jit(solution)/shard_map/ppermute | solution.py:60
  573.3 9.0 %collective-permute-done.69 = bf16[2,2,176,160]{2,3,1,0:T(8,128)(2,1)S(1)} collective-permute-done((bf16[2,2,176,160]{2,3,1,0:T(8,128)(2,1)S(1)}, bf16[2,2,176,160]{2,3,1,0:T(8,128)(2,1)S(1)}, u32[]{:S(2)}, u32[]{:S(2)}) %collective-permute-start.69) | collective-permute-done | bytes 225312 | tf_op jit(solution)/shard_map/ppermute | solution.py:49
  594.7 5.9 collective-permute-done.71
  607.9 16.5 %reduce-scatter.5.cloned.1.call-done = bf16[256,1920]{1,0:T(8,128)(2,1)} async-done(((bf16[1024,1920]{1,0:T(8,128)(2,1)}), bf16[256,1920]{1,0:T(8,128)(2,1)}) %reduce-scatter.5.cloned.1.call-update) | async-done | bytes 983056 | tf_op jit(solution)/shard_map/reduce_scatter | solution.py:246
  633.2 5.5 collective-permute-done.62
  (597 shorter events, 225.6 us)
Async XLA Ops:
  7.2 129.8 %all-gather.4.cloned.1.call-start = ((), (), s32[]{:S(2)}) async-start(), calls=%async_computation.2 | async-start | bytes 8847360 | tf_op jit(solution)/shard_map/all_gather | solution.py:205
  9.4 10.8 %collective-permute-start.2 = (bf16[64,1920]{1,0:T(8,128)(2,1)S(1)}, bf16[64,1920]{1,0:T(8,128)(2,1)S(1)}, u32[]{:S(2)}, u32[]{:S(2)}) collective-permute-start(bf16[64,1920]{1,0:T(8,128)(2,1)S(1)} %pad_maximum_fusion.34), channel_id=1, source_target_pairs={{0,17},{1,16},{2,19},{3,18},{4,21},{5,20},{6,23},{7,22},{8,25},{9,... | collective-permute-start | bytes 737288 | tf_op jit(solution)/shard_map/ppermute | solution.py:60
  13.4 11.2 %collective-permute-start.1 = (bf16[64,1920]{1,0:T(8,128)(2,1)S(1)}, bf16[64,1920]{1,0:T(8,128)(2,1)S(1)}, u32[]{:S(2)}, u32[]{:S(2)}) collective-permute-start(bf16[64,1920]{1,0:T(8,128)(2,1)S(1)} %pad_maximum_fusion.33), channel_id=1, source_target_pairs={{0,16},{1,17},{2,18},{3,19},{4,20},{5,21},{6,22},{7,23},{8,24},{9,... | collective-permute-start | bytes 737288 | tf_op jit(solution)/shard_map/ppermute | solution.py:60
  14.0 10.9 %collective-permute-start = (bf16[64,1920]{1,0:T(8,128)(2,1)S(1)}, bf16[64,1920]{1,0:T(8,128)(2,1)S(1)}, u32[]{:S(2)}, u32[]{:S(2)}) collective-permute-start(bf16[64,1920]{1,0:T(8,128)(2,1)S(1)} %pad_maximum_fusion.32), channel_id=1, source_target_pairs={{0,1},{1,0},{2,3},{3,2},{4,5},{5,4},{6,7},{7,6},{8,9},{9,8},{10,11... | collective-permute-start | bytes 737288 | tf_op jit(solution)/shard_map/ppermute | solution.py:60
  26.3 237.9 %all-gather.6.cloned.1.call-start = ((), (), s32[]{:S(2)}) async-start(), calls=%async_computation.3 | async-start | bytes 14155776 | tf_op jit(solution)/shard_map/all_gather | solution.py:205
  26.4 11.7 %collective-permute-start.3 = (s32[2,768]{1,0:T(2,128)S(1)}, s32[2,768]{1,0:T(2,128)S(1)}, u32[]{:S(2)}, u32[]{:S(2)}) collective-permute-start(s32[2,768]{1,0:T(2,128)S(1)} %copy-done.106), channel_id=1, source_target_pairs={{0,16},{8,24},{16,0},{24,8},{1,17},{9,25},{17,1},{25,9},{2,18},{10... | collective-permute-start | bytes 18440 | tf_op jit(solution)/shard_map/ppermute | solution.py:49
  32.6 13.0 %collective-permute-start.5 = (bf16[416,160]{1,0:T(8,128)(2,1)}, bf16[416,160]{1,0:T(8,128)(2,1)S(1)}, u32[]{:S(2)}, u32[]{:S(2)}) collective-permute-start(bf16[416,160]{1,0:T(8,128)(2,1)} %fusion.203), channel_id=1, source_target_pairs={{0,2},{1,3},{2,4},{3,5},{4,6},{5,7},{6,0},{7,1},{8,10},{9,11},{10,... | collective-permute-start | bytes 399368 | tf_op jit(solution)/shard_map/ppermute | solution.py:49
  34.1 26.6 %collective-permute-start.6 = (bf16[416,160]{1,0:T(8,128)(2,1)}, bf16[416,160]{1,0:T(8,128)(2,1)}, u32[]{:S(2)}, u32[]{:S(2)}) collective-permute-start(bf16[416,160]{1,0:T(8,128)(2,1)} %fusion.203), channel_id=1, source_target_pairs={{0,4},{1,5},{2,6},{3,7},{4,0},{5,1},{6,2},{7,3},{8,12},{9,13},{10,... | collective-permute-start | bytes 399368 | tf_op jit(solution)/shard_map/ppermute | solution.py:49
  36.7 25.4 %collective-permute-start.7 = (bf16[416,160]{1,0:T(8,128)(2,1)}, bf16[416,160]{1,0:T(8,128)(2,1)}, u32[]{:S(2)}, u32[]{:S(2)}) collective-permute-start(bf16[416,160]{1,0:T(8,128)(2,1)} %fusion.203), channel_id=1, source_target_pairs={{0,6},{1,7},{2,0},{3,1},{4,2},{5,3},{6,4},{7,5},{8,14},{9,15},{10,... | collective-permute-start | bytes 399368 | tf_op jit(solution)/shard_map/ppermute | solution.py:49
  40.3 22.5 %collective-permute-start.8 = (bf16[2,96,2048]{2,1,0:T(8,128)(2,1)}, bf16[2,96,2048]{2,1,0:T(8,128)(2,1)S(1)}, u32[]{:S(2)}, u32[]{:S(2)}) collective-permute-start(bf16[2,96,2048]{2,1,0:T(8,128)(2,1)} %shard_map.305.refs_0_), channel_id=1, source_target_pairs={{0,16},{8,24},{16,0},{24,8},{1,17},{9,25},{17,1},{25,9},{2,18},{10... | collective-permute-start | bytes 2359304 | tf_op jit(solution)/shard_map/ppermute | solution.py:49
  40.9 21.9 %collective-permute-start.4 = (bf16[2,96,2048]{2,1,0:T(8,128)(2,1)}, bf16[2,96,2048]{2,1,0:T(8,128)(2,1)S(1)}, u32[]{:S(2)}, u32[]{:S(2)}) collective-permute-start(bf16[2,96,2048]{2,1,0:T(8,128)(2,1)} %shard_map.305.refs_0_), channel_id=1, source_target_pairs={{0,1},{1,0},{2,3},{3,2},{4,5},{5,4},{6,7},{7,6},{8,9},{9,8},{10,11... | collective-permute-start | bytes 2359304 | tf_op jit(solution)/shard_map/ppermute | solution.py:49
  45.6 38.6 %collective-permute-start.30 = (bf16[64,4608]{1,0:T(8,128)(2,1)S(1)}, bf16[64,4608]{1,0:T(8,128)(2,1)S(1)}, u32[]{:S(2)}, u32[]{:S(2)}) collective-permute-start(bf16[64,4608]{1,0:T(8,128)(2,1)S(1)} %pad_maximum_fusion.22), channel_id=1, source_target_pairs={{0,16},{1,17},{2,18},{3,19},{4,20},{5,21},{6,22},{7,23},{8,24},{9,... | collective-permute-start | bytes 1769480 | tf_op jit(solution)/shard_map/ppermute | solution.py:60
  60.7 23.4 %collective-permute-start.31 = (bf16[64,4608]{1,0:T(8,128)(2,1)S(1)}, bf16[64,4608]{1,0:T(8,128)(2,1)S(1)}, u32[]{:S(2)}, u32[]{:S(2)}) collective-permute-start(bf16[64,4608]{1,0:T(8,128)(2,1)S(1)} %pad_maximum_fusion.23), channel_id=1, source_target_pairs={{0,17},{1,16},{2,19},{3,18},{4,21},{5,20},{6,23},{7,22},{8,25},{9,... | collective-permute-start | bytes 1769480 | tf_op jit(solution)/shard_map/ppermute | solution.py:60
  62.2 26.1 %collective-permute-start.29 = (bf16[64,4608]{1,0:T(8,128)(2,1)S(1)}, bf16[64,4608]{1,0:T(8,128)(2,1)S(1)}, u32[]{:S(2)}, u32[]{:S(2)}) collective-permute-start(bf16[64,4608]{1,0:T(8,128)(2,1)S(1)} %pad_maximum_fusion.21), channel_id=1, source_target_pairs={{0,1},{1,0},{2,3},{3,2},{4,5},{5,4},{6,7},{7,6},{8,9},{9,8},{10,11... | collective-permute-start | bytes 1769480 | tf_op jit(solution)/shard_map/ppermute | solution.py:60
  91.8 226.0 %all-gather.8.cloned.1.call-start = ((), (), s32[]{:S(2)}) async-start(), calls=%async_computation.4 | async-start | bytes 7077888 | tf_op jit(solution)/shard_map/all_gather | solution.py:205
  93.4 10.9 %collective-permute-start.11 = (bf16[2,416,160]{2,1,0:T(8,128)(2,1)S(1)}, bf16[2,416,160]{2,1,0:T(8,128)(2,1)}, u32[]{:S(2)}, u32[]{:S(2)}) collective-permute-start(bf16[2,416,160]{2,1,0:T(8,128)(2,1)S(1)} %pad_maximum_fusion.28), channel_id=1, source_target_pairs={{0,1},{1,0},{2,3},{3,2},{4,5},{5,4},{6,7},{7,6},{8,9},{9,8},{10,11... | collective-permute-start | bytes 798728 | tf_op jit(solution)/shard_map/ppermute | solution.py:49
  95.1 28.7 %collective-permute-start.14 = (bf16[2,8,2048]{2,1,0:T(8,128)(2,1)S(1)}, bf16[2,8,2048]{2,1,0:T(8,128)(2,1)S(1)}, u32[]{:S(2)}, u32[]{:S(2)}) collective-permute-start(bf16[2,8,2048]{2,1,0:T(8,128)(2,1)S(1)} %slice.559), channel_id=1, source_target_pairs={{1,3},{3,5},{5,7},{9,11},{11,13},{13,15},{17,19},{19,21},{21,23},{... | collective-permute-start | bytes 196616 | tf_op jit(solution)/shard_map/ppermute | solution.py:70
  95.7 28.1 %collective-permute-start.13 = (bf16[2,8,2048]{2,1,0:T(8,128)(2,1)S(1)}, bf16[2,8,2048]{2,1,0:T(8,128)(2,1)S(1)}, u32[]{:S(2)}, u32[]{:S(2)}) collective-permute-start(bf16[2,8,2048]{2,1,0:T(8,128)(2,1)S(1)} %slice.559), channel_id=1, source_target_pairs={{1,2},{3,4},{5,6},{9,10},{11,12},{13,14},{17,18},{19,20},{21,22},{... | collective-permute-start | bytes 196616 | tf_op jit(solution)/shard_map/ppermute | solution.py:70
  109.6 21.9 %collective-permute-start.10 = (bf16[96,2048]{1,0:T(8,128)(2,1)}, bf16[96,2048]{1,0:T(8,128)(2,1)S(1)}, u32[]{:S(2)}, u32[]{:S(2)}) collective-permute-start(bf16[96,2048]{1,0:T(8,128)(2,1)} %slice_bitcast_fusion.30), channel_id=1, source_target_pairs={{0,1},{1,0},{2,3},{3,2},{4,5},{5,4},{6,7},{7,6},{8,9},{9,8},{10,11... | collective-permute-start | bytes 1179656 | tf_op jit(solution)/shard_map/ppermute | solution.py:49
  114.5 17.0 %collective-permute-start.9 = (bf16[96,2048]{1,0:T(8,128)(2,1)}, bf16[96,2048]{1,0:T(8,128)(2,1)S(1)}, u32[]{:S(2)}, u32[]{:S(2)}) collective-permute-start(bf16[96,2048]{1,0:T(8,128)(2,1)} %slice_bitcast_fusion.31), channel_id=1, source_target_pairs={{0,16},{8,24},{16,0},{24,8},{1,17},{9,25},{17,1},{25,9},{2,18},{10... | collective-permute-start | bytes 1179656 | tf_op jit(solution)/shard_map/ppermute | solution.py:49
  124.5 10.3 %collective-permute-start.15 = (bf16[2,8,2048]{2,1,0:T(8,128)(2,1)}, bf16[2,8,2048]{2,1,0:T(8,128)(2,1)}, u32[]{:S(2)}, u32[]{:S(2)}) collective-permute-start(bf16[2,8,2048]{2,1,0:T(8,128)(2,1)} %add.509), channel_id=1, source_target_pairs={{0,16},{8,24},{16,0},{24,8},{1,17},{9,25},{17,1},{25,9},{2,18},{10... | collective-permute-start | bytes 196616 | tf_op jit(solution)/shard_map/ppermute | solution.py:49
  156.4 15.9 %collective-permute-start.16 = (f32[4,2,640]{2,1,0:T(2,128)S(1)}, f32[4,2,640]{2,1,0:T(2,128)S(1)}, u32[]{:S(2)}, u32[]{:S(2)}) collective-permute-start(f32[4,2,640]{2,1,0:T(2,128)S(1)} %slice.435), channel_id=1, source_target_pairs={{0,2},{1,3},{2,4},{3,5},{4,6},{5,7},{8,10},{9,11},{10,12},{11,13},... | collective-permute-start | bytes 61448 | tf_op jit(solution)/shard_map/ppermute | solution.py:49
  161.5 10.9 %collective-permute-start.17 = (f32[4,2,640]{2,1,0:T(2,128)S(1)}, f32[4,2,640]{2,1,0:T(2,128)S(1)}, u32[]{:S(2)}, u32[]{:S(2)}) collective-permute-start(f32[4,2,640]{2,1,0:T(2,128)S(1)} %slice.435), channel_id=1, source_target_pairs={{0,4},{1,5},{2,6},{3,7},{8,12},{9,13},{10,14},{11,15},{16,20},{17,... | collective-permute-start | bytes 61448 | tf_op jit(solution)/shard_map/ppermute | solution.py:49
  169.2 19.0 %collective-permute-start.20 = (bf16[2,96,2048]{2,1,0:T(8,128)(2,1)}, bf16[2,96,2048]{2,1,0:T(8,128)(2,1)S(1)}, u32[]{:S(2)}, u32[]{:S(2)}) collective-permute-start(bf16[2,96,2048]{2,1,0:T(8,128)(2,1)} %shard_map.310.refs_0_), channel_id=1, source_target_pairs={{0,16},{8,24},{16,0},{24,8},{1,17},{9,25},{17,1},{25,9},{2,18},{10... | collective-permute-start | bytes 2359304 | tf_op jit(solution)/shard_map/ppermute | solution.py:49
  170.3 19.0 %collective-permute-start.19 = (bf16[2,96,2048]{2,1,0:T(8,128)(2,1)}, bf16[2,96,2048]{2,1,0:T(8,128)(2,1)}, u32[]{:S(2)}, u32[]{:S(2)}) collective-permute-start(bf16[2,96,2048]{2,1,0:T(8,128)(2,1)} %shard_map.310.refs_0_), channel_id=1, source_target_pairs={{0,1},{1,0},{2,3},{3,2},{4,5},{5,4},{6,7},{7,6},{8,9},{9,8},{10,11... | collective-permute-start | bytes 2359304 | tf_op jit(solution)/shard_map/ppermute | solution.py:49
  195.0 17.9 %collective-permute-start.21 = (bf16[2,96,2048]{2,1,0:T(8,128)(2,1)}, bf16[2,96,2048]{2,1,0:T(8,128)(2,1)S(1)}, u32[]{:S(2)}, u32[]{:S(2)}) collective-permute-start(bf16[2,96,2048]{2,1,0:T(8,128)(2,1)} %slice_bitcast_fusion.22), channel_id=1, source_target_pairs={{0,16},{8,24},{16,0},{24,8},{1,17},{9,25},{17,1},{25,9},{2,18},{10... | collective-permute-start | bytes 2359304 | tf_op jit(solution)/shard_map/ppermute | solution.py:49
  196.7 17.4 %collective-permute-start.23 = (bf16[2,96,2048]{2,1,0:T(8,128)(2,1)}, bf16[2,96,2048]{2,1,0:T(8,128)(2,1)S(1)}, u32[]{:S(2)}, u32[]{:S(2)}) collective-permute-start(bf16[2,96,2048]{2,1,0:T(8,128)(2,1)} %slice_bitcast_fusion.19), channel_id=1, source_target_pairs={{0,1},{1,0},{2,3},{3,2},{4,5},{5,4},{6,7},{7,6},{8,9},{9,8},{10,11... | collective-permute-start | bytes 2359304 | tf_op jit(solution)/shard_map/ppermute | solution.py:49
  200.2 339.4 %reduce-scatter.3.cloned.1.call-start = ((), (), s32[]{:S(2)}) async-start(), calls=%async_computation.5 | async-start | bytes 11796480 | tf_op jit(solution)/shard_map/reduce_scatter | solution.py:246
  226.5 20.5 %collective-permute-start.25 = (bf16[2,96,2048]{2,1,0:T(8,128)(2,1)S(1)}, bf16[2,96,2048]{2,1,0:T(8,128)(2,1)S(1)}, u32[]{:S(2)}, u32[]{:S(2)}) collective-permute-start(bf16[2,96,2048]{2,1,0:T(8,128)(2,1)S(1)} %multiply_convert_fusion.3.refs_0_), channel_id=1, source_target_pairs={{0,1},{1,0},{2,3},{3,2},{4,5},{5,4},{6,7},{7,6},{8,9},{9,8},{10,11... | collective-permute-start | bytes 2359304 | tf_op jit(solution)/shard_map/ppermute | solution.py:49
  227.9 21.4 %collective-permute-start.26 = (bf16[2,96,2048]{2,1,0:T(8,128)(2,1)S(1)}, bf16[2,96,2048]{2,1,0:T(8,128)(2,1)S(1)}, u32[]{:S(2)}, u32[]{:S(2)}) collective-permute-start(bf16[2,96,2048]{2,1,0:T(8,128)(2,1)S(1)} %multiply_convert_fusion.3.refs_0_), channel_id=1, source_target_pairs={{0,16},{8,24},{16,0},{24,8},{1,17},{9,25},{17,1},{25,9},{2,18},{10... | collective-permute-start | bytes 2359304 | tf_op jit(solution)/shard_map/ppermute | solution.py:49
  231.1 23.5 %collective-permute-start.33 = (bf16[96,2048]{1,0:T(8,128)(2,1)}, bf16[96,2048]{1,0:T(8,128)(2,1)}, u32[]{:S(2)}, u32[]{:S(2)}) collective-permute-start(bf16[96,2048]{1,0:T(8,128)(2,1)} %slice_bitcast_fusion.28), channel_id=1, source_target_pairs={{0,1},{1,0},{2,3},{3,2},{4,5},{5,4},{6,7},{7,6},{8,9},{9,8},{10,11... | collective-permute-start | bytes 1179656 | tf_op jit(solution)/shard_map/ppermute | solution.py:49
  232.5 23.3 %collective-permute-start.32 = (bf16[96,2048]{1,0:T(8,128)(2,1)}, bf16[96,2048]{1,0:T(8,128)(2,1)}, u32[]{:S(2)}, u32[]{:S(2)}) collective-permute-start(bf16[96,2048]{1,0:T(8,128)(2,1)} %slice_bitcast_fusion.29), channel_id=1, source_target_pairs={{0,16},{8,24},{16,0},{24,8},{1,17},{9,25},{17,1},{25,9},{2,18},{10... | collective-permute-start | bytes 1179656 | tf_op jit(solution)/shard_map/ppermute | solution.py:49
  247.8 12.4 %collective-permute-start.27 = (bf16[96,2048]{1,0:T(8,128)(2,1)}, bf16[96,2048]{1,0:T(8,128)(2,1)S(1)}, u32[]{:S(2)}, u32[]{:S(2)}) collective-permute-start(bf16[96,2048]{1,0:T(8,128)(2,1)} %slice_bitcast_fusion.25), channel_id=1, source_target_pairs={{0,16},{8,24},{16,0},{24,8},{1,17},{9,25},{17,1},{25,9},{2,18},{10... | collective-permute-start | bytes 1179656 | tf_op jit(solution)/shard_map/ppermute | solution.py:49
  250.3 9.9 %collective-permute-start.28 = (bf16[96,2048]{1,0:T(8,128)(2,1)}, bf16[96,2048]{1,0:T(8,128)(2,1)}, u32[]{:S(2)}, u32[]{:S(2)}) collective-permute-start(bf16[96,2048]{1,0:T(8,128)(2,1)} %slice_bitcast_fusion.24), channel_id=1, source_target_pairs={{0,1},{1,0},{2,3},{3,2},{4,5},{5,4},{6,7},{7,6},{8,9},{9,8},{10,11... | collective-permute-start | bytes 1179656 | tf_op jit(solution)/shard_map/ppermute | solution.py:49
  280.4 14.1 %collective-permute-start.34 = (bf16[1024,1024]{1,0:T(8,128)(2,1)}, bf16[1024,1024]{1,0:T(8,128)(2,1)}, u32[]{:S(2)}, u32[]{:S(2)}) collective-permute-start(bf16[1024,1024]{1,0:T(8,128)(2,1)} %convolution_convert_fusion.4), channel_id=1, source_target_pairs={{0,8},{8,0},{16,24},{24,16},{1,9},{9,1},{17,25},{25,17},{2,10},{10... | collective-permute-start | bytes 6291464 | tf_op jit(solution)/shard_map/ppermute | solution.py:49
  291.6 19.3 %collective-permute-start.35 = (bf16[1024,2048]{1,0:T(8,128)(2,1)}, bf16[1024,2048]{1,0:T(8,128)(2,1)}, u32[]{:S(2)}, u32[]{:S(2)}) collective-permute-start(bf16[1024,2048]{1,0:T(8,128)(2,1)} %convolution_convert_fusion.1), channel_id=1, source_target_pairs={{0,8},{8,0},{16,24},{24,16},{1,9},{9,1},{17,25},{25,17},{2,10},{10... | collective-permute-start | bytes 12582920 | tf_op jit(solution)/shard_map/ppermute | solution.py:49
  333.0 13.1 %collective-permute-start.38 = (bf16[1024,1024]{1,0:T(8,128)(2,1)S(1)}, bf16[1024,1024]{1,0:T(8,128)(2,1)S(1)}, u32[]{:S(2)}, u32[]{:S(2)}) collective-permute-start(bf16[1024,1024]{1,0:T(8,128)(2,1)S(1)} %convolution_convert_fusion.3), channel_id=1, source_target_pairs={{0,8},{8,0},{16,24},{24,16},{1,9},{9,1},{17,25},{25,17},{2,10},{10... | collective-permute-start | bytes 6291464 | tf_op jit(solution)/shard_map/ppermute | solution.py:49
  342.6 20.1 %collective-permute-start.40 = (bf16[2,96,2048]{2,1,0:T(8,128)(2,1)}, bf16[2,96,2048]{2,1,0:T(8,128)(2,1)S(1)}, u32[]{:S(2)}, u32[]{:S(2)}) collective-permute-start(bf16[2,96,2048]{2,1,0:T(8,128)(2,1)} %slice_bitcast_fusion.13), channel_id=1, source_target_pairs={{0,1},{1,0},{2,3},{3,2},{4,5},{5,4},{6,7},{7,6},{8,9},{9,8},{10,11... | collective-permute-start | bytes 2359304 | tf_op jit(solution)/shard_map/ppermute | solution.py:49
  344.9 19.9 %collective-permute-start.37 = (bf16[2,96,2048]{2,1,0:T(8,128)(2,1)}, bf16[2,96,2048]{2,1,0:T(8,128)(2,1)}, u32[]{:S(2)}, u32[]{:S(2)}) collective-permute-start(bf16[2,96,2048]{2,1,0:T(8,128)(2,1)} %slice_bitcast_fusion.16), channel_id=1, source_target_pairs={{0,16},{8,24},{16,0},{24,8},{1,17},{9,25},{17,1},{25,9},{2,18},{10... | collective-permute-start | bytes 2359304 | tf_op jit(solution)/shard_map/ppermute | solution.py:49
  354.0 270.3 %reduce-scatter.5.cloned.1.call-start = ((), (), s32[]{:S(2)}) async-start(), calls=%async_computation.6 | async-start | bytes 4915200 | tf_op jit(solution)/shard_map/reduce_scatter | solution.py:246
  367.0 10.4 %collective-permute-start.39 = (bf16[96,2048]{1,0:T(8,128)(2,1)S(1)}, bf16[96,2048]{1,0:T(8,128)(2,1)S(1)}, u32[]{:S(2)}, u32[]{:S(2)}) collective-permute-start(bf16[96,2048]{1,0:T(8,128)(2,1)S(1)} %fusion.118), channel_id=1, source_target_pairs={{0,1},{1,0},{2,3},{3,2},{4,5},{5,4},{6,7},{7,6},{8,9},{9,8},{10,11... | collective-permute-start | bytes 1179656 | tf_op jit(solution)/shard_map/ppermute | solution.py:49
  367.8 10.1 %collective-permute-start.41 = (bf16[96,2048]{1,0:T(8,128)(2,1)S(1)}, bf16[96,2048]{1,0:T(8,128)(2,1)S(1)}, u32[]{:S(2)}, u32[]{:S(2)}) collective-permute-start(bf16[96,2048]{1,0:T(8,128)(2,1)S(1)} %fusion.119), channel_id=1, source_target_pairs={{0,16},{8,24},{16,0},{24,8},{1,17},{9,25},{17,1},{25,9},{2,18},{10... | collective-permute-start | bytes 1179656 | tf_op jit(solution)/shard_map/ppermute | solution.py:49
  379.6 17.7 %collective-permute-start.43 = (bf16[2,96,2048]{2,1,0:T(8,128)(2,1)S(1)}, bf16[2,96,2048]{2,1,0:T(8,128)(2,1)S(1)}, u32[]{:S(2)}, u32[]{:S(2)}) collective-permute-start(bf16[2,96,2048]{2,1,0:T(8,128)(2,1)S(1)} %fusion.165.refs_0_), channel_id=1, source_target_pairs={{0,16},{8,24},{16,0},{24,8},{1,17},{9,25},{17,1},{25,9},{2,18},{10... | collective-permute-start | bytes 2359304 | tf_op jit(solution)/shard_map/ppermute | solution.py:49
  381.1 18.4 %collective-permute-start.42 = (bf16[2,96,2048]{2,1,0:T(8,128)(2,1)S(1)}, bf16[2,96,2048]{2,1,0:T(8,128)(2,1)S(1)}, u32[]{:S(2)}, u32[]{:S(2)}) collective-permute-start(bf16[2,96,2048]{2,1,0:T(8,128)(2,1)S(1)} %fusion.165.refs_0_), channel_id=1, source_target_pairs={{0,1},{1,0},{2,3},{3,2},{4,5},{5,4},{6,7},{7,6},{8,9},{9,8},{10,11... | collective-permute-start | bytes 2359304 | tf_op jit(solution)/shard_map/ppermute | solution.py:49
  427.2 14.3 %collective-permute-start.50 = (f32[4,2,640]{2,1,0:T(2,128)S(1)}, f32[4,2,640]{2,1,0:T(2,128)S(1)}, u32[]{:S(2)}, u32[]{:S(2)}) collective-permute-start(f32[4,2,640]{2,1,0:T(2,128)S(1)} %slice.487), channel_id=1, source_target_pairs={{2,0},{3,1},{4,2},{5,3},{6,4},{7,5},{10,8},{11,9},{12,10},{13,11},... | collective-permute-start | bytes 61448 | tf_op jit(solution)/shard_map/ppermute | solution.py:49
  428.5 13.0 %collective-permute-start.51 = (f32[4,2,640]{2,1,0:T(2,128)S(1)}, f32[4,2,640]{2,1,0:T(2,128)S(1)}, u32[]{:S(2)}, u32[]{:S(2)}) collective-permute-start(f32[4,2,640]{2,1,0:T(2,128)S(1)} %slice.487), channel_id=1, source_target_pairs={{4,0},{5,1},{6,2},{7,3},{12,8},{13,9},{14,10},{15,11},{20,16},{21,... | collective-permute-start | bytes 61448 | tf_op jit(solution)/shard_map/ppermute | solution.py:49
  429.8 11.7 %collective-permute-start.52 = (f32[4,2,640]{2,1,0:T(2,128)S(1)}, f32[4,2,640]{2,1,0:T(2,128)S(1)}, u32[]{:S(2)}, u32[]{:S(2)}) collective-permute-start(f32[4,2,640]{2,1,0:T(2,128)S(1)} %slice.487), channel_id=1, source_target_pairs={{6,0},{7,1},{14,8},{15,9},{22,16},{23,17},{30,24},{31,25}} | collective-permute-start | bytes 61448 | tf_op jit(solution)/shard_map/ppermute | solution.py:49
  439.4 35.0 %collective-permute-start.46 = (bf16[2,96,2048]{2,1,0:T(8,128)(2,1)}, bf16[2,96,2048]{2,1,0:T(8,128)(2,1)}, u32[]{:S(2)}, u32[]{:S(2)}) collective-permute-start(bf16[2,96,2048]{2,1,0:T(8,128)(2,1)} %slice_bitcast_fusion.10), channel_id=1, source_target_pairs={{0,16},{8,24},{16,0},{24,8},{1,17},{9,25},{17,1},{25,9},{2,18},{10... | collective-permute-start | bytes 2359304 | tf_op jit(solution)/shard_map/ppermute | solution.py:49
  440.6 33.8 %collective-permute-start.48 = (bf16[2,96,2048]{2,1,0:T(8,128)(2,1)}, bf16[2,96,2048]{2,1,0:T(8,128)(2,1)}, u32[]{:S(2)}, u32[]{:S(2)}) collective-permute-start(bf16[2,96,2048]{2,1,0:T(8,128)(2,1)} %slice_bitcast_fusion.7), channel_id=1, source_target_pairs={{0,1},{1,0},{2,3},{3,2},{4,5},{5,4},{6,7},{7,6},{8,9},{9,8},{10,11... | collective-permute-start | bytes 2359304 | tf_op jit(solution)/shard_map/ppermute | solution.py:49
  452.6 11.5 %collective-permute-start.53 = (f32[4,8,640]{2,1,0:T(8,128)}, f32[4,8,640]{2,1,0:T(8,128)}, u32[]{:S(2)}, u32[]{:S(2)}) collective-permute-start(f32[4,8,640]{2,1,0:T(8,128)} %get-tuple-element.132), channel_id=1, source_target_pairs={{2,0},{3,1},{4,2},{5,3},{6,4},{7,5},{10,8},{11,9},{12,10},{13,11},... | collective-permute-start | bytes 245768 | tf_op jit(solution)/shard_map/ppermute | solution.py:49
  492.8 18.3 %collective-permute-start.55 = (bf16[1024,1280]{1,0:T(8,128)(2,1)}, bf16[1024,1280]{1,0:T(8,128)(2,1)}, u32[]{:S(2)}, u32[]{:S(2)}) collective-permute-start(bf16[1024,1280]{1,0:T(8,128)(2,1)} %convolution_convert_fusion), channel_id=1, source_target_pairs={{0,8},{8,0},{16,24},{24,16},{1,9},{9,1},{17,25},{25,17},{2,10},{10... | collective-permute-start | bytes 7864328 | tf_op jit(solution)/shard_map/ppermute | solution.py:49
  495.3 12.2 %collective-permute-start.56 = (bf16[1024,640]{1,0:T(8,128)(2,1)}, bf16[1024,640]{1,0:T(8,128)(2,1)}, u32[]{:S(2)}, u32[]{:S(2)}) collective-permute-start(bf16[1024,640]{1,0:T(8,128)(2,1)} %convolution_convert_fusion.5), channel_id=1, source_target_pairs={{0,8},{8,0},{16,24},{24,16},{1,9},{9,1},{17,25},{25,17},{2,10},{10... | collective-permute-start | bytes 3932168 | tf_op jit(solution)/shard_map/ppermute | solution.py:49
  503.7 20.3 %collective-permute-start.59 = (bf16[2,96,2048]{2,1,0:T(8,128)(2,1)}, bf16[2,96,2048]{2,1,0:T(8,128)(2,1)}, u32[]{:S(2)}, u32[]{:S(2)}) collective-permute-start(bf16[2,96,2048]{2,1,0:T(8,128)(2,1)} %slice_bitcast_fusion.1), channel_id=1, source_target_pairs={{0,1},{1,0},{2,3},{3,2},{4,5},{5,4},{6,7},{7,6},{8,9},{9,8},{10,11... | collective-permute-start | bytes 2359304 | tf_op jit(solution)/shard_map/ppermute | solution.py:49
  504.7 20.0 %collective-permute-start.54 = (bf16[2,96,2048]{2,1,0:T(8,128)(2,1)}, bf16[2,96,2048]{2,1,0:T(8,128)(2,1)}, u32[]{:S(2)}, u32[]{:S(2)}) collective-permute-start(bf16[2,96,2048]{2,1,0:T(8,128)(2,1)} %slice_bitcast_fusion.4), channel_id=1, source_target_pairs={{0,16},{8,24},{16,0},{24,8},{1,17},{9,25},{17,1},{25,9},{2,18},{10... | collective-permute-start | bytes 2359304 | tf_op jit(solution)/shard_map/ppermute | solution.py:49
  505.4 67.9 %collective-permute-start.64 = (bf16[2,2,176,160]{2,3,1,0:T(8,128)(2,1)S(1)}, bf16[2,2,176,160]{2,3,1,0:T(8,128)(2,1)}, u32[]{:S(2)}, u32[]{:S(2)}) collective-permute-start(bf16[2,2,176,160]{2,3,1,0:T(8,128)(2,1)S(1)} %fusion.111), channel_id=1, source_target_pairs={{0,2},{1,3},{2,4},{3,5},{4,6},{5,7},{6,0},{7,1},{8,10},{9,11},{10,... | collective-permute-start | bytes 675848 | tf_op jit(solution)/shard_map/ppermute | solution.py:49
  507.5 65.8 %collective-permute-start.68 = (bf16[2,2,176,160]{2,3,1,0:T(8,128)(2,1)S(1)}, bf16[2,2,176,160]{2,3,1,0:T(8,128)(2,1)}, u32[]{:S(2)}, u32[]{:S(2)}) collective-permute-start(bf16[2,2,176,160]{2,3,1,0:T(8,128)(2,1)S(1)} %fusion.111), channel_id=1, source_target_pairs={{0,4},{1,5},{2,6},{3,7},{4,0},{5,1},{6,2},{7,3},{8,12},{9,13},{10,... | collective-permute-start | bytes 675848 | tf_op jit(solution)/shard_map/ppermute | solution.py:49
  527.1 10.5 %collective-permute-start.58 = (bf16[96,2048]{1,0:T(8,128)(2,1)S(1)}, bf16[96,2048]{1,0:T(8,128)(2,1)S(1)}, u32[]{:S(2)}, u32[]{:S(2)}) collective-permute-start(bf16[96,2048]{1,0:T(8,128)(2,1)S(1)} %fusion.122), channel_id=1, source_target_pairs={{0,1},{1,0},{2,3},{3,2},{4,5},{5,4},{6,7},{7,6},{8,9},{9,8},{10,11... | collective-permute-start | bytes 1179656 | tf_op jit(solution)/shard_map/ppermute | solution.py:49
  528.4 10.2 %collective-permute-start.60 = (bf16[96,2048]{1,0:T(8,128)(2,1)S(1)}, bf16[96,2048]{1,0:T(8,128)(2,1)S(1)}, u32[]{:S(2)}, u32[]{:S(2)}) collective-permute-start(bf16[96,2048]{1,0:T(8,128)(2,1)S(1)} %fusion.123), channel_id=1, source_target_pairs={{0,16},{8,24},{16,0},{24,8},{1,17},{9,25},{17,1},{25,9},{2,18},{10... | collective-permute-start | bytes 1179656 | tf_op jit(solution)/shard_map/ppermute | solution.py:49
  542.4 16.6 %collective-permute-start.65 = (bf16[64,4608]{1,0:T(8,128)(2,1)}, bf16[64,4608]{1,0:T(8,128)(2,1)}, u32[]{:S(2)}, u32[]{:S(2)}) collective-permute-start(bf16[64,4608]{1,0:T(8,128)(2,1)} %get-tuple-element.171), channel_id=1, source_target_pairs={{0,1},{1,0},{2,3},{3,2},{4,5},{5,4},{6,7},{7,6},{8,9},{9,8},{10,11... | collective-permute-start | bytes 1769480 | tf_op jit(solution)/shard_map/ppermute | solution.py:60
  543.5 26.5 %collective-permute-start.66 = (bf16[64,4608]{1,0:T(8,128)(2,1)}, bf16[64,4608]{1,0:T(8,128)(2,1)}, u32[]{:S(2)}, u32[]{:S(2)}) collective-permute-start(bf16[64,4608]{1,0:T(8,128)(2,1)} %get-tuple-element.173), channel_id=1, source_target_pairs={{0,16},{1,17},{2,18},{3,19},{4,20},{5,21},{6,22},{7,23},{8,24},{9,... | collective-permute-start | bytes 1769480 | tf_op jit(solution)/shard_map/ppermute | solution.py:60
  544.2 25.8 %collective-permute-start.67 = (bf16[64,4608]{1,0:T(8,128)(2,1)}, bf16[64,4608]{1,0:T(8,128)(2,1)}, u32[]{:S(2)}, u32[]{:S(2)}) collective-permute-start(bf16[64,4608]{1,0:T(8,128)(2,1)} %get-tuple-element.172), channel_id=1, source_target_pairs={{0,17},{1,16},{2,19},{3,18},{4,21},{5,20},{6,23},{7,22},{8,25},{9,... | collective-permute-start | bytes 1769480 | tf_op jit(solution)/shard_map/ppermute | solution.py:60
  558.9 23.4 %collective-permute-start.69 = (bf16[2,2,176,160]{2,3,1,0:T(8,128)(2,1)S(1)}, bf16[2,2,176,160]{2,3,1,0:T(8,128)(2,1)S(1)}, u32[]{:S(2)}, u32[]{:S(2)}) collective-permute-start(bf16[2,2,176,160]{2,3,1,0:T(8,128)(2,1)S(1)} %fusion.111), channel_id=1, source_target_pairs={{0,6},{1,7},{2,0},{3,1},{4,2},{5,3},{6,4},{7,5},{8,14},{9,15},{10,... | collective-permute-start | bytes 675848 | tf_op jit(solution)/shard_map/ppermute | solution.py:49
  589.8 10.8 %collective-permute-start.71 = (bf16[2,2,176,160]{2,3,1,0:T(8,128)(2,1)}, bf16[2,2,176,160]{2,3,1,0:T(8,128)(2,1)S(1)}, u32[]{:S(2)}, u32[]{:S(2)}) collective-permute-start(bf16[2,2,176,160]{2,3,1,0:T(8,128)(2,1)} %add_convert_fusion.7), channel_id=1, source_target_pairs={{0,16},{1,17},{2,18},{3,19},{4,20},{5,21},{6,22},{7,23},{8,24},{9,... | collective-permute-start | bytes 675848 | tf_op jit(solution)/shard_map/ppermute | solution.py:60
  627.1 11.6 %collective-permute-start.62 = (bf16[64,1920]{1,0:T(8,128)(2,1)S(1)}, bf16[64,1920]{1,0:T(8,128)(2,1)S(1)}, u32[]{:S(2)}, u32[]{:S(2)}) collective-permute-start(bf16[64,1920]{1,0:T(8,128)(2,1)S(1)} %get-tuple-element.222), channel_id=1, source_target_pairs={{0,16},{1,17},{2,18},{3,19},{4,20},{5,21},{6,22},{7,23},{8,24},{9,... | collective-permute-start | bytes 737288 | tf_op jit(solution)/shard_map/ppermute | solution.py:60
  (144 other events, 1149.7 us)
Sparse Core Ops, SparseCore 0:
  26.4 93.8 all-gather.3
  122.5 117.9 all-gather.5
  242.1 64.5 all-gather.7
  354.1 166.3 reduce-scatter.2
  546.1 78.1 reduce-scatter.4

commit v5 on v4

--- a/solution.py
+++ b/solution.py
@@ -670,19 +670,6 @@
     ahead = grid.rows_ahead(own_rows[:, step - HALO :], vec)
     ahead = jnp.stack([ahead] + [grid.shift(ahead, "y", r) for r in range(1, ny)], axis=1)
     ahead = ahead.reshape(chains * HALO, depth)
-    pieces = [gained(mlp_gate, gain_mlp), gained(mlp_up, gain_mlp), mlp_down]
-    pieces = [after(p, weights_in) for p in pieces]
-    weights_ff = grid.columns_of(pieces, *in_hop).reshape(plane, -1)
-    wide = ff_width - ff_width // 3
-    ff_cuts = [
-        grid.all_rows(
-            jnp.concatenate(
-                [weights_ff[:, i * ff_width + lo : i * ff_width + hi] for i in range(3)], axis=1
-            )
-        )
-        for lo, hi in ((0, wide), (wide, ff_width))
-    ]
-
     segments = jnp.stack([seg_ids, *beside], axis=1)
     padded = jnp.pad(segments, ((0, 0), (0, 0), (HALO, 0)), constant_values=-1)
     near = lax.dynamic_slice_in_dim(padded, z * length, length + HALO, 2)
@@ -693,6 +680,19 @@
     same = jnp.stack(same + [jnp.zeros_like(same[0])] * (8 - TAPS), axis=-1)
     same = same.reshape(chains, length, 8)
     order = ((x - jnp.arange(nx, dtype=jnp.int32)) % nx).astype(jnp.int32)
+
+    pieces = [gained(mlp_gate, gain_mlp), gained(mlp_up, gain_mlp), mlp_down]
+    pieces = [after(p, weights_in) for p in pieces]
+    weights_ff = grid.columns_of(pieces, *in_hop, same).reshape(plane, -1)
+    wide = ff_width - ff_width // 3
+    ff_cuts = [
+        grid.all_rows(
+            jnp.concatenate(
+                [weights_ff[:, i * ff_width + lo : i * ff_width + hi] for i in range(3)], axis=1
+            )
+        )
+        for lo, hi in ((0, wide), (wide, ff_width))
+    ]
 
     mix_all = after(mix_all, vec, same)
     mix_x, mix_y, mix_out = (mix_all[:, i * width : (i + 1) * width] for i in range(3))
@@ -807,13 +807,12 @@
         [(length + HALO, width), (length + 2 * HALO, width)],
         flops=8 * chains * length * width * width,
     )
-    behind = grid.shift(head, "z", -1, wrap=False)
+    behind = after(grid.shift(head, "z", -1, wrap=False), block_out)
     chunk = lax.broadcasted_iota(jnp.int32, (1, nx, 1, 1), 1)
     tail = jnp.pad(behind, ((0, 0), (step - HALO, 0), (0, 0)))[:, None]
     d_drive = d_drive + jnp.where(chunk == (x - (nx - 1)) % nx, tail, 0.0)
     grad_drive = d_drive.astype(BF16).reshape(chains * length, width)
     part_in = (mix_back(grad_pre_y, mix_y) + mix_back(grad_drive, mix_x)).astype(BF16)
-    part_in = after(part_in, block_out)
     both = jnp.concatenate([grad_pre_y, grad_drive], axis=1)
     sum_in = WeightSum(grid, normed, after(both, part_in))
     sum_out = WeightSum(grid, grad_branch, after(mixed, part_in))

time: 657 us -> 652 us (level)
  waiting for transfers between devices: 231 us -> 212 us
  starting transfers between devices: 88 us -> 101 us
    ppermute x57, starting transfers between devices: 68.7 us -> 80.5 us  [shift(): return lax.ppermute(value, axis, pairs)]
    ppermute x57, waiting for transfers between devices: 141 us -> 131 us  [shift(): return lax.ppermute(value, axis, pairs)]
    ppermute x15, waiting for transfers between devices: 74 us -> 64.8 us  [shift_plane(): return lax.ppermute(value, ('seq', 'blk'), pairs)]
    unnamed x266 -> x272, local copies, waits for them, and re-layouts: 26.9 us -> 27.4 us
  transfers between devices with their start and end apart: 79 -> 79, of which waited for: 39 -> 39; matrix products, arithmetic and copies ran while one was open for 34% -> 35% of each run, Pallas kernels for 7% -> 8%
where the time goes in v5:
time: 652 us; the launch traced here: 646 us
  waiting for transfers between devices  212 us (33%)
  matrix products  129 us (20%)
  starting transfers between devices  101 us (15%)
  local copies, waits for them, and re-layouts  71.1 us (11%)
  other arithmetic  67.8 us (10%)
  Pallas kernels  48.7 us (7%)
  between operations  16.6 us (3%)
    ppermute x57, waiting for transfers between devices, shift(): return lax.ppermute(value, axis, pairs)  131 us
    ppermute x57, starting transfers between devices, shift(): return lax.ppermute(value, axis, pairs)  80.5 us
    ppermute x15, waiting for transfers between devices, shift_plane(): return lax.ppermute(value, ('seq', 'blk'), pairs)  64.8 us
    dot_general x8, matrix products, mix(): return jnp.dot(left, right, preferred_element_type=F32)  44.7 us
    dot_general x7, matrix products, mix_back(): lax.dot_general(left, right, (((1,), (1,)), ((), ())), preferred_element_...  41.6 us
    dot_general x12, matrix products, product(): lax.dot_general(cut, self.right, (((0,), (0,)), ((), ())), preferred_elem...  40.2 us
    pallas_call x3, Pallas kernels, scan_call(): pl.pallas_call(kernel, grid=(chains,), in_specs=specs, out_specs=out_spec...  28.6 us
    unnamed x272, local copies, waits for them, and re-layouts  27.4 us
  transfers between devices with their start and end apart: 79, of which 39 were waited for; matrix products, arithmetic and copies ran while one was open for 35% of the time, Pallas kernels for 8%

profile of v5, /device:TPU:0, one launch (start us, length us, event | category | flops | bytes accessed | tf_op | source)
XLA Modules:
  0.0 645.8 jit_solution(12727153710803263480)
XLA Ops:
  9.4 4.0 collective-permute-start.2
  14.2 6.1 collective-permute-done.2
  20.2 4.4 collective-permute-done.1
  34.1 2.6 collective-permute-start.6
  46.8 14.0 %collective-permute-done.6 = bf16[416,160]{1,0:T(8,128)(2,1)} collective-permute-done((bf16[416,160]{1,0:T(8,128)(2,1)}, bf16[416,160]{1,0:T(8,128)(2,1)}, u32[]{:S(2)}, u32[]{:S(2)}) %collective-permute-start.6) | collective-permute-done | bytes 133152 | tf_op jit(solution)/shard_map/ppermute | solution.py:49
  66.8 7.5 %collective-permute-done.29 = bf16[64,4608]{1,0:T(8,128)(2,1)} collective-permute-done((bf16[64,4608]{1,0:T(8,128)(2,1)}, bf16[64,4608]{1,0:T(8,128)(2,1)}, u32[]{:S(2)}, u32[]{:S(2)}) %collective-permute-start.29) | collective-permute-done | bytes 589856 | tf_op jit(solution)/shard_map/ppermute | solution.py:60
  74.3 14.4 %collective-permute-done.30 = bf16[64,4608]{1,0:T(8,128)(2,1)} collective-permute-done((bf16[64,4608]{1,0:T(8,128)(2,1)}, bf16[64,4608]{1,0:T(8,128)(2,1)}, u32[]{:S(2)}, u32[]{:S(2)}) %collective-permute-start.30) | collective-permute-done | bytes 589856 | tf_op jit(solution)/shard_map/ppermute | solution.py:60
  100.3 6.8 %collective-permute-done.11 = bf16[2,416,160]{2,1,0:T(8,128)(2,1)} collective-permute-done((bf16[2,416,160]{2,1,0:T(8,128)(2,1)S(1)}, bf16[2,416,160]{2,1,0:T(8,128)(2,1)}, u32[]{:S(2)}, u32[]{:S(2)}) %collective-permute-start.11) | collective-permute-done | bytes 266272 | tf_op jit(solution)/shard_map/ppermute | solution.py:49
  112.4 6.9 %collective-permute-start.10 = (bf16[96,2048]{1,0:T(8,128)(2,1)}, bf16[96,2048]{1,0:T(8,128)(2,1)S(1)}, u32[]{:S(2)}, u32[]{:S(2)}) collective-permute-start(bf16[96,2048]{1,0:T(8,128)(2,1)} %slice_bitcast_fusion.30), channel_id=1, source_target_pairs={{0,1},{1,0},{2,3},{3,2},{4,5},{5,4},{6,7},{7,6},{8,9},{9,8},{10,11... | collective-permute-start | bytes 1179656 | tf_op jit(solution)/shard_map/ppermute | solution.py:49
  129.4 2.9 collective-permute-done.9.refs_3_
  139.4 5.5 fusion.71
  145.0 10.3 %shard_map.309 = (f32[4,192,640]{2,1,0:T(8,128)S(1)}, f32[4,192,640]{2,1,0:T(8,128)}, f32[4,192,640]{2,1,0:T(8,128)}, f32[4,2,96,640]{3,2,1,0:T(8,128)}, f32[4,2...) custom-call(s32[2]{0:T(128)S(1)} %and_select_fusion.order, bf16[4,2,96,640]{3,2,1,0:T(8,128)(2,1)S(1)} %bitcast.509, ...), custom_call_target="tpu_custom_call" | custom-call | flops 2516582400 | bytes 12660744 | tf_op jit(solution)/shard_map/pallas_call | solution.py:573
  158.9 7.0 %collective-permute-start.17 = (f32[4,2,640]{2,1,0:T(2,128)S(1)}, f32[4,2,640]{2,1,0:T(2,128)S(1)}, u32[]{:S(2)}, u32[]{:S(2)}) collective-permute-start(f32[4,2,640]{2,1,0:T(2,128)S(1)} %slice.435), channel_id=1, source_target_pairs={{0,4},{1,5},{2,6},{3,7},{8,12},{9,13},{10,14},{11,15},{16,20},{17,... | collective-permute-start | bytes 61448 | tf_op jit(solution)/shard_map/ppermute | solution.py:49
  172.5 2.6 add_convert_fusion.6
  175.7 6.3 fusion.37
  182.0 6.1 collective-permute-done.20.refs_2_
  188.7 4.7 convolution_convert_fusion.2
  200.4 11.9 %collective-permute-done.21 = bf16[2,96,2048]{2,1,0:T(8,128)(2,1)S(1)} collective-permute-done((bf16[2,96,2048]{2,1,0:T(8,128)(2,1)}, bf16[2,96,2048]{2,1,0:T(8,128)(2,1)S(1)}, u32[]{:S(2)}, u32[]{:S(2)}) %collective-permute-start.21) | collective-permute-done | bytes 786464 | tf_op jit(solution)/shard_map/ppermute | solution.py:49
  218.1 5.8 collective-permute-done.22
  232.0 13.9 %collective-permute-done.25.refs_1_ = bf16[2,96,2048]{2,1,0:T(8,128)(2,1)S(1)} collective-permute-done((bf16[2,96,2048]{2,1,0:T(8,128)(2,1)S(1)}, bf16[2,96,2048]{2,1,0:T(8,128)(2,1)S(1)}, u32[]{:S(2)}, u32[]{:S(2)}) %collective-permute-start.25) | collective-permute-done | bytes 786464 | tf_op jit(solution)/shard_map/ppermute | solution.py:49
  250.3 2.9 collective-permute-done.33.refs_4_
  254.9 2.6 shard_map.312
  265.2 9.1 %fusion.12 = bf16[768,2048]{1,0:T(8,128)(2,1)S(1)} fusion(bf16[768,2048]{1,0:T(8,128)(2,1)S(1)} %bitcast.497, bf16[2048,3072]{1,0:T(8,128)(2,1)} %all-gather.6.cloned.1.call-done), kind=kOutput, calls=%fused_computation.28 | convolution fusion | flops 6444023808 | bytes 14680064 | tf_op jit(solution)/shard_map/dot_general | solution.py:592
  276.2 3.1 convolution_convert_fusion.4
  279.4 5.6 fusion.18
  285.0 5.7 convolution_convert_fusion.1
  294.0 4.7 convert_add_fusion.2
  298.8 11.1 %fusion = f32[768,2048]{1,0:T(8,128)} fusion(bf16[768,2048]{1,0:T(8,128)(2,1)S(1)} %pad_maximum_fusion.2, bf16[2048,3072]{1,0:T(8,128)(2,1)} %all-gather.6.cloned.1.call-done), kind=kOutput, calls=%fused_computation.2 | convolution fusion | flops 6442450944 | bytes 17825792 | tf_op jit(solution)/shard_map/dot_general | solution.py:596
  309.9 6.9 %convert_add_fusion = bf16[1024,2048]{1,0:T(8,128)(2,1)} fusion(bf16[1024,2048]{1,0:T(8,128)(2,1)} %collective-permute-done.35, bf16[768,2048]{1,0:T(8,128)(2,1)S(1)} %pad_maximum_fusion.2, bf16[768,2048]{1,0:T(8,128)(2,1)S(1)} %bitcast.499, s32[]{:T(128)S(6)} %select_n.600), kind=kOutput, calls=%fused_computation.1 | convolution fusion | flops 3227516928 | bytes 13107204 | tf_op jit(solution)/shard_map/dot_general | solution.py:231
  316.8 6.6 %fusion.45 = bf16[768,1024]{1,0:T(8,128)(2,1)S(1)} fusion(bf16[768,2048]{1,0:T(8,128)(2,1)} %bitcast.496, bf16[2048,1536]{1,0:T(8,128)(2,1)} %all-gather.8.cloned.1.call-done), kind=kOutput, calls=%fused_computation.92 | convolution fusion | flops 3222011904 | bytes 8912896 | tf_op jit(solution)/shard_map/dot_general | solution.py:592
  327.2 2.9 fusion.55
  334.9 5.6 fusion.9
  347.1 5.6 pad_maximum_fusion
  352.8 8.9 %collective-permute-done.40 = bf16[2,96,2048]{2,1,0:T(8,128)(2,1)S(1)} collective-permute-done((bf16[2,96,2048]{2,1,0:T(8,128)(2,1)}, bf16[2,96,2048]{2,1,0:T(8,128)(2,1)S(1)}, u32[]{:S(2)}, u32[]{:S(2)}) %collective-permute-start.40) | collective-permute-done | bytes 786464 | tf_op jit(solution)/shard_map/ppermute | solution.py:49
  368.5 7.2 %collective-permute-done.39 = bf16[96,2048]{1,0:T(8,128)(2,1)S(1)} collective-permute-done((bf16[96,2048]{1,0:T(8,128)(2,1)S(1)}, bf16[96,2048]{1,0:T(8,128)(2,1)S(1)}, u32[]{:S(2)}, u32[]{:S(2)}) %collective-permute-start.39) | collective-permute-done | bytes 393248 | tf_op jit(solution)/shard_map/ppermute | solution.py:49
  381.1 5.7 fusion.167
  386.8 3.5 add_convert_fusion.1
  390.2 6.1 collective-permute-done.43.refs_2_
  402.9 3.2 collective-permute-done.45.refs_4_
  411.7 6.6 %multiply_convert_fusion.1 = (bf16[768,640]{1,0:T(8,128)(2,1)S(1)}, bf16[768,640]{1,0:T(8,128)(2,1)S(1)}) fusion(f32[768,640]{1,0:T(8,128)S(1)} %copy-done.125, bf16[4,2,96,640]{3,2,1,0:T(8,128)(2,1)S(1)} %copy-done.85, bf16[768,2048]{1,0:T(8,128)(2,1)S(1)} %bitcast.493, bf16[2048,1920]{1,0:T(8,128)(2,1)} %all-gather.4.cloned.1.call-done), kind=kOutput, calls=%fused_computation.81 | convolution fusion | flops 2025553920 | bytes 10682368 | tf_op jit(solution)/shard_map/dot_general | solution.py:592
  418.4 7.3 %shard_map.315 = (f32[4,192,640]{2,1,0:T(8,128)S(1)}, f32[4,192,640]{2,1,0:T(8,128)S(1)}, f32[4,8,640]{2,1,0:T(8,128)S(1)}) custom-call(s32[2]{0:T(128)S(1)} %and_select_fusion.order, bf16[4,2,96,640]{3,2,1,0:T(8,128)(2,1)S(1)} %bitcast.508, f32[4,192,8]{2,1,0:T(8,128)S(1)} %copy-done.3, f32[8,640]{1,0:T(8,128)S(1)} %copy-done.37, ...), custom_call_target="tpu_custom_call" | custom-call | flops 19660800 | bytes 7008264 | tf_op jit(solution)/shard_map/pallas_call | solution.py:573
  434.4 6.5 fusion.27
  441.0 11.0 %shard_map.316 = (f32[4,2,96,640]{3,2,1,0:T(8,128)}, f32[4,8,640]{2,1,0:T(8,128)}, bf16[4,192,640]{2,1,0:T(8,128)(2,1)S(1)}, bf16[4,192,640]{2,1,0:T(8,128)(2,1)S(1)}, f32[8,640]{1,0:T(8,128)S(1)}) custom-call(s32[2]{0:T(128)S(1)} %and_select_fusion.order, bf16[4,2,96,640]{3,2,1,0:T(8,128)(2,1)S(1)} %bitcast.510, f32[4,8,640]{2,1,0:T(8,128)S(1)} %copy-done.39, ...), custom_call_target="tpu_custom_call" | custom-call | flops 2516582400 | bytes 20566024 | tf_op jit(solution)/shard_map/pallas_call | solution.py:573
  456.4 2.5 convert_add_fusion.9
  460.3 6.5 %collective-permute-done.47 = bf16[96,2048]{1,0:T(8,128)(2,1)S(1)} collective-permute-done((bf16[96,2048]{1,0:T(8,128)(2,1)S(1)}, bf16[96,2048]{1,0:T(8,128)(2,1)S(1)}, u32[]{:S(2)}, u32[]{:S(2)}) %collective-permute-start.47) | collective-permute-done | bytes 393248 | tf_op jit(solution)/shard_map/ppermute | solution.py:49
  471.7 4.8 add_convert_fusion
  476.7 2.9 copy-done.6
  479.6 3.9 convolution_convert_fusion
  483.5 2.5 convolution_convert_fusion.5
  495.9 3.0 collective-permute-start.64
  498.9 4.1 collective-permute-start.68
  503.0 3.5 add_convert_fusion.4
  506.6 4.0 add_convert_fusion.2
  515.6 2.4 convert_add_fusion.7
  519.3 9.2 %collective-permute-done.58 = bf16[96,2048]{1,0:T(8,128)(2,1)S(1)} collective-permute-done((bf16[96,2048]{1,0:T(8,128)(2,1)S(1)}, bf16[96,2048]{1,0:T(8,128)(2,1)S(1)}, u32[]{:S(2)}, u32[]{:S(2)}) %collective-permute-start.58) | collective-permute-done | bytes 393248 | tf_op jit(solution)/shard_map/ppermute | solution.py:49
  530.5 2.8 dynamic-slice_bitcast_fusion.2
  537.2 12.7 %collective-permute-done.65 = bf16[64,4608]{1,0:T(8,128)(2,1)} collective-permute-done((bf16[64,4608]{1,0:T(8,128)(2,1)}, bf16[64,4608]{1,0:T(8,128)(2,1)}, u32[]{:S(2)}, u32[]{:S(2)}) %collective-permute-start.65) | collective-permute-done | bytes 589856 | tf_op jit(solution)/shard_map/ppermute | solution.py:60
  549.9 6.2 collective-permute-start.69
  556.1 4.5 collective-permute-done.66
  563.9 13.0 %collective-permute-done.69 = bf16[2,2,176,160]{2,3,1,0:T(8,128)(2,1)S(1)} collective-permute-done((bf16[2,2,176,160]{2,3,1,0:T(8,128)(2,1)S(1)}, bf16[2,2,176,160]{2,3,1,0:T(8,128)(2,1)S(1)}, u32[]{:S(2)}, u32[]{:S(2)}) %collective-permute-start.69) | collective-permute-done | bytes 225312 | tf_op jit(solution)/shard_map/ppermute | solution.py:49
  586.5 3.2 collective-permute-done.70
  590.7 5.7 collective-permute-done.71
  603.6 15.9 %reduce-scatter.5.cloned.1.call-done = bf16[256,1920]{1,0:T(8,128)(2,1)} async-done(((bf16[1024,1920]{1,0:T(8,128)(2,1)}), bf16[256,1920]{1,0:T(8,128)(2,1)}) %reduce-scatter.5.cloned.1.call-update) | async-done | bytes 983056 | tf_op jit(solution)/shard_map/reduce_scatter | solution.py:246
  628.4 5.5 collective-permute-done.62
  (603 shorter events, 228.7 us)
Async XLA Ops:
  7.2 129.9 %all-gather.4.cloned.1.call-start = ((), (), s32[]{:S(2)}) async-start(), calls=%async_computation.2 | async-start | bytes 8847360 | tf_op jit(solution)/shard_map/all_gather | solution.py:205
  9.4 10.8 %collective-permute-start.2 = (bf16[64,1920]{1,0:T(8,128)(2,1)S(1)}, bf16[64,1920]{1,0:T(8,128)(2,1)S(1)}, u32[]{:S(2)}, u32[]{:S(2)}) collective-permute-start(bf16[64,1920]{1,0:T(8,128)(2,1)S(1)} %pad_maximum_fusion.34), channel_id=1, source_target_pairs={{0,17},{1,16},{2,19},{3,18},{4,21},{5,20},{6,23},{7,22},{8,25},{9,... | collective-permute-start | bytes 737288 | tf_op jit(solution)/shard_map/ppermute | solution.py:60
  13.4 11.2 %collective-permute-start.1 = (bf16[64,1920]{1,0:T(8,128)(2,1)S(1)}, bf16[64,1920]{1,0:T(8,128)(2,1)S(1)}, u32[]{:S(2)}, u32[]{:S(2)}) collective-permute-start(bf16[64,1920]{1,0:T(8,128)(2,1)S(1)} %pad_maximum_fusion.33), channel_id=1, source_target_pairs={{0,16},{1,17},{2,18},{3,19},{4,20},{5,21},{6,22},{7,23},{8,24},{9,... | collective-permute-start | bytes 737288 | tf_op jit(solution)/shard_map/ppermute | solution.py:60
  14.0 10.9 %collective-permute-start = (bf16[64,1920]{1,0:T(8,128)(2,1)S(1)}, bf16[64,1920]{1,0:T(8,128)(2,1)S(1)}, u32[]{:S(2)}, u32[]{:S(2)}) collective-permute-start(bf16[64,1920]{1,0:T(8,128)(2,1)S(1)} %pad_maximum_fusion.32), channel_id=1, source_target_pairs={{0,1},{1,0},{2,3},{3,2},{4,5},{5,4},{6,7},{7,6},{8,9},{9,8},{10,11... | collective-permute-start | bytes 737288 | tf_op jit(solution)/shard_map/ppermute | solution.py:60
  26.3 237.0 %all-gather.6.cloned.1.call-start = ((), (), s32[]{:S(2)}) async-start(), calls=%async_computation.3 | async-start | bytes 14155776 | tf_op jit(solution)/shard_map/all_gather | solution.py:205
  26.4 11.7 %collective-permute-start.3 = (s32[2,768]{1,0:T(2,128)S(1)}, s32[2,768]{1,0:T(2,128)S(1)}, u32[]{:S(2)}, u32[]{:S(2)}) collective-permute-start(s32[2,768]{1,0:T(2,128)S(1)} %copy-done.110), channel_id=1, source_target_pairs={{0,16},{8,24},{16,0},{24,8},{1,17},{9,25},{17,1},{25,9},{2,18},{10... | collective-permute-start | bytes 18440 | tf_op jit(solution)/shard_map/ppermute | solution.py:49
  32.6 13.7 %collective-permute-start.5 = (bf16[416,160]{1,0:T(8,128)(2,1)}, bf16[416,160]{1,0:T(8,128)(2,1)S(1)}, u32[]{:S(2)}, u32[]{:S(2)}) collective-permute-start(bf16[416,160]{1,0:T(8,128)(2,1)} %fusion.203), channel_id=1, source_target_pairs={{0,2},{1,3},{2,4},{3,5},{4,6},{5,7},{6,0},{7,1},{8,10},{9,11},{10,... | collective-permute-start | bytes 399368 | tf_op jit(solution)/shard_map/ppermute | solution.py:49
  34.1 26.6 %collective-permute-start.6 = (bf16[416,160]{1,0:T(8,128)(2,1)}, bf16[416,160]{1,0:T(8,128)(2,1)}, u32[]{:S(2)}, u32[]{:S(2)}) collective-permute-start(bf16[416,160]{1,0:T(8,128)(2,1)} %fusion.203), channel_id=1, source_target_pairs={{0,4},{1,5},{2,6},{3,7},{4,0},{5,1},{6,2},{7,3},{8,12},{9,13},{10,... | collective-permute-start | bytes 399368 | tf_op jit(solution)/shard_map/ppermute | solution.py:49
  36.7 25.3 %collective-permute-start.7 = (bf16[416,160]{1,0:T(8,128)(2,1)}, bf16[416,160]{1,0:T(8,128)(2,1)}, u32[]{:S(2)}, u32[]{:S(2)}) collective-permute-start(bf16[416,160]{1,0:T(8,128)(2,1)} %fusion.203), channel_id=1, source_target_pairs={{0,6},{1,7},{2,0},{3,1},{4,2},{5,3},{6,4},{7,5},{8,14},{9,15},{10,... | collective-permute-start | bytes 399368 | tf_op jit(solution)/shard_map/ppermute | solution.py:49
  40.3 26.5 %collective-permute-start.8 = (bf16[2,96,2048]{2,1,0:T(8,128)(2,1)}, bf16[2,96,2048]{2,1,0:T(8,128)(2,1)S(1)}, u32[]{:S(2)}, u32[]{:S(2)}) collective-permute-start(bf16[2,96,2048]{2,1,0:T(8,128)(2,1)} %shard_map.305.refs_0_), channel_id=1, source_target_pairs={{0,16},{8,24},{16,0},{24,8},{1,17},{9,25},{17,1},{25,9},{2,18},{10... | collective-permute-start | bytes 2359304 | tf_op jit(solution)/shard_map/ppermute | solution.py:49
  40.9 25.9 %collective-permute-start.4 = (bf16[2,96,2048]{2,1,0:T(8,128)(2,1)}, bf16[2,96,2048]{2,1,0:T(8,128)(2,1)S(1)}, u32[]{:S(2)}, u32[]{:S(2)}) collective-permute-start(bf16[2,96,2048]{2,1,0:T(8,128)(2,1)} %shard_map.305.refs_0_), channel_id=1, source_target_pairs={{0,1},{1,0},{2,3},{3,2},{4,5},{5,4},{6,7},{7,6},{8,9},{9,8},{10,11... | collective-permute-start | bytes 2359304 | tf_op jit(solution)/shard_map/ppermute | solution.py:49
  46.2 28.0 %collective-permute-start.29 = (bf16[64,4608]{1,0:T(8,128)(2,1)}, bf16[64,4608]{1,0:T(8,128)(2,1)}, u32[]{:S(2)}, u32[]{:S(2)}) collective-permute-start(bf16[64,4608]{1,0:T(8,128)(2,1)} %pad_maximum_fusion.21), channel_id=1, source_target_pairs={{0,1},{1,0},{2,3},{3,2},{4,5},{5,4},{6,7},{7,6},{8,9},{9,8},{10,11... | collective-permute-start | bytes 1769480 | tf_op jit(solution)/shard_map/ppermute | solution.py:60
  60.7 27.9 %collective-permute-start.30 = (bf16[64,4608]{1,0:T(8,128)(2,1)}, bf16[64,4608]{1,0:T(8,128)(2,1)}, u32[]{:S(2)}, u32[]{:S(2)}) collective-permute-start(bf16[64,4608]{1,0:T(8,128)(2,1)} %pad_maximum_fusion.22), channel_id=1, source_target_pairs={{0,16},{1,17},{2,18},{3,19},{4,20},{5,21},{6,22},{7,23},{8,24},{9,... | collective-permute-start | bytes 1769480 | tf_op jit(solution)/shard_map/ppermute | solution.py:60
  62.1 26.6 %collective-permute-start.31 = (bf16[64,4608]{1,0:T(8,128)(2,1)}, bf16[64,4608]{1,0:T(8,128)(2,1)}, u32[]{:S(2)}, u32[]{:S(2)}) collective-permute-start(bf16[64,4608]{1,0:T(8,128)(2,1)} %pad_maximum_fusion.23), channel_id=1, source_target_pairs={{0,17},{1,16},{2,19},{3,18},{4,21},{5,20},{6,23},{7,22},{8,25},{9,... | collective-permute-start | bytes 1769480 | tf_op jit(solution)/shard_map/ppermute | solution.py:60
  94.7 222.1 %all-gather.8.cloned.1.call-start = ((), (), s32[]{:S(2)}) async-start(), calls=%async_computation.4 | async-start | bytes 7077888 | tf_op jit(solution)/shard_map/all_gather | solution.py:205
  96.3 10.8 %collective-permute-start.11 = (bf16[2,416,160]{2,1,0:T(8,128)(2,1)S(1)}, bf16[2,416,160]{2,1,0:T(8,128)(2,1)}, u32[]{:S(2)}, u32[]{:S(2)}) collective-permute-start(bf16[2,416,160]{2,1,0:T(8,128)(2,1)S(1)} %pad_maximum_fusion.28), channel_id=1, source_target_pairs={{0,1},{1,0},{2,3},{3,2},{4,5},{5,4},{6,7},{7,6},{8,9},{9,8},{10,11... | collective-permute-start | bytes 798728 | tf_op jit(solution)/shard_map/ppermute | solution.py:49
  97.2 29.1 %collective-permute-start.14 = (bf16[2,8,2048]{2,1,0:T(8,128)(2,1)}, bf16[2,8,2048]{2,1,0:T(8,128)(2,1)}, u32[]{:S(2)}, u32[]{:S(2)}) collective-permute-start(bf16[2,8,2048]{2,1,0:T(8,128)(2,1)} %slice.559), channel_id=1, source_target_pairs={{1,3},{3,5},{5,7},{9,11},{11,13},{13,15},{17,19},{19,21},{21,23},{... | collective-permute-start | bytes 196616 | tf_op jit(solution)/shard_map/ppermute | solution.py:70
  98.5 27.8 %collective-permute-start.13 = (bf16[2,8,2048]{2,1,0:T(8,128)(2,1)}, bf16[2,8,2048]{2,1,0:T(8,128)(2,1)}, u32[]{:S(2)}, u32[]{:S(2)}) collective-permute-start(bf16[2,8,2048]{2,1,0:T(8,128)(2,1)} %slice.559), channel_id=1, source_target_pairs={{1,2},{3,4},{5,6},{9,10},{11,12},{13,14},{17,18},{19,20},{21,22},{... | collective-permute-start | bytes 196616 | tf_op jit(solution)/shard_map/ppermute | solution.py:70
  112.4 17.0 %collective-permute-start.10 = (bf16[96,2048]{1,0:T(8,128)(2,1)}, bf16[96,2048]{1,0:T(8,128)(2,1)S(1)}, u32[]{:S(2)}, u32[]{:S(2)}) collective-permute-start(bf16[96,2048]{1,0:T(8,128)(2,1)} %slice_bitcast_fusion.30), channel_id=1, source_target_pairs={{0,1},{1,0},{2,3},{3,2},{4,5},{5,4},{6,7},{7,6},{8,9},{9,8},{10,11... | collective-permute-start | bytes 1179656 | tf_op jit(solution)/shard_map/ppermute | solution.py:49
  120.1 12.2 %collective-permute-start.9 = (bf16[96,2048]{1,0:T(8,128)(2,1)}, bf16[96,2048]{1,0:T(8,128)(2,1)S(1)}, u32[]{:S(2)}, u32[]{:S(2)}) collective-permute-start(bf16[96,2048]{1,0:T(8,128)(2,1)} %slice_bitcast_fusion.31), channel_id=1, source_target_pairs={{0,16},{8,24},{16,0},{24,8},{1,17},{9,25},{17,1},{25,9},{2,18},{10... | collective-permute-start | bytes 1179656 | tf_op jit(solution)/shard_map/ppermute | solution.py:49
  156.5 15.3 %collective-permute-start.16 = (f32[4,2,640]{2,1,0:T(2,128)S(1)}, f32[4,2,640]{2,1,0:T(2,128)S(1)}, u32[]{:S(2)}, u32[]{:S(2)}) collective-permute-start(f32[4,2,640]{2,1,0:T(2,128)S(1)} %slice.435), channel_id=1, source_target_pairs={{0,2},{1,3},{2,4},{3,5},{4,6},{5,7},{8,10},{9,11},{10,12},{11,13},... | collective-permute-start | bytes 61448 | tf_op jit(solution)/shard_map/ppermute | solution.py:49
  158.9 12.9 %collective-permute-start.17 = (f32[4,2,640]{2,1,0:T(2,128)S(1)}, f32[4,2,640]{2,1,0:T(2,128)S(1)}, u32[]{:S(2)}, u32[]{:S(2)}) collective-permute-start(f32[4,2,640]{2,1,0:T(2,128)S(1)} %slice.435), channel_id=1, source_target_pairs={{0,4},{1,5},{2,6},{3,7},{8,12},{9,13},{10,14},{11,15},{16,20},{17,... | collective-permute-start | bytes 61448 | tf_op jit(solution)/shard_map/ppermute | solution.py:49
  169.6 18.5 %collective-permute-start.20 = (bf16[2,96,2048]{2,1,0:T(8,128)(2,1)}, bf16[2,96,2048]{2,1,0:T(8,128)(2,1)S(1)}, u32[]{:S(2)}, u32[]{:S(2)}) collective-permute-start(bf16[2,96,2048]{2,1,0:T(8,128)(2,1)} %shard_map.310.refs_0_), channel_id=1, source_target_pairs={{0,16},{8,24},{16,0},{24,8},{1,17},{9,25},{17,1},{25,9},{2,18},{10... | collective-permute-start | bytes 2359304 | tf_op jit(solution)/shard_map/ppermute | solution.py:49
  169.6 19.1 %collective-permute-start.19 = (bf16[2,96,2048]{2,1,0:T(8,128)(2,1)}, bf16[2,96,2048]{2,1,0:T(8,128)(2,1)}, u32[]{:S(2)}, u32[]{:S(2)}) collective-permute-start(bf16[2,96,2048]{2,1,0:T(8,128)(2,1)} %shard_map.310.refs_0_), channel_id=1, source_target_pairs={{0,1},{1,0},{2,3},{3,2},{4,5},{5,4},{6,7},{7,6},{8,9},{9,8},{10,11... | collective-permute-start | bytes 2359304 | tf_op jit(solution)/shard_map/ppermute | solution.py:49
  194.5 17.8 %collective-permute-start.21 = (bf16[2,96,2048]{2,1,0:T(8,128)(2,1)}, bf16[2,96,2048]{2,1,0:T(8,128)(2,1)S(1)}, u32[]{:S(2)}, u32[]{:S(2)}) collective-permute-start(bf16[2,96,2048]{2,1,0:T(8,128)(2,1)} %slice_bitcast_fusion.22), channel_id=1, source_target_pairs={{0,16},{8,24},{16,0},{24,8},{1,17},{9,25},{17,1},{25,9},{2,18},{10... | collective-permute-start | bytes 2359304 | tf_op jit(solution)/shard_map/ppermute | solution.py:49
  196.7 17.0 %collective-permute-start.23 = (bf16[2,96,2048]{2,1,0:T(8,128)(2,1)}, bf16[2,96,2048]{2,1,0:T(8,128)(2,1)S(1)}, u32[]{:S(2)}, u32[]{:S(2)}) collective-permute-start(bf16[2,96,2048]{2,1,0:T(8,128)(2,1)} %slice_bitcast_fusion.19), channel_id=1, source_target_pairs={{0,1},{1,0},{2,3},{3,2},{4,5},{5,4},{6,7},{7,6},{8,9},{9,8},{10,11... | collective-permute-start | bytes 2359304 | tf_op jit(solution)/shard_map/ppermute | solution.py:49
  200.3 330.2 %reduce-scatter.3.cloned.1.call-start = ((), (), s32[]{:S(2)}) async-start(), calls=%async_computation.5 | async-start | bytes 11796480 | tf_op jit(solution)/shard_map/reduce_scatter | solution.py:246
  225.4 20.5 %collective-permute-start.25 = (bf16[2,96,2048]{2,1,0:T(8,128)(2,1)S(1)}, bf16[2,96,2048]{2,1,0:T(8,128)(2,1)S(1)}, u32[]{:S(2)}, u32[]{:S(2)}) collective-permute-start(bf16[2,96,2048]{2,1,0:T(8,128)(2,1)S(1)} %multiply_convert_fusion.3.refs_0_), channel_id=1, source_target_pairs={{0,1},{1,0},{2,3},{3,2},{4,5},{5,4},{6,7},{7,6},{8,9},{9,8},{10,11... | collective-permute-start | bytes 2359304 | tf_op jit(solution)/shard_map/ppermute | solution.py:49
  227.6 20.7 %collective-permute-start.26 = (bf16[2,96,2048]{2,1,0:T(8,128)(2,1)S(1)}, bf16[2,96,2048]{2,1,0:T(8,128)(2,1)S(1)}, u32[]{:S(2)}, u32[]{:S(2)}) collective-permute-start(bf16[2,96,2048]{2,1,0:T(8,128)(2,1)S(1)} %multiply_convert_fusion.3.refs_0_), channel_id=1, source_target_pairs={{0,16},{8,24},{16,0},{24,8},{1,17},{9,25},{17,1},{25,9},{2,18},{10... | collective-permute-start | bytes 2359304 | tf_op jit(solution)/shard_map/ppermute | solution.py:49
  230.5 22.7 %collective-permute-start.33 = (bf16[96,2048]{1,0:T(8,128)(2,1)}, bf16[96,2048]{1,0:T(8,128)(2,1)}, u32[]{:S(2)}, u32[]{:S(2)}) collective-permute-start(bf16[96,2048]{1,0:T(8,128)(2,1)} %slice_bitcast_fusion.28), channel_id=1, source_target_pairs={{0,1},{1,0},{2,3},{3,2},{4,5},{5,4},{6,7},{7,6},{8,9},{9,8},{10,11... | collective-permute-start | bytes 1179656 | tf_op jit(solution)/shard_map/ppermute | solution.py:49
  231.5 23.5 %collective-permute-start.32 = (bf16[96,2048]{1,0:T(8,128)(2,1)}, bf16[96,2048]{1,0:T(8,128)(2,1)}, u32[]{:S(2)}, u32[]{:S(2)}) collective-permute-start(bf16[96,2048]{1,0:T(8,128)(2,1)} %slice_bitcast_fusion.29), channel_id=1, source_target_pairs={{0,16},{8,24},{16,0},{24,8},{1,17},{9,25},{17,1},{25,9},{2,18},{10... | collective-permute-start | bytes 1179656 | tf_op jit(solution)/shard_map/ppermute | solution.py:49
  246.8 12.6 %collective-permute-start.27 = (bf16[96,2048]{1,0:T(8,128)(2,1)}, bf16[96,2048]{1,0:T(8,128)(2,1)S(1)}, u32[]{:S(2)}, u32[]{:S(2)}) collective-permute-start(bf16[96,2048]{1,0:T(8,128)(2,1)} %slice_bitcast_fusion.25), channel_id=1, source_target_pairs={{0,16},{8,24},{16,0},{24,8},{1,17},{9,25},{17,1},{25,9},{2,18},{10... | collective-permute-start | bytes 1179656 | tf_op jit(solution)/shard_map/ppermute | solution.py:49
  279.4 14.1 %collective-permute-start.34 = (bf16[1024,1024]{1,0:T(8,128)(2,1)}, bf16[1024,1024]{1,0:T(8,128)(2,1)}, u32[]{:S(2)}, u32[]{:S(2)}) collective-permute-start(bf16[1024,1024]{1,0:T(8,128)(2,1)} %convolution_convert_fusion.4), channel_id=1, source_target_pairs={{0,8},{8,0},{16,24},{24,16},{1,9},{9,1},{17,25},{25,17},{2,10},{10... | collective-permute-start | bytes 6291464 | tf_op jit(solution)/shard_map/ppermute | solution.py:49
  290.7 19.2 %collective-permute-start.35 = (bf16[1024,2048]{1,0:T(8,128)(2,1)}, bf16[1024,2048]{1,0:T(8,128)(2,1)}, u32[]{:S(2)}, u32[]{:S(2)}) collective-permute-start(bf16[1024,2048]{1,0:T(8,128)(2,1)} %convolution_convert_fusion.1), channel_id=1, source_target_pairs={{0,8},{8,0},{16,24},{24,16},{1,9},{9,1},{17,25},{25,17},{2,10},{10... | collective-permute-start | bytes 12582920 | tf_op jit(solution)/shard_map/ppermute | solution.py:49
  331.9 13.0 %collective-permute-start.38 = (bf16[1024,1024]{1,0:T(8,128)(2,1)S(1)}, bf16[1024,1024]{1,0:T(8,128)(2,1)S(1)}, u32[]{:S(2)}, u32[]{:S(2)}) collective-permute-start(bf16[1024,1024]{1,0:T(8,128)(2,1)S(1)} %convolution_convert_fusion.3), channel_id=1, source_target_pairs={{0,8},{8,0},{16,24},{24,16},{1,9},{9,1},{17,25},{25,17},{2,10},{10... | collective-permute-start | bytes 6291464 | tf_op jit(solution)/shard_map/ppermute | solution.py:49
  341.5 20.1 %collective-permute-start.40 = (bf16[2,96,2048]{2,1,0:T(8,128)(2,1)}, bf16[2,96,2048]{2,1,0:T(8,128)(2,1)S(1)}, u32[]{:S(2)}, u32[]{:S(2)}) collective-permute-start(bf16[2,96,2048]{2,1,0:T(8,128)(2,1)} %slice_bitcast_fusion.13), channel_id=1, source_target_pairs={{0,1},{1,0},{2,3},{3,2},{4,5},{5,4},{6,7},{7,6},{8,9},{9,8},{10,11... | collective-permute-start | bytes 2359304 | tf_op jit(solution)/shard_map/ppermute | solution.py:49
  343.1 20.0 %collective-permute-start.37 = (bf16[2,96,2048]{2,1,0:T(8,128)(2,1)}, bf16[2,96,2048]{2,1,0:T(8,128)(2,1)}, u32[]{:S(2)}, u32[]{:S(2)}) collective-permute-start(bf16[2,96,2048]{2,1,0:T(8,128)(2,1)} %slice_bitcast_fusion.16), channel_id=1, source_target_pairs={{0,16},{8,24},{16,0},{24,8},{1,17},{9,25},{17,1},{25,9},{2,18},{10... | collective-permute-start | bytes 2359304 | tf_op jit(solution)/shard_map/ppermute | solution.py:49
  352.7 266.8 %reduce-scatter.5.cloned.1.call-start = ((), (), s32[]{:S(2)}) async-start(), calls=%async_computation.6 | async-start | bytes 4915200 | tf_op jit(solution)/shard_map/reduce_scatter | solution.py:246
  365.3 10.5 %collective-permute-start.39 = (bf16[96,2048]{1,0:T(8,128)(2,1)S(1)}, bf16[96,2048]{1,0:T(8,128)(2,1)S(1)}, u32[]{:S(2)}, u32[]{:S(2)}) collective-permute-start(bf16[96,2048]{1,0:T(8,128)(2,1)S(1)} %fusion.118), channel_id=1, source_target_pairs={{0,1},{1,0},{2,3},{3,2},{4,5},{5,4},{6,7},{7,6},{8,9},{9,8},{10,11... | collective-permute-start | bytes 1179656 | tf_op jit(solution)/shard_map/ppermute | solution.py:49
  366.7 10.2 %collective-permute-start.41 = (bf16[96,2048]{1,0:T(8,128)(2,1)S(1)}, bf16[96,2048]{1,0:T(8,128)(2,1)S(1)}, u32[]{:S(2)}, u32[]{:S(2)}) collective-permute-start(bf16[96,2048]{1,0:T(8,128)(2,1)S(1)} %fusion.119), channel_id=1, source_target_pairs={{0,16},{8,24},{16,0},{24,8},{1,17},{9,25},{17,1},{25,9},{2,18},{10... | collective-permute-start | bytes 1179656 | tf_op jit(solution)/shard_map/ppermute | solution.py:49
  378.5 17.8 %collective-permute-start.43 = (bf16[2,96,2048]{2,1,0:T(8,128)(2,1)S(1)}, bf16[2,96,2048]{2,1,0:T(8,128)(2,1)S(1)}, u32[]{:S(2)}, u32[]{:S(2)}) collective-permute-start(bf16[2,96,2048]{2,1,0:T(8,128)(2,1)S(1)} %fusion.165.refs_0_), channel_id=1, source_target_pairs={{0,16},{8,24},{16,0},{24,8},{1,17},{9,25},{17,1},{25,9},{2,18},{10... | collective-permute-start | bytes 2359304 | tf_op jit(solution)/shard_map/ppermute | solution.py:49
  380.3 17.7 %collective-permute-start.42 = (bf16[2,96,2048]{2,1,0:T(8,128)(2,1)S(1)}, bf16[2,96,2048]{2,1,0:T(8,128)(2,1)S(1)}, u32[]{:S(2)}, u32[]{:S(2)}) collective-permute-start(bf16[2,96,2048]{2,1,0:T(8,128)(2,1)S(1)} %fusion.165.refs_0_), channel_id=1, source_target_pairs={{0,1},{1,0},{2,3},{3,2},{4,5},{5,4},{6,7},{7,6},{8,9},{9,8},{10,11... | collective-permute-start | bytes 2359304 | tf_op jit(solution)/shard_map/ppermute | solution.py:49
  425.7 15.2 %collective-permute-start.50 = (f32[4,2,640]{2,1,0:T(2,128)S(1)}, f32[4,2,640]{2,1,0:T(2,128)S(1)}, u32[]{:S(2)}, u32[]{:S(2)}) collective-permute-start(f32[4,2,640]{2,1,0:T(2,128)S(1)} %slice.487), channel_id=1, source_target_pairs={{2,0},{3,1},{4,2},{5,3},{6,4},{7,5},{10,8},{11,9},{12,10},{13,11},... | collective-permute-start | bytes 61448 | tf_op jit(solution)/shard_map/ppermute | solution.py:49
  427.0 13.9 %collective-permute-start.51 = (f32[4,2,640]{2,1,0:T(2,128)S(1)}, f32[4,2,640]{2,1,0:T(2,128)S(1)}, u32[]{:S(2)}, u32[]{:S(2)}) collective-permute-start(f32[4,2,640]{2,1,0:T(2,128)S(1)} %slice.487), channel_id=1, source_target_pairs={{4,0},{5,1},{6,2},{7,3},{12,8},{13,9},{14,10},{15,11},{20,16},{21,... | collective-permute-start | bytes 61448 | tf_op jit(solution)/shard_map/ppermute | solution.py:49
  428.3 12.6 %collective-permute-start.52 = (f32[4,2,640]{2,1,0:T(2,128)S(1)}, f32[4,2,640]{2,1,0:T(2,128)S(1)}, u32[]{:S(2)}, u32[]{:S(2)}) collective-permute-start(f32[4,2,640]{2,1,0:T(2,128)S(1)} %slice.487), channel_id=1, source_target_pairs={{6,0},{7,1},{14,8},{15,9},{22,16},{23,17},{30,24},{31,25}} | collective-permute-start | bytes 61448 | tf_op jit(solution)/shard_map/ppermute | solution.py:49
  430.5 25.9 %collective-permute-start.46 = (bf16[2,96,2048]{2,1,0:T(8,128)(2,1)}, bf16[2,96,2048]{2,1,0:T(8,128)(2,1)}, u32[]{:S(2)}, u32[]{:S(2)}) collective-permute-start(bf16[2,96,2048]{2,1,0:T(8,128)(2,1)} %slice_bitcast_fusion.10), channel_id=1, source_target_pairs={{0,16},{8,24},{16,0},{24,8},{1,17},{9,25},{17,1},{25,9},{2,18},{10... | collective-permute-start | bytes 2359304 | tf_op jit(solution)/shard_map/ppermute | solution.py:49
  433.2 23.3 %collective-permute-start.48 = (bf16[2,96,2048]{2,1,0:T(8,128)(2,1)}, bf16[2,96,2048]{2,1,0:T(8,128)(2,1)}, u32[]{:S(2)}, u32[]{:S(2)}) collective-permute-start(bf16[2,96,2048]{2,1,0:T(8,128)(2,1)} %slice_bitcast_fusion.7), channel_id=1, source_target_pairs={{0,1},{1,0},{2,3},{3,2},{4,5},{5,4},{6,7},{7,6},{8,9},{9,8},{10,11... | collective-permute-start | bytes 2359304 | tf_op jit(solution)/shard_map/ppermute | solution.py:49
  452.0 17.3 %collective-permute-start.53 = (f32[4,8,640]{2,1,0:T(8,128)}, f32[4,8,640]{2,1,0:T(8,128)}, u32[]{:S(2)}, u32[]{:S(2)}) collective-permute-start(f32[4,8,640]{2,1,0:T(8,128)} %get-tuple-element.132), channel_id=1, source_target_pairs={{2,0},{3,1},{4,2},{5,3},{6,4},{7,5},{10,8},{11,9},{12,10},{13,11},... | collective-permute-start | bytes 245768 | tf_op jit(solution)/shard_map/ppermute | solution.py:49
  483.4 23.1 %collective-permute-start.55 = (bf16[1024,1280]{1,0:T(8,128)(2,1)}, bf16[1024,1280]{1,0:T(8,128)(2,1)}, u32[]{:S(2)}, u32[]{:S(2)}) collective-permute-start(bf16[1024,1280]{1,0:T(8,128)(2,1)} %convolution_convert_fusion), channel_id=1, source_target_pairs={{0,8},{8,0},{16,24},{24,16},{1,9},{9,1},{17,25},{25,17},{2,10},{10... | collective-permute-start | bytes 7864328 | tf_op jit(solution)/shard_map/ppermute | solution.py:49
  486.0 13.0 %collective-permute-start.56 = (bf16[1024,640]{1,0:T(8,128)(2,1)}, bf16[1024,640]{1,0:T(8,128)(2,1)}, u32[]{:S(2)}, u32[]{:S(2)}) collective-permute-start(bf16[1024,640]{1,0:T(8,128)(2,1)} %convolution_convert_fusion.5), channel_id=1, source_target_pairs={{0,8},{8,0},{16,24},{24,16},{1,9},{9,1},{17,25},{25,17},{2,10},{10... | collective-permute-start | bytes 3932168 | tf_op jit(solution)/shard_map/ppermute | solution.py:49
  494.4 20.2 %collective-permute-start.59 = (bf16[2,96,2048]{2,1,0:T(8,128)(2,1)}, bf16[2,96,2048]{2,1,0:T(8,128)(2,1)}, u32[]{:S(2)}, u32[]{:S(2)}) collective-permute-start(bf16[2,96,2048]{2,1,0:T(8,128)(2,1)} %slice_bitcast_fusion.1), channel_id=1, source_target_pairs={{0,1},{1,0},{2,3},{3,2},{4,5},{5,4},{6,7},{7,6},{8,9},{9,8},{10,11... | collective-permute-start | bytes 2359304 | tf_op jit(solution)/shard_map/ppermute | solution.py:49
  495.6 20.0 %collective-permute-start.54 = (bf16[2,96,2048]{2,1,0:T(8,128)(2,1)}, bf16[2,96,2048]{2,1,0:T(8,128)(2,1)}, u32[]{:S(2)}, u32[]{:S(2)}) collective-permute-start(bf16[2,96,2048]{2,1,0:T(8,128)(2,1)} %slice_bitcast_fusion.4), channel_id=1, source_target_pairs={{0,16},{8,24},{16,0},{24,8},{1,17},{9,25},{17,1},{25,9},{2,18},{10... | collective-permute-start | bytes 2359304 | tf_op jit(solution)/shard_map/ppermute | solution.py:49
  495.9 68.0 %collective-permute-start.64 = (bf16[2,2,176,160]{2,3,1,0:T(8,128)(2,1)S(1)}, bf16[2,2,176,160]{2,3,1,0:T(8,128)(2,1)}, u32[]{:S(2)}, u32[]{:S(2)}) collective-permute-start(bf16[2,2,176,160]{2,3,1,0:T(8,128)(2,1)S(1)} %fusion.111), channel_id=1, source_target_pairs={{0,2},{1,3},{2,4},{3,5},{4,6},{5,7},{6,0},{7,1},{8,10},{9,11},{10,... | collective-permute-start | bytes 675848 | tf_op jit(solution)/shard_map/ppermute | solution.py:49
  498.9 65.0 %collective-permute-start.68 = (bf16[2,2,176,160]{2,3,1,0:T(8,128)(2,1)S(1)}, bf16[2,2,176,160]{2,3,1,0:T(8,128)(2,1)}, u32[]{:S(2)}, u32[]{:S(2)}) collective-permute-start(bf16[2,2,176,160]{2,3,1,0:T(8,128)(2,1)S(1)} %fusion.111), channel_id=1, source_target_pairs={{0,4},{1,5},{2,6},{3,7},{4,0},{5,1},{6,2},{7,3},{8,12},{9,13},{10,... | collective-permute-start | bytes 675848 | tf_op jit(solution)/shard_map/ppermute | solution.py:49
  518.1 10.5 %collective-permute-start.58 = (bf16[96,2048]{1,0:T(8,128)(2,1)S(1)}, bf16[96,2048]{1,0:T(8,128)(2,1)S(1)}, u32[]{:S(2)}, u32[]{:S(2)}) collective-permute-start(bf16[96,2048]{1,0:T(8,128)(2,1)S(1)} %fusion.122), channel_id=1, source_target_pairs={{0,1},{1,0},{2,3},{3,2},{4,5},{5,4},{6,7},{7,6},{8,9},{9,8},{10,11... | collective-permute-start | bytes 1179656 | tf_op jit(solution)/shard_map/ppermute | solution.py:49
  519.0 10.5 %collective-permute-start.60 = (bf16[96,2048]{1,0:T(8,128)(2,1)S(1)}, bf16[96,2048]{1,0:T(8,128)(2,1)S(1)}, u32[]{:S(2)}, u32[]{:S(2)}) collective-permute-start(bf16[96,2048]{1,0:T(8,128)(2,1)S(1)} %fusion.123), channel_id=1, source_target_pairs={{0,16},{8,24},{16,0},{24,8},{1,17},{9,25},{17,1},{25,9},{2,18},{10... | collective-permute-start | bytes 1179656 | tf_op jit(solution)/shard_map/ppermute | solution.py:49
  533.3 16.6 %collective-permute-start.65 = (bf16[64,4608]{1,0:T(8,128)(2,1)}, bf16[64,4608]{1,0:T(8,128)(2,1)}, u32[]{:S(2)}, u32[]{:S(2)}) collective-permute-start(bf16[64,4608]{1,0:T(8,128)(2,1)} %get-tuple-element.171), channel_id=1, source_target_pairs={{0,1},{1,0},{2,3},{3,2},{4,5},{5,4},{6,7},{7,6},{8,9},{9,8},{10,11... | collective-permute-start | bytes 1769480 | tf_op jit(solution)/shard_map/ppermute | solution.py:60
  534.2 26.4 %collective-permute-start.66 = (bf16[64,4608]{1,0:T(8,128)(2,1)}, bf16[64,4608]{1,0:T(8,128)(2,1)}, u32[]{:S(2)}, u32[]{:S(2)}) collective-permute-start(bf16[64,4608]{1,0:T(8,128)(2,1)} %get-tuple-element.173), channel_id=1, source_target_pairs={{0,16},{1,17},{2,18},{3,19},{4,20},{5,21},{6,22},{7,23},{8,24},{9,... | collective-permute-start | bytes 1769480 | tf_op jit(solution)/shard_map/ppermute | solution.py:60
  534.5 26.0 %collective-permute-start.67 = (bf16[64,4608]{1,0:T(8,128)(2,1)}, bf16[64,4608]{1,0:T(8,128)(2,1)}, u32[]{:S(2)}, u32[]{:S(2)}) collective-permute-start(bf16[64,4608]{1,0:T(8,128)(2,1)} %get-tuple-element.172), channel_id=1, source_target_pairs={{0,17},{1,16},{2,19},{3,18},{4,21},{5,20},{6,23},{7,22},{8,25},{9,... | collective-permute-start | bytes 1769480 | tf_op jit(solution)/shard_map/ppermute | solution.py:60
  549.9 27.1 %collective-permute-start.69 = (bf16[2,2,176,160]{2,3,1,0:T(8,128)(2,1)S(1)}, bf16[2,2,176,160]{2,3,1,0:T(8,128)(2,1)S(1)}, u32[]{:S(2)}, u32[]{:S(2)}) collective-permute-start(bf16[2,2,176,160]{2,3,1,0:T(8,128)(2,1)S(1)} %fusion.111), channel_id=1, source_target_pairs={{0,6},{1,7},{2,0},{3,1},{4,2},{5,3},{6,4},{7,5},{8,14},{9,15},{10,... | collective-permute-start | bytes 675848 | tf_op jit(solution)/shard_map/ppermute | solution.py:49
  578.9 10.8 %collective-permute-start.70 = (bf16[2,2,176,160]{2,3,1,0:T(8,128)(2,1)}, bf16[2,2,176,160]{2,3,1,0:T(8,128)(2,1)S(1)}, u32[]{:S(2)}, u32[]{:S(2)}) collective-permute-start(bf16[2,2,176,160]{2,3,1,0:T(8,128)(2,1)} %add_convert_fusion.7), channel_id=1, source_target_pairs={{0,1},{1,0},{2,3},{3,2},{4,5},{5,4},{6,7},{7,6},{8,9},{9,8},{10,11... | collective-permute-start | bytes 675848 | tf_op jit(solution)/shard_map/ppermute | solution.py:60
  584.5 11.8 %collective-permute-start.71 = (bf16[2,2,176,160]{2,3,1,0:T(8,128)(2,1)}, bf16[2,2,176,160]{2,3,1,0:T(8,128)(2,1)S(1)}, u32[]{:S(2)}, u32[]{:S(2)}) collective-permute-start(bf16[2,2,176,160]{2,3,1,0:T(8,128)(2,1)} %add_convert_fusion.7), channel_id=1, source_target_pairs={{0,16},{1,17},{2,18},{3,19},{4,20},{5,21},{6,22},{7,23},{8,24},{9,... | collective-permute-start | bytes 675848 | tf_op jit(solution)/shard_map/ppermute | solution.py:60
  586.0 10.3 %collective-permute-start.72 = (bf16[2,2,176,160]{2,3,1,0:T(8,128)(2,1)}, bf16[2,2,176,160]{2,3,1,0:T(8,128)(2,1)S(1)}, u32[]{:S(2)}, u32[]{:S(2)}) collective-permute-start(bf16[2,2,176,160]{2,3,1,0:T(8,128)(2,1)} %add_convert_fusion.7), channel_id=1, source_target_pairs={{0,17},{1,16},{2,19},{3,18},{4,21},{5,20},{6,23},{7,22},{8,25},{9,... | collective-permute-start | bytes 675848 | tf_op jit(solution)/shard_map/ppermute | solution.py:60
  622.3 11.6 %collective-permute-start.62 = (bf16[64,1920]{1,0:T(8,128)(2,1)S(1)}, bf16[64,1920]{1,0:T(8,128)(2,1)S(1)}, u32[]{:S(2)}, u32[]{:S(2)}) collective-permute-start(bf16[64,1920]{1,0:T(8,128)(2,1)S(1)} %get-tuple-element.222), channel_id=1, source_target_pairs={{0,16},{1,17},{2,18},{3,19},{4,20},{5,21},{6,22},{7,23},{8,24},{9,... | collective-permute-start | bytes 737288 | tf_op jit(solution)/shard_map/ppermute | solution.py:60
  (147 other events, 1286.0 us)
Sparse Core Ops, SparseCore 0:
  26.4 93.8 all-gather.3
  122.5 117.9 all-gather.5
  242.1 64.5 all-gather.7
  352.8 170.9 reduce-scatter.2
  537.1 82.3 reduce-scatter.4
